TPU v7x, 32 devices: a whole 2x2x4 slice. The times are simulated.
32 devices in a mesh: img: 4 (over z), txt: 8 (over y, x, core).
Axes of the slice: x: 2, y: 2, z: 4, core: 2. Of those that a mesh axis runs over, the one named last changes fastest.
Arguments:
- teacher_image: bfloat16 [4096, 1280], P(('img', 'txt')), may hold values from -24 to 24
- teacher_text: bfloat16 [4096, 1280], P(('txt', 'img')), may hold values from -24 to 24
- student_image: bfloat16 [4096, 512], P(('img', 'txt')), may hold values from -24 to 24
- student_text: bfloat16 [4096, 512], P(('txt', 'img')), may hold values from -24 to 24
Outputs:
- loss: float32 [], replicated
- image_grad: float32 [4096, 512], P(('img', 'txt'))
- text_grad: float32 [4096, 512], P(('txt', 'img'))
All inputs are finite; a program needn't handle non-finite values.
Results may differ from a plain program's by a relative error of at most 0.0012.
Values may be sent and summed in bfloat16 or wider, within the bound.
No kernel may reach another device: no remote copies, remote signals or barrier semaphores. Data moves between devices by JAX's collectives and lax.ppermute only.
A program may use at most 128 MiB of HBM per device.

v0:
```python
import math

import jax
import jax.numpy as jnp
from jax import lax
from jax.sharding import PartitionSpec as P


def pair_logits(
    image_teacher, image_student, text_teacher, text_student, scale_teacher, scale_student
):
    teacher_logit = (
        jnp.einsum("rd,cd->rc", image_teacher, text_teacher, preferred_element_type=jnp.float32)
        * scale_teacher
    )
    student_logit = (
        jnp.einsum("rd,cd->rc", image_student, text_student, preferred_element_type=jnp.float32)
        * scale_student
    )
    return (teacher_logit, student_logit)


def fold_columns(column_peak, column_total, logit):
    new_peak = jnp.maximum(column_peak, jnp.max(logit, axis=0))
    new_total = column_total * jnp.exp(column_peak - new_peak) + jnp.sum(
        jnp.exp(logit - new_peak[None, :]), axis=0
    )
    return (new_peak, new_total)


def split_delta(delta):
    delta_high = delta.astype(jnp.bfloat16)
    widened = lax.optimization_barrier(delta_high).astype(jnp.float32)
    delta_low = (delta - widened).astype(jnp.bfloat16)
    return (delta_high, delta_low)


def row_blocks(piece_rows):
    step_rows = math.gcd(piece_rows, 512)
    return [(offset, step_rows) for offset in range(0, piece_rows, step_rows)]


def local(teacher_image, teacher_text, student_image, student_text):
    scale_teacher = teacher_image.shape[1] ** (-0.5)
    scale_student = student_image.shape[1] ** (-0.5)
    text_teacher, text_student = (
        lax.all_gather(teacher_text, "img", axis=0, tiled=True),
        lax.all_gather(student_text, "img", axis=0, tiled=True),
    )
    tile_rows = teacher_image.shape[0] * lax.axis_size("txt")
    tile_cols = text_teacher.shape[0]
    row_empty = jnp.zeros((tile_rows,), jnp.float32)
    column_peak_empty = jnp.full((tile_cols,), -jnp.inf, jnp.float32)
    column_total_empty = jnp.zeros((tile_cols,), jnp.float32)
    image_teacher, image_student = (
        lax.all_gather(teacher_image, "txt", axis=0, tiled=True),
        lax.all_gather(student_image, "txt", axis=0, tiled=True),
    )
    pieces = (image_teacher, image_student)
    teacher_row_peak = row_empty
    teacher_row_total = row_empty
    student_row_peak = row_empty
    student_row_total = row_empty
    teacher_column_peak = column_peak_empty
    teacher_column_total = column_total_empty
    student_column_peak = column_peak_empty
    student_column_total = column_total_empty
    for offset, count in row_blocks(pieces[0].shape[0]):
        teacher_logit, student_logit = pair_logits(
            pieces[0][offset : offset + count],
            pieces[1][offset : offset + count],
            text_teacher,
            text_student,
            scale_teacher,
            scale_student,
        )
        row_start = 0 + offset
        top_teacher = jnp.max(teacher_logit, axis=1)
        top_student = jnp.max(student_logit, axis=1)
        teacher_row_peak = lax.dynamic_update_slice_in_dim(
            teacher_row_peak, top_teacher, row_start, 0
        )
        student_row_peak = lax.dynamic_update_slice_in_dim(
            student_row_peak, top_student, row_start, 0
        )
        teacher_row_total = lax.dynamic_update_slice_in_dim(
            teacher_row_total,
            jnp.sum(jnp.exp(teacher_logit - top_teacher[:, None]), axis=1),
            row_start,
            0,
        )
        student_row_total = lax.dynamic_update_slice_in_dim(
            student_row_total,
            jnp.sum(jnp.exp(student_logit - top_student[:, None]), axis=1),
            row_start,
            0,
        )
        teacher_column_peak, teacher_column_total = fold_columns(
            teacher_column_peak, teacher_column_total, teacher_logit
        )
        student_column_peak, student_column_total = fold_columns(
            student_column_peak, student_column_total, student_logit
        )
    local_stats = (
        teacher_row_peak,
        teacher_row_total,
        student_row_peak,
        student_row_total,
        teacher_column_peak,
        teacher_column_total,
        student_column_peak,
        student_column_total,
    )
    (
        teacher_row_peak,
        teacher_row_total,
        student_row_peak,
        student_row_total,
        teacher_column_peak,
        teacher_column_total,
        student_column_peak,
        student_column_total,
    ) = local_stats
    row_top_teacher, row_top_student = lax.pmax((teacher_row_peak, student_row_peak), "txt")
    row_sum_teacher, row_sum_student = lax.psum(
        (
            teacher_row_total * jnp.exp(teacher_row_peak - row_top_teacher),
            student_row_total * jnp.exp(student_row_peak - row_top_student),
        ),
        "txt",
    )
    column_top_teacher, column_top_student = lax.pmax(
        (teacher_column_peak, student_column_peak), "img"
    )
    column_sum_teacher, column_sum_student = lax.psum(
        (
            teacher_column_total * jnp.exp(teacher_column_peak - column_top_teacher),
            student_column_total * jnp.exp(student_column_peak - column_top_student),
        ),
        "img",
    )
    teacher_row_lse = row_top_teacher + jnp.log(row_sum_teacher)
    student_row_lse = row_top_student + jnp.log(row_sum_student)
    teacher_column_lse = column_top_teacher + jnp.log(column_sum_teacher)
    student_column_lse = column_top_student + jnp.log(column_sum_student)
    pieces = (image_teacher, image_student)
    image_total = jnp.zeros((tile_rows, student_image.shape[1]), jnp.float32)
    text_total = jnp.zeros((tile_cols, student_image.shape[1]), jnp.float32)
    divergence = jnp.zeros((), jnp.float32)
    for offset, count in row_blocks(pieces[0].shape[0]):
        block_student = pieces[1][offset : offset + count]
        teacher_logit, student_logit = pair_logits(
            pieces[0][offset : offset + count],
            block_student,
            text_teacher,
            text_student,
            scale_teacher,
            scale_student,
        )
        row_start = 0 + offset
        lse_teacher = lax.dynamic_slice_in_dim(teacher_row_lse, row_start, count)
        lse_student = lax.dynamic_slice_in_dim(student_row_lse, row_start, count)
        teacher_row_prob = jnp.exp(teacher_logit - lse_teacher[:, None])
        student_row_prob = jnp.exp(student_logit - lse_student[:, None])
        teacher_column_prob = jnp.exp(teacher_logit - teacher_column_lse[None, :])
        student_column_prob = jnp.exp(student_logit - student_column_lse[None, :])
        difference = teacher_logit - student_logit
        divergence = (
            divergence
            + jnp.sum(teacher_row_prob * difference)
            + jnp.sum(teacher_column_prob * difference)
        )
        delta = student_row_prob - teacher_row_prob + (student_column_prob - teacher_column_prob)
        delta_high, delta_low = split_delta(delta)
        image_part = jnp.dot(
            delta_high, text_student, preferred_element_type=jnp.float32
        ) + jnp.dot(delta_low, text_student, preferred_element_type=jnp.float32)
        image_total = lax.dynamic_update_slice_in_dim(image_total, image_part, row_start, 0)
        text_total = (
            text_total
            + jnp.einsum("rc,rd->cd", delta_high, block_student, preferred_element_type=jnp.float32)
            + jnp.einsum("rc,rd->cd", delta_low, block_student, preferred_element_type=jnp.float32)
        )
    image_total, text_total, divergence = (image_total, text_total, divergence)
    row_share = teacher_image.shape[0]
    column_share = teacher_text.shape[0]
    row_gap = jnp.sum(
        lax.dynamic_slice_in_dim(
            student_row_lse - teacher_row_lse, lax.axis_index("txt") * row_share, row_share
        )
    )
    column_gap = jnp.sum(
        lax.dynamic_slice_in_dim(
            student_column_lse - teacher_column_lse,
            lax.axis_index("img") * column_share,
            column_share,
        )
    )
    total = lax.psum(divergence + row_gap + column_gap, ("img", "txt"))
    pair_count = tile_rows * lax.axis_size("img")
    loss = total / (2.0 * pair_count)
    image_grad = (
        lax.psum_scatter(image_total, "txt", scatter_dimension=0, tiled=True) * scale_student
    )
    text_grad = lax.psum_scatter(text_total, "img", scatter_dimension=0, tiled=True) * scale_student
    return (loss, image_grad, text_grad)


def solution(mesh):
    in_specs = (
        P(("img", "txt"), None),
        P(("txt", "img"), None),
        P(("img", "txt"), None),
        P(("txt", "img"), None),
    )
    out_specs = (P(), P(("img", "txt"), None), P(("txt", "img"), None))
    return jax.shard_map(local, mesh=mesh, in_specs=in_specs, out_specs=out_specs, check_vma=False)
```

profile of v0, /device:TPU:0, one launch (start us, length us, event | category | flops | bytes accessed | tf_op | source)
XLA Modules:
  0.0 250.6 jit_solution(8795059823378958672)
XLA Ops:
  7.2 0.7 all-gather.8.cloned.1.call-update
  7.9 0.7 all-gather.6.cloned.1.call-update
  8.7 0.7 all-gather.4.cloned.1.call-update
  9.4 17.6 %all_gather.15 = bf16[512,512]{1,0:T(8,128)(2,1)S(1)} all-gather(bf16[128,512]{1,0:T(8,128)(2,1)} %param.7), channel_id=1, replica_groups=mesh['img'=4,'txt'=8] {'img'}, dimensions={0}, use_global_device_ids=true | all-gather | bytes 655360 | tf_op jit(solution)/shard_map/all_gather | solution.py:48
  27.0 9.1 %all-gather.8.cloned.1.call-done = bf16[1024,512]{1,0:T(8,128)(2,1)} async-done(((bf16[128,512]{1,0:T(8,128)(2,1)}), bf16[1024,512]{1,0:T(8,128)(2,1)}) %all-gather.8.cloned.1.call-update) | async-done | bytes 1048592 | tf_op jit(solution)/shard_map/all_gather | solution.py:57
  36.1 1.7 fusion.20
  37.8 0.6 fusion.19
  38.4 0.5 fusion.9
  38.9 31.5 %all-gather.6.cloned.1.call-done = bf16[512,1280]{1,0:T(8,128)(2,1)} async-done(((bf16[128,1280]{1,0:T(8,128)(2,1)}), bf16[512,1280]{1,0:T(8,128)(2,1)}) %all-gather.6.cloned.1.call-update) | async-done | bytes 1310736 | tf_op jit(solution)/shard_map/all_gather | solution.py:47
  70.4 31.0 %all-gather.4.cloned.1.call-done = bf16[1024,1280]{1,0:T(8,128)(2,1)} async-done(((bf16[128,1280]{1,0:T(8,128)(2,1)}), bf16[1024,1280]{1,0:T(8,128)(2,1)}) %all-gather.4.cloned.1.call-update) | async-done | bytes 2621456 | tf_op jit(solution)/shard_map/all_gather | solution.py:56
  101.4 3.7 %fusion.11 = (f32[512]{0:T(512)S(1)}, f32[512]{0:T(512)S(1)}, f32[512,512]{1,0:T(8,128)}) fusion(bf16[512,1280]{1,0:T(8,128)(2,1)} %all-gather.6.cloned.1.call-done, bf16[1024,1280]{1,0:T(8,128)(2,1)} %all-gather.4.cloned.1.call-done), kind=kOutput, calls=%fused_computation.55 | convolution fusion | flops 671874048 | bytes 3674112 | tf_op jit(solution)/shard_map/rd,cd->rc/dot_general | solution.py:13
  105.2 1.9 fusion.12
  107.1 11.7 %all-reduce.2 = (f32[512]{0:T(512)S(1)}, f32[512]{0:T(512)S(1)}) all-reduce(f32[512]{0:T(512)S(1)} %max.22, f32[512]{0:T(512)S(1)} %max.23), channel_id=1, replica_groups=mesh['img'=4,'txt'=8] {'img'}, use_global_device_ids=true, to_apply=%region_9.0 | all-reduce | flops 1024 | bytes 8192 | tf_op jit(solution)/shard_map/pmax | solution.py:132
  118.7 2.5 exponential_reduce_fusion.4
  121.2 8.4 %psum.36 = f32[512]{0:T(512)S(1)} all-reduce(f32[512]{0:T(512)S(1)} %exponential_multiply_fusion.1), channel_id=1, replica_groups=mesh['img'=4,'txt'=8] {'img'}, use_global_device_ids=true, to_apply=%region_12.0 | all-reduce | flops 512 | bytes 4096 | tf_op jit(solution)/shard_map/psum | solution.py:135
  129.6 12.1 %all-reduce.1 = (f32[1024]{0:T(1024)S(1)}, f32[1024]{0:T(1024)S(1)}) all-reduce(f32[1024]{0:T(1024)S(1)} %pad_maximum_fusion.1, f32[1024]{0:T(1024)S(1)} %pad_maximum_fusion.2), channel_id=1, replica_groups=mesh['img'=4,'txt'=8] {'txt'}, use_global_device_ids=true, to_apply=%region_2.0 | all-reduce | flops 2048 | bytes 16384 | tf_op jit(solution)/shard_map/pmax | solution.py:124
  141.8 12.0 %all-reduce = (f32[1024]{0:T(1024)S(1)}, f32[1024]{0:T(1024)S(1)}) all-reduce(f32[1024]{0:T(1024)S(1)} %maximum_multiply_fusion, f32[1024]{0:T(1024)S(1)} %maximum_multiply_fusion.1), channel_id=1, replica_groups=mesh['img'=4,'txt'=8] {'txt'}, use_global_device_ids=true, to_apply=%region_5.0 | all-reduce | flops 2048 | bytes 16384 | tf_op jit(solution)/shard_map/psum | solution.py:125
  153.9 3.4 %multiply_reduce_fusion = (f32[]{:T(128)}, f32[]{:T(128)}, f32[512]{0:T(512)S(1)}, f32[512]{0:T(512)S(1)}, f32[]{:T(128)}, /*index=5*/f32[]{:T(128)}) fusion(f32[512,512]{1,0:T(8,128)} %get-tuple-element.46, f32[512]{0:T(512)S(1)} %log_add_fusion.3, f32[512,512]{1,0:T(8,128)S(1)} %get-tuple-element.50, f32[512]{0:T(512)S(1)} %get-tuple-element.44, ...), kind=kLoop, calls=%fused_computation.20 | loop fusion | flops 4717564 | bytes 4208656 | tf_op jit(solution)/shard_map/reduce_sum | solution.py:171
  157.3 10.3 %psum.38 = f32[512]{0:T(512)S(1)} all-reduce(f32[512]{0:T(512)S(1)} %exponential_multiply_fusion), channel_id=1, replica_groups=mesh['img'=4,'txt'=8] {'img'}, use_global_device_ids=true, to_apply=%region_28.0 | all-reduce | flops 512 | bytes 4096 | tf_op jit(solution)/shard_map/psum | solution.py:135
  167.6 2.7 %fusion.13 = (bf16[512,512]{1,0:T(8,128)(2,1)S(1)}, f32[512,512]{1,0:T(8,128)S(1)}, bf16[512,512]{1,0:T(8,128)(2,1)S(1)}, f32[512,512]{1,0:T(8,128)S(1)}) fusion(f32[512,512]{1,0:T(8,128)} %get-tuple-element.45, f32[512]{0:T(512)S(1)} %log_add_fusion.3, f32[512,512]{1,0:T(8,128)} %copy-done, f32[512]{0:T(512)S(1)} %get-tuple-element.35, ...), kind=kLoop, calls=%fused_computation.57 | loop fusion | flops 4194304 | bytes 7352320 | tf_op jit(solution)/shard_map/convert_element_type | solution.py:32
  170.8 0.5 convolution_add_fusion.2
  171.4 0.5 convolution_add_fusion.1
  171.8 1.5 convolution_add_fusion
  174.3 0.8 copy-done.4
  175.5 0.8 copy-done.2
  176.7 1.5 pad_maximum_fusion
  180.8 0.7 dynamic-slice_reduce_fusion.1
  182.1 0.7 dynamic-slice_reduce_fusion
  183.4 37.7 %psum.39 = f32[]{:T(128)} all-reduce(f32[]{:T(128)S(6)} %add.94), channel_id=1, replica_groups=mesh['img'=4,'txt'=8] {'img','txt'}, use_global_device_ids=true, to_apply=%region_30.0 | all-reduce | flops 1 | bytes 8 | tf_op jit(solution)/shard_map/psum | solution.py:199
  221.9 1.7 broadcast_multiply_fusion
  223.5 17.7 %reduce-scatter.3.cloned.1.call-done = f32[128,512]{1,0:T(8,128)} async-done(((f32[1024,512]{1,0:T(8,128)}), f32[128,512]{1,0:T(8,128)}) %reduce-scatter.3.cloned.1.call-update) | async-done | bytes 262160 | tf_op jit(solution)/shard_map/reduce_scatter | solution.py:203
  241.2 1.7 broadcast_multiply_fusion.1
  (42 shorter events, 2.6 us)
Async XLA Ops:
  7.2 28.9 %all-gather.8.cloned.1.call-start = ((), (), s32[]{:S(2)}) async-start(), calls=%async_computation.4 | async-start | bytes 1179648 | tf_op jit(solution)/shard_map/all_gather | solution.py:57
  7.9 62.5 %all-gather.6.cloned.1.call-start = ((), (), s32[]{:S(2)}) async-start(), calls=%async_computation.3 | async-start | bytes 1638400 | tf_op jit(solution)/shard_map/all_gather | solution.py:47
  8.6 92.8 %all-gather.4.cloned.1.call-start = ((), (), s32[]{:S(2)}) async-start(), calls=%async_computation.2 | async-start | bytes 2949120 | tf_op jit(solution)/shard_map/all_gather | solution.py:56
  9.4 212.5 %reduce-scatter.5.cloned.1.call-start = ((), (), s32[]{:S(2)}) async-start(), calls=%async_computation.6 | async-start | bytes 1310720 | tf_op jit(solution)/shard_map/reduce_scatter | solution.py:205
  36.1 1.7 copy-start.5
  38.4 115.5 %copy-start = (f32[512,512]{1,0:T(8,128)}, f32[512,512]{1,0:T(8,128)S(1)}, u32[]{:S(2)}) copy-start(f32[512,512]{1,0:T(8,128)S(1)} %get-tuple-element.48) | copy-start | bytes 3145732
  101.4 3.7 %copy-start.7 = (bf16[1024,1280]{1,0:T(8,128)(2,1)S(1)}, bf16[1024,1280]{1,0:T(8,128)(2,1)}, u32[]{:S(2)}) copy-start(bf16[1024,1280]{1,0:T(8,128)(2,1)} %all-gather.4.cloned.1.call-done) | copy-start | bytes 7864324
  101.4 3.7 %copy-start.8 = (bf16[512,1280]{1,0:T(8,128)(2,1)S(1)}, bf16[512,1280]{1,0:T(8,128)(2,1)}, u32[]{:S(2)}) copy-start(bf16[512,1280]{1,0:T(8,128)(2,1)} %all-gather.6.cloned.1.call-done) | copy-start | bytes 3932164
  167.6 2.8 %copy-start.6 = (bf16[1024,512]{1,0:T(8,128)(2,1)S(1)}, bf16[1024,512]{1,0:T(8,128)(2,1)}, u32[]{:S(2)}) copy-start(bf16[1024,512]{1,0:T(8,128)(2,1)} %all-gather.8.cloned.1.call-done) | copy-start | bytes 3145732
  170.3 1.0 copy-start.1
  170.3 1.5 copy-start.3
  173.3 67.9 %reduce-scatter.3.cloned.1.call-start = ((), (), s32[]{:S(2)}) async-start(), calls=%async_computation.5 | async-start | bytes 2359296 | tf_op jit(solution)/shard_map/reduce_scatter | solution.py:203
  173.8 1.2 copy-start.4
  175.1 1.2 copy-start.2
Sparse Core Ops, SparseCore 0:
  9.9 26.1 all-gather.7
  37.7 32.6 all-gather.5
  72.3 29.0 all-gather.3
  173.5 24.3 reduce-scatter.4
  201.3 39.8 reduce-scatter.2
where the time goes:
time: 251 us
  blocking collectives  110 us (44%)
  waiting for transfers between devices  91.4 us (36%)
  between operations  19.6 us (8%)
  other arithmetic  15.4 us (6%)
  matrix products  12.5 us (5%)
    psum x1, blocking collectives, local(): total = lax.psum(divergence + row_gap + column_gap, ('img', 'txt'))  37.7 us
    all_gather x1, waiting for transfers between devices, local(): lax.all_gather(teacher_text, 'img', axis=0, tiled=True)  31.5 us
    all_gather x1, waiting for transfers between devices, local(): lax.all_gather(teacher_image, 'txt', axis=0, tiled=True)  31 us
    psum x2, blocking collectives, local(): lax.psum((teacher_column_total * jnp.exp(teacher_column_peak - column_top...  18.8 us
    reduce_scatter x1, waiting for transfers between devices, local(): lax.psum_scatter(image_total, 'txt', scatter_dimension=0, tiled=True)  17.7 us
    all_gather x1, blocking collectives, local(): lax.all_gather(student_text, 'img', axis=0, tiled=True)  17.6 us
    pmax x1, blocking collectives, local(): lax.pmax((teacher_row_peak, student_row_peak), 'txt')  12.1 us
    psum x1, blocking collectives, local(): lax.psum((teacher_row_total * jnp.exp(teacher_row_peak - row_top_teacher)...  12 us
  transfers between devices with their start and end apart: 5, of which 4 were waited for; matrix products, arithmetic and copies ran while one was open for 4% of the time, Pallas kernels for 0%

commit v1 on v0

v1 whole, which is shorter than its diff:
```python
import functools

import jax
import jax.numpy as jnp
import numpy as np
from jax import lax
from jax.experimental import pallas as pl
from jax.experimental.pallas import tpu as pltpu
from jax.sharding import Mesh, PartitionSpec as P

F32 = jnp.float32
BF16 = jnp.bfloat16
LINES = 8
EXTRA = 8
PARAMS = pltpu.CompilerParams(vmem_limit_bytes=56 * 2**20)
VMEM = pl.BlockSpec(memory_space=pltpu.VMEM)
SMEM = pl.BlockSpec(memory_space=pltpu.SMEM)


def matmul(a, b, da, db):
    return lax.dot_general(a, b, (((da,), (db,)), ((), ())), preferred_element_type=F32)


def pack_lines(values, shape, axis):
    index = lax.broadcasted_iota(jnp.int32, shape, axis)
    out = jnp.zeros(shape, F32)
    for k, value in enumerate(values):
        out = jnp.where(index == k, value, out)
    return out


def stats_kernel(cfg, rank, *refs):
    nr, nc, b, tw, scale_t, scale_s = cfg
    images, texts = refs[:nr], refs[nr : nr + nc]
    tl_ref, sl_ref, row_ref, col_ref, text = refs[nr + nc :]
    for p in range(nc):
        text[p * b : (p + 1) * b, :] = texts[p][...]
    step = 2 if nr % 2 == 0 else 1
    count = step * b
    peak_t = peak_s = None
    for p in range(0, nr, step):
        block = jnp.concatenate([images[p + k][...] for k in range(step)], 0)
        tl = matmul(block[:, :tw], text[:, :tw], 1, 1) * scale_t
        sl = matmul(block[:, tw:], text[:, tw:], 1, 1) * scale_s
        tl_ref[p * b : p * b + count, :] = tl
        sl_ref[p * b : p * b + count, :] = sl
        top_t, top_s = jnp.max(tl, 0, keepdims=True), jnp.max(sl, 0, keepdims=True)
        peak_t = top_t if peak_t is None else jnp.maximum(peak_t, top_t)
        peak_s = top_s if peak_s is None else jnp.maximum(peak_s, top_s)
        mt, ms = jnp.max(tl, 1, keepdims=True), jnp.max(sl, 1, keepdims=True)
        et = jnp.exp(tl - mt)
        sum_t = jnp.sum(et, 1, keepdims=True)
        gap = jnp.sum(et * (tl - sl), 1, keepdims=True)
        sum_s = jnp.sum(jnp.exp(sl - ms), 1, keepdims=True)
        lines = pack_lines((mt + jnp.log(sum_t), ms + jnp.log(sum_s), gap / sum_t), (count, 128), 1)
        for k in range(step):
            place = pl.ds(pl.multiple_of((rank[0] ^ (p + k)) * b, b), b)
            flat = jnp.transpose(lines[k * b : (k + 1) * b])[:LINES]
            for q in range(nr):
                row_ref[q * LINES : (q + 1) * LINES, place] = flat
    sum_t = sum_s = gap = None
    for p in range(0, nr, step):
        tl, sl = tl_ref[p * b : p * b + count, :], sl_ref[p * b : p * b + count, :]
        et = jnp.exp(tl - peak_t)
        parts = [
            jnp.sum(et, 0, keepdims=True),
            jnp.sum(jnp.exp(sl - peak_s), 0, keepdims=True),
            jnp.sum(et * (tl - sl), 0, keepdims=True),
        ]
        sum_t, sum_s, gap = parts if p == 0 else [x + y for x, y in zip((sum_t, sum_s, gap), parts)]
    lines = (peak_t + jnp.log(sum_t), peak_s + jnp.log(sum_s), gap / sum_t)
    for p in range(nc):
        place = pl.ds(pl.multiple_of((rank[1] ^ p) * b, b), b)
        flat = pack_lines([x[:, p * b : (p + 1) * b] for x in lines], (LINES, b), 0)
        for q in range(nc):
            col_ref[q * LINES : (q + 1) * LINES, place] = flat


def combine(parts, n):
    tiles = [parts[k * LINES : (k + 1) * LINES, :] for k in range(n)]
    peak = functools.reduce(jnp.maximum, tiles)
    weights = [jnp.exp(x - peak) for x in tiles]
    total = functools.reduce(jnp.add, weights)
    lse = peak + jnp.log(total)
    gap = functools.reduce(jnp.add, [w[0:1] * x[2:3] for w, x in zip(weights, tiles)])
    return lse, jnp.sum(gap / total[0:1] + lse[1:2] - lse[0:1], axis=(0, 1), keepdims=True)


def gradient_kernel(cfg, rank, *refs):
    nr, nc, b, tw, scale = cfg
    images, texts = refs[:nr], refs[nr : nr + nc]
    tl_ref, sl_ref, row_parts, col_parts = refs[nr + nc : nr + nc + 4]
    image_keep, image_send, text_keep, text_send, lse_ref, text, image, high_ref, low_ref = refs[nr + nc + 4 :]
    row_lse, row_share = combine(row_parts, nr)
    col_lse, col_share = combine(col_parts, nc)
    lse_ref[...] = row_lse
    for p in range(nc):
        text[p * b : (p + 1) * b, :] = texts[p][:, tw:]
    for p in range(nr):
        image[p * b : (p + 1) * b, :] = images[p][:, tw:]
    columns = [[None, None] for _ in range(nc)]
    for p in range(nc):
        place = rank[1] ^ p
        for k in range(2):
            piece = col_lse[k : k + 1, :b]
            for q in range(1, nc):
                piece = jnp.where(place == q, col_lse[k : k + 1, q * b : (q + 1) * b], piece)
            columns[p][k] = piece
    col_t = jnp.concatenate([c[0] for c in columns], 1)
    col_s = jnp.concatenate([c[1] for c in columns], 1)
    half = nr // 2
    for p in range(nr):
        place = pl.ds(pl.multiple_of((rank[0] ^ p) * b, b), b)
        row = jnp.transpose(lse_ref[:, place])
        tl, sl = tl_ref[p * b : (p + 1) * b, :], sl_ref[p * b : (p + 1) * b, :]
        delta = (jnp.exp(sl - row[:, 1:2]) - jnp.exp(tl - row[:, 0:1])) + (jnp.exp(sl - col_s) - jnp.exp(tl - col_t))
        high = delta.astype(BF16)
        high_ref[p * b : (p + 1) * b, :] = high
        low_ref[p * b : (p + 1) * b, :] = (delta - high.astype(F32)).astype(BF16)
    for p in range(nr):
        rows = slice(p * b, (p + 1) * b)
        part = (matmul(high_ref[rows, :], text[...], 1, 0) + matmul(low_ref[rows, :], text[...], 1, 0)) * scale
        if p < half:
            image_keep[rows, :] = part
        else:
            image_send[(p - half) * b : (p - half + 1) * b, :] = part
    half = nc // 2
    for p in range(nc):
        cols = slice(p * b, (p + 1) * b)
        part = (matmul(high_ref[:, cols], image[...], 0, 0) + matmul(low_ref[:, cols], image[...], 0, 0)) * scale
        if p < half:
            text_keep[cols, :] = part
        else:
            text_send[(p - half) * b : (p - half + 1) * b, :] = part
    for ref, share in ((image_keep, col_share), (image_send, col_share), (text_keep, row_share), (text_send, row_share)):
        ref[ref.shape[0] - EXTRA :, :] = jnp.broadcast_to(share, (EXTRA, ref.shape[1]))


def swap(bit, x):
    return lax.ppermute(x, bit, [(0, 1), (1, 0)])


def gather(bits, x):
    blocks = [x]
    for bit in bits:
        blocks = blocks + [swap(bit, y) for y in blocks]
    return blocks


def scatter_sum(bits, keep, send, b):
    for k in reversed(range(len(bits))):
        total = keep + swap(bits[k], send)
        if k:
            rows = total.shape[0] - EXTRA
            send = total[rows // 2 :]
            keep = jnp.concatenate([total[: rows // 2], total[rows:]])
    return total[:b], total[b, 0]


def local(image_bits, text_bits, teacher_image, teacher_text, student_image, student_text):
    b, tw = teacher_image.shape
    sw = student_image.shape[1]
    nr, nc = 1 << len(image_bits), 1 << len(text_bits)
    r, c = nr * b, nc * b
    images = gather(image_bits, jnp.concatenate([teacher_image, student_image], 1))
    texts = gather(text_bits, jnp.concatenate([teacher_text, student_text], 1))
    row_axes, col_axes = image_bits[::-1], text_bits[::-1]
    rank = jnp.stack([lax.axis_index(row_axes), lax.axis_index(col_axes)]).astype(jnp.int32)
    blocks = images + texts
    specs = [SMEM] + [VMEM] * len(blocks)
    out = lambda *shape: jax.ShapeDtypeStruct(shape, F32)
    flops = 2 * r * c * (tw + sw)
    tl, sl, row_lines, col_lines = pl.pallas_call(
        functools.partial(stats_kernel, (nr, nc, b, tw, tw**-0.5, sw**-0.5)),
        out_shape=[out(r, c), out(r, c), out(nr * LINES, r), out(nc * LINES, c)],
        in_specs=specs,
        out_specs=[VMEM] * 4,
        scratch_shapes=[pltpu.VMEM((c, tw + sw), BF16)],
        compiler_params=PARAMS,
        cost_estimate=pl.CostEstimate(flops=flops, bytes_accessed=8 * r * c, transcendentals=4 * r * c),
    )(rank, *blocks)
    row_lines = lax.all_to_all(row_lines, row_axes, 0, 0, tiled=True)
    col_lines = lax.all_to_all(col_lines, col_axes, 0, 0, tiled=True)
    ir, ic = r // 2 + EXTRA, c // 2 + EXTRA
    image_keep, image_send, text_keep, text_send = pl.pallas_call(
        functools.partial(gradient_kernel, (nr, nc, b, tw, sw**-0.5)),
        out_shape=[out(ir, sw), out(ir, sw), out(ic, sw), out(ic, sw)],
        in_specs=specs + [VMEM] * 4,
        out_specs=[VMEM] * 4,
        scratch_shapes=[
            pltpu.VMEM((LINES, r), F32),
            pltpu.VMEM((c, sw), BF16),
            pltpu.VMEM((r, sw), BF16),
            pltpu.VMEM((r, c), BF16),
            pltpu.VMEM((r, c), BF16),
        ],
        compiler_params=PARAMS,
        cost_estimate=pl.CostEstimate(flops=8 * r * c * sw, bytes_accessed=8 * r * c, transcendentals=4 * r * c),
    )(rank, *blocks, tl, sl, row_lines, col_lines)
    image_grad, col_share = scatter_sum(image_bits, image_keep, image_send, b)
    text_grad, row_share = scatter_sum(text_bits, text_keep, text_send, b)
    pairs = b << (len(image_bits) + len(text_bits))
    return ((row_share + col_share) / (2.0 * pairs), image_grad, text_grad)


def solution(mesh):
    bits = {axis: [f"{axis}{k}" for k in reversed(range(mesh.shape[axis].bit_length() - 1))] for axis in ("img", "txt")}
    names = bits["img"] + bits["txt"]
    cube = Mesh(np.asarray(mesh.devices).reshape((2,) * len(names)), names)
    text_bits = [x for x in bits["img"] if int(x[3:]) >= 1] + [x for x in bits["txt"] if int(x[3:]) % 2 == 1]
    image_bits = [x for x in names if x not in text_bits]
    image, text = P(tuple(names), None), P(tuple(bits["txt"] + bits["img"]), None)
    return jax.shard_map(
        functools.partial(local, tuple(image_bits), tuple(text_bits)),
        mesh=cube,
        in_specs=(image, text, image, text),
        out_specs=(P(), image, text),
        check_vma=False,
    )
```

time: 251 us -> 113 us (0.45)
  blocking collectives: 110 us -> 20.3 us
  waiting for transfers between devices: 91.4 us -> 50.9 us
  between operations: 19.6 us -> 3.18 us
  Pallas kernels: 0 us -> 16.1 us
  starting transfers between devices: 0.19 us -> 15.1 us
  other arithmetic: 15.4 us -> 2.36 us
  matrix products: 12.5 us -> 0 us
  local copies, waits for them, and re-layouts: 1.6 us -> 4.66 us
    all_gather x3 -> x0, waiting for transfers between devices: 71.6 us -> none  [the longest x1 31.5 us: local(): lax.all_gather(teacher_text, 'img', axis=0, tiled=True)]
    psum x4 -> x0, blocking collectives: 68.5 us -> none  [the longest x1 37.7 us: local(): total = lax.psum(divergence + row_gap + column_gap, ('img', 'txt'))]
    ppermute x0 -> x15, waiting for transfers between devices: none -> 50.9 us  [swap(): return lax.ppermute(x, bit, [(0, 1), (1, 0)])]
    pmax x2 -> x0, blocking collectives: 23.8 us -> none  [the longest x1 12.1 us: local(): lax.pmax((teacher_row_peak, student_row_peak), 'txt')]
    all_to_all x0 -> x2, blocking collectives: none -> 20.3 us  [the longest x1 10.6 us: local(): row_lines = lax.all_to_all(row_lines, row_axes, 0, 0, tiled=True)]
    reduce_scatter x2 -> x0, waiting for transfers between devices: 17.7 us -> none  [the longest x1 17.7 us: local(): lax.psum_scatter(image_total, 'txt', scatter_dimension=0, tiled=True)]
    all_gather x1 -> x0, blocking collectives: 17.6 us -> none  [local(): lax.all_gather(student_text, 'img', axis=0, tiled=True)]
    pallas_call x0 -> x2, Pallas kernels: none -> 16.1 us  [the longest x1 8.78 us: local(): pl.pallas_call(functools.partial(gradient_kernel, (nr, nc, b, tw, sw ** (...]
  transfers between devices with their start and end apart: 5 -> 15, of which waited for: 4 -> 9; matrix products, arithmetic and copies ran while one was open for 4% -> 3% of each run, Pallas kernels for 0% -> 0%
where the time goes in v1:
time: 113 us
  waiting for transfers between devices  50.9 us (45%)
  blocking collectives  20.3 us (18%)
  Pallas kernels  16.1 us (14%)
  starting transfers between devices  15.1 us (13%)
  local copies, waits for them, and re-layouts  4.66 us (4%)
  between operations  3.18 us (3%)
  other arithmetic  2.36 us (2%)
    ppermute x15, waiting for transfers between devices, swap(): return lax.ppermute(x, bit, [(0, 1), (1, 0)])  50.9 us
    ppermute x15, starting transfers between devices, swap(): return lax.ppermute(x, bit, [(0, 1), (1, 0)])  15.1 us
    all_to_all x1, blocking collectives, local(): row_lines = lax.all_to_all(row_lines, row_axes, 0, 0, tiled=True)  10.6 us
    all_to_all x1, blocking collectives, local(): col_lines = lax.all_to_all(col_lines, col_axes, 0, 0, tiled=True)  9.71 us
    pallas_call x1, Pallas kernels, local(): pl.pallas_call(functools.partial(gradient_kernel, (nr, nc, b, tw, sw ** (...  8.78 us
    pallas_call x1, Pallas kernels, local(): pl.pallas_call(functools.partial(stats_kernel, (nr, nc, b, tw, tw ** (-0....  7.3 us
    slice x4, local copies, waits for them, and re-layouts, scatter_sum(): return (total[:b], total[b, 0])  2.47 us
  transfers between devices with their start and end apart: 15, of which 9 were waited for; matrix products, arithmetic and copies ran while one was open for 3% of the time, Pallas kernels for 0%

profile of v1, /device:TPU:0, one launch (start us, length us, event | category | flops | bytes accessed | tf_op | source)
XLA Modules:
  0.0 112.6 jit_solution(17844219679128698286)
XLA Ops:
  0.7 1.0 constant_dynamic-update-slice_fusion.1
  1.7 0.9 constant_dynamic-update-slice_fusion.refs_0_
  2.6 3.1 %collective-permute-start = (bf16[128,1792]{1,0:T(8,128)(2,1)S(1)}, bf16[128,1792]{1,0:T(8,128)(2,1)S(1)}, u32[]{:S(2)}, u32[]{:S(2)}) collective-permute-start(bf16[128,1792]{1,0:T(8,128)(2,1)S(1)} %constant_dynamic-update-slice_fusion.refs_0_), channel_id=1, source_target_pairs={{0,8},{8,0},{1,9},{9,1},{2,10},{10,2},{3,11},{11,3},{4,12},{12,4},... | collective-permute-start | bytes 1376264 | tf_op jit(solution)/shard_map/ppermute | solution.py:140
  5.8 1.6 %collective-permute-start.8 = (bf16[128,1792]{1,0:T(8,128)(2,1)S(1)}, bf16[128,1792]{1,0:T(8,128)(2,1)S(1)}, u32[]{:S(2)}, u32[]{:S(2)}) collective-permute-start(bf16[128,1792]{1,0:T(8,128)(2,1)S(1)} %constant_dynamic-update-slice_fusion.2.refs_8_), channel_id=1, source_target_pairs={{0,2},{2,0},{1,3},{3,1},{4,6},{6,4},{5,7},{7,5},{8,10},{10,8},{9,1... | collective-permute-start | bytes 1376264 | tf_op jit(solution)/shard_map/ppermute | solution.py:140
  7.3 2.6 %collective-permute-start.7 = (bf16[128,1792]{1,0:T(8,128)(2,1)S(1)}, bf16[128,1792]{1,0:T(8,128)(2,1)S(1)}, u32[]{:S(2)}, u32[]{:S(2)}) collective-permute-start(bf16[128,1792]{1,0:T(8,128)(2,1)S(1)} %constant_dynamic-update-slice_fusion.2.refs_8_), channel_id=1, source_target_pairs={{0,16},{16,0},{1,17},{17,1},{2,18},{18,2},{3,19},{19,3},{4,20},{20... | collective-permute-start | bytes 1376264 | tf_op jit(solution)/shard_map/ppermute | solution.py:140
  9.9 1.5 %collective-permute-start.1 = (bf16[128,1792]{1,0:T(8,128)(2,1)S(1)}, bf16[128,1792]{1,0:T(8,128)(2,1)S(1)}, u32[]{:S(2)}, u32[]{:S(2)}) collective-permute-start(bf16[128,1792]{1,0:T(8,128)(2,1)S(1)} %constant_dynamic-update-slice_fusion.refs_0_), channel_id=1, source_target_pairs={{0,4},{4,0},{1,5},{5,1},{2,6},{6,2},{3,7},{7,3},{8,12},{12,8},{9,1... | collective-permute-start | bytes 1376264 | tf_op jit(solution)/shard_map/ppermute | solution.py:140
  11.5 13.2 %collective-permute-done.refs_1_ = bf16[128,1792]{1,0:T(8,128)(2,1)S(1)} collective-permute-done((bf16[128,1792]{1,0:T(8,128)(2,1)S(1)}, bf16[128,1792]{1,0:T(8,128)(2,1)S(1)}, u32[]{:S(2)}, u32[]{:S(2)}) %collective-permute-start) | collective-permute-done | bytes 458784 | tf_op jit(solution)/shard_map/ppermute | solution.py:140
  24.6 1.7 %collective-permute-start.2 = (bf16[128,1792]{1,0:T(8,128)(2,1)S(1)}, bf16[128,1792]{1,0:T(8,128)(2,1)S(1)}, u32[]{:S(2)}, u32[]{:S(2)}) collective-permute-start(bf16[128,1792]{1,0:T(8,128)(2,1)S(1)} %collective-permute-done.refs_1_), channel_id=1, source_target_pairs={{0,4},{4,0},{1,5},{5,1},{2,6},{6,2},{3,7},{7,3},{8,12},{12,8},{9,1... | collective-permute-start | bytes 1376264 | tf_op jit(solution)/shard_map/ppermute | solution.py:140
  26.3 0.5 collective-permute-start.4
  26.8 3.0 %collective-permute-done.7.refs_9_ = bf16[128,1792]{1,0:T(8,128)(2,1)S(1)} collective-permute-done((bf16[128,1792]{1,0:T(8,128)(2,1)S(1)}, bf16[128,1792]{1,0:T(8,128)(2,1)S(1)}, u32[]{:S(2)}, u32[]{:S(2)}) %collective-permute-start.7) | collective-permute-done | bytes 458784 | tf_op jit(solution)/shard_map/ppermute | solution.py:140
  29.8 0.5 collective-permute-start.9
  30.4 6.0 %collective-permute-done.2.refs_3_ = bf16[128,1792]{1,0:T(8,128)(2,1)S(1)} collective-permute-done((bf16[128,1792]{1,0:T(8,128)(2,1)S(1)}, bf16[128,1792]{1,0:T(8,128)(2,1)S(1)}, u32[]{:S(2)}, u32[]{:S(2)}) %collective-permute-start.2) | collective-permute-done | bytes 458784 | tf_op jit(solution)/shard_map/ppermute | solution.py:140
  36.3 0.7 pad_add_fusion.rank
  37.0 3.1 %collective-permute-done.9.refs_11_ = bf16[128,1792]{1,0:T(8,128)(2,1)} collective-permute-done((bf16[128,1792]{1,0:T(8,128)(2,1)S(1)}, bf16[128,1792]{1,0:T(8,128)(2,1)}, u32[]{:S(2)}, u32[]{:S(2)}) %collective-permute-start.9) | collective-permute-done | bytes 458784 | tf_op jit(solution)/shard_map/ppermute | solution.py:140
  40.2 7.3 %shard_map.67 = (f32[1024,512]{1,0:T(8,128)}, f32[1024,512]{1,0:T(8,128)}, f32[64,1024]{1,0:T(8,128)}, f32[32,512]{1,0:T(8,128)}) custom-call(s32[2]{0:T(128)} %pad_add_fusion.rank, bf16[128,1792]{1,0:T(8,128)(2,1)} %copy-done, bf16[128,1792]{1,0:T(8,128)(2,1)} %copy-done.3, bf16[128,1792]{1,0:T(8,128)(2,1)} %copy-done.6, bf16[128,1792]{1,0:T(8,128)(2,1)} %copy-done.7, ...), custom_call_target="tpu_custom_call" | custom-call | flops 1879048192 | bytes 4194304 | tf_op jit(solution)/shard_map/pallas_call | solution.py:173
  47.5 9.7 %all_to_all.22 = f32[4,8,512]{2,1,0:T(8,128)} all-to-all(f32[4,8,512]{2,1,0:T(8,128)} %bitcast.10), channel_id=1, replica_groups=mesh['img1'=2,'img0'=2,'txt2'=2,'txt1'=2,'txt0'=2] {'txt1','img1'}, dimensions={0} | all-to-all | bytes 131072 | tf_op jit(solution)/shard_map/all_to_all | solution.py:183
  57.2 10.6 %all_to_all.23 = f32[8,8,1024]{2,1,0:T(8,128)} all-to-all(f32[8,8,1024]{2,1,0:T(8,128)} %bitcast.9), channel_id=1, replica_groups=mesh['img1'=2,'img0'=2,'txt2'=2,'txt1'=2,'txt0'=2] {'txt0','txt2','img0'}, dimensions={0} | all-to-all | bytes 524288 | tf_op jit(solution)/shard_map/all_to_all | solution.py:182
  67.8 8.8 %shard_map.68 = (f32[520,512]{1,0:T(8,128)}, f32[520,512]{1,0:T(8,128)}, f32[264,512]{1,0:T(8,128)}, f32[264,512]{1,0:T(8,128)}) custom-call(s32[2]{0:T(128)} %pad_add_fusion.rank, bf16[128,1792]{1,0:T(8,128)(2,1)} %copy-done, bf16[128,1792]{1,0:T(8,128)(2,1)} %copy-done.3, bf16[128,1792]{1,0:T(8,128)(2,1)} %copy-done.6, bf16[128,1792]{1,0:T(8,128)(2,1)} %copy-done.7, ...), custom_call_target="tpu_custom_call" | custom-call | flops 2147483648 | bytes 4194304 | tf_op jit(solution)/shard_map/pallas_call | solution.py:185
  76.8 0.7 collective-permute-start.10
  77.5 2.0 %collective-permute-done.12 = f32[520,512]{1,0:T(8,128)S(1)} collective-permute-done((f32[520,512]{1,0:T(8,128)}, f32[520,512]{1,0:T(8,128)S(1)}, u32[]{:S(2)}, u32[]{:S(2)}) %collective-permute-start.12) | collective-permute-done | bytes 1064992 | tf_op jit(solution)/shard_map/ppermute | solution.py:140
  79.5 1.4 %add.33 = f32[520,512]{1,0:T(8,128)S(1)} add(f32[520,512]{1,0:T(8,128)} %get-tuple-element.17, f32[520,512]{1,0:T(8,128)S(1)} %collective-permute-done.12) | non-fusion elementwise | flops 266240 | bytes 3194880 | tf_op jit(solution)/shard_map/add | solution.py:152
  81.0 1.0 collective-permute-start.13
  82.0 9.5 %collective-permute-done.10 = f32[264,512]{1,0:T(8,128)S(1)} collective-permute-done((f32[264,512]{1,0:T(8,128)}, f32[264,512]{1,0:T(8,128)S(1)}, u32[]{:S(2)}, u32[]{:S(2)}) %collective-permute-start.10) | collective-permute-done | bytes 540704 | tf_op jit(solution)/shard_map/ppermute | solution.py:140
  91.6 0.8 collective-permute-start.11
  92.5 2.9 %collective-permute-done.13 = f32[264,512]{1,0:T(8,128)S(1)} collective-permute-done((f32[264,512]{1,0:T(8,128)S(1)}, f32[264,512]{1,0:T(8,128)S(1)}, u32[]{:S(2)}, u32[]{:S(2)}) %collective-permute-start.13) | collective-permute-done | bytes 540704 | tf_op jit(solution)/shard_map/ppermute | solution.py:140
  95.5 0.9 collective-permute-start.14
  96.5 10.3 %collective-permute-done.11 = f32[136,512]{1,0:T(8,128)S(1)} collective-permute-done((f32[136,512]{1,0:T(8,128)S(1)}, f32[136,512]{1,0:T(8,128)S(1)}, u32[]{:S(2)}, u32[]{:S(2)}) %collective-permute-start.11) | collective-permute-done | bytes 278560 | tf_op jit(solution)/shard_map/ppermute | solution.py:140
  106.8 0.5 slice.55
  107.3 0.7 slice.64
  108.1 0.9 collective-permute-done.14
  109.0 0.5 slice.62
  109.5 0.7 slice.63
  (45 shorter events, 0.7 us)
Async XLA Ops:
  0.6 5.1 %copy-start.8 = (bf16[128,1280]{1,0:T(8,128)(2,1)S(1)}, bf16[128,1280]{1,0:T(8,128)(2,1)}, u32[]{:S(2)}) copy-start(bf16[128,1280]{1,0:T(8,128)(2,1)} %param.5) | copy-start | bytes 983044
  0.6 5.1 %copy-start.9 = (bf16[128,512]{1,0:T(8,128)(2,1)S(1)}, bf16[128,512]{1,0:T(8,128)(2,1)}, u32[]{:S(2)}) copy-start(bf16[128,512]{1,0:T(8,128)(2,1)} %param.7) | copy-start | bytes 393220
  2.6 37.5 %copy-start = (bf16[128,1792]{1,0:T(8,128)(2,1)}, bf16[128,1792]{1,0:T(8,128)(2,1)S(1)}, u32[]{:S(2)}) copy-start(bf16[128,1792]{1,0:T(8,128)(2,1)S(1)} %constant_dynamic-update-slice_fusion.refs_0_) | copy-start | bytes 1376260
  2.6 22.0 %collective-permute-start = (bf16[128,1792]{1,0:T(8,128)(2,1)S(1)}, bf16[128,1792]{1,0:T(8,128)(2,1)S(1)}, u32[]{:S(2)}, u32[]{:S(2)}) collective-permute-start(bf16[128,1792]{1,0:T(8,128)(2,1)S(1)} %constant_dynamic-update-slice_fusion.refs_0_), channel_id=1, source_target_pairs={{0,8},{8,0},{1,9},{9,1},{2,10},{10,2},{3,11},{11,3},{4,12},{12,4},... | collective-permute-start | bytes 1376264 | tf_op jit(solution)/shard_map/ppermute | solution.py:140
  5.8 34.4 %copy-start.1 = (bf16[128,1792]{1,0:T(8,128)(2,1)}, bf16[128,1792]{1,0:T(8,128)(2,1)S(1)}, u32[]{:S(2)}) copy-start(bf16[128,1792]{1,0:T(8,128)(2,1)S(1)} %constant_dynamic-update-slice_fusion.2.refs_8_) | copy-start | bytes 1376260
  5.8 20.5 %collective-permute-start.8 = (bf16[128,1792]{1,0:T(8,128)(2,1)S(1)}, bf16[128,1792]{1,0:T(8,128)(2,1)S(1)}, u32[]{:S(2)}, u32[]{:S(2)}) collective-permute-start(bf16[128,1792]{1,0:T(8,128)(2,1)S(1)} %constant_dynamic-update-slice_fusion.2.refs_8_), channel_id=1, source_target_pairs={{0,2},{2,0},{1,3},{3,1},{4,6},{6,4},{5,7},{7,5},{8,10},{10,8},{9,1... | collective-permute-start | bytes 1376264 | tf_op jit(solution)/shard_map/ppermute | solution.py:140
  7.3 22.5 %collective-permute-start.7 = (bf16[128,1792]{1,0:T(8,128)(2,1)S(1)}, bf16[128,1792]{1,0:T(8,128)(2,1)S(1)}, u32[]{:S(2)}, u32[]{:S(2)}) collective-permute-start(bf16[128,1792]{1,0:T(8,128)(2,1)S(1)} %constant_dynamic-update-slice_fusion.2.refs_8_), channel_id=1, source_target_pairs={{0,16},{16,0},{1,17},{17,1},{2,18},{18,2},{3,19},{19,3},{4,20},{20... | collective-permute-start | bytes 1376264 | tf_op jit(solution)/shard_map/ppermute | solution.py:140
  9.9 20.4 %collective-permute-start.1 = (bf16[128,1792]{1,0:T(8,128)(2,1)S(1)}, bf16[128,1792]{1,0:T(8,128)(2,1)S(1)}, u32[]{:S(2)}, u32[]{:S(2)}) collective-permute-start(bf16[128,1792]{1,0:T(8,128)(2,1)S(1)} %constant_dynamic-update-slice_fusion.refs_0_), channel_id=1, source_target_pairs={{0,4},{4,0},{1,5},{5,1},{2,6},{6,2},{3,7},{7,3},{8,12},{12,8},{9,1... | collective-permute-start | bytes 1376264 | tf_op jit(solution)/shard_map/ppermute | solution.py:140
  24.6 15.6 %copy-start.3 = (bf16[128,1792]{1,0:T(8,128)(2,1)}, bf16[128,1792]{1,0:T(8,128)(2,1)S(1)}, u32[]{:S(2)}) copy-start(bf16[128,1792]{1,0:T(8,128)(2,1)S(1)} %collective-permute-done.refs_1_) | copy-start | bytes 1376260
  24.6 11.7 %collective-permute-start.2 = (bf16[128,1792]{1,0:T(8,128)(2,1)S(1)}, bf16[128,1792]{1,0:T(8,128)(2,1)S(1)}, u32[]{:S(2)}, u32[]{:S(2)}) collective-permute-start(bf16[128,1792]{1,0:T(8,128)(2,1)S(1)} %collective-permute-done.refs_1_), channel_id=1, source_target_pairs={{0,4},{4,0},{1,5},{5,1},{2,6},{6,2},{3,7},{7,3},{8,12},{12,8},{9,1... | collective-permute-start | bytes 1376264 | tf_op jit(solution)/shard_map/ppermute | solution.py:140
  26.3 10.7 %collective-permute-start.3 = (bf16[128,1792]{1,0:T(8,128)(2,1)S(1)}, bf16[128,1792]{1,0:T(8,128)(2,1)}, u32[]{:S(2)}, u32[]{:S(2)}) collective-permute-start(bf16[128,1792]{1,0:T(8,128)(2,1)S(1)} %constant_dynamic-update-slice_fusion.refs_0_), channel_id=1, source_target_pairs={{0,1},{1,0},{2,3},{3,2},{4,5},{5,4},{6,7},{7,6},{8,9},{9,8},{10,11... | collective-permute-start | bytes 1376264 | tf_op jit(solution)/shard_map/ppermute | solution.py:140
  26.3 13.9 %copy-start.4 = (bf16[128,1792]{1,0:T(8,128)(2,1)}, bf16[128,1792]{1,0:T(8,128)(2,1)S(1)}, u32[]{:S(2)}) copy-start(bf16[128,1792]{1,0:T(8,128)(2,1)S(1)} %collective-permute-done.8.refs_10_) | copy-start | bytes 1376260
  26.3 13.8 %collective-permute-start.4 = (bf16[128,1792]{1,0:T(8,128)(2,1)S(1)}, bf16[128,1792]{1,0:T(8,128)(2,1)}, u32[]{:S(2)}, u32[]{:S(2)}) collective-permute-start(bf16[128,1792]{1,0:T(8,128)(2,1)S(1)} %collective-permute-done.refs_1_), channel_id=1, source_target_pairs={{0,1},{1,0},{2,3},{3,2},{4,5},{5,4},{6,7},{7,6},{8,9},{9,8},{10,11... | collective-permute-start | bytes 1376264 | tf_op jit(solution)/shard_map/ppermute | solution.py:140
  29.8 10.4 %copy-start.5 = (bf16[128,1792]{1,0:T(8,128)(2,1)}, bf16[128,1792]{1,0:T(8,128)(2,1)S(1)}, u32[]{:S(2)}) copy-start(bf16[128,1792]{1,0:T(8,128)(2,1)S(1)} %collective-permute-done.7.refs_9_) | copy-start | bytes 1376260
  29.8 10.3 %collective-permute-start.9 = (bf16[128,1792]{1,0:T(8,128)(2,1)S(1)}, bf16[128,1792]{1,0:T(8,128)(2,1)}, u32[]{:S(2)}, u32[]{:S(2)}) collective-permute-start(bf16[128,1792]{1,0:T(8,128)(2,1)S(1)} %collective-permute-done.7.refs_9_), channel_id=1, source_target_pairs={{0,2},{2,0},{1,3},{3,1},{4,6},{6,4},{5,7},{7,5},{8,10},{10,8},{9,1... | collective-permute-start | bytes 1376264 | tf_op jit(solution)/shard_map/ppermute | solution.py:140
  30.4 9.9 %copy-start.6 = (bf16[128,1792]{1,0:T(8,128)(2,1)}, bf16[128,1792]{1,0:T(8,128)(2,1)S(1)}, u32[]{:S(2)}) copy-start(bf16[128,1792]{1,0:T(8,128)(2,1)S(1)} %collective-permute-done.1.refs_2_) | copy-start | bytes 1376260
  30.4 9.8 %collective-permute-start.5 = (bf16[128,1792]{1,0:T(8,128)(2,1)S(1)}, bf16[128,1792]{1,0:T(8,128)(2,1)}, u32[]{:S(2)}, u32[]{:S(2)}) collective-permute-start(bf16[128,1792]{1,0:T(8,128)(2,1)S(1)} %collective-permute-done.1.refs_2_), channel_id=1, source_target_pairs={{0,1},{1,0},{2,3},{3,2},{4,5},{5,4},{6,7},{7,6},{8,9},{9,8},{10,11... | collective-permute-start | bytes 1376264 | tf_op jit(solution)/shard_map/ppermute | solution.py:140
  36.3 3.9 %copy-start.7 = (bf16[128,1792]{1,0:T(8,128)(2,1)}, bf16[128,1792]{1,0:T(8,128)(2,1)S(1)}, u32[]{:S(2)}) copy-start(bf16[128,1792]{1,0:T(8,128)(2,1)S(1)} %collective-permute-done.2.refs_3_) | copy-start | bytes 1376260
  36.3 3.8 %collective-permute-start.6 = (bf16[128,1792]{1,0:T(8,128)(2,1)S(1)}, bf16[128,1792]{1,0:T(8,128)(2,1)}, u32[]{:S(2)}, u32[]{:S(2)}) collective-permute-start(bf16[128,1792]{1,0:T(8,128)(2,1)S(1)} %collective-permute-done.2.refs_3_), channel_id=1, source_target_pairs={{0,1},{1,0},{2,3},{3,2},{4,5},{5,4},{6,7},{7,6},{8,9},{9,8},{10,11... | collective-permute-start | bytes 1376264 | tf_op jit(solution)/shard_map/ppermute | solution.py:140
  76.6 2.9 %collective-permute-start.12 = (f32[520,512]{1,0:T(8,128)}, f32[520,512]{1,0:T(8,128)S(1)}, u32[]{:S(2)}, u32[]{:S(2)}) collective-permute-start(f32[520,512]{1,0:T(8,128)} %get-tuple-element.18), channel_id=1, source_target_pairs={{0,1},{1,0},{2,3},{3,2},{4,5},{5,4},{6,7},{7,6},{8,9},{9,8},{10,11... | collective-permute-start | bytes 3194888 | tf_op jit(solution)/shard_map/ppermute | solution.py:140
  76.8 14.7 %collective-permute-start.10 = (f32[264,512]{1,0:T(8,128)}, f32[264,512]{1,0:T(8,128)S(1)}, u32[]{:S(2)}, u32[]{:S(2)}) collective-permute-start(f32[264,512]{1,0:T(8,128)} %get-tuple-element.16), channel_id=1, source_target_pairs={{0,2},{2,0},{1,3},{3,1},{4,6},{6,4},{5,7},{7,5},{8,10},{10,8},{9,1... | collective-permute-start | bytes 1622024 | tf_op jit(solution)/shard_map/ppermute | solution.py:140
  81.0 10.6 %copy-start.2 = (f32[264,512]{1,0:T(8,128)S(1)}, f32[264,512]{1,0:T(8,128)}, u32[]{:S(2)}) copy-start(f32[264,512]{1,0:T(8,128)} %get-tuple-element.15) | copy-start | bytes 1622020
  81.0 14.4 %collective-permute-start.13 = (f32[264,512]{1,0:T(8,128)S(1)}, f32[264,512]{1,0:T(8,128)S(1)}, u32[]{:S(2)}, u32[]{:S(2)}) collective-permute-start(f32[264,512]{1,0:T(8,128)S(1)} %slice.58), channel_id=1, source_target_pairs={{0,4},{4,0},{1,5},{5,1},{2,6},{6,2},{3,7},{7,3},{8,12},{12,8},{9,1... | collective-permute-start | bytes 1622024 | tf_op jit(solution)/shard_map/ppermute | solution.py:140
  91.6 15.1 %collective-permute-start.11 = (f32[136,512]{1,0:T(8,128)S(1)}, f32[136,512]{1,0:T(8,128)S(1)}, u32[]{:S(2)}, u32[]{:S(2)}) collective-permute-start(f32[136,512]{1,0:T(8,128)S(1)} %slice.54), channel_id=1, source_target_pairs={{0,16},{16,0},{1,17},{17,1},{2,18},{18,2},{3,19},{19,3},{4,20},{20... | collective-permute-start | bytes 835592 | tf_op jit(solution)/shard_map/ppermute | solution.py:140
  95.5 13.4 %collective-permute-start.14 = (f32[136,512]{1,0:T(8,128)S(1)}, f32[136,512]{1,0:T(8,128)S(1)}, u32[]{:S(2)}, u32[]{:S(2)}) collective-permute-start(f32[136,512]{1,0:T(8,128)S(1)} %slice.61), channel_id=1, source_target_pairs={{0,8},{8,0},{1,9},{9,1},{2,10},{10,2},{3,11},{11,3},{4,12},{12,4},... | collective-permute-start | bytes 835592 | tf_op jit(solution)/shard_map/ppermute | solution.py:140

commit v2 on v1

v2 whole, which is shorter than its diff:
```python
import functools

import jax
import jax.numpy as jnp
import numpy as np
from jax import lax
from jax.experimental import pallas as pl
from jax.experimental.pallas import tpu as pltpu
from jax.sharding import Mesh, PartitionSpec as P

F32 = jnp.float32
BF16 = jnp.bfloat16
F16 = jnp.float16
LINES = 8
EXTRA = 16
PARAMS = pltpu.CompilerParams(vmem_limit_bytes=56 * 2**20)
VMEM = pl.BlockSpec(memory_space=pltpu.VMEM)


def matmul(a, b, da, db):
    return lax.dot_general(a, b, (((da,), (db,)), ((), ())), preferred_element_type=F32)


def block(k, b):
    return slice(k * b, (k + 1) * b)


def only(k, value, shape, axis):
    return jnp.where(lax.broadcasted_iota(jnp.int32, shape, axis) == k, value, 0.0)


def row_lse(logit):
    peak = jnp.max(logit, 1, keepdims=True)
    return peak + jnp.log(jnp.sum(jnp.exp(logit - peak), 1, keepdims=True))


def logit_kernel(nr, nc, b, scale, line, *refs):
    images, texts, refs = refs[:nr], refs[nr : nr + nc], refs[nr + nc :]
    before, refs = (refs[0], refs[1:]) if line else (None, refs)
    logit_ref, row_ref, text = refs
    for p in range(nc):
        text[block(p, b), :] = texts[p][...]
    step = 2 if nr % 2 == 0 else 1
    for p in range(0, nr, step):
        image = jnp.concatenate([x[...] for x in images[p : p + step]], 0)
        logit = matmul(image, text[...], 1, 1) * scale
        logit_ref[p * b : (p + step) * b, :] = logit
        lse = only(line, row_lse(logit), (step * b, 128), 1)
        for k in range(step):
            flat = jnp.transpose(lse[block(k, b)])[:LINES]
            row_ref[:, block(p + k, b)] = flat + before[:, block(p + k, b)] if line else flat


def column_kernel(line, *refs):
    logit_ref, refs = refs[0], refs[1:]
    before, refs = (refs[0], refs[1:]) if line else (None, refs)
    col_ref = refs[0]
    step = min(256, logit_ref.shape[0])
    chunks = [slice(k, k + step) for k in range(0, logit_ref.shape[0], step)]
    peak = functools.reduce(jnp.maximum, [jnp.max(logit_ref[x, :], 0, keepdims=True) for x in chunks])
    total = functools.reduce(
        jnp.add, [jnp.sum(jnp.exp(logit_ref[x, :] - peak), 0, keepdims=True) for x in chunks]
    )
    lse = only(line, peak + jnp.log(total), col_ref.shape, 0)
    col_ref[...] = lse + before[...] if line else lse


def merge(x, y):
    peak = jnp.maximum(x, y)
    return peak + jnp.log(jnp.exp(x - peak) + jnp.exp(y - peak))


def merge_kernel(b, flips, *refs):
    n = len(flips)
    for k, flip in enumerate(flips):
        own, come, out = refs[2 * k], refs[2 * k + 1], refs[2 * n + k]
        for p in range(own.shape[1] // b):
            out[:, block(p, b)] = merge(own[:, block(p, b)], come[:, block(p ^ flip, b)])


def image_kernel(nr, nc, b, scale, *refs):
    texts, refs = refs[:nc], refs[nc:]
    tl_ref, sl_ref, row_own, row_come, col_own, col_come, keep, send, high_ref, low_ref, share, top, text = refs
    for p in range(nc):
        text[block(p, b), :] = texts[p][...]
    cols = [merge(col_own[:, block(p, b)], col_come[:, block(p ^ 1, b)]) for p in range(nc)]
    col_t = jnp.concatenate([x[0:1] for x in cols], 1)
    col_s = jnp.concatenate([x[1:2] for x in cols], 1)
    gap = cols[0][1:2] - cols[0][0:1]
    half = nr // 2
    total = high_end = None
    for p in range(nr):
        rows = merge(row_own[:, block(p, b)], row_come[:, block(p ^ 1, b)])
        if p == 0:
            gap = gap + (rows[1:2] - rows[0:1])
        row = jnp.transpose(rows)
        tl, sl = tl_ref[block(p, b), :], sl_ref[block(p, b), :]
        row_t, col_prob_t = jnp.exp(tl - row[:, 0:1]), jnp.exp(tl - col_t)
        delta = (jnp.exp(sl - row[:, 1:2]) - row_t) + (jnp.exp(sl - col_s) - col_prob_t)
        part = jnp.sum((row_t + col_prob_t) * (tl - sl), 0, keepdims=True)
        total = part if total is None else total + part
        high = delta.astype(BF16)
        low = (delta - high.astype(F32)).astype(BF16)
        high_ref[block(p, b), :] = high
        low_ref[block(p, b), :] = low
        part = (matmul(high, text[...], 1, 0) + matmul(low, text[...], 1, 0)) * scale
        peak = jnp.max(jnp.abs(part), 0, keepdims=True)
        high_end = peak if high_end is None else jnp.maximum(high_end, peak)
        if p < half:
            keep[block(p, b), :] = part
        else:
            send[block(p - half, b), :] = part
    share[...] = jnp.broadcast_to(jnp.sum(total, 1, keepdims=True) + jnp.sum(gap, 1, keepdims=True), share.shape)
    high_end = jnp.max(high_end, 1, keepdims=True)
    top[...] = jnp.broadcast_to(high_end, top.shape)
    send[half * b :, :] = jnp.broadcast_to(high_end, (send.shape[0] - half * b, send.shape[1]))


def text_kernel(nr, nc, b, scale, *refs):
    images, refs = refs[:nr], refs[nr:]
    high_ref, low_ref, keep, send, top, image = refs
    for p in range(nr):
        image[block(p, b), :] = images[p][...]
    half = nc // 2
    high_end = None
    for p in range(nc):
        high, low = high_ref[:, block(p, b)], low_ref[:, block(p, b)]
        part = (matmul(high, image[...], 0, 0) + matmul(low, image[...], 0, 0)) * scale
        peak = jnp.max(jnp.abs(part), axis=(0, 1), keepdims=True)
        high_end = peak if high_end is None else jnp.maximum(high_end, peak)
        if p < half:
            keep[block(p, b), :] = part
        else:
            send[block(p - half, b), :] = part
    top[...] = jnp.broadcast_to(high_end, top.shape)


def call(kernel, outs, args, scratch=(), flops=0, transcendentals=0):
    shapes = [jax.ShapeDtypeStruct(s, d) for s, d in outs]
    size = sum(x.size * x.dtype.itemsize for x in list(args) + shapes)
    return pl.pallas_call(
        kernel,
        out_shape=shapes,
        in_specs=[VMEM] * len(args),
        out_specs=[VMEM] * len(shapes),
        scratch_shapes=[pltpu.VMEM(s, d) for s, d in scratch],
        compiler_params=PARAMS,
        cost_estimate=pl.CostEstimate(flops=flops, bytes_accessed=size, transcendentals=transcendentals),
    )(*args)


def swap(bit, x):
    return lax.ppermute(x, bit, [(0, 1), (1, 0)])


def after(x, done):
    return lax.optimization_barrier((x, done))[0]


def gather(bits, teacher, student):
    teachers, students = [teacher], [student]
    for bit in bits:
        first = swap(bit, teacher)
        second = swap(bit, after(student, first))
        teachers = teachers + [first] + [swap(bit, after(x, second)) for x in teachers[1:]]
        students = students + [second] + [swap(bit, x) for x in students[1:]]
    return teachers, students


def message(x, bound):
    power = jnp.ceil(jnp.log2(jnp.maximum(bound, 1e-30)))
    return jnp.concatenate([(x * jnp.exp2(14.0 - power)).astype(F16), jnp.full((EXTRA, x.shape[1]), power, F16)])


def add_message(keep, come, bound):
    rows = come.shape[0] - EXTRA
    power = come[rows, 0].astype(F32)
    return keep + come[:rows].astype(F32) * jnp.exp2(power - 14.0), bound + jnp.exp2(power)


def halves(x):
    return x[: x.shape[0] // 2], x[x.shape[0] // 2 :]


def local(image_bits, text_bits, teacher_image, teacher_text, student_image, student_text):
    b, tw = teacher_image.shape
    sw = student_image.shape[1]
    nr, nc = 1 << len(image_bits), 1 << len(text_bits)
    r, c = nr * b, nc * b
    ti, si = gather(image_bits, teacher_image, student_image)
    tt, st = gather(text_bits, teacher_text, student_text)
    tl, rows = call(
        functools.partial(logit_kernel, nr, nc, b, tw**-0.5, 0),
        [((r, c), F32), ((LINES, r), F32)], ti + tt, [((c, tw), BF16)], 2 * r * c * tw, r * c,
    )
    (cols,) = call(functools.partial(column_kernel, 0), [((LINES, c), F32)], [tl], (), 4 * r * c, r * c)
    sl, rows = call(
        functools.partial(logit_kernel, nr, nc, b, sw**-0.5, 1),
        [((r, c), F32), ((LINES, r), F32)], si + st + [rows], [((c, sw), BF16)], 2 * r * c * sw, r * c,
    )
    (cols,) = call(functools.partial(column_kernel, 1), [((LINES, c), F32)], [sl, cols], (), 4 * r * c, r * c)
    rounds = max(len(image_bits), len(text_bits))
    row_come = col_come = None
    for k in reversed(range(rounds)):
        todo = []
        if k < len(image_bits):
            row_come = swap(image_bits[k], rows)
            todo.append((rows, row_come))
        if k < len(text_bits):
            col_come = swap(text_bits[k], cols)
            todo.append((cols, col_come))
        if k:
            args = [x for pair in todo for x in pair]
            outs = list(call(
                functools.partial(merge_kernel, b, [1 << k] * len(todo)), [(x.shape, F32) for x, _ in todo], args)
            )
            if k < len(text_bits):
                cols = outs.pop()
            if k < len(image_bits):
                rows = outs.pop()
    lanes = ((8, 128), F32)
    keep, send, high, low, share, top = call(
        functools.partial(image_kernel, nr, nc, b, sw**-0.5),
        [((r // 2, sw), F32), ((r // 2 + 8, sw), F32), ((r, c), BF16), ((r, c), BF16), lanes, lanes],
        st + [tl, sl, rows, row_come, cols, col_come], [((c, sw), BF16)], 4 * r * c * sw, 4 * r * c,
    )
    come = swap(image_bits[-1], send)
    share_bits = list(text_bits[:1] + image_bits[:1] + text_bits[1:] + image_bits[1:])
    share = share + swap(share_bits.pop(), share)
    text_keep, text_send, text_top = call(
        functools.partial(text_kernel, nr, nc, b, sw**-0.5),
        [((c // 2, sw), F32), ((c // 2, sw), F32), lanes], si + [high, low], [((r, sw), BF16)], 4 * r * c * sw,
    )
    text_bound, image_bound = text_top[0, 0], top[0, 0] + come[r // 2, 0]
    text_note = message(text_send, text_bound)
    text_come = swap(text_bits[-1], text_note)
    image_keep, image_send = halves(keep + come[: r // 2])
    image_note = message(image_send, image_bound)
    image_come = swap(image_bits[-2], image_note)
    share = after(share, image_note)
    share = share + swap(share_bits.pop(), share)
    text_total, text_bound = add_message(text_keep, after(text_come, image_note), text_bound)
    image_total, image_bound = add_message(image_keep, image_come, image_bound)
    for k in reversed(range(max(len(text_bits) - 1, len(image_bits) - 2))):
        if k < len(text_bits) - 1:
            text_keep, text_send = halves(text_total)
            text_note = message(text_send, text_bound)
            text_come = swap(text_bits[k], text_note)
        if k < len(image_bits) - 2:
            image_keep, image_send = halves(image_total)
            image_note = message(image_send, image_bound)
            image_come = swap(image_bits[k], image_note)
        if k < len(text_bits) - 1:
            text_total, text_bound = add_message(text_keep, after(text_come, image_note), text_bound)
        if k < len(image_bits) - 2:
            image_total, image_bound = add_message(image_keep, after(image_come, text_note), image_bound)
    share = after(share, (text_note, image_note))
    while share_bits:
        share = share + swap(share_bits.pop(), share)
    image_grad, text_grad = image_total, text_total
    pairs = b << (len(image_bits) + len(text_bits))
    return (share[0, 0] / (2.0 * pairs), image_grad, text_grad)


def solution(mesh):
    bits = {axis: [f"{axis}{k}" for k in reversed(range(mesh.shape[axis].bit_length() - 1))] for axis in ("img", "txt")}
    names = bits["img"] + bits["txt"]
    cube = Mesh(np.asarray(mesh.devices).reshape((2,) * len(names)), names)
    text_bits = [x for x in bits["img"] if int(x[3:]) >= 1] + [x for x in bits["txt"] if int(x[3:]) % 2 == 1]
    image_bits = [x for x in names if x not in text_bits]
    image, text = P(tuple(names), None), P(tuple(bits["txt"] + bits["img"]), None)
    return jax.shard_map(
        functools.partial(local, tuple(image_bits), tuple(text_bits)),
        mesh=cube,
        in_specs=(image, text, image, text),
        out_specs=(P(), image, text),
        check_vma=False,
    )
```

time: 113 us -> 135 us (1.19)
  blocking collectives: 20.3 us -> 0 us
  starting transfers between devices: 15.1 us -> 33.3 us
  Pallas kernels: 16.1 us -> 27.3 us
  local copies, waits for them, and re-layouts: 4.66 us -> 10.6 us
  between operations: 3.18 us -> 8.58 us
    all_to_all x2 -> x0, blocking collectives: 20.3 us -> none  [the longest x1 10.6 us: local(): row_lines = lax.all_to_all(row_lines, row_axes, 0, 0, tiled=True)]
    ppermute x15 -> x35, starting transfers between devices: 15.1 us -> 33.3 us  [swap(): return lax.ppermute(x, bit, [(0, 1), (1, 0)])]
    pallas_call x2 -> x8, Pallas kernels: 16.1 us -> 27.3 us  [call(): pl.pallas_call(kernel, out_shape=shapes, in_specs=[VMEM] * len(args), out...]
    unnamed x22 -> x56, local copies, waits for them, and re-layouts: 1.11 us -> 4.84 us
    slice x13 -> x8, local copies, waits for them, and re-layouts: 2.62 us -> 5.62 us  [the longest x3 3.05 us: local(): text_bound, image_bound = (text_top[0, 0], top[0, 0] + come[r // 2, 0])]
    ppermute x15 -> x35, waiting for transfers between devices: 50.9 us -> 52.1 us  [swap(): return lax.ppermute(x, bit, [(0, 1), (1, 0)])]
  transfers between devices with their start and end apart: 15 -> 35, of which waited for: 9 -> 15; matrix products, arithmetic and copies ran while one was open for 3% -> 5% of each run, Pallas kernels for 0% -> 11%
where the time goes in v2:
time: 135 us; the launch traced here: 134 us
  waiting for transfers between devices  52.1 us (39%)
  starting transfers between devices  33.3 us (25%)
  Pallas kernels  27.3 us (20%)
  local copies, waits for them, and re-layouts  10.6 us (8%)
  between operations  8.58 us (6%)
  other arithmetic  2.47 us (2%)
    ppermute x35, waiting for transfers between devices, swap(): return lax.ppermute(x, bit, [(0, 1), (1, 0)])  52.1 us
    ppermute x35, starting transfers between devices, swap(): return lax.ppermute(x, bit, [(0, 1), (1, 0)])  33.3 us
    pallas_call x8, Pallas kernels, call(): pl.pallas_call(kernel, out_shape=shapes, in_specs=[VMEM] * len(args), out...  27.3 us
    unnamed x56, local copies, waits for them, and re-layouts  4.84 us
    slice x3, local copies, waits for them, and re-layouts, local(): text_bound, image_bound = (text_top[0, 0], top[0, 0] + come[r // 2, 0])  3.05 us
  transfers between devices with their start and end apart: 35, of which 15 were waited for; matrix products, arithmetic and copies ran while one was open for 5% of the time, Pallas kernels for 11%

profile of v2, /device:TPU:0, one launch (start us, length us, event | category | flops | bytes accessed | tf_op | source)
XLA Modules:
  0.0 134.5 jit_solution(10998414232024530879)
XLA Ops:
  0.6 3.0 %collective-permute-start.6 = (bf16[128,1280]{1,0:T(8,128)(2,1)}, bf16[128,1280]{1,0:T(8,128)(2,1)S(1)}, u32[]{:S(2)}, u32[]{:S(2)}) collective-permute-start(bf16[128,1280]{1,0:T(8,128)(2,1)} %refs_0_.4), channel_id=1, source_target_pairs={{0,4},{4,0},{1,5},{5,1},{2,6},{6,2},{3,7},{7,3},{8,12},{12,8},{9,1... | collective-permute-start | bytes 983048 | tf_op jit(solution)/shard_map/ppermute | solution.py:153
  3.7 1.6 %collective-permute-start.5 = (bf16[128,1280]{1,0:T(8,128)(2,1)}, bf16[128,1280]{1,0:T(8,128)(2,1)S(1)}, u32[]{:S(2)}, u32[]{:S(2)}) collective-permute-start(bf16[128,1280]{1,0:T(8,128)(2,1)} %refs_0_.4), channel_id=1, source_target_pairs={{0,8},{8,0},{1,9},{9,1},{2,10},{10,2},{3,11},{11,3},{4,12},{12,4},... | collective-permute-start | bytes 983048 | tf_op jit(solution)/shard_map/ppermute | solution.py:153
  6.7 4.8 %collective-permute-done.6.refs_2_ = bf16[128,1280]{1,0:T(8,128)(2,1)S(1)} collective-permute-done((bf16[128,1280]{1,0:T(8,128)(2,1)}, bf16[128,1280]{1,0:T(8,128)(2,1)S(1)}, u32[]{:S(2)}, u32[]{:S(2)}) %collective-permute-start.6) | collective-permute-done | bytes 327712 | tf_op jit(solution)/shard_map/ppermute | solution.py:153
  11.6 1.7 %collective-permute-start.7 = (bf16[128,512]{1,0:T(8,128)(2,1)}, bf16[128,512]{1,0:T(8,128)(2,1)S(1)}, u32[]{:S(2)}, u32[]{:S(2)}) collective-permute-start(bf16[128,512]{1,0:T(8,128)(2,1)} %refs_0_.7), channel_id=1, source_target_pairs={{0,4},{4,0},{1,5},{5,1},{2,6},{6,2},{3,7},{7,3},{8,12},{12,8},{9,1... | collective-permute-start | bytes 393224 | tf_op jit(solution)/shard_map/ppermute | solution.py:153
  13.3 2.6 %collective-permute-start = (bf16[128,1280]{1,0:T(8,128)(2,1)}, bf16[128,1280]{1,0:T(8,128)(2,1)S(1)}, u32[]{:S(2)}, u32[]{:S(2)}) collective-permute-start(bf16[128,1280]{1,0:T(8,128)(2,1)} %refs_8_.2), channel_id=1, source_target_pairs={{0,16},{16,0},{1,17},{17,1},{2,18},{18,2},{3,19},{19,3},{4,20},{20... | collective-permute-start | bytes 983048 | tf_op jit(solution)/shard_map/ppermute | solution.py:153
  16.8 1.7 %collective-permute-start.8 = (bf16[128,1280]{1,0:T(8,128)(2,1)S(1)}, bf16[128,1280]{1,0:T(8,128)(2,1)S(1)}, u32[]{:S(2)}, u32[]{:S(2)}) collective-permute-start(bf16[128,1280]{1,0:T(8,128)(2,1)S(1)} %collective-permute-done.5.refs_1_), channel_id=1, source_target_pairs={{0,4},{4,0},{1,5},{5,1},{2,6},{6,2},{3,7},{7,3},{8,12},{12,8},{9,1... | collective-permute-start | bytes 983048 | tf_op jit(solution)/shard_map/ppermute | solution.py:153
  18.5 1.5 %collective-permute-start.3 = (bf16[128,512]{1,0:T(8,128)(2,1)}, bf16[128,512]{1,0:T(8,128)(2,1)S(1)}, u32[]{:S(2)}, u32[]{:S(2)}) collective-permute-start(bf16[128,512]{1,0:T(8,128)(2,1)} %refs_0_.6), channel_id=1, source_target_pairs={{0,2},{2,0},{1,3},{3,1},{4,6},{6,4},{5,7},{7,5},{8,10},{10,8},{9,1... | collective-permute-start | bytes 393224 | tf_op jit(solution)/shard_map/ppermute | solution.py:153
  20.0 9.7 %collective-permute-done.refs_9_ = bf16[128,1280]{1,0:T(8,128)(2,1)S(1)} collective-permute-done((bf16[128,1280]{1,0:T(8,128)(2,1)}, bf16[128,1280]{1,0:T(8,128)(2,1)S(1)}, u32[]{:S(2)}, u32[]{:S(2)}) %collective-permute-start) | collective-permute-done | bytes 327712 | tf_op jit(solution)/shard_map/ppermute | solution.py:153
  29.8 1.6 %collective-permute-start.14 = (bf16[128,1280]{1,0:T(8,128)(2,1)S(1)}, bf16[128,1280]{1,0:T(8,128)(2,1)S(1)}, u32[]{:S(2)}, u32[]{:S(2)}) collective-permute-start(bf16[128,1280]{1,0:T(8,128)(2,1)S(1)} %collective-permute-done.refs_9_), channel_id=1, source_target_pairs={{0,2},{2,0},{1,3},{3,1},{4,6},{6,4},{5,7},{7,5},{8,10},{10,8},{9,1... | collective-permute-start | bytes 983048 | tf_op jit(solution)/shard_map/ppermute | solution.py:153
  31.9 6.6 %collective-permute-done.1.refs_9_.refs_1_ = bf16[128,512]{1,0:T(8,128)(2,1)S(1)} collective-permute-done((bf16[128,512]{1,0:T(8,128)(2,1)}, bf16[128,512]{1,0:T(8,128)(2,1)S(1)}, u32[]{:S(2)}, u32[]{:S(2)}) %collective-permute-start.1) | collective-permute-done | bytes 131104 | tf_op jit(solution)/shard_map/ppermute | solution.py:153
  38.6 5.2 %collective-permute-done.15.refs_1_ = bf16[128,512]{1,0:T(8,128)(2,1)S(1)} collective-permute-done((bf16[128,512]{1,0:T(8,128)(2,1)}, bf16[128,512]{1,0:T(8,128)(2,1)S(1)}, u32[]{:S(2)}, u32[]{:S(2)}) %collective-permute-start.15) | collective-permute-done | bytes 131104 | tf_op jit(solution)/shard_map/ppermute | solution.py:153
  44.2 4.5 %collective-permute-done.16.refs_3_ = bf16[128,512]{1,0:T(8,128)(2,1)S(1)} collective-permute-done((bf16[128,512]{1,0:T(8,128)(2,1)S(1)}, bf16[128,512]{1,0:T(8,128)(2,1)S(1)}, u32[]{:S(2)}, u32[]{:S(2)}) %collective-permute-start.16) | collective-permute-done | bytes 131104 | tf_op jit(solution)/shard_map/ppermute | solution.py:153
  48.7 1.6 %collective-permute-start.4 = (bf16[128,512]{1,0:T(8,128)(2,1)S(1)}, bf16[128,512]{1,0:T(8,128)(2,1)S(1)}, u32[]{:S(2)}, u32[]{:S(2)}) collective-permute-start(bf16[128,512]{1,0:T(8,128)(2,1)S(1)} %collective-permute-done.1.refs_9_.refs_1_), channel_id=1, source_target_pairs={{0,2},{2,0},{1,3},{3,1},{4,6},{6,4},{5,7},{7,5},{8,10},{10,8},{9,1... | collective-permute-start | bytes 393224 | tf_op jit(solution)/shard_map/ppermute | solution.py:153
  51.9 5.0 %shard_map.67 = (f32[1024,512]{1,0:T(8,128)}, f32[8,1024]{1,0:T(8,128)}) custom-call(bf16[128,1280]{1,0:T(8,128)(2,1)} %refs_0_.4, bf16[128,1280]{1,0:T(8,128)(2,1)} %copy-done.12, bf16[128,1280]{1,0:T(8,128)(2,1)} %copy-done.11, bf16[128,1280]{1,0:T(8,128)(2,1)} %copy-done.16, bf16[128,1280]{1,0:T(8,128)(2,1)} %copy-done.14, bf16[128,1280]{1,0:T(8,128)(2,1)} %copy-done.18, ...), custom_call_target="tpu_custom_call" | custom-call | flops 1342177280 | bytes 6062080 | tf_op jit(solution)/shard_map/pallas_call | solution.py:141
  57.7 3.6 %shard_map.68 = (f32[1024,512]{1,0:T(8,128)}, f32[8,1024]{1,0:T(8,128)}) custom-call(bf16[128,512]{1,0:T(8,128)(2,1)} %refs_0_.7, bf16[128,512]{1,0:T(8,128)(2,1)} %copy-done.23, bf16[128,512]{1,0:T(8,128)(2,1)} %copy-done.21, bf16[128,512]{1,0:T(8,128)(2,1)} %copy-done.24, bf16[128,512]{1,0:T(8,128)(2,1)} %copy-done.22, bf16[128,512]{1,0:T(8,128)(2,1)} %copy-done.26, ...), custom_call_target="tpu_custom_call" | custom-call | flops 536870912 | bytes 3735552 | tf_op jit(solution)/shard_map/pallas_call | solution.py:141
  65.3 2.7 %shard_map.70.refs_1_ = f32[8,512]{1,0:T(8,128)} custom-call(f32[1024,512]{1,0:T(8,128)} %get-tuple-element.42.refs_0_.refs_4_), custom_call_target="tpu_custom_call" | custom-call | flops 2097152 | bytes 2113536 | tf_op jit(solution)/shard_map/pallas_call | solution.py:141
  68.0 2.7 %shard_map.71.refs_2_ = f32[8,512]{1,0:T(8,128)} custom-call(f32[1024,512]{1,0:T(8,128)} %get-tuple-element.45.refs_0_.refs_5_, f32[8,512]{1,0:T(8,128)} %shard_map.70.refs_1_), custom_call_target="tpu_custom_call" | custom-call | flops 2097152 | bytes 2129920 | tf_op jit(solution)/shard_map/pallas_call | solution.py:141
  71.3 3.4 %collective-permute-done.22.refs_3_ = f32[8,512]{1,0:T(8,128)S(1)} collective-permute-done((f32[8,512]{1,0:T(8,128)}, f32[8,512]{1,0:T(8,128)S(1)}, u32[]{:S(2)}, u32[]{:S(2)}) %collective-permute-start.22) | collective-permute-done | bytes 16416 | tf_op jit(solution)/shard_map/ppermute | solution.py:153
  77.3 1.8 %collective-permute-start.24 = (f32[8,512]{1,0:T(8,128)}, f32[8,512]{1,0:T(8,128)S(1)}, u32[]{:S(2)}, u32[]{:S(2)}) collective-permute-start(f32[8,512]{1,0:T(8,128)} %get-tuple-element.48.refs_8_), channel_id=1, source_target_pairs={{0,16},{16,0},{1,17},{17,1},{2,18},{18,2},{3,19},{19,3},{4,20},{20... | collective-permute-start | bytes 49160 | tf_op jit(solution)/shard_map/ppermute | solution.py:153
  79.1 3.1 %collective-permute-done.24.refs_9_ = f32[8,512]{1,0:T(8,128)S(1)} collective-permute-done((f32[8,512]{1,0:T(8,128)}, f32[8,512]{1,0:T(8,128)S(1)}, u32[]{:S(2)}, u32[]{:S(2)}) %collective-permute-start.24) | collective-permute-done | bytes 16416 | tf_op jit(solution)/shard_map/ppermute | solution.py:153
  83.4 6.5 %shard_map.73 = (f32[512,512]{1,0:T(8,128)}, f32[520,512]{1,0:T(8,128)}, bf16[1024,512]{1,0:T(8,128)(2,1)}, bf16[1024,512]{1,0:T(8,128)(2,1)}, f32[8,128]{1,0:T(8,128)}, /*index=5*/f32[8,128]{1,0:T(8,128)}) custom-call(bf16[128,512]{1,0:T(8,128)(2,1)} %refs_0_.6, bf16[128,512]{1,0:T(8,128)(2,1)} %copy-done.3, bf16[128,512]{1,0:T(8,128)(2,1)} %copy-done.2, ...), custom_call_target="tpu_custom_call" | custom-call | flops 1073741824 | bytes 9035776 | tf_op jit(solution)/shard_map/pallas_call | solution.py:141
  91.1 4.0 %shard_map.74 = (f32[256,512]{1,0:T(8,128)}, f32[256,512]{1,0:T(8,128)}, f32[8,128]{1,0:T(8,128)}) custom-call(bf16[128,512]{1,0:T(8,128)(2,1)} %refs_0_.7, bf16[128,512]{1,0:T(8,128)(2,1)} %copy-done.23, bf16[128,512]{1,0:T(8,128)(2,1)} %copy-done.21, bf16[128,512]{1,0:T(8,128)(2,1)} %copy-done.24, bf16[128,512]{1,0:T(8,128)(2,1)} %copy-done.22, ...), custom_call_target="tpu_custom_call" | custom-call | flops 1073741824 | bytes 4198400 | tf_op jit(solution)/shard_map/pallas_call | solution.py:141
  101.1 1.6 %collective-permute-start.29 = (f16[272,512]{1,0:T(8,128)(2,1)S(1)}, f16[272,512]{1,0:T(8,128)(2,1)S(1)}, u32[]{:S(2)}, u32[]{:S(2)}) collective-permute-start(f16[272,512]{1,0:T(8,128)(2,1)S(1)} %concatenate.12), channel_id=1, source_target_pairs={{0,4},{4,0},{1,5},{5,1},{2,6},{6,2},{3,7},{7,3},{8,12},{12,8},{9,1... | collective-permute-start | bytes 835592 | tf_op jit(solution)/shard_map/ppermute | solution.py:153
  102.7 4.7 %collective-permute-done.28 = f16[272,512]{1,0:T(8,128)(2,1)S(1)} collective-permute-done((f16[272,512]{1,0:T(8,128)(2,1)S(1)}, f16[272,512]{1,0:T(8,128)(2,1)S(1)}, u32[]{:S(2)}, u32[]{:S(2)}) %collective-permute-start.28) | collective-permute-done | bytes 278560 | tf_op jit(solution)/shard_map/ppermute | solution.py:153
  109.6 1.8 %collective-permute-start.34 = (f16[144,512]{1,0:T(8,128)(2,1)S(1)}, f16[144,512]{1,0:T(8,128)(2,1)S(1)}, u32[]{:S(2)}, u32[]{:S(2)}) collective-permute-start(f16[144,512]{1,0:T(8,128)(2,1)S(1)} %concatenate.14), channel_id=1, source_target_pairs={{0,16},{16,0},{1,17},{17,1},{2,18},{18,2},{3,19},{19,3},{4,20},{20... | collective-permute-start | bytes 442376 | tf_op jit(solution)/shard_map/ppermute | solution.py:153
  114.8 1.5 %collective-permute-start.27 = (f32[8,128]{1,0:T(8,128)S(1)}, f32[8,128]{1,0:T(8,128)S(1)}, u32[]{:S(2)}, u32[]{:S(2)}) collective-permute-start(f32[8,128]{1,0:T(8,128)S(1)} %add.62), channel_id=1, source_target_pairs={{0,4},{4,0},{1,5},{5,1},{2,6},{6,2},{3,7},{7,3},{8,12},{12,8},{9,1... | collective-permute-start | bytes 12296 | tf_op jit(solution)/shard_map/ppermute | solution.py:153
  116.3 2.1 %collective-permute-done.27 = f32[8,128]{1,0:T(8,128)S(1)} collective-permute-done((f32[8,128]{1,0:T(8,128)S(1)}, f32[8,128]{1,0:T(8,128)S(1)}, u32[]{:S(2)}, u32[]{:S(2)}) %collective-permute-start.27) | collective-permute-done | bytes 4128 | tf_op jit(solution)/shard_map/ppermute | solution.py:153
  118.4 1.5 %collective-permute-start.30 = (f32[8,128]{1,0:T(8,128)S(1)}, f32[8,128]{1,0:T(8,128)S(1)}, u32[]{:S(2)}, u32[]{:S(2)}) collective-permute-start(f32[8,128]{1,0:T(8,128)S(1)} %add.65), channel_id=1, source_target_pairs={{0,2},{2,0},{1,3},{3,1},{4,6},{6,4},{5,7},{7,5},{8,10},{10,8},{9,1... | collective-permute-start | bytes 12296 | tf_op jit(solution)/shard_map/ppermute | solution.py:153
  119.9 2.1 %collective-permute-done.30 = f32[8,128]{1,0:T(8,128)S(1)} collective-permute-done((f32[8,128]{1,0:T(8,128)S(1)}, f32[8,128]{1,0:T(8,128)S(1)}, u32[]{:S(2)}, u32[]{:S(2)}) %collective-permute-start.30) | collective-permute-done | bytes 4128 | tf_op jit(solution)/shard_map/ppermute | solution.py:153
  122.0 1.5 %collective-permute-start.31 = (f32[8,128]{1,0:T(8,128)S(1)}, f32[8,128]{1,0:T(8,128)S(1)}, u32[]{:S(2)}, u32[]{:S(2)}) collective-permute-start(f32[8,128]{1,0:T(8,128)S(1)} %add.72), channel_id=1, source_target_pairs={{0,8},{8,0},{1,9},{9,1},{2,10},{10,2},{3,11},{11,3},{4,12},{12,4},... | collective-permute-start | bytes 12296 | tf_op jit(solution)/shard_map/ppermute | solution.py:153
  123.5 2.1 %collective-permute-done.31 = f32[8,128]{1,0:T(8,128)S(1)} collective-permute-done((f32[8,128]{1,0:T(8,128)S(1)}, f32[8,128]{1,0:T(8,128)S(1)}, u32[]{:S(2)}, u32[]{:S(2)}) %collective-permute-start.31) | collective-permute-done | bytes 4128 | tf_op jit(solution)/shard_map/ppermute | solution.py:153
  125.6 2.7 %collective-permute-start.32 = (f32[8,128]{1,0:T(8,128)S(1)}, f32[8,128]{1,0:T(8,128)S(1)}, u32[]{:S(2)}, u32[]{:S(2)}) collective-permute-start(f32[8,128]{1,0:T(8,128)S(1)} %add.73), channel_id=1, source_target_pairs={{0,16},{16,0},{1,17},{17,1},{2,18},{18,2},{3,19},{19,3},{4,20},{20... | collective-permute-start | bytes 12296 | tf_op jit(solution)/shard_map/ppermute | solution.py:153
  (127 shorter events, 25.4 us)
Async XLA Ops:
  0.6 11.0 %collective-permute-start.6 = (bf16[128,1280]{1,0:T(8,128)(2,1)}, bf16[128,1280]{1,0:T(8,128)(2,1)S(1)}, u32[]{:S(2)}, u32[]{:S(2)}) collective-permute-start(bf16[128,1280]{1,0:T(8,128)(2,1)} %refs_0_.4), channel_id=1, source_target_pairs={{0,4},{4,0},{1,5},{5,1},{2,6},{6,2},{3,7},{7,3},{8,12},{12,8},{9,1... | collective-permute-start | bytes 983048 | tf_op jit(solution)/shard_map/ppermute | solution.py:153
  3.7 12.3 %collective-permute-start.5 = (bf16[128,1280]{1,0:T(8,128)(2,1)}, bf16[128,1280]{1,0:T(8,128)(2,1)S(1)}, u32[]{:S(2)}, u32[]{:S(2)}) collective-permute-start(bf16[128,1280]{1,0:T(8,128)(2,1)} %refs_0_.4), channel_id=1, source_target_pairs={{0,8},{8,0},{1,9},{9,1},{2,10},{10,2},{3,11},{11,3},{4,12},{12,4},... | collective-permute-start | bytes 983048 | tf_op jit(solution)/shard_map/ppermute | solution.py:153
  5.2 13.3 %collective-permute-start.2 = (bf16[128,1280]{1,0:T(8,128)(2,1)}, bf16[128,1280]{1,0:T(8,128)(2,1)S(1)}, u32[]{:S(2)}, u32[]{:S(2)}) collective-permute-start(bf16[128,1280]{1,0:T(8,128)(2,1)} %refs_8_.2), channel_id=1, source_target_pairs={{0,2},{2,0},{1,3},{3,1},{4,6},{6,4},{5,7},{7,5},{8,10},{10,8},{9,1... | collective-permute-start | bytes 983048 | tf_op jit(solution)/shard_map/ppermute | solution.py:153
  6.7 13.3 %collective-permute-start.9 = (bf16[128,1280]{1,0:T(8,128)(2,1)}, bf16[128,1280]{1,0:T(8,128)(2,1)S(1)}, u32[]{:S(2)}, u32[]{:S(2)}) collective-permute-start(bf16[128,1280]{1,0:T(8,128)(2,1)} %refs_0_.4), channel_id=1, source_target_pairs={{0,1},{1,0},{2,3},{3,2},{4,5},{5,4},{6,7},{7,6},{8,9},{9,8},{10,11... | collective-permute-start | bytes 983048 | tf_op jit(solution)/shard_map/ppermute | solution.py:153
  11.6 5.2 %collective-permute-start.7 = (bf16[128,512]{1,0:T(8,128)(2,1)}, bf16[128,512]{1,0:T(8,128)(2,1)S(1)}, u32[]{:S(2)}, u32[]{:S(2)}) collective-permute-start(bf16[128,512]{1,0:T(8,128)(2,1)} %refs_0_.7), channel_id=1, source_target_pairs={{0,4},{4,0},{1,5},{5,1},{2,6},{6,2},{3,7},{7,3},{8,12},{12,8},{9,1... | collective-permute-start | bytes 393224 | tf_op jit(solution)/shard_map/ppermute | solution.py:153
  13.3 16.4 %collective-permute-start = (bf16[128,1280]{1,0:T(8,128)(2,1)}, bf16[128,1280]{1,0:T(8,128)(2,1)S(1)}, u32[]{:S(2)}, u32[]{:S(2)}) collective-permute-start(bf16[128,1280]{1,0:T(8,128)(2,1)} %refs_8_.2), channel_id=1, source_target_pairs={{0,16},{16,0},{1,17},{17,1},{2,18},{18,2},{3,19},{19,3},{4,20},{20... | collective-permute-start | bytes 983048 | tf_op jit(solution)/shard_map/ppermute | solution.py:153
  16.8 15.1 %collective-permute-start.8 = (bf16[128,1280]{1,0:T(8,128)(2,1)S(1)}, bf16[128,1280]{1,0:T(8,128)(2,1)S(1)}, u32[]{:S(2)}, u32[]{:S(2)}) collective-permute-start(bf16[128,1280]{1,0:T(8,128)(2,1)S(1)} %collective-permute-done.5.refs_1_), channel_id=1, source_target_pairs={{0,4},{4,0},{1,5},{5,1},{2,6},{6,2},{3,7},{7,3},{8,12},{12,8},{9,1... | collective-permute-start | bytes 983048 | tf_op jit(solution)/shard_map/ppermute | solution.py:153
  18.5 11.3 %collective-permute-start.3 = (bf16[128,512]{1,0:T(8,128)(2,1)}, bf16[128,512]{1,0:T(8,128)(2,1)S(1)}, u32[]{:S(2)}, u32[]{:S(2)}) collective-permute-start(bf16[128,512]{1,0:T(8,128)(2,1)} %refs_0_.6), channel_id=1, source_target_pairs={{0,2},{2,0},{1,3},{3,1},{4,6},{6,4},{5,7},{7,5},{8,10},{10,8},{9,1... | collective-permute-start | bytes 393224 | tf_op jit(solution)/shard_map/ppermute | solution.py:153
  20.0 11.3 %collective-permute-start.10 = (bf16[128,512]{1,0:T(8,128)(2,1)}, bf16[128,512]{1,0:T(8,128)(2,1)S(1)}, u32[]{:S(2)}, u32[]{:S(2)}) collective-permute-start(bf16[128,512]{1,0:T(8,128)(2,1)} %refs_0_.7), channel_id=1, source_target_pairs={{0,1},{1,0},{2,3},{3,2},{4,5},{5,4},{6,7},{7,6},{8,9},{9,8},{10,11... | collective-permute-start | bytes 393224 | tf_op jit(solution)/shard_map/ppermute | solution.py:153
  29.8 8.8 %collective-permute-start.1 = (bf16[128,512]{1,0:T(8,128)(2,1)}, bf16[128,512]{1,0:T(8,128)(2,1)S(1)}, u32[]{:S(2)}, u32[]{:S(2)}) collective-permute-start(bf16[128,512]{1,0:T(8,128)(2,1)} %refs_0_.6), channel_id=1, source_target_pairs={{0,16},{16,0},{1,17},{17,1},{2,18},{18,2},{3,19},{19,3},{4,20},{20... | collective-permute-start | bytes 393224 | tf_op jit(solution)/shard_map/ppermute | solution.py:153
  29.8 18.9 %collective-permute-start.14 = (bf16[128,1280]{1,0:T(8,128)(2,1)S(1)}, bf16[128,1280]{1,0:T(8,128)(2,1)S(1)}, u32[]{:S(2)}, u32[]{:S(2)}) collective-permute-start(bf16[128,1280]{1,0:T(8,128)(2,1)S(1)} %collective-permute-done.refs_9_), channel_id=1, source_target_pairs={{0,2},{2,0},{1,3},{3,1},{4,6},{6,4},{5,7},{7,5},{8,10},{10,8},{9,1... | collective-permute-start | bytes 983048 | tf_op jit(solution)/shard_map/ppermute | solution.py:153
  31.3 18.9 %collective-permute-start.11 = (bf16[128,1280]{1,0:T(8,128)(2,1)S(1)}, bf16[128,1280]{1,0:T(8,128)(2,1)S(1)}, u32[]{:S(2)}, u32[]{:S(2)}) collective-permute-start(bf16[128,1280]{1,0:T(8,128)(2,1)S(1)} %collective-permute-done.5.refs_1_), channel_id=1, source_target_pairs={{0,1},{1,0},{2,3},{3,2},{4,5},{5,4},{6,7},{7,6},{8,9},{9,8},{10,11... | collective-permute-start | bytes 983048 | tf_op jit(solution)/shard_map/ppermute | solution.py:153
  31.3 19.1 %collective-permute-start.12 = (bf16[128,1280]{1,0:T(8,128)(2,1)S(1)}, bf16[128,1280]{1,0:T(8,128)(2,1)S(1)}, u32[]{:S(2)}, u32[]{:S(2)}) collective-permute-start(bf16[128,1280]{1,0:T(8,128)(2,1)S(1)} %collective-permute-done.6.refs_2_), channel_id=1, source_target_pairs={{0,1},{1,0},{2,3},{3,2},{4,5},{5,4},{6,7},{7,6},{8,9},{9,8},{10,11... | collective-permute-start | bytes 983048 | tf_op jit(solution)/shard_map/ppermute | solution.py:153
  31.9 19.0 %collective-permute-start.13 = (bf16[128,1280]{1,0:T(8,128)(2,1)S(1)}, bf16[128,1280]{1,0:T(8,128)(2,1)S(1)}, u32[]{:S(2)}, u32[]{:S(2)}) collective-permute-start(bf16[128,1280]{1,0:T(8,128)(2,1)S(1)} %collective-permute-done.8.refs_3_), channel_id=1, source_target_pairs={{0,1},{1,0},{2,3},{3,2},{4,5},{5,4},{6,7},{7,6},{8,9},{9,8},{10,11... | collective-permute-start | bytes 983048 | tf_op jit(solution)/shard_map/ppermute | solution.py:153
  38.6 5.2 %collective-permute-start.15 = (bf16[128,512]{1,0:T(8,128)(2,1)}, bf16[128,512]{1,0:T(8,128)(2,1)S(1)}, u32[]{:S(2)}, u32[]{:S(2)}) collective-permute-start(bf16[128,512]{1,0:T(8,128)(2,1)} %refs_0_.7), channel_id=1, source_target_pairs={{0,8},{8,0},{1,9},{9,1},{2,10},{10,2},{3,11},{11,3},{4,12},{12,4},... | collective-permute-start | bytes 393224 | tf_op jit(solution)/shard_map/ppermute | solution.py:153
  43.7 5.0 %collective-permute-start.16 = (bf16[128,512]{1,0:T(8,128)(2,1)S(1)}, bf16[128,512]{1,0:T(8,128)(2,1)S(1)}, u32[]{:S(2)}, u32[]{:S(2)}) collective-permute-start(bf16[128,512]{1,0:T(8,128)(2,1)S(1)} %collective-permute-done.15.refs_1_), channel_id=1, source_target_pairs={{0,4},{4,0},{1,5},{5,1},{2,6},{6,2},{3,7},{7,3},{8,12},{12,8},{9,1... | collective-permute-start | bytes 393224 | tf_op jit(solution)/shard_map/ppermute | solution.py:153
  48.7 8.2 %collective-permute-start.18 = (bf16[128,512]{1,0:T(8,128)(2,1)S(1)}, bf16[128,512]{1,0:T(8,128)(2,1)S(1)}, u32[]{:S(2)}, u32[]{:S(2)}) collective-permute-start(bf16[128,512]{1,0:T(8,128)(2,1)S(1)} %collective-permute-done.7.refs_2_), channel_id=1, source_target_pairs={{0,1},{1,0},{2,3},{3,2},{4,5},{5,4},{6,7},{7,6},{8,9},{9,8},{10,11... | collective-permute-start | bytes 393224 | tf_op jit(solution)/shard_map/ppermute | solution.py:153
  48.7 8.2 %collective-permute-start.4 = (bf16[128,512]{1,0:T(8,128)(2,1)S(1)}, bf16[128,512]{1,0:T(8,128)(2,1)S(1)}, u32[]{:S(2)}, u32[]{:S(2)}) collective-permute-start(bf16[128,512]{1,0:T(8,128)(2,1)S(1)} %collective-permute-done.1.refs_9_.refs_1_), channel_id=1, source_target_pairs={{0,2},{2,0},{1,3},{3,1},{4,6},{6,4},{5,7},{7,5},{8,10},{10,8},{9,1... | collective-permute-start | bytes 393224 | tf_op jit(solution)/shard_map/ppermute | solution.py:153
  50.3 6.7 %collective-permute-start.17 = (bf16[128,512]{1,0:T(8,128)(2,1)S(1)}, bf16[128,512]{1,0:T(8,128)(2,1)S(1)}, u32[]{:S(2)}, u32[]{:S(2)}) collective-permute-start(bf16[128,512]{1,0:T(8,128)(2,1)S(1)} %collective-permute-done.15.refs_1_), channel_id=1, source_target_pairs={{0,1},{1,0},{2,3},{3,2},{4,5},{5,4},{6,7},{7,6},{8,9},{9,8},{10,11... | collective-permute-start | bytes 393224 | tf_op jit(solution)/shard_map/ppermute | solution.py:153
  50.5 6.5 %collective-permute-start.19 = (bf16[128,512]{1,0:T(8,128)(2,1)S(1)}, bf16[128,512]{1,0:T(8,128)(2,1)S(1)}, u32[]{:S(2)}, u32[]{:S(2)}) collective-permute-start(bf16[128,512]{1,0:T(8,128)(2,1)S(1)} %collective-permute-done.16.refs_3_), channel_id=1, source_target_pairs={{0,1},{1,0},{2,3},{3,2},{4,5},{5,4},{6,7},{7,6},{8,9},{9,8},{10,11... | collective-permute-start | bytes 393224 | tf_op jit(solution)/shard_map/ppermute | solution.py:153
  64.8 9.9 %collective-permute-start.21 = (f32[8,1024]{1,0:T(8,128)}, f32[8,1024]{1,0:T(8,128)S(1)}, u32[]{:S(2)}, u32[]{:S(2)}) collective-permute-start(f32[8,1024]{1,0:T(8,128)} %shard_map.69.refs_0_), channel_id=1, source_target_pairs={{0,4},{4,0},{1,5},{5,1},{2,6},{6,2},{3,7},{7,3},{8,12},{12,8},{9,1... | collective-permute-start | bytes 98312 | tf_op jit(solution)/shard_map/ppermute | solution.py:153
  70.7 3.9 %collective-permute-start.22 = (f32[8,512]{1,0:T(8,128)}, f32[8,512]{1,0:T(8,128)S(1)}, u32[]{:S(2)}, u32[]{:S(2)}) collective-permute-start(f32[8,512]{1,0:T(8,128)} %shard_map.71.refs_2_), channel_id=1, source_target_pairs={{0,2},{2,0},{1,3},{3,1},{4,6},{6,4},{5,7},{7,5},{8,10},{10,8},{9,1... | collective-permute-start | bytes 49160 | tf_op jit(solution)/shard_map/ppermute | solution.py:153
  77.3 4.9 %collective-permute-start.23 = (f32[8,1024]{1,0:T(8,128)}, f32[8,1024]{1,0:T(8,128)S(1)}, u32[]{:S(2)}, u32[]{:S(2)}) collective-permute-start(f32[8,1024]{1,0:T(8,128)} %get-tuple-element.47.refs_6_), channel_id=1, source_target_pairs={{0,8},{8,0},{1,9},{9,1},{2,10},{10,2},{3,11},{11,3},{4,12},{12,4},... | collective-permute-start | bytes 98312 | tf_op jit(solution)/shard_map/ppermute | solution.py:153
  77.3 4.8 %collective-permute-start.24 = (f32[8,512]{1,0:T(8,128)}, f32[8,512]{1,0:T(8,128)S(1)}, u32[]{:S(2)}, u32[]{:S(2)}) collective-permute-start(f32[8,512]{1,0:T(8,128)} %get-tuple-element.48.refs_8_), channel_id=1, source_target_pairs={{0,16},{16,0},{1,17},{17,1},{2,18},{18,2},{3,19},{19,3},{4,20},{20... | collective-permute-start | bytes 49160 | tf_op jit(solution)/shard_map/ppermute | solution.py:153
  89.8 9.1 %collective-permute-start.26 = (f32[520,512]{1,0:T(8,128)}, f32[520,512]{1,0:T(8,128)S(1)}, u32[]{:S(2)}, u32[]{:S(2)}) collective-permute-start(f32[520,512]{1,0:T(8,128)} %get-tuple-element.51), channel_id=1, source_target_pairs={{0,1},{1,0},{2,3},{3,2},{4,5},{5,4},{6,7},{7,6},{8,9},{9,8},{10,11... | collective-permute-start | bytes 3194888 | tf_op jit(solution)/shard_map/ppermute | solution.py:153
  98.3 9.1 %collective-permute-start.28 = (f16[272,512]{1,0:T(8,128)(2,1)S(1)}, f16[272,512]{1,0:T(8,128)(2,1)S(1)}, u32[]{:S(2)}, u32[]{:S(2)}) collective-permute-start(f16[272,512]{1,0:T(8,128)(2,1)S(1)} %concatenate.13), channel_id=1, source_target_pairs={{0,2},{2,0},{1,3},{3,1},{4,6},{6,4},{5,7},{7,5},{8,10},{10,8},{9,1... | collective-permute-start | bytes 835592 | tf_op jit(solution)/shard_map/ppermute | solution.py:153
  101.1 10.3 %collective-permute-start.29 = (f16[272,512]{1,0:T(8,128)(2,1)S(1)}, f16[272,512]{1,0:T(8,128)(2,1)S(1)}, u32[]{:S(2)}, u32[]{:S(2)}) collective-permute-start(f16[272,512]{1,0:T(8,128)(2,1)S(1)} %concatenate.12), channel_id=1, source_target_pairs={{0,4},{4,0},{1,5},{5,1},{2,6},{6,2},{3,7},{7,3},{8,12},{12,8},{9,1... | collective-permute-start | bytes 835592 | tf_op jit(solution)/shard_map/ppermute | solution.py:153
  109.6 18.6 %collective-permute-start.34 = (f16[144,512]{1,0:T(8,128)(2,1)S(1)}, f16[144,512]{1,0:T(8,128)(2,1)S(1)}, u32[]{:S(2)}, u32[]{:S(2)}) collective-permute-start(f16[144,512]{1,0:T(8,128)(2,1)S(1)} %concatenate.14), channel_id=1, source_target_pairs={{0,16},{16,0},{1,17},{17,1},{2,18},{18,2},{3,19},{19,3},{4,20},{20... | collective-permute-start | bytes 442376 | tf_op jit(solution)/shard_map/ppermute | solution.py:153
  113.0 18.3 %collective-permute-start.33 = (f16[144,512]{1,0:T(8,128)(2,1)S(1)}, f16[144,512]{1,0:T(8,128)(2,1)S(1)}, u32[]{:S(2)}, u32[]{:S(2)}) collective-permute-start(f16[144,512]{1,0:T(8,128)(2,1)S(1)} %concatenate.15), channel_id=1, source_target_pairs={{0,8},{8,0},{1,9},{9,1},{2,10},{10,2},{3,11},{11,3},{4,12},{12,4},... | collective-permute-start | bytes 442376 | tf_op jit(solution)/shard_map/ppermute | solution.py:153
  114.8 3.6 %collective-permute-start.27 = (f32[8,128]{1,0:T(8,128)S(1)}, f32[8,128]{1,0:T(8,128)S(1)}, u32[]{:S(2)}, u32[]{:S(2)}) collective-permute-start(f32[8,128]{1,0:T(8,128)S(1)} %add.62), channel_id=1, source_target_pairs={{0,4},{4,0},{1,5},{5,1},{2,6},{6,2},{3,7},{7,3},{8,12},{12,8},{9,1... | collective-permute-start | bytes 12296 | tf_op jit(solution)/shard_map/ppermute | solution.py:153
  118.4 3.6 %collective-permute-start.30 = (f32[8,128]{1,0:T(8,128)S(1)}, f32[8,128]{1,0:T(8,128)S(1)}, u32[]{:S(2)}, u32[]{:S(2)}) collective-permute-start(f32[8,128]{1,0:T(8,128)S(1)} %add.65), channel_id=1, source_target_pairs={{0,2},{2,0},{1,3},{3,1},{4,6},{6,4},{5,7},{7,5},{8,10},{10,8},{9,1... | collective-permute-start | bytes 12296 | tf_op jit(solution)/shard_map/ppermute | solution.py:153
  125.6 4.5 %collective-permute-start.32 = (f32[8,128]{1,0:T(8,128)S(1)}, f32[8,128]{1,0:T(8,128)S(1)}, u32[]{:S(2)}, u32[]{:S(2)}) collective-permute-start(f32[8,128]{1,0:T(8,128)S(1)} %add.73), channel_id=1, source_target_pairs={{0,16},{16,0},{1,17},{17,1},{2,18},{18,2},{3,19},{19,3},{4,20},{20... | collective-permute-start | bytes 12296 | tf_op jit(solution)/shard_map/ppermute | solution.py:153
  (31 other events, 343.9 us)

commit v3 on v1

v3 whole, which is shorter than its diff:
```python
import functools

import jax
import jax.numpy as jnp
import numpy as np
from jax import lax
from jax.experimental import pallas as pl
from jax.experimental.pallas import tpu as pltpu
from jax.sharding import Mesh, PartitionSpec as P

F32 = jnp.float32
BF16 = jnp.bfloat16
F16 = jnp.float16
LOG2E = 1.4426950408889634
LN2 = 0.6931471805599453
LINES = 8
KINDS = 3
PARAMS = pltpu.CompilerParams(vmem_limit_bytes=56 * 2**20)
VMEM = pl.BlockSpec(memory_space=pltpu.VMEM)
SMEM = pl.BlockSpec(memory_space=pltpu.SMEM)


def matmul(a, b, da, db):
    return lax.dot_general(a, b, (((da,), (db,)), ((), ())), preferred_element_type=F32)


def block(k, b):
    return slice(k * b, (k + 1) * b)


def stack_rows(values, shape, axis, first=0):
    index = lax.broadcasted_iota(jnp.int32, shape, axis) - first
    out = jnp.zeros(shape, F32)
    for k, value in enumerate(values):
        out = jnp.where(index == k, value, out)
    return out


def tree(op, items):
    while len(items) > 1:
        items = [op(x, y) for x, y in zip(items[::2], items[1::2])]
    return items[0]


def stats_kernel(image_forms, text_forms, b, tw, scale_t, scale_s, core, *refs):
    nr, nc = len(image_forms), len(text_forms)
    ti, si, refs = views(refs, image_forms, tw)
    tt, st, refs = views(refs, text_forms, tw)
    tl_ref, sl_ref, row_ref, swap_ref, col_ref, text_t, text_s = refs
    for p in range(nc):
        text_t[block(p, b), :] = tt[p][...]
        text_s[block(p, b), :] = st[p][...]
    step = 2 if nr % 2 == 0 else 1
    count = step * b
    peak_t = peak_s = None
    for p in range(0, nr, step):
        rows = slice(p * b, p * b + count)
        tl = matmul(jnp.concatenate([x[...] for x in ti[p : p + step]], 0), text_t[...], 1, 1) * (scale_t * LOG2E)
        sl = matmul(jnp.concatenate([x[...] for x in si[p : p + step]], 0), text_s[...], 1, 1) * (scale_s * LOG2E)
        tl_ref[rows, :] = tl
        sl_ref[rows, :] = sl
        top_t, top_s = jnp.max(tl, 0, keepdims=True), jnp.max(sl, 0, keepdims=True)
        peak_t = top_t if peak_t is None else jnp.maximum(peak_t, top_t)
        peak_s = top_s if peak_s is None else jnp.maximum(peak_s, top_s)
        mt, ms = jnp.max(tl, 1, keepdims=True), jnp.max(sl, 1, keepdims=True)
        et = jnp.exp2(tl - mt)
        sum_t = jnp.sum(et, 1, keepdims=True)
        gap = jnp.sum(et * (tl - sl), 1, keepdims=True)
        sum_s = jnp.sum(jnp.exp2(sl - ms), 1, keepdims=True)
        lines = (mt + jnp.log2(sum_t), ms + jnp.log2(sum_s), gap / sum_t)
        lines = stack_rows(lines, (count, 128), 1, core[0] * KINDS)
        for k in range(step):
            flat = jnp.transpose(lines[block(k, b)])[:LINES]
            row_ref[:, block(p + k, b)] = flat
            swap_ref[:, block((p + k) ^ (nr // 2), b)] = flat
    sum_t = sum_s = gap = None
    for p in range(0, nr, step):
        tl, sl = tl_ref[p * b : p * b + count, :], sl_ref[p * b : p * b + count, :]
        et = jnp.exp2(tl - peak_t)
        parts = [
            jnp.sum(et, 0, keepdims=True),
            jnp.sum(jnp.exp2(sl - peak_s), 0, keepdims=True),
            jnp.sum(et * (tl - sl), 0, keepdims=True),
        ]
        sum_t, sum_s, gap = parts if p == 0 else [x + y for x, y in zip((sum_t, sum_s, gap), parts)]
    lines = (peak_t + jnp.log2(sum_t), peak_s + jnp.log2(sum_s), gap / sum_t)
    col_ref[...] = stack_rows(lines, col_ref.shape, 0)


def combine(tiles, terms):
    lses = []
    for kind in (1, 0):
        peak = tree(jnp.maximum, [x[kind] for x in tiles])
        weights = [jnp.exp2(x[kind] - peak) for x in tiles]
        total = tree(jnp.add, weights)
        lses.append(peak + jnp.log2(total))
    for k, (w, x) in enumerate(zip(weights, tiles)):
        terms[k : k + 1, :] = w * x[2]
    gap = tree(jnp.add, [terms[k : k + 1, :] for k in range(len(tiles))])
    return lses[1], lses[0], gap / total + (lses[0] - lses[1])


def sum_blocks(x, b):
    parts = [jnp.sum(x[:, block(p, b)], axis=(0, 1), keepdims=True) for p in range(x.shape[1] // b)]
    return tree(jnp.add, parts) * LN2


def gradient_kernel(image_forms, text_forms, b, tw, scale, *refs):
    nr, nc = len(image_forms), len(text_forms)
    si, refs = refs[:nr], refs[nr:]
    st, refs = refs[:nc], refs[nc:]
    tl_ref, sl_ref, refs = refs[0], refs[1], refs[2:]
    row_parts, refs = refs[: nr // 2], refs[nr // 2 :]
    col_parts, refs = refs[:nc], refs[nc:]
    image_keep, image_send, text_keep, text_send, image_extra, text_extra, refs = *refs[:6], refs[6:]
    text, image, high_ref, low_ref, row_terms, col_terms = refs
    for p in range(nc):
        text[block(p, b), :] = st[p][...] if text_forms[p] == 2 else st[p][:, tw:]
    for p in range(nr):
        image[block(p, b), :] = si[p][...] if image_forms[p] == 2 else si[p][:, tw:]
    tiles = []
    for q in range(nr // 2):
        x = jnp.concatenate([row_parts[q][:, block(p ^ q, b)] for p in range(nr)], 1)
        for core in range(2):
            tiles.append([x[core * KINDS + k : core * KINDS + k + 1, :] for k in range(KINDS)])
    row_t, row_s, terms = combine(tiles, row_terms)
    row_share = sum_blocks(terms, b)
    rows = stack_rows((row_t, row_s), (LINES, nr * b), 0)
    tiles = []
    for q in range(nc):
        x = jnp.concatenate([col_parts[q][:, block(p ^ q, b)] for p in range(nc)], 1)
        tiles.append([x[k : k + 1, :] for k in range(KINDS)])
    col_t, col_s, terms = combine(tiles, col_terms)
    col_share = sum_blocks(terms, b)
    half = nr // 2
    for p in range(nr):
        row = jnp.transpose(rows[:, block(p, b)])
        tl, sl = tl_ref[block(p, b), :], sl_ref[block(p, b), :]
        delta = (jnp.exp2(sl - row[:, 1:2]) - jnp.exp2(tl - row[:, 0:1])) + (
            jnp.exp2(sl - col_s) - jnp.exp2(tl - col_t)
        )
        high = delta.astype(BF16)
        high_ref[block(p, b), :] = high
        low_ref[block(p, b), :] = (delta - high.astype(F32)).astype(BF16)
    step = 2 if half % 2 == 0 else 1
    bound = None
    for p in range(0, nr, step):
        rows = slice(p * b, (p + step) * b)
        part = (matmul(high_ref[rows, :], text[...], 1, 0) + matmul(low_ref[rows, :], text[...], 1, 0)) * scale
        peak = jnp.max(jnp.abs(part), 0, keepdims=True)
        bound = peak if bound is None else jnp.maximum(bound, peak)
        if p < half:
            image_keep[rows, :] = part
        else:
            image_send[(p - half) * b : (p - half + step) * b, :] = part
    extra = stack_rows((bound, col_share), image_extra.shape, 0)
    image_extra[...] = extra
    image_send[half * b :, :] = extra
    half = nc // 2
    step = 2 if half % 2 == 0 else 1
    bound = None
    for p in range(0, nc, step):
        cols = slice(p * b, (p + step) * b)
        part = (matmul(high_ref[:, cols], image[...], 0, 0) + matmul(low_ref[:, cols], image[...], 0, 0)) * scale
        peak = jnp.max(jnp.abs(part), 0, keepdims=True)
        bound = peak if bound is None else jnp.maximum(bound, peak)
        if p < half:
            text_keep[cols, :] = part
        else:
            text_send[(p - half) * b : (p - half + step) * b, :] = part
    text_extra[...] = stack_rows((bound, row_share), text_extra.shape, 0)


def call(kernel, outs, args, scratch=(), flops=0, transcendentals=0):
    shapes = [jax.ShapeDtypeStruct(s, d) for s, d in outs]
    size = sum(x.size * x.dtype.itemsize for x in list(args) + shapes)
    return pl.pallas_call(
        kernel,
        out_shape=shapes,
        in_specs=[SMEM if x.dtype == jnp.int32 else VMEM for x in args],
        out_specs=[VMEM] * len(shapes),
        scratch_shapes=[pltpu.VMEM(s, d) for s, d in scratch],
        compiler_params=PARAMS,
        cost_estimate=pl.CostEstimate(flops=flops, bytes_accessed=size, transcendentals=transcendentals),
    )(*args)


def swap(bits, x):
    perm = [(i, i ^ ((1 << len(bits)) - 1)) for i in range(1 << len(bits))]
    return lax.ppermute(x, bits, perm)


def subset(bits, q):
    return tuple(b for k, b in enumerate(bits) if q >> k & 1)


def after(x, done):
    return lax.optimization_barrier((x, done))[0]


def together(*groups):
    return lax.optimization_barrier(groups)


def gather(image_bits, text_bits, image, text):
    groups = []
    for bits, (teacher, student) in ((image_bits, image), (text_bits, text)):
        both = jnp.concatenate([teacher, student], 1)
        groups.append((bits, teacher, student, both))
    come = [{0: [swap(bits[:1], teacher)]} for bits, teacher, _, _ in groups]
    for (bits, _, _, both), got in zip(groups, come):
        for k in range(1, len(bits)):
            got[1 << k] = [swap(bits[k : k + 1], both)]
    come = [{1 if p == 0 else p: x for p, x in got.items()} for got in come]
    students = [group[2] for group in groups]
    for stage in range(1, max(len(image_bits), len(text_bits)) + 1):
        come, students = together(come, students)
        new = [{p: list(x) for p, x in got.items()} for got in come]
        for n, (bits, _, _, _) in enumerate(groups):
            if stage == 1:
                new[n][1].append(swap(bits[:1], students[n]))
            for k in range(1, len(bits)):
                for p in range(1, 1 << k):
                    have, sent = come[n].get(p, []), new[n].setdefault(p | 1 << k, [])
                    sent.extend(swap(bits[k : k + 1], x) for x in have[len(sent) :])
        come = new
    blocks = []
    for (bits, teacher, student, _), got in zip(groups, come):
        blocks.append([(teacher, student)] + [tuple(got[p]) for p in range(1, 1 << len(bits))])
    return blocks


def flatten(blocks):
    return [x for parts in blocks for x in parts]


def views(refs, forms, tw):
    teachers, students = [], []
    for form in forms:
        if form == 1:
            teachers.append(refs[0].at[:, :tw])
            students.append(refs[0].at[:, tw:])
        else:
            teachers.append(refs[0])
            students.append(refs[1])
        refs = refs[form:]
    return teachers, students, refs


def power_of(extra):
    return jnp.ceil(jnp.log2(jnp.maximum(extra[0:1], 1e-30)))


def narrow(x, extra):
    return (x * jnp.exp2(14.0 - power_of(extra))).astype(F16)


def add_sum(keep, come, extra):
    body, other = come
    return keep + body.astype(F32) * jnp.exp2(power_of(other) - 14.0), extra + other


def halves(x):
    return x[: x.shape[0] // 2], x[x.shape[0] // 2 :]


def local(image_bits, text_bits, teacher_image, teacher_text, student_image, student_text):
    b, tw = teacher_image.shape
    sw = student_image.shape[1]
    nr, nc = 1 << len(image_bits), 1 << len(text_bits)
    r, c = nr * b, nc * b
    pair, others = image_bits[-1:], image_bits[:-1]
    images, texts = gather(image_bits, text_bits, (teacher_image, student_image), (teacher_text, student_text))
    forms = [len(x) for x in images], [len(x) for x in texts]
    core = lax.axis_index(pair).astype(jnp.int32).reshape(1)
    tl, sl, rows, rows_swapped, cols = call(
        functools.partial(stats_kernel, *forms, b, tw, tw**-0.5, sw**-0.5),
        [((r, c), F32), ((r, c), F32), ((LINES, r), F32), ((LINES, r), F32), ((LINES, c), F32)],
        [core] + flatten(images + texts), [((c, tw), BF16), ((c, sw), BF16)], 2 * r * c * (tw + sw), 4 * r * c,
    )
    other = swap(pair, rows_swapped)
    col_parts = [cols] + [swap(subset(text_bits, q), cols) for q in range(1, nc)]
    rows = rows + other
    row_parts = [rows] + [swap(subset(others, q), rows) for q in range(1, nr // 2)]
    lines = ((LINES, sw), F32)
    image_keep, image_send, text_keep, text_send, image_extra, text_extra = call(
        functools.partial(gradient_kernel, *forms, b, tw, sw**-0.5),
        [((r // 2, sw), F32), ((r // 2 + LINES, sw), F32), ((c // 2, sw), F32), ((c // 2, sw), F32), lines, lines],
        [x[-1] for x in images + texts] + [tl, sl] + row_parts + col_parts,
        [((c, sw), BF16), ((r, sw), BF16), ((r, c), BF16), ((r, c), BF16), ((nr, r), F32), ((max(nc, 8), c), F32)],
        8 * r * c * sw, 4 * r * c,
    )
    come = swap(pair, image_send)
    image_keep, image_send = halves(image_keep + come[: r // 2])
    image_extra = image_extra + come[r // 2 :]
    for k in reversed(range(max(len(text_bits), len(others)))):
        todo = {}
        if k < len(text_bits):
            todo["text"] = [narrow(text_send, text_extra), text_extra]
        if k < len(others):
            todo["image"] = [narrow(image_send, image_extra), image_extra]
        (todo,) = together(todo)
        if k < len(text_bits):
            text_come = [swap(text_bits[k : k + 1], x) for x in todo["text"]]
        if k < len(others):
            image_come = [swap(others[k : k + 1], x) for x in todo["image"]]
        if k < len(text_bits):
            text_total, text_extra = add_sum(text_keep, text_come, text_extra)
            text_keep, text_send = halves(text_total)
        if k < len(others):
            image_total, image_extra = add_sum(image_keep, image_come, image_extra)
            image_keep, image_send = halves(image_total)
    pairs = b << (len(image_bits) + len(text_bits))
    loss = (image_extra[1, 0] + text_extra[1, 0]) / (2.0 * pairs)
    return (loss, image_total, text_total)


def solution(mesh):
    bits = {axis: [f"{axis}{k}" for k in reversed(range(mesh.shape[axis].bit_length() - 1))] for axis in ("img", "txt")}
    names = bits["img"] + bits["txt"]
    cube = Mesh(np.asarray(mesh.devices).reshape((2,) * len(names)), names)
    text_bits = [x for x in bits["img"] if int(x[3:]) >= 1] + [x for x in bits["txt"] if int(x[3:]) % 2 == 1]
    image_bits = [x for x in names if x not in text_bits]
    image, text = P(tuple(names), None), P(tuple(bits["txt"] + bits["img"]), None)
    return jax.shard_map(
        functools.partial(local, tuple(image_bits), tuple(text_bits)),
        mesh=cube,
        in_specs=(image, text, image, text),
        out_specs=(P(), image, text),
        check_vma=False,
    )
```

time: 113 us -> 109 us (0.965)
  blocking collectives: 20.3 us -> 0 us
  starting transfers between devices: 15.1 us -> 31.2 us
  other arithmetic: 2.36 us -> 7.81 us
  waiting for transfers between devices: 50.9 us -> 45.9 us
  between operations: 3.18 us -> 4.81 us
    all_to_all x2 -> x0, blocking collectives: 20.3 us -> none  [the longest x1 10.6 us: local(): row_lines = lax.all_to_all(row_lines, row_axes, 0, 0, tiled=True)]
    ppermute x15 -> x32, starting transfers between devices: 15.1 us -> 31.2 us  [swap(): return lax.ppermute(x, bits, perm)]
    ppermute x15 -> x32, waiting for transfers between devices: 50.9 us -> 45.9 us  [swap(): return lax.ppermute(x, bits, perm)]
    add x5 -> x9, other arithmetic: 1.69 us -> 4.6 us  [the longest x4 1.67 us: add_sum(): keep + body.astype(F32) * jnp.exp2(power_of(other) - 14.0)]
    convert_element_type x0 -> x4, other arithmetic: none -> 1.21 us  [narrow(): return (x * jnp.exp2(14.0 - power_of(extra))).astype(F16)]
    concatenate x0 -> x1, other arithmetic: none -> 1.14 us  [gather(): both = jnp.concatenate([teacher, student], 1)]
    slice x13 -> x4, local copies, waits for them, and re-layouts: 2.62 us -> 2.05 us  [local(): loss = (image_extra[1, 0] + text_extra[1, 0]) / (2.0 * pairs)]
  transfers between devices with their start and end apart: 15 -> 32, of which waited for: 9 -> 16; matrix products, arithmetic and copies ran while one was open for 3% -> 5% of each run, Pallas kernels for 0% -> 0%
where the time goes in v3:
time: 109 us; the launch traced here: 108 us
  waiting for transfers between devices  45.9 us (42%)
  starting transfers between devices  31.2 us (29%)
  Pallas kernels  15.2 us (14%)
  other arithmetic  7.81 us (7%)
  between operations  4.81 us (4%)
  local copies, waits for them, and re-layouts  3.58 us (3%)
    ppermute x32, waiting for transfers between devices, swap(): return lax.ppermute(x, bits, perm)  45.9 us
    ppermute x32, starting transfers between devices, swap(): return lax.ppermute(x, bits, perm)  31.2 us
    pallas_call x2, Pallas kernels, call(): pl.pallas_call(kernel, out_shape=shapes, in_specs=[SMEM if x.dtype == jnp...  15.2 us
  transfers between devices with their start and end apart: 32, of which 16 were waited for; matrix products, arithmetic and copies ran while one was open for 5% of the time, Pallas kernels for 0%

profile of v3, /device:TPU:0, one launch (start us, length us, event | category | flops | bytes accessed | tf_op | source)
XLA Modules:
  0.0 108.5 jit_solution(5162536145823279839)
XLA Ops:
  0.7 1.1 %pad_maximum_fusion = bf16[128,1792]{1,0:T(8,128)(2,1)S(1)} fusion(bf16[128,512]{1,0:T(8,128)(2,1)} %refs_8_.1, bf16[128,1280]{1,0:T(8,128)(2,1)} %refs_13_.1), kind=kLoop, calls=%fused_computation.6 | loop fusion | flops 917504 | bytes 917504 | tf_op jit(solution)/shard_map/concatenate | solution.py:208
  1.8 3.0 %collective-permute-start.4 = (bf16[128,1792]{1,0:T(8,128)(2,1)S(1)}, bf16[128,1792]{1,0:T(8,128)(2,1)S(1)}, u32[]{:S(2)}, u32[]{:S(2)}) collective-permute-start(bf16[128,1792]{1,0:T(8,128)(2,1)S(1)} %pad_maximum_fusion), channel_id=1, source_target_pairs={{0,2},{2,0},{1,3},{3,1},{4,6},{6,4},{5,7},{7,5},{8,10},{10,8},{9,1... | collective-permute-start | bytes 1376264 | tf_op jit(solution)/shard_map/ppermute | solution.py:190
  5.0 1.6 %collective-permute-start.1 = (bf16[128,1792]{1,0:T(8,128)(2,1)S(1)}, bf16[128,1792]{1,0:T(8,128)(2,1)S(1)}, u32[]{:S(2)}, u32[]{:S(2)}) collective-permute-start(bf16[128,1792]{1,0:T(8,128)(2,1)S(1)} %constant_dynamic-update-slice_fusion), channel_id=1, source_target_pairs={{0,4},{4,0},{1,5},{5,1},{2,6},{6,2},{3,7},{7,3},{8,12},{12,8},{9,1... | collective-permute-start | bytes 1376264 | tf_op jit(solution)/shard_map/ppermute | solution.py:190
  6.6 1.6 %collective-permute-start = (bf16[128,1280]{1,0:T(8,128)(2,1)S(1)}, bf16[128,1280]{1,0:T(8,128)(2,1)S(1)}, u32[]{:S(2)}, u32[]{:S(2)}) collective-permute-start(bf16[128,1280]{1,0:T(8,128)(2,1)S(1)} %copy-done.2), channel_id=1, source_target_pairs={{0,8},{8,0},{1,9},{9,1},{2,10},{10,2},{3,11},{11,3},{4,12},{12,4},... | collective-permute-start | bytes 983048 | tf_op jit(solution)/shard_map/ppermute | solution.py:190
  8.1 2.6 %collective-permute-start.3 = (bf16[128,1280]{1,0:T(8,128)(2,1)S(1)}, bf16[128,1280]{1,0:T(8,128)(2,1)S(1)}, u32[]{:S(2)}, u32[]{:S(2)}) collective-permute-start(bf16[128,1280]{1,0:T(8,128)(2,1)S(1)} %copy-done.1), channel_id=1, source_target_pairs={{0,16},{16,0},{1,17},{17,1},{2,18},{18,2},{3,19},{19,3},{4,20},{20... | collective-permute-start | bytes 983048 | tf_op jit(solution)/shard_map/ppermute | solution.py:190
  10.7 12.5 %collective-permute-done.refs_2_ = bf16[128,1280]{1,0:T(8,128)(2,1)S(1)} collective-permute-done((bf16[128,1280]{1,0:T(8,128)(2,1)S(1)}, bf16[128,1280]{1,0:T(8,128)(2,1)S(1)}, u32[]{:S(2)}, u32[]{:S(2)}) %collective-permute-start) | collective-permute-done | bytes 327712 | tf_op jit(solution)/shard_map/ppermute | solution.py:190
  23.2 2.4 %collective-permute-done.3.refs_15_ = bf16[128,1280]{1,0:T(8,128)(2,1)S(1)} collective-permute-done((bf16[128,1280]{1,0:T(8,128)(2,1)S(1)}, bf16[128,1280]{1,0:T(8,128)(2,1)S(1)}, u32[]{:S(2)}, u32[]{:S(2)}) %collective-permute-start.3) | collective-permute-done | bytes 327712 | tf_op jit(solution)/shard_map/ppermute | solution.py:190
  27.4 5.0 %collective-permute-done.5.refs_3_.refs_1_ = bf16[128,512]{1,0:T(8,128)(2,1)S(1)} collective-permute-done((bf16[128,512]{1,0:T(8,128)(2,1)S(1)}, bf16[128,512]{1,0:T(8,128)(2,1)S(1)}, u32[]{:S(2)}, u32[]{:S(2)}) %collective-permute-start.5) | collective-permute-done | bytes 131104 | tf_op jit(solution)/shard_map/ppermute | solution.py:190
  32.5 1.3 %collective-permute-start.9 = (bf16[128,512]{1,0:T(8,128)(2,1)S(1)}, bf16[128,512]{1,0:T(8,128)(2,1)S(1)}, u32[]{:S(2)}, u32[]{:S(2)}) collective-permute-start(bf16[128,512]{1,0:T(8,128)(2,1)S(1)} %copy-done.3), channel_id=1, source_target_pairs={{0,16},{16,0},{1,17},{17,1},{2,18},{18,2},{3,19},{19,3},{4,20},{20... | collective-permute-start | bytes 393224 | tf_op jit(solution)/shard_map/ppermute | solution.py:190
  33.8 6.9 %collective-permute-done.9.refs_16_.refs_9_ = bf16[128,512]{1,0:T(8,128)(2,1)S(1)} collective-permute-done((bf16[128,512]{1,0:T(8,128)(2,1)S(1)}, bf16[128,512]{1,0:T(8,128)(2,1)S(1)}, u32[]{:S(2)}, u32[]{:S(2)}) %collective-permute-start.9) | collective-permute-done | bytes 131104 | tf_op jit(solution)/shard_map/ppermute | solution.py:190
  41.6 1.5 %collective-permute-start.14 = (bf16[128,512]{1,0:T(8,128)(2,1)S(1)}, bf16[128,512]{1,0:T(8,128)(2,1)S(1)}, u32[]{:S(2)}, u32[]{:S(2)}) collective-permute-start(bf16[128,512]{1,0:T(8,128)(2,1)S(1)} %collective-permute-done.9.refs_16_.refs_9_), channel_id=1, source_target_pairs={{0,2},{2,0},{1,3},{3,1},{4,6},{6,4},{5,7},{7,5},{8,10},{10,8},{9,1... | collective-permute-start | bytes 393224 | tf_op jit(solution)/shard_map/ppermute | solution.py:190
  43.2 1.5 %collective-permute-start.11 = (bf16[128,512]{1,0:T(8,128)(2,1)S(1)}, bf16[128,512]{1,0:T(8,128)(2,1)}, u32[]{:S(2)}, u32[]{:S(2)}) collective-permute-start(bf16[128,512]{1,0:T(8,128)(2,1)S(1)} %collective-permute-done.5.refs_3_.refs_1_), channel_id=1, source_target_pairs={{0,4},{4,0},{1,5},{5,1},{2,6},{6,2},{3,7},{7,3},{8,12},{12,8},{9,1... | collective-permute-start | bytes 393224 | tf_op jit(solution)/shard_map/ppermute | solution.py:190
  44.7 2.7 %collective-permute-done.14.refs_19_.refs_11_ = bf16[128,512]{1,0:T(8,128)(2,1)S(1)} collective-permute-done((bf16[128,512]{1,0:T(8,128)(2,1)S(1)}, bf16[128,512]{1,0:T(8,128)(2,1)S(1)}, u32[]{:S(2)}, u32[]{:S(2)}) %collective-permute-start.14) | collective-permute-done | bytes 131104 | tf_op jit(solution)/shard_map/ppermute | solution.py:190
  47.4 1.7 %collective-permute-done.11.refs_6_.refs_3_ = bf16[128,512]{1,0:T(8,128)(2,1)} collective-permute-done((bf16[128,512]{1,0:T(8,128)(2,1)S(1)}, bf16[128,512]{1,0:T(8,128)(2,1)}, u32[]{:S(2)}, u32[]{:S(2)}) %collective-permute-start.11) | collective-permute-done | bytes 131104 | tf_op jit(solution)/shard_map/ppermute | solution.py:190
  49.2 1.7 %collective-permute-done.15.refs_12_.refs_7_ = bf16[128,512]{1,0:T(8,128)(2,1)} collective-permute-done((bf16[128,512]{1,0:T(8,128)(2,1)}, bf16[128,512]{1,0:T(8,128)(2,1)}, u32[]{:S(2)}, u32[]{:S(2)}) %collective-permute-start.15) | collective-permute-done | bytes 131104 | tf_op jit(solution)/shard_map/ppermute | solution.py:190
  50.9 7.5 %shard_map.67 = (f32[1024,512]{1,0:T(8,128)}, f32[1024,512]{1,0:T(8,128)}, f32[8,1024]{1,0:T(8,128)}, f32[8,1024]{1,0:T(8,128)}, f32[8,512]{1,0:T(8,128)}) custom-call(s32[1]{0:T(128)} %bitcast.core, bf16[128,1280]{1,0:T(8,128)(2,1)} %refs_0_.2, bf16[128,512]{1,0:T(8,128)(2,1)} %refs_0_.3, bf16[128,1280]{1,0:T(8,128)(2,1)} %copy-done.11, ...), custom_call_target="tpu_custom_call" | custom-call | flops 1879048192 | bytes 9781252 | tf_op jit(solution)/shard_map/pallas_call | solution.py:177
  58.7 1.3 %collective-permute-done.16 = f32[8,1024]{1,0:T(8,128)S(1)} collective-permute-done((f32[8,1024]{1,0:T(8,128)}, f32[8,1024]{1,0:T(8,128)S(1)}, u32[]{:S(2)}, u32[]{:S(2)}) %collective-permute-start.16) | collective-permute-done | bytes 32800 | tf_op jit(solution)/shard_map/ppermute | solution.py:190
  60.7 2.8 %collective-permute-start.19 = (f32[8,1024]{1,0:T(8,128)S(1)}, f32[8,1024]{1,0:T(8,128)S(1)}, u32[]{:S(2)}, u32[]{:S(2)}) collective-permute-start(f32[8,1024]{1,0:T(8,128)S(1)} %add.41.refs_14_), channel_id=1, source_target_pairs={{0,12},{4,8},{8,4},{12,0},{1,13},{5,9},{9,5},{13,1},{2,14},{6,10},... | collective-permute-start | bytes 98312 | tf_op jit(solution)/shard_map/ppermute | solution.py:190
  64.2 1.5 %collective-permute-start.21 = (f32[8,512]{1,0:T(8,128)}, f32[8,512]{1,0:T(8,128)S(1)}, u32[]{:S(2)}, u32[]{:S(2)}) collective-permute-start(f32[8,512]{1,0:T(8,128)} %get-tuple-element.92.refs_18_), channel_id=1, source_target_pairs={{0,2},{2,0},{1,3},{3,1},{4,6},{6,4},{5,7},{7,5},{8,10},{10,8},{9,1... | collective-permute-start | bytes 49160 | tf_op jit(solution)/shard_map/ppermute | solution.py:190
  65.7 1.7 %collective-permute-start.20 = (f32[8,512]{1,0:T(8,128)}, f32[8,512]{1,0:T(8,128)S(1)}, u32[]{:S(2)}, u32[]{:S(2)}) collective-permute-start(f32[8,512]{1,0:T(8,128)} %get-tuple-element.92.refs_18_), channel_id=1, source_target_pairs={{0,16},{16,0},{1,17},{17,1},{2,18},{18,2},{3,19},{19,3},{4,20},{20... | collective-permute-start | bytes 49160 | tf_op jit(solution)/shard_map/ppermute | solution.py:190
  68.1 2.4 %collective-permute-done.20.refs_19_ = f32[8,512]{1,0:T(8,128)S(1)} collective-permute-done((f32[8,512]{1,0:T(8,128)}, f32[8,512]{1,0:T(8,128)S(1)}, u32[]{:S(2)}, u32[]{:S(2)}) %collective-permute-start.20) | collective-permute-done | bytes 16416 | tf_op jit(solution)/shard_map/ppermute | solution.py:190
  71.2 7.7 %shard_map.68 = (f32[512,512]{1,0:T(8,128)}, f32[520,512]{1,0:T(8,128)}, f32[256,512]{1,0:T(8,128)}, f32[256,512]{1,0:T(8,128)}, f32[8,512]{1,0:T(8,128)}, /*index=5*/f32[8,512]{1,0:T(8,128)}) custom-call(bf16[128,512]{1,0:T(8,128)(2,1)} %refs_0_.3, bf16[128,512]{1,0:T(8,128)(2,1)} %copy-done.17, bf16[128,1792]{1,0:T(8,128)(2,1)} %copy-done.9, ...), custom_call_target="tpu_custom_call" | custom-call | flops 2147483648 | bytes 10469376 | tf_op jit(solution)/shard_map/pallas_call | solution.py:177
  79.7 1.1 %multiply_convert_fusion = f16[256,512]{1,0:T(8,128)(2,1)S(1)} fusion(f32[256,512]{1,0:T(8,128)} %get-tuple-element.96, f32[512]{0:T(512)S(1)} %bitcast.17), kind=kLoop, calls=%fused_computation.5 | loop fusion | flops 262144 | bytes 788480 | tf_op jit(solution)/shard_map/convert_element_type | solution.py:255
  80.8 1.0 collective-permute-done.23
  82.6 1.4 %slice_add_fusion = f32[512,512]{1,0:T(8,128)S(1)} fusion(f32[512,512]{1,0:T(8,128)} %get-tuple-element.95, f32[520,512]{1,0:T(8,128)S(1)} %collective-permute-done.23), kind=kLoop, calls=%fused_computation | loop fusion | flops 262144 | bytes 3145728 | tf_op jit(solution)/shard_map/add | solution.py:294
  84.1 1.5 %collective-permute-start.24 = (f32[8,512]{1,0:T(8,128)S(1)}, f32[8,512]{1,0:T(8,128)S(1)}, u32[]{:S(2)}, u32[]{:S(2)}) collective-permute-start(f32[8,512]{1,0:T(8,128)S(1)} %slice_add_fusion.4), channel_id=1, source_target_pairs={{0,4},{4,0},{1,5},{5,1},{2,6},{6,2},{3,7},{7,3},{8,12},{12,8},{9,1... | collective-permute-start | bytes 49160 | tf_op jit(solution)/shard_map/ppermute | solution.py:190
  86.7 1.5 %collective-permute-start.26 = (f16[256,512]{1,0:T(8,128)(2,1)S(1)}, f16[256,512]{1,0:T(8,128)(2,1)S(1)}, u32[]{:S(2)}, u32[]{:S(2)}) collective-permute-start(f16[256,512]{1,0:T(8,128)(2,1)S(1)} %multiply_convert_fusion), channel_id=1, source_target_pairs={{0,2},{2,0},{1,3},{3,1},{4,6},{6,4},{5,7},{7,5},{8,10},{10,8},{9,1... | collective-permute-start | bytes 786440 | tf_op jit(solution)/shard_map/ppermute | solution.py:190
  88.2 1.1 %collective-permute-done.27 = f32[8,512]{1,0:T(8,128)S(1)} collective-permute-done((f32[8,512]{1,0:T(8,128)S(1)}, f32[8,512]{1,0:T(8,128)S(1)}, u32[]{:S(2)}, u32[]{:S(2)}) %collective-permute-start.27) | collective-permute-done | bytes 16416 | tf_op jit(solution)/shard_map/ppermute | solution.py:190
  89.4 4.6 %collective-permute-done.25 = f16[256,512]{1,0:T(8,128)(2,1)S(1)} collective-permute-done((f16[256,512]{1,0:T(8,128)(2,1)S(1)}, f16[256,512]{1,0:T(8,128)(2,1)S(1)}, u32[]{:S(2)}, u32[]{:S(2)}) %collective-permute-start.25) | collective-permute-done | bytes 262176 | tf_op jit(solution)/shard_map/ppermute | solution.py:190
  94.5 1.9 %collective-permute-start.28 = (f32[8,512]{1,0:T(8,128)S(1)}, f32[8,512]{1,0:T(8,128)S(1)}, u32[]{:S(2)}, u32[]{:S(2)}) collective-permute-start(f32[8,512]{1,0:T(8,128)S(1)} %add.44), channel_id=1, source_target_pairs={{0,8},{8,0},{1,9},{9,1},{2,10},{10,2},{3,11},{11,3},{4,12},{12,4},... | collective-permute-start | bytes 49160 | tf_op jit(solution)/shard_map/ppermute | solution.py:190
  96.5 1.2 %collective-permute-start.29 = (f32[8,512]{1,0:T(8,128)S(1)}, f32[8,512]{1,0:T(8,128)S(1)}, u32[]{:S(2)}, u32[]{:S(2)}) collective-permute-start(f32[8,512]{1,0:T(8,128)S(1)} %add.47), channel_id=1, source_target_pairs={{0,16},{16,0},{1,17},{17,1},{2,18},{18,2},{3,19},{19,3},{4,20},{20... | collective-permute-start | bytes 49160 | tf_op jit(solution)/shard_map/ppermute | solution.py:190
  99.3 1.3 %collective-permute-start.31 = (f16[128,512]{1,0:T(8,128)(2,1)S(1)}, f16[128,512]{1,0:T(8,128)(2,1)S(1)}, u32[]{:S(2)}, u32[]{:S(2)}) collective-permute-start(f16[128,512]{1,0:T(8,128)(2,1)S(1)} %fusion.1), channel_id=1, source_target_pairs={{0,16},{16,0},{1,17},{17,1},{2,18},{18,2},{3,19},{19,3},{4,20},{20... | collective-permute-start | bytes 393224 | tf_op jit(solution)/shard_map/ppermute | solution.py:190
  (116 shorter events, 15.2 us)
Async XLA Ops:
  1.8 23.8 %collective-permute-start.4 = (bf16[128,1792]{1,0:T(8,128)(2,1)S(1)}, bf16[128,1792]{1,0:T(8,128)(2,1)S(1)}, u32[]{:S(2)}, u32[]{:S(2)}) collective-permute-start(bf16[128,1792]{1,0:T(8,128)(2,1)S(1)} %pad_maximum_fusion), channel_id=1, source_target_pairs={{0,2},{2,0},{1,3},{3,1},{4,6},{6,4},{5,7},{7,5},{8,10},{10,8},{9,1... | collective-permute-start | bytes 1376264 | tf_op jit(solution)/shard_map/ppermute | solution.py:190
  4.9 20.7 %collective-permute-start.2 = (bf16[128,1792]{1,0:T(8,128)(2,1)S(1)}, bf16[128,1792]{1,0:T(8,128)(2,1)S(1)}, u32[]{:S(2)}, u32[]{:S(2)}) collective-permute-start(bf16[128,1792]{1,0:T(8,128)(2,1)S(1)} %constant_dynamic-update-slice_fusion), channel_id=1, source_target_pairs={{0,1},{1,0},{2,3},{3,2},{4,5},{5,4},{6,7},{7,6},{8,9},{9,8},{10,11... | collective-permute-start | bytes 1376264 | tf_op jit(solution)/shard_map/ppermute | solution.py:190
  5.0 20.7 %collective-permute-start.1 = (bf16[128,1792]{1,0:T(8,128)(2,1)S(1)}, bf16[128,1792]{1,0:T(8,128)(2,1)S(1)}, u32[]{:S(2)}, u32[]{:S(2)}) collective-permute-start(bf16[128,1792]{1,0:T(8,128)(2,1)S(1)} %constant_dynamic-update-slice_fusion), channel_id=1, source_target_pairs={{0,4},{4,0},{1,5},{5,1},{2,6},{6,2},{3,7},{7,3},{8,12},{12,8},{9,1... | collective-permute-start | bytes 1376264 | tf_op jit(solution)/shard_map/ppermute | solution.py:190
  6.6 16.7 %collective-permute-start = (bf16[128,1280]{1,0:T(8,128)(2,1)S(1)}, bf16[128,1280]{1,0:T(8,128)(2,1)S(1)}, u32[]{:S(2)}, u32[]{:S(2)}) collective-permute-start(bf16[128,1280]{1,0:T(8,128)(2,1)S(1)} %copy-done.2), channel_id=1, source_target_pairs={{0,8},{8,0},{1,9},{9,1},{2,10},{10,2},{3,11},{11,3},{4,12},{12,4},... | collective-permute-start | bytes 983048 | tf_op jit(solution)/shard_map/ppermute | solution.py:190
  8.1 17.5 %collective-permute-start.3 = (bf16[128,1280]{1,0:T(8,128)(2,1)S(1)}, bf16[128,1280]{1,0:T(8,128)(2,1)S(1)}, u32[]{:S(2)}, u32[]{:S(2)}) collective-permute-start(bf16[128,1280]{1,0:T(8,128)(2,1)S(1)} %copy-done.1), channel_id=1, source_target_pairs={{0,16},{16,0},{1,17},{17,1},{2,18},{18,2},{3,19},{19,3},{4,20},{20... | collective-permute-start | bytes 983048 | tf_op jit(solution)/shard_map/ppermute | solution.py:190
  25.6 15.1 %collective-permute-start.8 = (bf16[128,1792]{1,0:T(8,128)(2,1)S(1)}, bf16[128,1792]{1,0:T(8,128)(2,1)S(1)}, u32[]{:S(2)}, u32[]{:S(2)}) collective-permute-start(bf16[128,1792]{1,0:T(8,128)(2,1)S(1)} %collective-permute-done.1.refs_4_.refs_2_), channel_id=1, source_target_pairs={{0,1},{1,0},{2,3},{3,2},{4,5},{5,4},{6,7},{7,6},{8,9},{9,8},{10,11... | collective-permute-start | bytes 1376264 | tf_op jit(solution)/shard_map/ppermute | solution.py:190
  25.7 15.0 %collective-permute-start.10 = (bf16[128,1280]{1,0:T(8,128)(2,1)S(1)}, bf16[128,1280]{1,0:T(8,128)(2,1)S(1)}, u32[]{:S(2)}, u32[]{:S(2)}) collective-permute-start(bf16[128,1280]{1,0:T(8,128)(2,1)S(1)} %collective-permute-done.3.refs_15_), channel_id=1, source_target_pairs={{0,2},{2,0},{1,3},{3,1},{4,6},{6,4},{5,7},{7,5},{8,10},{10,8},{9,1... | collective-permute-start | bytes 983048 | tf_op jit(solution)/shard_map/ppermute | solution.py:190
  26.3 14.4 %collective-permute-start.7 = (bf16[128,1280]{1,0:T(8,128)(2,1)S(1)}, bf16[128,1280]{1,0:T(8,128)(2,1)S(1)}, u32[]{:S(2)}, u32[]{:S(2)}) collective-permute-start(bf16[128,1280]{1,0:T(8,128)(2,1)S(1)} %collective-permute-done.refs_2_), channel_id=1, source_target_pairs={{0,1},{1,0},{2,3},{3,2},{4,5},{5,4},{6,7},{7,6},{8,9},{9,8},{10,11... | collective-permute-start | bytes 983048 | tf_op jit(solution)/shard_map/ppermute | solution.py:190
  26.5 14.2 %collective-permute-start.6 = (bf16[128,1280]{1,0:T(8,128)(2,1)S(1)}, bf16[128,1280]{1,0:T(8,128)(2,1)S(1)}, u32[]{:S(2)}, u32[]{:S(2)}) collective-permute-start(bf16[128,1280]{1,0:T(8,128)(2,1)S(1)} %collective-permute-done.refs_2_), channel_id=1, source_target_pairs={{0,4},{4,0},{1,5},{5,1},{2,6},{6,2},{3,7},{7,3},{8,12},{12,8},{9,1... | collective-permute-start | bytes 983048 | tf_op jit(solution)/shard_map/ppermute | solution.py:190
  27.0 5.5 %collective-permute-start.5 = (bf16[128,512]{1,0:T(8,128)(2,1)S(1)}, bf16[128,512]{1,0:T(8,128)(2,1)S(1)}, u32[]{:S(2)}, u32[]{:S(2)}) collective-permute-start(bf16[128,512]{1,0:T(8,128)(2,1)S(1)} %copy-done.4), channel_id=1, source_target_pairs={{0,8},{8,0},{1,9},{9,1},{2,10},{10,2},{3,11},{11,3},{4,12},{12,4},... | collective-permute-start | bytes 393224 | tf_op jit(solution)/shard_map/ppermute | solution.py:190
  32.5 8.2 %collective-permute-start.9 = (bf16[128,512]{1,0:T(8,128)(2,1)S(1)}, bf16[128,512]{1,0:T(8,128)(2,1)S(1)}, u32[]{:S(2)}, u32[]{:S(2)}) collective-permute-start(bf16[128,512]{1,0:T(8,128)(2,1)S(1)} %copy-done.3), channel_id=1, source_target_pairs={{0,16},{16,0},{1,17},{17,1},{2,18},{18,2},{3,19},{19,3},{4,20},{20... | collective-permute-start | bytes 393224 | tf_op jit(solution)/shard_map/ppermute | solution.py:190
  41.5 7.6 %collective-permute-start.13 = (bf16[128,1280]{1,0:T(8,128)(2,1)S(1)}, bf16[128,1280]{1,0:T(8,128)(2,1)S(1)}, u32[]{:S(2)}, u32[]{:S(2)}) collective-permute-start(bf16[128,1280]{1,0:T(8,128)(2,1)S(1)} %collective-permute-done.6.refs_5_), channel_id=1, source_target_pairs={{0,1},{1,0},{2,3},{3,2},{4,5},{5,4},{6,7},{7,6},{8,9},{9,8},{10,11... | collective-permute-start | bytes 983048 | tf_op jit(solution)/shard_map/ppermute | solution.py:190
  41.6 5.8 %collective-permute-start.14 = (bf16[128,512]{1,0:T(8,128)(2,1)S(1)}, bf16[128,512]{1,0:T(8,128)(2,1)S(1)}, u32[]{:S(2)}, u32[]{:S(2)}) collective-permute-start(bf16[128,512]{1,0:T(8,128)(2,1)S(1)} %collective-permute-done.9.refs_16_.refs_9_), channel_id=1, source_target_pairs={{0,2},{2,0},{1,3},{3,1},{4,6},{6,4},{5,7},{7,5},{8,10},{10,8},{9,1... | collective-permute-start | bytes 393224 | tf_op jit(solution)/shard_map/ppermute | solution.py:190
  43.1 4.3 %collective-permute-start.12 = (bf16[128,512]{1,0:T(8,128)(2,1)S(1)}, bf16[128,512]{1,0:T(8,128)(2,1)S(1)}, u32[]{:S(2)}, u32[]{:S(2)}) collective-permute-start(bf16[128,512]{1,0:T(8,128)(2,1)S(1)} %collective-permute-done.5.refs_3_.refs_1_), channel_id=1, source_target_pairs={{0,1},{1,0},{2,3},{3,2},{4,5},{5,4},{6,7},{7,6},{8,9},{9,8},{10,11... | collective-permute-start | bytes 393224 | tf_op jit(solution)/shard_map/ppermute | solution.py:190
  43.2 5.9 %collective-permute-start.11 = (bf16[128,512]{1,0:T(8,128)(2,1)S(1)}, bf16[128,512]{1,0:T(8,128)(2,1)}, u32[]{:S(2)}, u32[]{:S(2)}) collective-permute-start(bf16[128,512]{1,0:T(8,128)(2,1)S(1)} %collective-permute-done.5.refs_3_.refs_1_), channel_id=1, source_target_pairs={{0,4},{4,0},{1,5},{5,1},{2,6},{6,2},{3,7},{7,3},{8,12},{12,8},{9,1... | collective-permute-start | bytes 393224 | tf_op jit(solution)/shard_map/ppermute | solution.py:190
  49.1 1.8 %collective-permute-start.15 = (bf16[128,512]{1,0:T(8,128)(2,1)}, bf16[128,512]{1,0:T(8,128)(2,1)}, u32[]{:S(2)}, u32[]{:S(2)}) collective-permute-start(bf16[128,512]{1,0:T(8,128)(2,1)} %collective-permute-done.11.refs_6_.refs_3_), channel_id=1, source_target_pairs={{0,1},{1,0},{2,3},{3,2},{4,5},{5,4},{6,7},{7,6},{8,9},{9,8},{10,11... | collective-permute-start | bytes 393224 | tf_op jit(solution)/shard_map/ppermute | solution.py:190
  58.5 1.5 %collective-permute-start.16 = (f32[8,1024]{1,0:T(8,128)}, f32[8,1024]{1,0:T(8,128)S(1)}, u32[]{:S(2)}, u32[]{:S(2)}) collective-permute-start(f32[8,1024]{1,0:T(8,128)} %get-tuple-element.91), channel_id=1, source_target_pairs={{0,1},{1,0},{2,3},{3,2},{4,5},{5,4},{6,7},{7,6},{8,9},{9,8},{10,11... | collective-permute-start | bytes 98312 | tf_op jit(solution)/shard_map/ppermute | solution.py:190
  58.7 7.0 %collective-permute-start.22 = (f32[8,512]{1,0:T(8,128)}, f32[8,512]{1,0:T(8,128)S(1)}, u32[]{:S(2)}, u32[]{:S(2)}) collective-permute-start(f32[8,512]{1,0:T(8,128)} %get-tuple-element.92.refs_18_), channel_id=1, source_target_pairs={{0,18},{2,16},{16,2},{18,0},{1,19},{3,17},{17,3},{19,1},{4,22},{6,... | collective-permute-start | bytes 49160 | tf_op jit(solution)/shard_map/ppermute | solution.py:190
  60.7 9.8 %collective-permute-start.19 = (f32[8,1024]{1,0:T(8,128)S(1)}, f32[8,1024]{1,0:T(8,128)S(1)}, u32[]{:S(2)}, u32[]{:S(2)}) collective-permute-start(f32[8,1024]{1,0:T(8,128)S(1)} %add.41.refs_14_), channel_id=1, source_target_pairs={{0,12},{4,8},{8,4},{12,0},{1,13},{5,9},{9,5},{13,1},{2,14},{6,10},... | collective-permute-start | bytes 98312 | tf_op jit(solution)/shard_map/ppermute | solution.py:190
  63.5 7.0 %collective-permute-start.18 = (f32[8,1024]{1,0:T(8,128)S(1)}, f32[8,1024]{1,0:T(8,128)S(1)}, u32[]{:S(2)}, u32[]{:S(2)}) collective-permute-start(f32[8,1024]{1,0:T(8,128)S(1)} %add.41.refs_14_), channel_id=1, source_target_pairs={{0,4},{4,0},{1,5},{5,1},{2,6},{6,2},{3,7},{7,3},{8,12},{12,8},{9,1... | collective-permute-start | bytes 98312 | tf_op jit(solution)/shard_map/ppermute | solution.py:190
  64.0 6.5 %collective-permute-start.17 = (f32[8,1024]{1,0:T(8,128)S(1)}, f32[8,1024]{1,0:T(8,128)S(1)}, u32[]{:S(2)}, u32[]{:S(2)}) collective-permute-start(f32[8,1024]{1,0:T(8,128)S(1)} %add.41.refs_14_), channel_id=1, source_target_pairs={{0,8},{8,0},{1,9},{9,1},{2,10},{10,2},{3,11},{11,3},{4,12},{12,4},... | collective-permute-start | bytes 98312 | tf_op jit(solution)/shard_map/ppermute | solution.py:190
  64.2 3.9 %collective-permute-start.21 = (f32[8,512]{1,0:T(8,128)}, f32[8,512]{1,0:T(8,128)S(1)}, u32[]{:S(2)}, u32[]{:S(2)}) collective-permute-start(f32[8,512]{1,0:T(8,128)} %get-tuple-element.92.refs_18_), channel_id=1, source_target_pairs={{0,2},{2,0},{1,3},{3,1},{4,6},{6,4},{5,7},{7,5},{8,10},{10,8},{9,1... | collective-permute-start | bytes 49160 | tf_op jit(solution)/shard_map/ppermute | solution.py:190
  65.7 4.8 %collective-permute-start.20 = (f32[8,512]{1,0:T(8,128)}, f32[8,512]{1,0:T(8,128)S(1)}, u32[]{:S(2)}, u32[]{:S(2)}) collective-permute-start(f32[8,512]{1,0:T(8,128)} %get-tuple-element.92.refs_18_), channel_id=1, source_target_pairs={{0,16},{16,0},{1,17},{17,1},{2,18},{18,2},{3,19},{19,3},{4,20},{20... | collective-permute-start | bytes 49160 | tf_op jit(solution)/shard_map/ppermute | solution.py:190
  78.8 3.0 %collective-permute-start.23 = (f32[520,512]{1,0:T(8,128)}, f32[520,512]{1,0:T(8,128)S(1)}, u32[]{:S(2)}, u32[]{:S(2)}) collective-permute-start(f32[520,512]{1,0:T(8,128)} %get-tuple-element.94), channel_id=1, source_target_pairs={{0,1},{1,0},{2,3},{3,2},{4,5},{5,4},{6,7},{7,6},{8,9},{9,8},{10,11... | collective-permute-start | bytes 3194888 | tf_op jit(solution)/shard_map/ppermute | solution.py:190
  84.1 4.1 %collective-permute-start.24 = (f32[8,512]{1,0:T(8,128)S(1)}, f32[8,512]{1,0:T(8,128)S(1)}, u32[]{:S(2)}, u32[]{:S(2)}) collective-permute-start(f32[8,512]{1,0:T(8,128)S(1)} %slice_add_fusion.4), channel_id=1, source_target_pairs={{0,4},{4,0},{1,5},{5,1},{2,6},{6,2},{3,7},{7,3},{8,12},{12,8},{9,1... | collective-permute-start | bytes 49160 | tf_op jit(solution)/shard_map/ppermute | solution.py:190
  85.5 3.8 %collective-permute-start.27 = (f32[8,512]{1,0:T(8,128)S(1)}, f32[8,512]{1,0:T(8,128)S(1)}, u32[]{:S(2)}, u32[]{:S(2)}) collective-permute-start(f32[8,512]{1,0:T(8,128)S(1)} %copy-done.6), channel_id=1, source_target_pairs={{0,2},{2,0},{1,3},{3,1},{4,6},{6,4},{5,7},{7,5},{8,10},{10,8},{9,1... | collective-permute-start | bytes 49160 | tf_op jit(solution)/shard_map/ppermute | solution.py:190
  86.2 7.8 %collective-permute-start.25 = (f16[256,512]{1,0:T(8,128)(2,1)S(1)}, f16[256,512]{1,0:T(8,128)(2,1)S(1)}, u32[]{:S(2)}, u32[]{:S(2)}) collective-permute-start(f16[256,512]{1,0:T(8,128)(2,1)S(1)} %fusion), channel_id=1, source_target_pairs={{0,4},{4,0},{1,5},{5,1},{2,6},{6,2},{3,7},{7,3},{8,12},{12,8},{9,1... | collective-permute-start | bytes 786440 | tf_op jit(solution)/shard_map/ppermute | solution.py:190
  86.7 7.7 %collective-permute-start.26 = (f16[256,512]{1,0:T(8,128)(2,1)S(1)}, f16[256,512]{1,0:T(8,128)(2,1)S(1)}, u32[]{:S(2)}, u32[]{:S(2)}) collective-permute-start(f16[256,512]{1,0:T(8,128)(2,1)S(1)} %multiply_convert_fusion), channel_id=1, source_target_pairs={{0,2},{2,0},{1,3},{3,1},{4,6},{6,4},{5,7},{7,5},{8,10},{10,8},{9,1... | collective-permute-start | bytes 786440 | tf_op jit(solution)/shard_map/ppermute | solution.py:190
  94.5 6.0 %collective-permute-start.28 = (f32[8,512]{1,0:T(8,128)S(1)}, f32[8,512]{1,0:T(8,128)S(1)}, u32[]{:S(2)}, u32[]{:S(2)}) collective-permute-start(f32[8,512]{1,0:T(8,128)S(1)} %add.44), channel_id=1, source_target_pairs={{0,8},{8,0},{1,9},{9,1},{2,10},{10,2},{3,11},{11,3},{4,12},{12,4},... | collective-permute-start | bytes 49160 | tf_op jit(solution)/shard_map/ppermute | solution.py:190
  96.5 5.9 %collective-permute-start.29 = (f32[8,512]{1,0:T(8,128)S(1)}, f32[8,512]{1,0:T(8,128)S(1)}, u32[]{:S(2)}, u32[]{:S(2)}) collective-permute-start(f32[8,512]{1,0:T(8,128)S(1)} %add.47), channel_id=1, source_target_pairs={{0,16},{16,0},{1,17},{17,1},{2,18},{18,2},{3,19},{19,3},{4,20},{20... | collective-permute-start | bytes 49160 | tf_op jit(solution)/shard_map/ppermute | solution.py:190
  98.7 6.3 %collective-permute-start.30 = (f16[128,512]{1,0:T(8,128)(2,1)S(1)}, f16[128,512]{1,0:T(8,128)(2,1)S(1)}, u32[]{:S(2)}, u32[]{:S(2)}) collective-permute-start(f16[128,512]{1,0:T(8,128)(2,1)S(1)} %fusion.2), channel_id=1, source_target_pairs={{0,8},{8,0},{1,9},{9,1},{2,10},{10,2},{3,11},{11,3},{4,12},{12,4},... | collective-permute-start | bytes 393224 | tf_op jit(solution)/shard_map/ppermute | solution.py:190
  99.3 7.3 %collective-permute-start.31 = (f16[128,512]{1,0:T(8,128)(2,1)S(1)}, f16[128,512]{1,0:T(8,128)(2,1)S(1)}, u32[]{:S(2)}, u32[]{:S(2)}) collective-permute-start(f16[128,512]{1,0:T(8,128)(2,1)S(1)} %fusion.1), channel_id=1, source_target_pairs={{0,16},{16,0},{1,17},{17,1},{2,18},{18,2},{3,19},{19,3},{4,20},{20... | collective-permute-start | bytes 393224 | tf_op jit(solution)/shard_map/ppermute | solution.py:190
  (27 other events, 266.2 us)

commit v4 on v3

v4 whole, which is shorter than its diff:
```python
import functools

import jax
import jax.numpy as jnp
import numpy as np
from jax import lax
from jax.experimental import pallas as pl
from jax.experimental.pallas import tpu as pltpu
from jax.sharding import Mesh, PartitionSpec as P

F32 = jnp.float32
BF16 = jnp.bfloat16
F16 = jnp.float16
LOG2E = 1.4426950408889634
LN2 = 0.6931471805599453
LINES = 8
KINDS = 3
PARAMS = pltpu.CompilerParams(vmem_limit_bytes=56 * 2**20)
VMEM = pl.BlockSpec(memory_space=pltpu.VMEM)
SMEM = pl.BlockSpec(memory_space=pltpu.SMEM)


def matmul(a, b, da, db):
    return lax.dot_general(a, b, (((da,), (db,)), ((), ())), preferred_element_type=F32)


def block(k, b):
    return slice(k * b, (k + 1) * b)


def stack_rows(values, shape, axis, first=0):
    index = lax.broadcasted_iota(jnp.int32, shape, axis) - first
    out = jnp.zeros(shape, F32)
    for k, value in enumerate(values):
        out = jnp.where(index == k, value, out)
    return out


def tree(op, items):
    while len(items) > 1:
        items = [op(x, y) for x, y in zip(items[::2], items[1::2])]
    return items[0]


def stats_kernel(nr, nc, b, scale_t, scale_s, core, *refs):
    ti, si, refs = refs[:nr], refs[nr : 2 * nr], refs[2 * nr :]
    tt, st, refs = refs[:nc], refs[nc : 2 * nc], refs[2 * nc :]
    tl_ref, sl_ref, row_ref, swap_ref, col_ref, text_t, text_s = refs
    for p in range(nc):
        text_t[block(p, b), :] = tt[p][...]
        text_s[block(p, b), :] = st[p][...]
    largest = [
        functools.reduce(jnp.maximum, [jnp.max(jnp.abs(x[...].astype(F32)), 0, keepdims=True) for x in xs])
        for xs in (si, st)
    ]
    width = largest[0].shape[1]

    def with_largest(flat, k):
        if (k + 1) * b > width:
            return flat
        return flat + stack_rows((largest[1][:, block(k, b)],), flat.shape, 0, 2 * KINDS + core[0])

    step = 2 if nr % 2 == 0 else 1
    count = step * b
    peak_t = peak_s = None
    for p in range(0, nr, step):
        rows = slice(p * b, p * b + count)
        tl = matmul(jnp.concatenate([x[...] for x in ti[p : p + step]], 0), text_t[...], 1, 1) * (scale_t * LOG2E)
        sl = matmul(jnp.concatenate([x[...] for x in si[p : p + step]], 0), text_s[...], 1, 1) * (scale_s * LOG2E)
        tl_ref[rows, :] = tl
        sl_ref[rows, :] = sl
        top_t, top_s = jnp.max(tl, 0, keepdims=True), jnp.max(sl, 0, keepdims=True)
        peak_t = top_t if peak_t is None else jnp.maximum(peak_t, top_t)
        peak_s = top_s if peak_s is None else jnp.maximum(peak_s, top_s)
        mt, ms = jnp.max(tl, 1, keepdims=True), jnp.max(sl, 1, keepdims=True)
        et = jnp.exp2(tl - mt)
        sum_t = jnp.sum(et, 1, keepdims=True)
        gap = jnp.sum(et * (tl - sl), 1, keepdims=True)
        sum_s = jnp.sum(jnp.exp2(sl - ms), 1, keepdims=True)
        lines = (mt + jnp.log2(sum_t), ms + jnp.log2(sum_s), gap / sum_t)
        lines = stack_rows(lines, (count, 128), 1, core[0] * KINDS)
        for k in range(step):
            flat = jnp.transpose(lines[block(k, b)])[:LINES]
            other = (p + k) ^ (nr // 2)
            row_ref[:, block(p + k, b)] = with_largest(flat, p + k)
            swap_ref[:, block(other, b)] = with_largest(flat, other)
    sum_t = sum_s = gap = None
    for p in range(0, nr, step):
        tl, sl = tl_ref[p * b : p * b + count, :], sl_ref[p * b : p * b + count, :]
        et = jnp.exp2(tl - peak_t)
        parts = [
            jnp.sum(et, 0, keepdims=True),
            jnp.sum(jnp.exp2(sl - peak_s), 0, keepdims=True),
            jnp.sum(et * (tl - sl), 0, keepdims=True),
        ]
        sum_t, sum_s, gap = parts if p == 0 else [x + y for x, y in zip((sum_t, sum_s, gap), parts)]
    lines = (peak_t + jnp.log2(sum_t), peak_s + jnp.log2(sum_s), gap / sum_t)
    images = largest[0]
    if col_ref.shape[1] > width:
        images = jnp.concatenate([images, jnp.zeros((1, col_ref.shape[1] - width), F32)], 1)
    col_ref[...] = stack_rows(lines + (images,), col_ref.shape, 0)


def combine(tiles, terms):
    lses = []
    for kind in (1, 0):
        peak = tree(jnp.maximum, [x[kind] for x in tiles])
        weights = [jnp.exp2(x[kind] - peak) for x in tiles]
        total = tree(jnp.add, weights)
        lses.append(peak + jnp.log2(total))
    for k, (w, x) in enumerate(zip(weights, tiles)):
        terms[k : k + 1, :] = w * x[2]
    gap = tree(jnp.add, [terms[k : k + 1, :] for k in range(len(tiles))])
    return lses[1], lses[0], gap / total + (lses[0] - lses[1])


def sum_blocks(x, b):
    parts = [jnp.sum(x[:, block(p, b)], axis=(0, 1), keepdims=True) for p in range(x.shape[1] // b)]
    return tree(jnp.add, parts) * LN2


def powers(largest, pairs, scale):
    bound = functools.reduce(jnp.maximum, largest) * ((1 + pairs) * scale)
    power = jnp.ceil(jnp.log2(jnp.maximum(bound, 1e-30)))
    return jnp.exp2(15.0 - power) * scale, jnp.exp2(power - 15.0)


def gradient_kernel(nr, nc, b, pairs, scale, *refs):
    si, refs = refs[:nr], refs[nr:]
    st, refs = refs[:nc], refs[nc:]
    tl_ref, sl_ref, refs = refs[0], refs[1], refs[2:]
    row_parts, refs = refs[: nr // 2], refs[nr // 2 :]
    col_parts, refs = refs[:nc], refs[nc:]
    image_keep, image_send, text_keep, text_send, back, image_share, text_share, refs = *refs[:7], refs[7:]
    width = back.shape[1]
    lines = [x[2 * KINDS + core : 2 * KINDS + core + 1, :width] for x in row_parts for core in range(2)]
    image_scale, image_back = powers(lines, pairs, scale)
    text_scale, text_back = powers([x[KINDS : KINDS + 1, :width] for x in col_parts], pairs, scale)
    back[...] = stack_rows((image_back, text_back), back.shape, 0)
    text, image, high_ref, low_ref, row_terms, col_terms = refs
    for p in range(nc):
        text[block(p, b), :] = st[p][...]
    for p in range(nr):
        image[block(p, b), :] = si[p][...]
    tiles = []
    for q in range(nr // 2):
        x = jnp.concatenate([row_parts[q][:, block(p ^ q, b)] for p in range(nr)], 1)
        for core in range(2):
            tiles.append([x[core * KINDS + k : core * KINDS + k + 1, :] for k in range(KINDS)])
    row_t, row_s, terms = combine(tiles, row_terms)
    row_share = sum_blocks(terms, b)
    rows = stack_rows((row_t, row_s), (LINES, nr * b), 0)
    tiles = []
    for q in range(nc):
        x = jnp.concatenate([col_parts[q][:, block(p ^ q, b)] for p in range(nc)], 1)
        tiles.append([x[k : k + 1, :] for k in range(KINDS)])
    col_t, col_s, terms = combine(tiles, col_terms)
    col_share = sum_blocks(terms, b)
    half = nr // 2
    for p in range(nr):
        row = jnp.transpose(rows[:, block(p, b)])
        tl, sl = tl_ref[block(p, b), :], sl_ref[block(p, b), :]
        delta = (jnp.exp2(sl - row[:, 1:2]) - jnp.exp2(tl - row[:, 0:1])) + (
            jnp.exp2(sl - col_s) - jnp.exp2(tl - col_t)
        )
        high = delta.astype(BF16)
        high_ref[block(p, b), :] = high
        low_ref[block(p, b), :] = (delta - high.astype(F32)).astype(BF16)
    image_share[...] = jnp.broadcast_to(col_share, image_share.shape)
    text_share[...] = jnp.broadcast_to(row_share, text_share.shape)
    step = 2 if half % 2 == 0 else 1
    for p in range(0, nr, step):
        rows = slice(p * b, (p + step) * b)
        part = (matmul(high_ref[rows, :], text[...], 1, 0) + matmul(low_ref[rows, :], text[...], 1, 0)) * image_scale
        if p < half:
            image_keep[rows, :] = part
        else:
            image_send[(p - half) * b : (p - half + step) * b, :] = part
    half = nc // 2
    step = 2 if half % 2 == 0 else 1
    for p in range(0, nc, step):
        cols = slice(p * b, (p + step) * b)
        part = (matmul(high_ref[:, cols], image[...], 0, 0) + matmul(low_ref[:, cols], image[...], 0, 0)) * text_scale
        if p < half:
            text_keep[cols, :] = part
        else:
            text_send[(p - half) * b : (p - half + step) * b, :] = part


def call(kernel, outs, args, scratch=(), flops=0, transcendentals=0):
    shapes = [jax.ShapeDtypeStruct(s, d) for s, d in outs]
    size = sum(x.size * x.dtype.itemsize for x in list(args) + shapes)
    return pl.pallas_call(
        kernel,
        out_shape=shapes,
        in_specs=[SMEM if x.dtype == jnp.int32 else VMEM for x in args],
        out_specs=[VMEM] * len(shapes),
        scratch_shapes=[pltpu.VMEM(s, d) for s, d in scratch],
        compiler_params=PARAMS,
        cost_estimate=pl.CostEstimate(flops=flops, bytes_accessed=size, transcendentals=transcendentals),
    )(*args)


def swap(bits, x):
    perm = [(i, i ^ ((1 << len(bits)) - 1)) for i in range(1 << len(bits))]
    return lax.ppermute(x, bits, perm)


def subset(bits, q):
    return tuple(b for k, b in enumerate(bits) if q >> k & 1)


def together(*groups):
    return lax.optimization_barrier(groups)


def stage_of(bits, pair, part, p):
    count = bin(p).count("1")
    late = count == 2 and pair in subset(bits, p)
    if part == 0:
        return 0 if count == 1 else count + (late and p & 1)
    return 1 if count == 1 and p > 1 else count + 1 + late


def gather(image_bits, text_bits, image, text):
    groups = [(image_bits, image), (text_bits, text)]
    have = {(n, part, 0): x for n, (_, own) in enumerate(groups) for part, x in enumerate(own)}
    stages = {}
    for n, (bits, _) in enumerate(groups):
        for part in range(2):
            for p in range(1, 1 << len(bits)):
                stages.setdefault(stage_of(bits, image_bits[-1], part, p), []).append((n, part, p))
    for stage in sorted(stages):
        top = {key: 1 << key[2].bit_length() - 1 for key in stages[stage]}
        sources = {key: have[key[0], key[1], key[2] ^ top[key]] for key in stages[stage]}
        if stage:
            gates = [x for key, x in have.items() if key[2] and (stage > 1 or key[2] > 1)]
            sources, _ = together(sources, gates)
        for key, x in sources.items():
            have[key] = swap(subset(groups[key[0]][0], top[key]), x)
    return [[have[n, part, p] for p in range(1 << len(bits))] for n, (bits, _) in enumerate(groups) for part in range(2)]


def halves(x):
    return x[: x.shape[0] // 2], x[x.shape[0] // 2 :]


def local(image_bits, text_bits, teacher_image, teacher_text, student_image, student_text):
    b, tw = teacher_image.shape
    sw = student_image.shape[1]
    nr, nc = 1 << len(image_bits), 1 << len(text_bits)
    r, c = nr * b, nc * b
    pair, others = image_bits[-1:], image_bits[:-1]
    ti, si, tt, st = gather(image_bits, text_bits, (teacher_image, student_image), (teacher_text, student_text))
    core = lax.axis_index(pair).astype(jnp.int32).reshape(1)
    tl, sl, rows, rows_swapped, cols = call(
        functools.partial(stats_kernel, nr, nc, b, tw**-0.5, sw**-0.5),
        [((r, c), F32), ((r, c), F32), ((LINES, r), F32), ((LINES, r), F32), ((LINES, c), F32)],
        [core] + ti + si + tt + st, [((c, tw), BF16), ((c, sw), BF16)], 2 * r * c * (tw + sw), 4 * r * c,
    )
    other = swap(pair, rows_swapped)
    col_parts = [cols] + [swap(subset(text_bits, q), cols) for q in range(1, nc)]
    rows = rows + other
    row_parts = [rows] + [swap(subset(others, q), rows) for q in range(1, nr // 2)]
    pairs = b << (len(image_bits) + len(text_bits))
    lanes = ((8, 128), F32)
    image_keep, image_send, text_keep, text_send, back, image_share, text_share = call(
        functools.partial(gradient_kernel, nr, nc, b, pairs, sw**-0.5),
        [((n, sw), F32) for n in (r // 2, r // 2, c // 2, c // 2)] + [((8, sw), F32), lanes, lanes],
        si + st + [tl, sl] + row_parts + col_parts,
        [((c, sw), BF16), ((r, sw), BF16), ((r, c), BF16), ((r, c), BF16), ((nr, r), F32), ((max(nc, 8), c), F32)],
        8 * r * c * sw, 4 * r * c,
    )
    image_keep, image_send = halves(image_keep + swap(pair, image_send))
    image_share = image_share + swap(pair, image_share)
    for k in reversed(range(max(len(text_bits), len(others)))):
        todo = {}
        if k < len(text_bits):
            todo["text"] = [text_send.astype(F16), text_share]
        if k < len(others):
            todo["image"] = [image_send.astype(F16), image_share]
        (todo,) = together(todo)
        if k < len(text_bits):
            come, share = [swap(text_bits[k : k + 1], x) for x in todo["text"]]
            text_total, text_share = text_keep + come.astype(F32), text_share + share
            text_keep, text_send = halves(text_total)
        if k < len(others):
            come, share = [swap(others[k : k + 1], x) for x in todo["image"]]
            image_total, image_share = image_keep + come.astype(F32), image_share + share
            image_keep, image_send = halves(image_total)
    loss = (image_share[0, 0] + text_share[0, 0]) / (2.0 * pairs)
    return (loss, image_total * back[0:1], text_total * back[1:2])


def solution(mesh):
    bits = {axis: [f"{axis}{k}" for k in reversed(range(mesh.shape[axis].bit_length() - 1))] for axis in ("img", "txt")}
    names = bits["img"] + bits["txt"]
    cube = Mesh(np.asarray(mesh.devices).reshape((2,) * len(names)), names)
    text_bits = [x for x in bits["img"] if int(x[3:]) >= 1] + [x for x in bits["txt"] if int(x[3:]) % 2 == 1]
    image_bits = [x for x in names if x not in text_bits]
    image, text = P(tuple(names), None), P(tuple(bits["txt"] + bits["img"]), None)
    return jax.shard_map(
        functools.partial(local, tuple(image_bits), tuple(text_bits)),
        mesh=cube,
        in_specs=(image, text, image, text),
        out_specs=(P(), image, text),
        check_vma=False,
    )
```

time: 109 us -> 103 us (0.945)
  waiting for transfers between devices: 45.9 us -> 38.3 us
  starting transfers between devices: 31.2 us -> 37.9 us
  other arithmetic: 7.81 us -> 5.76 us
  between operations: 4.81 us -> 3.4 us
    ppermute x32 -> x37, waiting for transfers between devices: 45.9 us -> 38.3 us  [swap(): return lax.ppermute(x, bits, perm)]
    ppermute x32 -> x37, starting transfers between devices: 31.2 us -> 37.9 us  [swap(): return lax.ppermute(x, bits, perm)]
    mul x0 -> x2, other arithmetic: none -> 1.49 us  [local(): return (loss, image_total * back[0:1], text_total * back[1:2])]
    add x8, other arithmetic: 3.84 us -> 2.35 us  [the longest x1 1.49 us: local(): image_keep, image_send = halves(image_keep + swap(pair, image_send))]
    concatenate x1 -> x0, other arithmetic: 1.14 us -> none  [gather(): both = jnp.concatenate([teacher, student], 1)]
  transfers between devices with their start and end apart: 32 -> 37, of which waited for: 16 -> 18; matrix products, arithmetic and copies ran while one was open for 5% -> 5% of each run, Pallas kernels for 0% -> 0%
where the time goes in v4:
time: 103 us
  waiting for transfers between devices  38.3 us (37%)
  starting transfers between devices  37.9 us (37%)
  Pallas kernels  14.6 us (14%)
  other arithmetic  5.76 us (6%)
  between operations  3.4 us (3%)
  local copies, waits for them, and re-layouts  3.05 us (3%)
    ppermute x37, waiting for transfers between devices, swap(): return lax.ppermute(x, bits, perm)  38.3 us
    ppermute x37, starting transfers between devices, swap(): return lax.ppermute(x, bits, perm)  37.9 us
    pallas_call x2, Pallas kernels, call(): pl.pallas_call(kernel, out_shape=shapes, in_specs=[SMEM if x.dtype == jnp...  14.6 us
  transfers between devices with their start and end apart: 37, of which 18 were waited for; matrix products, arithmetic and copies ran while one was open for 5% of the time, Pallas kernels for 0%

profile of v4, /device:TPU:0, one launch (start us, length us, event | category | flops | bytes accessed | tf_op | source)
XLA Modules:
  0.0 102.9 jit_solution(7208605217848531517)
XLA Ops:
  0.6 3.0 %collective-permute-start.4 = (bf16[128,1280]{1,0:T(8,128)(2,1)}, bf16[128,1280]{1,0:T(8,128)(2,1)S(1)}, u32[]{:S(2)}, u32[]{:S(2)}) collective-permute-start(bf16[128,1280]{1,0:T(8,128)(2,1)} %refs_16_.1), channel_id=1, source_target_pairs={{0,2},{2,0},{1,3},{3,1},{4,6},{6,4},{5,7},{7,5},{8,10},{10,8},{9,1... | collective-permute-start | bytes 983048 | tf_op jit(solution)/shard_map/ppermute | solution.py:206
  3.6 1.5 %collective-permute-start.1 = (bf16[128,1280]{1,0:T(8,128)(2,1)}, bf16[128,1280]{1,0:T(8,128)(2,1)S(1)}, u32[]{:S(2)}, u32[]{:S(2)}) collective-permute-start(bf16[128,1280]{1,0:T(8,128)(2,1)} %refs_0_.2), channel_id=1, source_target_pairs={{0,4},{4,0},{1,5},{5,1},{2,6},{6,2},{3,7},{7,3},{8,12},{12,8},{9,1... | collective-permute-start | bytes 983048 | tf_op jit(solution)/shard_map/ppermute | solution.py:206
  5.2 2.6 %collective-permute-start.2 = (bf16[128,1280]{1,0:T(8,128)(2,1)}, bf16[128,1280]{1,0:T(8,128)(2,1)S(1)}, u32[]{:S(2)}, u32[]{:S(2)}) collective-permute-start(bf16[128,1280]{1,0:T(8,128)(2,1)} %refs_16_.1), channel_id=1, source_target_pairs={{0,16},{16,0},{1,17},{17,1},{2,18},{18,2},{3,19},{19,3},{4,20},{20... | collective-permute-start | bytes 983048 | tf_op jit(solution)/shard_map/ppermute | solution.py:206
  7.7 1.6 %collective-permute-start = (bf16[128,1280]{1,0:T(8,128)(2,1)}, bf16[128,1280]{1,0:T(8,128)(2,1)S(1)}, u32[]{:S(2)}, u32[]{:S(2)}) collective-permute-start(bf16[128,1280]{1,0:T(8,128)(2,1)} %refs_0_.2), channel_id=1, source_target_pairs={{0,8},{8,0},{1,9},{9,1},{2,10},{10,2},{3,11},{11,3},{4,12},{12,4},... | collective-permute-start | bytes 983048 | tf_op jit(solution)/shard_map/ppermute | solution.py:206
  9.3 2.2 %collective-permute-done.4.refs_18_ = bf16[128,1280]{1,0:T(8,128)(2,1)S(1)} collective-permute-done((bf16[128,1280]{1,0:T(8,128)(2,1)}, bf16[128,1280]{1,0:T(8,128)(2,1)S(1)}, u32[]{:S(2)}, u32[]{:S(2)}) %collective-permute-start.4) | collective-permute-done | bytes 327712 | tf_op jit(solution)/shard_map/ppermute | solution.py:206
  11.6 1.5 %collective-permute-done.1.refs_2_ = bf16[128,1280]{1,0:T(8,128)(2,1)S(1)} collective-permute-done((bf16[128,1280]{1,0:T(8,128)(2,1)}, bf16[128,1280]{1,0:T(8,128)(2,1)S(1)}, u32[]{:S(2)}, u32[]{:S(2)}) %collective-permute-start.1) | collective-permute-done | bytes 327712 | tf_op jit(solution)/shard_map/ppermute | solution.py:206
  13.0 1.6 %collective-permute-start.5 = (bf16[128,512]{1,0:T(8,128)(2,1)}, bf16[128,512]{1,0:T(8,128)(2,1)S(1)}, u32[]{:S(2)}, u32[]{:S(2)}) collective-permute-start(bf16[128,512]{1,0:T(8,128)(2,1)} %refs_0_.3), channel_id=1, source_target_pairs={{0,4},{4,0},{1,5},{5,1},{2,6},{6,2},{3,7},{7,3},{8,12},{12,8},{9,1... | collective-permute-start | bytes 393224 | tf_op jit(solution)/shard_map/ppermute | solution.py:206
  15.1 8.4 %collective-permute-done.2.refs_17_ = bf16[128,1280]{1,0:T(8,128)(2,1)S(1)} collective-permute-done((bf16[128,1280]{1,0:T(8,128)(2,1)}, bf16[128,1280]{1,0:T(8,128)(2,1)S(1)}, u32[]{:S(2)}, u32[]{:S(2)}) %collective-permute-start.2) | collective-permute-done | bytes 327712 | tf_op jit(solution)/shard_map/ppermute | solution.py:206
  24.8 1.5 %collective-permute-start.8 = (bf16[128,512]{1,0:T(8,128)(2,1)}, bf16[128,512]{1,0:T(8,128)(2,1)}, u32[]{:S(2)}, u32[]{:S(2)}) collective-permute-start(bf16[128,512]{1,0:T(8,128)(2,1)} %refs_0_.3), channel_id=1, source_target_pairs={{0,8},{8,0},{1,9},{9,1},{2,10},{10,2},{3,11},{11,3},{4,12},{12,4},... | collective-permute-start | bytes 393224 | tf_op jit(solution)/shard_map/ppermute | solution.py:206
  26.3 2.3 %collective-permute-start.10 = (bf16[128,512]{1,0:T(8,128)(2,1)}, bf16[128,512]{1,0:T(8,128)(2,1)S(1)}, u32[]{:S(2)}, u32[]{:S(2)}) collective-permute-start(bf16[128,512]{1,0:T(8,128)(2,1)} %refs_8_.3), channel_id=1, source_target_pairs={{0,16},{16,0},{1,17},{17,1},{2,18},{18,2},{3,19},{19,3},{4,20},{20... | collective-permute-start | bytes 393224 | tf_op jit(solution)/shard_map/ppermute | solution.py:206
  28.6 4.4 %collective-permute-done.8.refs_9_.refs_1_ = bf16[128,512]{1,0:T(8,128)(2,1)} collective-permute-done((bf16[128,512]{1,0:T(8,128)(2,1)}, bf16[128,512]{1,0:T(8,128)(2,1)}, u32[]{:S(2)}, u32[]{:S(2)}) %collective-permute-start.8) | collective-permute-done | bytes 131104 | tf_op jit(solution)/shard_map/ppermute | solution.py:206
  33.0 2.6 %collective-permute-done.10.refs_21_.refs_9_ = bf16[128,512]{1,0:T(8,128)(2,1)S(1)} collective-permute-done((bf16[128,512]{1,0:T(8,128)(2,1)}, bf16[128,512]{1,0:T(8,128)(2,1)S(1)}, u32[]{:S(2)}, u32[]{:S(2)}) %collective-permute-start.10) | collective-permute-done | bytes 131104 | tf_op jit(solution)/shard_map/ppermute | solution.py:206
  36.2 1.5 %collective-permute-start.13 = (bf16[128,512]{1,0:T(8,128)(2,1)}, bf16[128,512]{1,0:T(8,128)(2,1)}, u32[]{:S(2)}, u32[]{:S(2)}) collective-permute-start(bf16[128,512]{1,0:T(8,128)(2,1)} %collective-permute-done.8.refs_9_.refs_1_), channel_id=1, source_target_pairs={{0,4},{4,0},{1,5},{5,1},{2,6},{6,2},{3,7},{7,3},{8,12},{12,8},{9,1... | collective-permute-start | bytes 393224 | tf_op jit(solution)/shard_map/ppermute | solution.py:206
  37.7 1.5 %collective-permute-start.16 = (bf16[128,512]{1,0:T(8,128)(2,1)S(1)}, bf16[128,512]{1,0:T(8,128)(2,1)S(1)}, u32[]{:S(2)}, u32[]{:S(2)}) collective-permute-start(bf16[128,512]{1,0:T(8,128)(2,1)S(1)} %collective-permute-done.10.refs_21_.refs_9_), channel_id=1, source_target_pairs={{0,2},{2,0},{1,3},{3,1},{4,6},{6,4},{5,7},{7,5},{8,10},{10,8},{9,1... | collective-permute-start | bytes 393224 | tf_op jit(solution)/shard_map/ppermute | solution.py:206
  39.2 2.8 %collective-permute-done.13.refs_11_.refs_3_ = bf16[128,512]{1,0:T(8,128)(2,1)} collective-permute-done((bf16[128,512]{1,0:T(8,128)(2,1)}, bf16[128,512]{1,0:T(8,128)(2,1)}, u32[]{:S(2)}, u32[]{:S(2)}) %collective-permute-start.13) | collective-permute-done | bytes 131104 | tf_op jit(solution)/shard_map/ppermute | solution.py:206
  45.6 7.7 %shard_map.67 = (f32[1024,512]{1,0:T(8,128)}, f32[1024,512]{1,0:T(8,128)}, f32[8,1024]{1,0:T(8,128)}, f32[8,1024]{1,0:T(8,128)}, f32[8,512]{1,0:T(8,128)}) custom-call(s32[1]{0:T(128)} %bitcast.core, bf16[128,1280]{1,0:T(8,128)(2,1)} %refs_0_.2, bf16[128,1280]{1,0:T(8,128)(2,1)} %copy-done.7, bf16[128,1280]{1,0:T(8,128)(2,1)} %copy-done.4, ...), custom_call_target="tpu_custom_call" | custom-call | flops 1879048192 | bytes 9781252 | tf_op jit(solution)/shard_map/pallas_call | solution.py:193
  53.6 1.3 %collective-permute-start.26 = (f32[8,512]{1,0:T(8,128)}, f32[8,512]{1,0:T(8,128)S(1)}, u32[]{:S(2)}, u32[]{:S(2)}) collective-permute-start(f32[8,512]{1,0:T(8,128)} %get-tuple-element.57.refs_18_), channel_id=1, source_target_pairs={{0,18},{2,16},{16,2},{18,0},{1,19},{3,17},{17,3},{19,1},{4,22},{6,... | collective-permute-start | bytes 49160 | tf_op jit(solution)/shard_map/ppermute | solution.py:206
  55.7 2.3 %collective-permute-start.23 = (f32[8,1024]{1,0:T(8,128)S(1)}, f32[8,1024]{1,0:T(8,128)S(1)}, u32[]{:S(2)}, u32[]{:S(2)}) collective-permute-start(f32[8,1024]{1,0:T(8,128)S(1)} %add.37.refs_14_), channel_id=1, source_target_pairs={{0,12},{4,8},{8,4},{12,0},{1,13},{5,9},{9,5},{13,1},{2,14},{6,10},... | collective-permute-start | bytes 98312 | tf_op jit(solution)/shard_map/ppermute | solution.py:206
  58.0 1.4 %collective-permute-start.22 = (f32[8,1024]{1,0:T(8,128)S(1)}, f32[8,1024]{1,0:T(8,128)S(1)}, u32[]{:S(2)}, u32[]{:S(2)}) collective-permute-start(f32[8,1024]{1,0:T(8,128)S(1)} %add.37.refs_14_), channel_id=1, source_target_pairs={{0,4},{4,0},{1,5},{5,1},{2,6},{6,2},{3,7},{7,3},{8,12},{12,8},{9,1... | collective-permute-start | bytes 98312 | tf_op jit(solution)/shard_map/ppermute | solution.py:206
  60.5 1.8 %collective-permute-start.24 = (f32[8,512]{1,0:T(8,128)}, f32[8,512]{1,0:T(8,128)S(1)}, u32[]{:S(2)}, u32[]{:S(2)}) collective-permute-start(f32[8,512]{1,0:T(8,128)} %get-tuple-element.57.refs_18_), channel_id=1, source_target_pairs={{0,16},{16,0},{1,17},{17,1},{2,18},{18,2},{3,19},{19,3},{4,20},{20... | collective-permute-start | bytes 49160 | tf_op jit(solution)/shard_map/ppermute | solution.py:206
  62.3 1.1 %collective-permute-done.25.refs_20_ = f32[8,512]{1,0:T(8,128)S(1)} collective-permute-done((f32[8,512]{1,0:T(8,128)}, f32[8,512]{1,0:T(8,128)S(1)}, u32[]{:S(2)}, u32[]{:S(2)}) %collective-permute-start.25) | collective-permute-done | bytes 16416 | tf_op jit(solution)/shard_map/ppermute | solution.py:206
  63.4 2.0 %collective-permute-done.24.refs_19_ = f32[8,512]{1,0:T(8,128)S(1)} collective-permute-done((f32[8,512]{1,0:T(8,128)}, f32[8,512]{1,0:T(8,128)S(1)}, u32[]{:S(2)}, u32[]{:S(2)}) %collective-permute-start.24) | collective-permute-done | bytes 16416 | tf_op jit(solution)/shard_map/ppermute | solution.py:206
  66.0 6.9 %shard_map.68 = (f32[512,512]{1,0:T(8,128)}, f32[512,512]{1,0:T(8,128)}, f32[256,512]{1,0:T(8,128)}, f32[256,512]{1,0:T(8,128)}, f32[8,512]{1,0:T(8,128)}, /*index=5*/f32[8,128]{1,0:T(8,128)}, f32[8,128]{1,0:T(8,128)}) custom-call(bf16[128,512]{1,0:T(8,128)(2,1)} %refs_0_.3, bf16[128,512]{1,0:T(8,128)(2,1)} %collective-permute-done.8.refs_9_.refs_1_, ...), custom_call_target="tpu_custom_call" | custom-call | flops 2147483648 | bytes 9134080 | tf_op jit(solution)/shard_map/pallas_call | solution.py:193
  74.6 1.3 %collective-permute-done.27 = f32[8,128]{1,0:T(8,128)S(1)} collective-permute-done((f32[8,128]{1,0:T(8,128)}, f32[8,128]{1,0:T(8,128)S(1)}, u32[]{:S(2)}, u32[]{:S(2)}) %collective-permute-start.27) | collective-permute-done | bytes 4128 | tf_op jit(solution)/shard_map/ppermute | solution.py:206
  76.5 1.5 %add.39 = f32[512,512]{1,0:T(8,128)S(1)} add(f32[512,512]{1,0:T(8,128)} %get-tuple-element.59, f32[512,512]{1,0:T(8,128)S(1)} %collective-permute-done.28) | non-fusion elementwise | flops 262144 | bytes 3145728 | tf_op jit(solution)/shard_map/add | solution.py:274
  78.7 1.4 %collective-permute-start.29 = (f32[8,128]{1,0:T(8,128)S(1)}, f32[8,128]{1,0:T(8,128)S(1)}, u32[]{:S(2)}, u32[]{:S(2)}) collective-permute-start(f32[8,128]{1,0:T(8,128)S(1)} %add.38), channel_id=1, source_target_pairs={{0,4},{4,0},{1,5},{5,1},{2,6},{6,2},{3,7},{7,3},{8,12},{12,8},{9,1... | collective-permute-start | bytes 12296 | tf_op jit(solution)/shard_map/ppermute | solution.py:206
  82.2 4.4 %collective-permute-done.29 = f32[8,128]{1,0:T(8,128)S(1)} collective-permute-done((f32[8,128]{1,0:T(8,128)S(1)}, f32[8,128]{1,0:T(8,128)S(1)}, u32[]{:S(2)}, u32[]{:S(2)}) %collective-permute-start.29) | collective-permute-done | bytes 4128 | tf_op jit(solution)/shard_map/ppermute | solution.py:206
  86.7 2.0 %collective-permute-done.31 = f16[256,512]{1,0:T(8,128)(2,1)S(1)} collective-permute-done((f16[256,512]{1,0:T(8,128)(2,1)S(1)}, f16[256,512]{1,0:T(8,128)(2,1)S(1)}, u32[]{:S(2)}, u32[]{:S(2)}) %collective-permute-start.31) | collective-permute-done | bytes 262176 | tf_op jit(solution)/shard_map/ppermute | solution.py:206
  88.8 2.1 %collective-permute-start.33 = (f32[8,128]{1,0:T(8,128)S(1)}, f32[8,128]{1,0:T(8,128)S(1)}, u32[]{:S(2)}, u32[]{:S(2)}) collective-permute-start(f32[8,128]{1,0:T(8,128)S(1)} %add.40), channel_id=1, source_target_pairs={{0,8},{8,0},{1,9},{9,1},{2,10},{10,2},{3,11},{11,3},{4,12},{12,4},... | collective-permute-start | bytes 12296 | tf_op jit(solution)/shard_map/ppermute | solution.py:206
  91.3 1.9 %collective-permute-start.35 = (f16[128,512]{1,0:T(8,128)(2,1)S(1)}, f16[128,512]{1,0:T(8,128)(2,1)S(1)}, u32[]{:S(2)}, u32[]{:S(2)}) collective-permute-start(f16[128,512]{1,0:T(8,128)(2,1)S(1)} %slice_convert_fusion.2), channel_id=1, source_target_pairs={{0,8},{8,0},{1,9},{9,1},{2,10},{10,2},{3,11},{11,3},{4,12},{12,4},... | collective-permute-start | bytes 393224 | tf_op jit(solution)/shard_map/ppermute | solution.py:206
  95.2 1.6 %collective-permute-done.34 = f32[8,128]{1,0:T(8,128)S(1)} collective-permute-done((f32[8,128]{1,0:T(8,128)S(1)}, f32[8,128]{1,0:T(8,128)S(1)}, u32[]{:S(2)}, u32[]{:S(2)}) %collective-permute-start.34) | collective-permute-done | bytes 4128 | tf_op jit(solution)/shard_map/ppermute | solution.py:206
  99.4 1.7 %collective-permute-done.36 = f16[128,512]{1,0:T(8,128)(2,1)S(1)} collective-permute-done((f16[128,512]{1,0:T(8,128)(2,1)S(1)}, f16[128,512]{1,0:T(8,128)(2,1)S(1)}, u32[]{:S(2)}, u32[]{:S(2)}) %collective-permute-start.36) | collective-permute-done | bytes 131104 | tf_op jit(solution)/shard_map/ppermute | solution.py:206
  (108 shorter events, 18.4 us)
Async XLA Ops:
  0.6 10.9 %collective-permute-start.4 = (bf16[128,1280]{1,0:T(8,128)(2,1)}, bf16[128,1280]{1,0:T(8,128)(2,1)S(1)}, u32[]{:S(2)}, u32[]{:S(2)}) collective-permute-start(bf16[128,1280]{1,0:T(8,128)(2,1)} %refs_16_.1), channel_id=1, source_target_pairs={{0,2},{2,0},{1,3},{3,1},{4,6},{6,4},{5,7},{7,5},{8,10},{10,8},{9,1... | collective-permute-start | bytes 983048 | tf_op jit(solution)/shard_map/ppermute | solution.py:206
  3.6 9.4 %collective-permute-start.1 = (bf16[128,1280]{1,0:T(8,128)(2,1)}, bf16[128,1280]{1,0:T(8,128)(2,1)S(1)}, u32[]{:S(2)}, u32[]{:S(2)}) collective-permute-start(bf16[128,1280]{1,0:T(8,128)(2,1)} %refs_0_.2), channel_id=1, source_target_pairs={{0,4},{4,0},{1,5},{5,1},{2,6},{6,2},{3,7},{7,3},{8,12},{12,8},{9,1... | collective-permute-start | bytes 983048 | tf_op jit(solution)/shard_map/ppermute | solution.py:206
  5.2 7.9 %collective-permute-start.3 = (bf16[128,1280]{1,0:T(8,128)(2,1)}, bf16[128,1280]{1,0:T(8,128)(2,1)S(1)}, u32[]{:S(2)}, u32[]{:S(2)}) collective-permute-start(bf16[128,1280]{1,0:T(8,128)(2,1)} %refs_0_.2), channel_id=1, source_target_pairs={{0,1},{1,0},{2,3},{3,2},{4,5},{5,4},{6,7},{7,6},{8,9},{9,8},{10,11... | collective-permute-start | bytes 983048 | tf_op jit(solution)/shard_map/ppermute | solution.py:206
  5.2 18.4 %collective-permute-start.2 = (bf16[128,1280]{1,0:T(8,128)(2,1)}, bf16[128,1280]{1,0:T(8,128)(2,1)S(1)}, u32[]{:S(2)}, u32[]{:S(2)}) collective-permute-start(bf16[128,1280]{1,0:T(8,128)(2,1)} %refs_16_.1), channel_id=1, source_target_pairs={{0,16},{16,0},{1,17},{17,1},{2,18},{18,2},{3,19},{19,3},{4,20},{20... | collective-permute-start | bytes 983048 | tf_op jit(solution)/shard_map/ppermute | solution.py:206
  7.7 16.0 %collective-permute-start = (bf16[128,1280]{1,0:T(8,128)(2,1)}, bf16[128,1280]{1,0:T(8,128)(2,1)S(1)}, u32[]{:S(2)}, u32[]{:S(2)}) collective-permute-start(bf16[128,1280]{1,0:T(8,128)(2,1)} %refs_0_.2), channel_id=1, source_target_pairs={{0,8},{8,0},{1,9},{9,1},{2,10},{10,2},{3,11},{11,3},{4,12},{12,4},... | collective-permute-start | bytes 983048 | tf_op jit(solution)/shard_map/ppermute | solution.py:206
  13.0 10.7 %collective-permute-start.5 = (bf16[128,512]{1,0:T(8,128)(2,1)}, bf16[128,512]{1,0:T(8,128)(2,1)S(1)}, u32[]{:S(2)}, u32[]{:S(2)}) collective-permute-start(bf16[128,512]{1,0:T(8,128)(2,1)} %refs_0_.3), channel_id=1, source_target_pairs={{0,4},{4,0},{1,5},{5,1},{2,6},{6,2},{3,7},{7,3},{8,12},{12,8},{9,1... | collective-permute-start | bytes 393224 | tf_op jit(solution)/shard_map/ppermute | solution.py:206
  14.6 9.1 %collective-permute-start.6 = (bf16[128,512]{1,0:T(8,128)(2,1)}, bf16[128,512]{1,0:T(8,128)(2,1)S(1)}, u32[]{:S(2)}, u32[]{:S(2)}) collective-permute-start(bf16[128,512]{1,0:T(8,128)(2,1)} %refs_0_.3), channel_id=1, source_target_pairs={{0,1},{1,0},{2,3},{3,2},{4,5},{5,4},{6,7},{7,6},{8,9},{9,8},{10,11... | collective-permute-start | bytes 393224 | tf_op jit(solution)/shard_map/ppermute | solution.py:206
  14.6 9.1 %collective-permute-start.7 = (bf16[128,512]{1,0:T(8,128)(2,1)}, bf16[128,512]{1,0:T(8,128)(2,1)}, u32[]{:S(2)}, u32[]{:S(2)}) collective-permute-start(bf16[128,512]{1,0:T(8,128)(2,1)} %refs_8_.3), channel_id=1, source_target_pairs={{0,2},{2,0},{1,3},{3,1},{4,6},{6,4},{5,7},{7,5},{8,10},{10,8},{9,1... | collective-permute-start | bytes 393224 | tf_op jit(solution)/shard_map/ppermute | solution.py:206
  23.7 11.9 %collective-permute-start.9 = (bf16[128,1280]{1,0:T(8,128)(2,1)S(1)}, bf16[128,1280]{1,0:T(8,128)(2,1)S(1)}, u32[]{:S(2)}, u32[]{:S(2)}) collective-permute-start(bf16[128,1280]{1,0:T(8,128)(2,1)S(1)} %collective-permute-done.refs_1_), channel_id=1, source_target_pairs={{0,4},{4,0},{1,5},{5,1},{2,6},{6,2},{3,7},{7,3},{8,12},{12,8},{9,1... | collective-permute-start | bytes 983048 | tf_op jit(solution)/shard_map/ppermute | solution.py:206
  24.3 11.3 %collective-permute-start.11 = (bf16[128,1280]{1,0:T(8,128)(2,1)S(1)}, bf16[128,1280]{1,0:T(8,128)(2,1)S(1)}, u32[]{:S(2)}, u32[]{:S(2)}) collective-permute-start(bf16[128,1280]{1,0:T(8,128)(2,1)S(1)} %collective-permute-done.1.refs_2_), channel_id=1, source_target_pairs={{0,1},{1,0},{2,3},{3,2},{4,5},{5,4},{6,7},{7,6},{8,9},{9,8},{10,11... | collective-permute-start | bytes 983048 | tf_op jit(solution)/shard_map/ppermute | solution.py:206
  24.3 11.3 %collective-permute-start.12 = (bf16[128,1280]{1,0:T(8,128)(2,1)S(1)}, bf16[128,1280]{1,0:T(8,128)(2,1)S(1)}, u32[]{:S(2)}, u32[]{:S(2)}) collective-permute-start(bf16[128,1280]{1,0:T(8,128)(2,1)S(1)} %collective-permute-done.2.refs_17_), channel_id=1, source_target_pairs={{0,2},{2,0},{1,3},{3,1},{4,6},{6,4},{5,7},{7,5},{8,10},{10,8},{9,1... | collective-permute-start | bytes 983048 | tf_op jit(solution)/shard_map/ppermute | solution.py:206
  24.8 8.2 %collective-permute-start.8 = (bf16[128,512]{1,0:T(8,128)(2,1)}, bf16[128,512]{1,0:T(8,128)(2,1)}, u32[]{:S(2)}, u32[]{:S(2)}) collective-permute-start(bf16[128,512]{1,0:T(8,128)(2,1)} %refs_0_.3), channel_id=1, source_target_pairs={{0,8},{8,0},{1,9},{9,1},{2,10},{10,2},{3,11},{11,3},{4,12},{12,4},... | collective-permute-start | bytes 393224 | tf_op jit(solution)/shard_map/ppermute | solution.py:206
  26.3 9.3 %collective-permute-start.10 = (bf16[128,512]{1,0:T(8,128)(2,1)}, bf16[128,512]{1,0:T(8,128)(2,1)S(1)}, u32[]{:S(2)}, u32[]{:S(2)}) collective-permute-start(bf16[128,512]{1,0:T(8,128)(2,1)} %refs_8_.3), channel_id=1, source_target_pairs={{0,16},{16,0},{1,17},{17,1},{2,18},{18,2},{3,19},{19,3},{4,20},{20... | collective-permute-start | bytes 393224 | tf_op jit(solution)/shard_map/ppermute | solution.py:206
  35.6 7.3 %collective-permute-start.14 = (bf16[128,1280]{1,0:T(8,128)(2,1)S(1)}, bf16[128,1280]{1,0:T(8,128)(2,1)S(1)}, u32[]{:S(2)}, u32[]{:S(2)}) collective-permute-start(bf16[128,1280]{1,0:T(8,128)(2,1)S(1)} %collective-permute-done.refs_1_), channel_id=1, source_target_pairs={{0,1},{1,0},{2,3},{3,2},{4,5},{5,4},{6,7},{7,6},{8,9},{9,8},{10,11... | collective-permute-start | bytes 983048 | tf_op jit(solution)/shard_map/ppermute | solution.py:206
  35.7 7.2 %collective-permute-start.15 = (bf16[128,1280]{1,0:T(8,128)(2,1)S(1)}, bf16[128,1280]{1,0:T(8,128)(2,1)S(1)}, u32[]{:S(2)}, u32[]{:S(2)}) collective-permute-start(bf16[128,1280]{1,0:T(8,128)(2,1)S(1)} %collective-permute-done.9.refs_3_), channel_id=1, source_target_pairs={{0,1},{1,0},{2,3},{3,2},{4,5},{5,4},{6,7},{7,6},{8,9},{9,8},{10,11... | collective-permute-start | bytes 983048 | tf_op jit(solution)/shard_map/ppermute | solution.py:206
  36.2 5.8 %collective-permute-start.13 = (bf16[128,512]{1,0:T(8,128)(2,1)}, bf16[128,512]{1,0:T(8,128)(2,1)}, u32[]{:S(2)}, u32[]{:S(2)}) collective-permute-start(bf16[128,512]{1,0:T(8,128)(2,1)} %collective-permute-done.8.refs_9_.refs_1_), channel_id=1, source_target_pairs={{0,4},{4,0},{1,5},{5,1},{2,6},{6,2},{3,7},{7,3},{8,12},{12,8},{9,1... | collective-permute-start | bytes 393224 | tf_op jit(solution)/shard_map/ppermute | solution.py:206
  37.7 5.2 %collective-permute-start.16 = (bf16[128,512]{1,0:T(8,128)(2,1)S(1)}, bf16[128,512]{1,0:T(8,128)(2,1)S(1)}, u32[]{:S(2)}, u32[]{:S(2)}) collective-permute-start(bf16[128,512]{1,0:T(8,128)(2,1)S(1)} %collective-permute-done.10.refs_21_.refs_9_), channel_id=1, source_target_pairs={{0,2},{2,0},{1,3},{3,1},{4,6},{6,4},{5,7},{7,5},{8,10},{10,8},{9,1... | collective-permute-start | bytes 393224 | tf_op jit(solution)/shard_map/ppermute | solution.py:206
  53.6 6.8 %collective-permute-start.26 = (f32[8,512]{1,0:T(8,128)}, f32[8,512]{1,0:T(8,128)S(1)}, u32[]{:S(2)}, u32[]{:S(2)}) collective-permute-start(f32[8,512]{1,0:T(8,128)} %get-tuple-element.57.refs_18_), channel_id=1, source_target_pairs={{0,18},{2,16},{16,2},{18,0},{1,19},{3,17},{17,3},{19,1},{4,22},{6,... | collective-permute-start | bytes 49160 | tf_op jit(solution)/shard_map/ppermute | solution.py:206
  55.7 9.7 %collective-permute-start.23 = (f32[8,1024]{1,0:T(8,128)S(1)}, f32[8,1024]{1,0:T(8,128)S(1)}, u32[]{:S(2)}, u32[]{:S(2)}) collective-permute-start(f32[8,1024]{1,0:T(8,128)S(1)} %add.37.refs_14_), channel_id=1, source_target_pairs={{0,12},{4,8},{8,4},{12,0},{1,13},{5,9},{9,5},{13,1},{2,14},{6,10},... | collective-permute-start | bytes 98312 | tf_op jit(solution)/shard_map/ppermute | solution.py:206
  58.0 7.3 %collective-permute-start.22 = (f32[8,1024]{1,0:T(8,128)S(1)}, f32[8,1024]{1,0:T(8,128)S(1)}, u32[]{:S(2)}, u32[]{:S(2)}) collective-permute-start(f32[8,1024]{1,0:T(8,128)S(1)} %add.37.refs_14_), channel_id=1, source_target_pairs={{0,4},{4,0},{1,5},{5,1},{2,6},{6,2},{3,7},{7,3},{8,12},{12,8},{9,1... | collective-permute-start | bytes 98312 | tf_op jit(solution)/shard_map/ppermute | solution.py:206
  59.4 5.9 %collective-permute-start.21 = (f32[8,1024]{1,0:T(8,128)S(1)}, f32[8,1024]{1,0:T(8,128)S(1)}, u32[]{:S(2)}, u32[]{:S(2)}) collective-permute-start(f32[8,1024]{1,0:T(8,128)S(1)} %add.37.refs_14_), channel_id=1, source_target_pairs={{0,8},{8,0},{1,9},{9,1},{2,10},{10,2},{3,11},{11,3},{4,12},{12,4},... | collective-permute-start | bytes 98312 | tf_op jit(solution)/shard_map/ppermute | solution.py:206
  59.4 3.9 %collective-permute-start.25 = (f32[8,512]{1,0:T(8,128)}, f32[8,512]{1,0:T(8,128)S(1)}, u32[]{:S(2)}, u32[]{:S(2)}) collective-permute-start(f32[8,512]{1,0:T(8,128)} %get-tuple-element.57.refs_18_), channel_id=1, source_target_pairs={{0,2},{2,0},{1,3},{3,1},{4,6},{6,4},{5,7},{7,5},{8,10},{10,8},{9,1... | collective-permute-start | bytes 49160 | tf_op jit(solution)/shard_map/ppermute | solution.py:206
  60.5 4.8 %collective-permute-start.24 = (f32[8,512]{1,0:T(8,128)}, f32[8,512]{1,0:T(8,128)S(1)}, u32[]{:S(2)}, u32[]{:S(2)}) collective-permute-start(f32[8,512]{1,0:T(8,128)} %get-tuple-element.57.refs_18_), channel_id=1, source_target_pairs={{0,16},{16,0},{1,17},{17,1},{2,18},{18,2},{3,19},{19,3},{4,20},{20... | collective-permute-start | bytes 49160 | tf_op jit(solution)/shard_map/ppermute | solution.py:206
  72.9 3.6 %collective-permute-start.28 = (f32[512,512]{1,0:T(8,128)}, f32[512,512]{1,0:T(8,128)S(1)}, u32[]{:S(2)}, u32[]{:S(2)}) collective-permute-start(f32[512,512]{1,0:T(8,128)} %get-tuple-element.60), channel_id=1, source_target_pairs={{0,1},{1,0},{2,3},{3,2},{4,5},{5,4},{6,7},{7,6},{8,9},{9,8},{10,11... | collective-permute-start | bytes 3145736 | tf_op jit(solution)/shard_map/ppermute | solution.py:206
  78.1 8.5 %collective-permute-start.30 = (f16[256,512]{1,0:T(8,128)(2,1)S(1)}, f16[256,512]{1,0:T(8,128)(2,1)S(1)}, u32[]{:S(2)}, u32[]{:S(2)}) collective-permute-start(f16[256,512]{1,0:T(8,128)(2,1)S(1)} %slice_convert_fusion), channel_id=1, source_target_pairs={{0,4},{4,0},{1,5},{5,1},{2,6},{6,2},{3,7},{7,3},{8,12},{12,8},{9,1... | collective-permute-start | bytes 786440 | tf_op jit(solution)/shard_map/ppermute | solution.py:206
  78.7 7.8 %collective-permute-start.29 = (f32[8,128]{1,0:T(8,128)S(1)}, f32[8,128]{1,0:T(8,128)S(1)}, u32[]{:S(2)}, u32[]{:S(2)}) collective-permute-start(f32[8,128]{1,0:T(8,128)S(1)} %add.38), channel_id=1, source_target_pairs={{0,4},{4,0},{1,5},{5,1},{2,6},{6,2},{3,7},{7,3},{8,12},{12,8},{9,1... | collective-permute-start | bytes 12296 | tf_op jit(solution)/shard_map/ppermute | solution.py:206
  80.2 6.4 %collective-permute-start.32 = (f32[8,128]{1,0:T(8,128)S(1)}, f32[8,128]{1,0:T(8,128)S(1)}, u32[]{:S(2)}, u32[]{:S(2)}) collective-permute-start(f32[8,128]{1,0:T(8,128)S(1)} %copy-done.2), channel_id=1, source_target_pairs={{0,2},{2,0},{1,3},{3,1},{4,6},{6,4},{5,7},{7,5},{8,10},{10,8},{9,1... | collective-permute-start | bytes 12296 | tf_op jit(solution)/shard_map/ppermute | solution.py:206
  81.2 7.6 %collective-permute-start.31 = (f16[256,512]{1,0:T(8,128)(2,1)S(1)}, f16[256,512]{1,0:T(8,128)(2,1)S(1)}, u32[]{:S(2)}, u32[]{:S(2)}) collective-permute-start(f16[256,512]{1,0:T(8,128)(2,1)S(1)} %convert_element_type.18), channel_id=1, source_target_pairs={{0,2},{2,0},{1,3},{3,1},{4,6},{6,4},{5,7},{7,5},{8,10},{10,8},{9,1... | collective-permute-start | bytes 786440 | tf_op jit(solution)/shard_map/ppermute | solution.py:206
  88.8 5.9 %collective-permute-start.33 = (f32[8,128]{1,0:T(8,128)S(1)}, f32[8,128]{1,0:T(8,128)S(1)}, u32[]{:S(2)}, u32[]{:S(2)}) collective-permute-start(f32[8,128]{1,0:T(8,128)S(1)} %add.40), channel_id=1, source_target_pairs={{0,8},{8,0},{1,9},{9,1},{2,10},{10,2},{3,11},{11,3},{4,12},{12,4},... | collective-permute-start | bytes 12296 | tf_op jit(solution)/shard_map/ppermute | solution.py:206
  90.9 5.9 %collective-permute-start.34 = (f32[8,128]{1,0:T(8,128)S(1)}, f32[8,128]{1,0:T(8,128)S(1)}, u32[]{:S(2)}, u32[]{:S(2)}) collective-permute-start(f32[8,128]{1,0:T(8,128)S(1)} %add.43), channel_id=1, source_target_pairs={{0,16},{16,0},{1,17},{17,1},{2,18},{18,2},{3,19},{19,3},{4,20},{20... | collective-permute-start | bytes 12296 | tf_op jit(solution)/shard_map/ppermute | solution.py:206
  91.3 7.3 %collective-permute-start.35 = (f16[128,512]{1,0:T(8,128)(2,1)S(1)}, f16[128,512]{1,0:T(8,128)(2,1)S(1)}, u32[]{:S(2)}, u32[]{:S(2)}) collective-permute-start(f16[128,512]{1,0:T(8,128)(2,1)S(1)} %slice_convert_fusion.2), channel_id=1, source_target_pairs={{0,8},{8,0},{1,9},{9,1},{2,10},{10,2},{3,11},{11,3},{4,12},{12,4},... | collective-permute-start | bytes 393224 | tf_op jit(solution)/shard_map/ppermute | solution.py:206
  94.0 7.0 %collective-permute-start.36 = (f16[128,512]{1,0:T(8,128)(2,1)S(1)}, f16[128,512]{1,0:T(8,128)(2,1)S(1)}, u32[]{:S(2)}, u32[]{:S(2)}) collective-permute-start(f16[128,512]{1,0:T(8,128)(2,1)S(1)} %slice_convert_fusion.1), channel_id=1, source_target_pairs={{0,16},{16,0},{1,17},{17,1},{2,18},{18,2},{3,19},{19,3},{4,20},{20... | collective-permute-start | bytes 393224 | tf_op jit(solution)/shard_map/ppermute | solution.py:206
  (28 other events, 276.0 us)

commit v5 on v4

--- a/solution.py
+++ b/solution.py
@@ -42,16 +42,15 @@
     return items[0]
 
 
-def stats_kernel(nr, nc, b, scale_t, scale_s, core, *refs):
-    ti, si, refs = refs[:nr], refs[nr : 2 * nr], refs[2 * nr :]
-    tt, st, refs = refs[:nc], refs[nc : 2 * nc], refs[2 * nc :]
+def stats_kernel(nr, nc, b, tw, scale_t, scale_s, core, *refs):
+    images, texts, refs = refs[:nr], refs[nr : nr + nc], refs[nr + nc :]
     tl_ref, sl_ref, row_ref, swap_ref, col_ref, text_t, text_s = refs
     for p in range(nc):
-        text_t[block(p, b), :] = tt[p][...]
-        text_s[block(p, b), :] = st[p][...]
+        text_t[block(p, b), :] = texts[p][:, :tw]
+        text_s[block(p, b), :] = texts[p][:, tw:]
     largest = [
-        functools.reduce(jnp.maximum, [jnp.max(jnp.abs(x[...].astype(F32)), 0, keepdims=True) for x in xs])
-        for xs in (si, st)
+        functools.reduce(jnp.maximum, [jnp.max(jnp.abs(x[:, tw:].astype(F32)), 0, keepdims=True) for x in xs])
+        for xs in (images, texts)
     ]
     width = largest[0].shape[1]
 
@@ -65,8 +64,8 @@
     peak_t = peak_s = None
     for p in range(0, nr, step):
         rows = slice(p * b, p * b + count)
-        tl = matmul(jnp.concatenate([x[...] for x in ti[p : p + step]], 0), text_t[...], 1, 1) * (scale_t * LOG2E)
-        sl = matmul(jnp.concatenate([x[...] for x in si[p : p + step]], 0), text_s[...], 1, 1) * (scale_s * LOG2E)
+        tl = matmul(jnp.concatenate([x[:, :tw] for x in images[p : p + step]], 0), text_t[...], 1, 1) * (scale_t * LOG2E)
+        sl = matmul(jnp.concatenate([x[:, tw:] for x in images[p : p + step]], 0), text_s[...], 1, 1) * (scale_s * LOG2E)
         tl_ref[rows, :] = tl
         sl_ref[rows, :] = sl
         top_t, top_s = jnp.max(tl, 0, keepdims=True), jnp.max(sl, 0, keepdims=True)
@@ -95,10 +94,10 @@
         ]
         sum_t, sum_s, gap = parts if p == 0 else [x + y for x, y in zip((sum_t, sum_s, gap), parts)]
     lines = (peak_t + jnp.log2(sum_t), peak_s + jnp.log2(sum_s), gap / sum_t)
-    images = largest[0]
+    most = largest[0]
     if col_ref.shape[1] > width:
-        images = jnp.concatenate([images, jnp.zeros((1, col_ref.shape[1] - width), F32)], 1)
-    col_ref[...] = stack_rows(lines + (images,), col_ref.shape, 0)
+        most = jnp.concatenate([most, jnp.zeros((1, col_ref.shape[1] - width), F32)], 1)
+    col_ref[...] = stack_rows(lines + (most,), col_ref.shape, 0)
 
 
 def combine(tiles, terms):
@@ -125,13 +124,13 @@
     return jnp.exp2(15.0 - power) * scale, jnp.exp2(power - 15.0)
 
 
-def gradient_kernel(nr, nc, b, pairs, scale, *refs):
-    si, refs = refs[:nr], refs[nr:]
-    st, refs = refs[:nc], refs[nc:]
+def gradient_kernel(nr, nc, b, tw, pairs, scale, *refs):
+    images, texts, refs = refs[:nr], refs[nr : nr + nc], refs[nr + nc :]
     tl_ref, sl_ref, refs = refs[0], refs[1], refs[2:]
     row_parts, refs = refs[: nr // 2], refs[nr // 2 :]
     col_parts, refs = refs[:nc], refs[nc:]
-    image_keep, image_send, text_keep, text_send, back, image_share, text_share, refs = *refs[:7], refs[7:]
+    image_parts, text_parts, refs = refs[:4], refs[4:6], refs[6:]
+    back, image_share, text_share, refs = *refs[:3], refs[3:]
     width = back.shape[1]
     lines = [x[2 * KINDS + core : 2 * KINDS + core + 1, :width] for x in row_parts for core in range(2)]
     image_scale, image_back = powers(lines, pairs, scale)
@@ -139,9 +138,9 @@
     back[...] = stack_rows((image_back, text_back), back.shape, 0)
     text, image, high_ref, low_ref, row_terms, col_terms = refs
     for p in range(nc):
-        text[block(p, b), :] = st[p][...]
+        text[block(p, b), :] = texts[p][:, tw:]
     for p in range(nr):
-        image[block(p, b), :] = si[p][...]
+        image[block(p, b), :] = images[p][:, tw:]
     tiles = []
     for q in range(nr // 2):
         x = jnp.concatenate([row_parts[q][:, block(p ^ q, b)] for p in range(nr)], 1)
@@ -156,7 +155,6 @@
         tiles.append([x[k : k + 1, :] for k in range(KINDS)])
     col_t, col_s, terms = combine(tiles, col_terms)
     col_share = sum_blocks(terms, b)
-    half = nr // 2
     for p in range(nr):
         row = jnp.transpose(rows[:, block(p, b)])
         tl, sl = tl_ref[block(p, b), :], sl_ref[block(p, b), :]
@@ -168,23 +166,16 @@
         low_ref[block(p, b), :] = (delta - high.astype(F32)).astype(BF16)
     image_share[...] = jnp.broadcast_to(col_share, image_share.shape)
     text_share[...] = jnp.broadcast_to(row_share, text_share.shape)
-    step = 2 if half % 2 == 0 else 1
-    for p in range(0, nr, step):
-        rows = slice(p * b, (p + step) * b)
-        part = (matmul(high_ref[rows, :], text[...], 1, 0) + matmul(low_ref[rows, :], text[...], 1, 0)) * image_scale
-        if p < half:
-            image_keep[rows, :] = part
-        else:
-            image_send[(p - half) * b : (p - half + step) * b, :] = part
+    quarter = nr // 4
+    for n in (3, 2, 1, 0):
+        rows = slice(n * quarter * b, (n + 1) * quarter * b)
+        part = matmul(high_ref[rows, :], text[...], 1, 0) + matmul(low_ref[rows, :], text[...], 1, 0)
+        image_parts[n][...] = part * image_scale
     half = nc // 2
-    step = 2 if half % 2 == 0 else 1
-    for p in range(0, nc, step):
-        cols = slice(p * b, (p + step) * b)
-        part = (matmul(high_ref[:, cols], image[...], 0, 0) + matmul(low_ref[:, cols], image[...], 0, 0)) * text_scale
-        if p < half:
-            text_keep[cols, :] = part
-        else:
-            text_send[(p - half) * b : (p - half + step) * b, :] = part
+    for n in (1, 0):
+        cols = slice(n * half * b, (n + 1) * half * b)
+        part = matmul(high_ref[:, cols], image[...], 0, 0) + matmul(low_ref[:, cols], image[...], 0, 0)
+        text_parts[n][...] = part * text_scale
 
 
 def call(kernel, outs, args, scratch=(), flops=0, transcendentals=0):
@@ -214,31 +205,11 @@
     return lax.optimization_barrier(groups)
 
 
-def stage_of(bits, pair, part, p):
-    count = bin(p).count("1")
-    late = count == 2 and pair in subset(bits, p)
-    if part == 0:
-        return 0 if count == 1 else count + (late and p & 1)
-    return 1 if count == 1 and p > 1 else count + 1 + late
-
-
-def gather(image_bits, text_bits, image, text):
-    groups = [(image_bits, image), (text_bits, text)]
-    have = {(n, part, 0): x for n, (_, own) in enumerate(groups) for part, x in enumerate(own)}
-    stages = {}
-    for n, (bits, _) in enumerate(groups):
-        for part in range(2):
-            for p in range(1, 1 << len(bits)):
-                stages.setdefault(stage_of(bits, image_bits[-1], part, p), []).append((n, part, p))
-    for stage in sorted(stages):
-        top = {key: 1 << key[2].bit_length() - 1 for key in stages[stage]}
-        sources = {key: have[key[0], key[1], key[2] ^ top[key]] for key in stages[stage]}
-        if stage:
-            gates = [x for key, x in have.items() if key[2] and (stage > 1 or key[2] > 1)]
-            sources, _ = together(sources, gates)
-        for key, x in sources.items():
-            have[key] = swap(subset(groups[key[0]][0], top[key]), x)
-    return [[have[n, part, p] for p in range(1 << len(bits))] for n, (bits, _) in enumerate(groups) for part in range(2)]
+def gather(bits, x):
+    blocks = [x]
+    for bit in bits:
+        blocks = blocks + [swap((bit,), y) for y in blocks]
+    return blocks
 
 
 def halves(x):
@@ -251,12 +222,13 @@
     nr, nc = 1 << len(image_bits), 1 << len(text_bits)
     r, c = nr * b, nc * b
     pair, others = image_bits[-1:], image_bits[:-1]
-    ti, si, tt, st = gather(image_bits, text_bits, (teacher_image, student_image), (teacher_text, student_text))
+    images = gather(image_bits, jnp.concatenate([teacher_image, student_image], 1))
+    texts = gather(text_bits, jnp.concatenate([teacher_text, student_text], 1))
     core = lax.axis_index(pair).astype(jnp.int32).reshape(1)
     tl, sl, rows, rows_swapped, cols = call(
-        functools.partial(stats_kernel, nr, nc, b, tw**-0.5, sw**-0.5),
+        functools.partial(stats_kernel, nr, nc, b, tw, tw**-0.5, sw**-0.5),
         [((r, c), F32), ((r, c), F32), ((LINES, r), F32), ((LINES, r), F32), ((LINES, c), F32)],
-        [core] + ti + si + tt + st, [((c, tw), BF16), ((c, sw), BF16)], 2 * r * c * (tw + sw), 4 * r * c,
+        [core] + images + texts, [((c, tw), BF16), ((c, sw), BF16)], 2 * r * c * (tw + sw), 4 * r * c,
     )
     other = swap(pair, rows_swapped)
     col_parts = [cols] + [swap(subset(text_bits, q), cols) for q in range(1, nc)]
@@ -264,30 +236,35 @@
     row_parts = [rows] + [swap(subset(others, q), rows) for q in range(1, nr // 2)]
     pairs = b << (len(image_bits) + len(text_bits))
     lanes = ((8, 128), F32)
-    image_keep, image_send, text_keep, text_send, back, image_share, text_share = call(
-        functools.partial(gradient_kernel, nr, nc, b, pairs, sw**-0.5),
-        [((n, sw), F32) for n in (r // 2, r // 2, c // 2, c // 2)] + [((8, sw), F32), lanes, lanes],
-        si + st + [tl, sl] + row_parts + col_parts,
+    near, far, other_near, other_far, text_keep, text_send, back, image_share, text_share = call(
+        functools.partial(gradient_kernel, nr, nc, b, tw, pairs, sw**-0.5),
+        [((r // 4, sw), F32)] * 4 + [((c // 2, sw), F32)] * 2 + [((8, sw), F32), lanes, lanes],
+        images + texts + [tl, sl] + row_parts + col_parts,
         [((c, sw), BF16), ((r, sw), BF16), ((r, c), BF16), ((r, c), BF16), ((nr, r), F32), ((max(nc, 8), c), F32)],
         8 * r * c * sw, 4 * r * c,
     )
-    image_keep, image_send = halves(image_keep + swap(pair, image_send))
+    image_send = far + swap(pair, other_far)
+    image_keep = near + swap(pair, other_near)
     image_share = image_share + swap(pair, image_share)
+    text_share = text_share + swap(text_bits[-1:], text_share)
     for k in reversed(range(max(len(text_bits), len(others)))):
         todo = {}
         if k < len(text_bits):
-            todo["text"] = [text_send.astype(F16), text_share]
+            todo["text"] = [text_send.astype(F16)]
+        if 0 < k < len(text_bits):
+            todo["text"].append(text_share)
         if k < len(others):
             todo["image"] = [image_send.astype(F16), image_share]
         (todo,) = together(todo)
         if k < len(text_bits):
-            come, share = [swap(text_bits[k : k + 1], x) for x in todo["text"]]
-            text_total, text_share = text_keep + come.astype(F32), text_share + share
+            text_total = text_keep + swap(text_bits[k : k + 1], todo["text"][0]).astype(F32)
             text_keep, text_send = halves(text_total)
+        if 0 < k < len(text_bits):
+            text_share = todo["text"][1] + swap(text_bits[k - 1 : k], todo["text"][1])
         if k < len(others):
-            come, share = [swap(others[k : k + 1], x) for x in todo["image"]]
-            image_total, image_share = image_keep + come.astype(F32), image_share + share
+            image_total = image_keep + swap(others[k : k + 1], todo["image"][0]).astype(F32)
             image_keep, image_send = halves(image_total)
+            image_share = todo["image"][1] + swap(others[k : k + 1], todo["image"][1])
     loss = (image_share[0, 0] + text_share[0, 0]) / (2.0 * pairs)
     return (loss, image_total * back[0:1], text_total * back[1:2])
 
@@ -296,8 +273,8 @@
     bits = {axis: [f"{axis}{k}" for k in reversed(range(mesh.shape[axis].bit_length() - 1))] for axis in ("img", "txt")}
     names = bits["img"] + bits["txt"]
     cube = Mesh(np.asarray(mesh.devices).reshape((2,) * len(names)), names)
-    text_bits = [x for x in bits["img"] if int(x[3:]) >= 1] + [x for x in bits["txt"] if int(x[3:]) % 2 == 1]
-    image_bits = [x for x in names if x not in text_bits]
+    image_bits = bits["img"][:-1] + [x for x in bits["txt"] if int(x[3:]) % 2 == 0]
+    text_bits = [x for x in names if x not in image_bits]
     image, text = P(tuple(names), None), P(tuple(bits["txt"] + bits["img"]), None)
     return jax.shard_map(
         functools.partial(local, tuple(image_bits), tuple(text_bits)),

time: 103 us -> 100 us (0.971)
  starting transfers between devices: 37.9 us -> 29.6 us
  local copies, waits for them, and re-layouts: 3.05 us -> 6.3 us
  Pallas kernels: 14.6 us -> 15.7 us
    ppermute x37 -> x28, starting transfers between devices: 37.9 us -> 29.6 us  [swap(): return lax.ppermute(x, bits, perm)]
    concatenate x0 -> x2, local copies, waits for them, and re-layouts: none -> 1.83 us  [the longest x1 0.92 us: local(): jnp.concatenate([teacher_image, student_image], 1)]
    unnamed x46 -> x34, local copies, waits for them, and re-layouts: 1.23 us -> 2.64 us
    convert_element_type x1 -> x2, other arithmetic: 1.08 us -> 2.3 us  [the longest x1 1.16 us: local(): todo['image'] = [image_send.astype(F16), image_share]]
    pallas_call x2, Pallas kernels: 14.6 us -> 15.7 us  [call(): pl.pallas_call(kernel, out_shape=shapes, in_specs=[SMEM if x.dtype == jnp...]
    ppermute x37 -> x28, waiting for transfers between devices: 38.3 us -> 38.5 us  [swap(): return lax.ppermute(x, bits, perm)]
  transfers between devices with their start and end apart: 37 -> 28, of which waited for: 18 -> 12; matrix products, arithmetic and copies ran while one was open for 5% -> 9% of each run, Pallas kernels for 0% -> 0%
where the time goes in v5:
time: 100 us; the launch traced here: 99.5 us
  waiting for transfers between devices  38.5 us (38%)
  starting transfers between devices  29.6 us (30%)
  Pallas kernels  15.7 us (16%)
  local copies, waits for them, and re-layouts  6.3 us (6%)
  other arithmetic  6.15 us (6%)
  between operations  3.29 us (3%)
    ppermute x28, waiting for transfers between devices, swap(): return lax.ppermute(x, bits, perm)  38.5 us
    ppermute x28, starting transfers between devices, swap(): return lax.ppermute(x, bits, perm)  29.6 us
    pallas_call x2, Pallas kernels, call(): pl.pallas_call(kernel, out_shape=shapes, in_specs=[SMEM if x.dtype == jnp...  15.7 us
    unnamed x34, local copies, waits for them, and re-layouts  2.64 us
  transfers between devices with their start and end apart: 28, of which 12 were waited for; matrix products, arithmetic and copies ran while one was open for 9% of the time, Pallas kernels for 0%

profile of v5, /device:TPU:0, one launch (start us, length us, event | category | flops | bytes accessed | tf_op | source)
XLA Modules:
  0.0 99.5 jit_solution(16658503000259347457)
XLA Ops:
  0.6 1.0 constant_dynamic-update-slice_fusion.1
  1.6 0.9 constant_dynamic-update-slice_fusion.refs_0_
  2.6 4.1 %collective-permute-start = (bf16[128,1792]{1,0:T(8,128)(2,1)S(1)}, bf16[128,1792]{1,0:T(8,128)(2,1)S(1)}, u32[]{:S(2)}, u32[]{:S(2)}) collective-permute-start(bf16[128,1792]{1,0:T(8,128)(2,1)S(1)} %constant_dynamic-update-slice_fusion.refs_0_), channel_id=1, source_target_pairs={{0,16},{16,0},{1,17},{17,1},{2,18},{18,2},{3,19},{19,3},{4,20},{20... | collective-permute-start | bytes 1376264 | tf_op jit(solution)/shard_map/ppermute | solution.py:197
  6.7 1.0 constant_dynamic-update-slice_fusion.3
  7.7 0.9 constant_dynamic-update-slice_fusion.2.refs_8_
  8.6 1.6 %collective-permute-start.8 = (bf16[128,1792]{1,0:T(8,128)(2,1)S(1)}, bf16[128,1792]{1,0:T(8,128)(2,1)S(1)}, u32[]{:S(2)}, u32[]{:S(2)}) collective-permute-start(bf16[128,1792]{1,0:T(8,128)(2,1)S(1)} %constant_dynamic-update-slice_fusion.2.refs_8_), channel_id=1, source_target_pairs={{0,2},{2,0},{1,3},{3,1},{4,6},{6,4},{5,7},{7,5},{8,10},{10,8},{9,1... | collective-permute-start | bytes 1376264 | tf_op jit(solution)/shard_map/ppermute | solution.py:197
  10.1 1.6 %collective-permute-start.7 = (bf16[128,1792]{1,0:T(8,128)(2,1)S(1)}, bf16[128,1792]{1,0:T(8,128)(2,1)S(1)}, u32[]{:S(2)}, u32[]{:S(2)}) collective-permute-start(bf16[128,1792]{1,0:T(8,128)(2,1)S(1)} %constant_dynamic-update-slice_fusion.2.refs_8_), channel_id=1, source_target_pairs={{0,8},{8,0},{1,9},{9,1},{2,10},{10,2},{3,11},{11,3},{4,12},{12,4},... | collective-permute-start | bytes 1376264 | tf_op jit(solution)/shard_map/ppermute | solution.py:197
  11.7 1.5 %collective-permute-start.1 = (bf16[128,1792]{1,0:T(8,128)(2,1)S(1)}, bf16[128,1792]{1,0:T(8,128)(2,1)S(1)}, u32[]{:S(2)}, u32[]{:S(2)}) collective-permute-start(bf16[128,1792]{1,0:T(8,128)(2,1)S(1)} %constant_dynamic-update-slice_fusion.refs_0_), channel_id=1, source_target_pairs={{0,4},{4,0},{1,5},{5,1},{2,6},{6,2},{3,7},{7,3},{8,12},{12,8},{9,1... | collective-permute-start | bytes 1376264 | tf_op jit(solution)/shard_map/ppermute | solution.py:197
  13.2 13.9 %collective-permute-done.refs_1_ = bf16[128,1792]{1,0:T(8,128)(2,1)S(1)} collective-permute-done((bf16[128,1792]{1,0:T(8,128)(2,1)S(1)}, bf16[128,1792]{1,0:T(8,128)(2,1)S(1)}, u32[]{:S(2)}, u32[]{:S(2)}) %collective-permute-start) | collective-permute-done | bytes 458784 | tf_op jit(solution)/shard_map/ppermute | solution.py:197
  27.1 1.6 %collective-permute-start.2 = (bf16[128,1792]{1,0:T(8,128)(2,1)S(1)}, bf16[128,1792]{1,0:T(8,128)(2,1)S(1)}, u32[]{:S(2)}, u32[]{:S(2)}) collective-permute-start(bf16[128,1792]{1,0:T(8,128)(2,1)S(1)} %collective-permute-done.refs_1_), channel_id=1, source_target_pairs={{0,4},{4,0},{1,5},{5,1},{2,6},{6,2},{3,7},{7,3},{8,12},{12,8},{9,1... | collective-permute-start | bytes 1376264 | tf_op jit(solution)/shard_map/ppermute | solution.py:197
  29.2 1.3 %collective-permute-done.7.refs_9_ = bf16[128,1792]{1,0:T(8,128)(2,1)S(1)} collective-permute-done((bf16[128,1792]{1,0:T(8,128)(2,1)S(1)}, bf16[128,1792]{1,0:T(8,128)(2,1)S(1)}, u32[]{:S(2)}, u32[]{:S(2)}) %collective-permute-start.7) | collective-permute-done | bytes 458784 | tf_op jit(solution)/shard_map/ppermute | solution.py:197
  31.1 7.7 %collective-permute-done.2.refs_3_ = bf16[128,1792]{1,0:T(8,128)(2,1)S(1)} collective-permute-done((bf16[128,1792]{1,0:T(8,128)(2,1)S(1)}, bf16[128,1792]{1,0:T(8,128)(2,1)S(1)}, u32[]{:S(2)}, u32[]{:S(2)}) %collective-permute-start.2) | collective-permute-done | bytes 458784 | tf_op jit(solution)/shard_map/ppermute | solution.py:197
  38.8 3.1 %collective-permute-done.9.refs_11_ = bf16[128,1792]{1,0:T(8,128)(2,1)} collective-permute-done((bf16[128,1792]{1,0:T(8,128)(2,1)S(1)}, bf16[128,1792]{1,0:T(8,128)(2,1)}, u32[]{:S(2)}, u32[]{:S(2)}) %collective-permute-start.9) | collective-permute-done | bytes 458784 | tf_op jit(solution)/shard_map/ppermute | solution.py:197
  41.9 7.7 %shard_map.67 = (f32[1024,512]{1,0:T(8,128)}, f32[1024,512]{1,0:T(8,128)}, f32[8,1024]{1,0:T(8,128)}, f32[8,1024]{1,0:T(8,128)}, f32[8,512]{1,0:T(8,128)}) custom-call(s32[1]{0:T(128)} %bitcast.core, bf16[128,1792]{1,0:T(8,128)(2,1)} %copy-done, bf16[128,1792]{1,0:T(8,128)(2,1)} %copy-done.4, bf16[128,1792]{1,0:T(8,128)(2,1)} %copy-done.7, ...), custom_call_target="tpu_custom_call" | custom-call | flops 1879048192 | bytes 9781252 | tf_op jit(solution)/shard_map/pallas_call | solution.py:184
  49.6 1.6 %collective-permute-start.16 = (f32[8,512]{1,0:T(8,128)}, f32[8,512]{1,0:T(8,128)S(1)}, u32[]{:S(2)}, u32[]{:S(2)}) collective-permute-start(f32[8,512]{1,0:T(8,128)} %get-tuple-element.28.refs_18_), channel_id=1, source_target_pairs={{0,10},{2,8},{8,2},{10,0},{1,11},{3,9},{9,3},{11,1},{4,14},{6,12},... | collective-permute-start | bytes 49160 | tf_op jit(solution)/shard_map/ppermute | solution.py:197
  52.0 4.1 %collective-permute-start.13 = (f32[8,1024]{1,0:T(8,128)S(1)}, f32[8,1024]{1,0:T(8,128)S(1)}, u32[]{:S(2)}, u32[]{:S(2)}) collective-permute-start(f32[8,1024]{1,0:T(8,128)S(1)} %add.40.refs_14_), channel_id=1, source_target_pairs={{0,20},{4,16},{16,4},{20,0},{1,21},{5,17},{17,5},{21,1},{2,22},{6,... | collective-permute-start | bytes 98312 | tf_op jit(solution)/shard_map/ppermute | solution.py:197
  57.7 1.1 %collective-permute-start.14 = (f32[8,512]{1,0:T(8,128)}, f32[8,512]{1,0:T(8,128)S(1)}, u32[]{:S(2)}, u32[]{:S(2)}) collective-permute-start(f32[8,512]{1,0:T(8,128)} %get-tuple-element.28.refs_18_), channel_id=1, source_target_pairs={{0,8},{8,0},{1,9},{9,1},{2,10},{10,2},{3,11},{11,3},{4,12},{12,4},... | collective-permute-start | bytes 49160 | tf_op jit(solution)/shard_map/ppermute | solution.py:197
  58.8 2.0 %collective-permute-done.15.refs_20_ = f32[8,512]{1,0:T(8,128)S(1)} collective-permute-done((f32[8,512]{1,0:T(8,128)}, f32[8,512]{1,0:T(8,128)S(1)}, u32[]{:S(2)}, u32[]{:S(2)}) %collective-permute-start.15) | collective-permute-done | bytes 16416 | tf_op jit(solution)/shard_map/ppermute | solution.py:197
  60.8 0.8 collective-permute-done.14.refs_19_
  62.6 8.1 %shard_map.68 = (f32[256,512]{1,0:T(8,128)}, f32[256,512]{1,0:T(8,128)}, f32[256,512]{1,0:T(8,128)}, f32[256,512]{1,0:T(8,128)}, f32[256,512]{1,0:T(8,128)}, /*i...) custom-call(bf16[128,1792]{1,0:T(8,128)(2,1)} %copy-done, ...), custom_call_target="tpu_custom_call" | custom-call | flops 2147483648 | bytes 13066240 | tf_op jit(solution)/shard_map/pallas_call | solution.py:184
  71.3 0.9 collective-permute-start.20
  72.2 1.1 %convert_element_type.21 = f16[256,512]{1,0:T(8,128)(2,1)S(1)} convert(f32[256,512]{1,0:T(8,128)} %get-tuple-element.34) | non-fusion elementwise | flops 131072 | bytes 786432 | tf_op jit(solution)/shard_map/convert_element_type | solution.py:253
  74.3 0.9 collective-permute-done.20
  75.8 1.2 %add_convert_fusion = f16[256,512]{1,0:T(8,128)(2,1)S(1)} fusion(f32[256,512]{1,0:T(8,128)} %get-tuple-element.31, f32[256,512]{1,0:T(8,128)S(1)} %collective-permute-done.18), kind=kLoop, calls=%fused_computation.2 | loop fusion | flops 262144 | bytes 1310720 | tf_op jit(solution)/shard_map/convert_element_type | solution.py:257
  77.0 1.2 %collective-permute-start.21 = (f16[256,512]{1,0:T(8,128)(2,1)S(1)}, f16[256,512]{1,0:T(8,128)(2,1)S(1)}, u32[]{:S(2)}, u32[]{:S(2)}) collective-permute-start(f16[256,512]{1,0:T(8,128)(2,1)S(1)} %add_convert_fusion), channel_id=1, source_target_pairs={{0,4},{4,0},{1,5},{5,1},{2,6},{6,2},{3,7},{7,3},{8,12},{12,8},{9,1... | collective-permute-start | bytes 786440 | tf_op jit(solution)/shard_map/ppermute | solution.py:197
  78.1 0.9 collective-permute-start.22
  79.9 1.0 %collective-permute-start.23 = (f16[256,512]{1,0:T(8,128)(2,1)S(1)}, f16[256,512]{1,0:T(8,128)(2,1)S(1)}, u32[]{:S(2)}, u32[]{:S(2)}) collective-permute-start(f16[256,512]{1,0:T(8,128)(2,1)S(1)} %convert_element_type.21), channel_id=1, source_target_pairs={{0,2},{2,0},{1,3},{3,1},{4,6},{6,4},{5,7},{7,5},{8,10},{10,8},{9,1... | collective-permute-start | bytes 786440 | tf_op jit(solution)/shard_map/ppermute | solution.py:197
  80.9 3.7 %collective-permute-done.22 = f32[8,128]{1,0:T(8,128)S(1)} collective-permute-done((f32[8,128]{1,0:T(8,128)S(1)}, f32[8,128]{1,0:T(8,128)S(1)}, u32[]{:S(2)}, u32[]{:S(2)}) %collective-permute-start.22) | collective-permute-done | bytes 4128 | tf_op jit(solution)/shard_map/ppermute | solution.py:197
  84.8 1.7 %collective-permute-done.23 = f16[256,512]{1,0:T(8,128)(2,1)S(1)} collective-permute-done((f16[256,512]{1,0:T(8,128)(2,1)S(1)}, f16[256,512]{1,0:T(8,128)(2,1)S(1)}, u32[]{:S(2)}, u32[]{:S(2)}) %collective-permute-start.23) | collective-permute-done | bytes 262176 | tf_op jit(solution)/shard_map/ppermute | solution.py:197
  86.6 3.0 %collective-permute-start.24 = (f32[8,128]{1,0:T(8,128)S(1)}, f32[8,128]{1,0:T(8,128)S(1)}, u32[]{:S(2)}, u32[]{:S(2)}) collective-permute-start(f32[8,128]{1,0:T(8,128)S(1)} %add.46), channel_id=1, source_target_pairs={{0,16},{16,0},{1,17},{17,1},{2,18},{18,2},{3,19},{19,3},{4,20},{20... | collective-permute-start | bytes 12296 | tf_op jit(solution)/shard_map/ppermute | solution.py:197
  91.0 1.2 %collective-permute-start.27 = (f16[128,512]{1,0:T(8,128)(2,1)S(1)}, f16[128,512]{1,0:T(8,128)(2,1)S(1)}, u32[]{:S(2)}, u32[]{:S(2)}) collective-permute-start(f16[128,512]{1,0:T(8,128)(2,1)S(1)} %slice_convert_fusion), channel_id=1, source_target_pairs={{0,8},{8,0},{1,9},{9,1},{2,10},{10,2},{3,11},{11,3},{4,12},{12,4},... | collective-permute-start | bytes 393224 | tf_op jit(solution)/shard_map/ppermute | solution.py:197
  94.0 2.9 %collective-permute-done.26 = f16[128,512]{1,0:T(8,128)(2,1)S(1)} collective-permute-done((f16[128,512]{1,0:T(8,128)(2,1)S(1)}, f16[128,512]{1,0:T(8,128)(2,1)S(1)}, u32[]{:S(2)}, u32[]{:S(2)}) %collective-permute-start.26) | collective-permute-done | bytes 131104 | tf_op jit(solution)/shard_map/ppermute | solution.py:197
  (79 shorter events, 11.1 us)
Async XLA Ops:
  2.5 39.3 %copy-start = (bf16[128,1792]{1,0:T(8,128)(2,1)}, bf16[128,1792]{1,0:T(8,128)(2,1)S(1)}, u32[]{:S(2)}) copy-start(bf16[128,1792]{1,0:T(8,128)(2,1)S(1)} %constant_dynamic-update-slice_fusion.refs_0_) | copy-start | bytes 1376260
  2.6 24.6 %collective-permute-start = (bf16[128,1792]{1,0:T(8,128)(2,1)S(1)}, bf16[128,1792]{1,0:T(8,128)(2,1)S(1)}, u32[]{:S(2)}, u32[]{:S(2)}) collective-permute-start(bf16[128,1792]{1,0:T(8,128)(2,1)S(1)} %constant_dynamic-update-slice_fusion.refs_0_), channel_id=1, source_target_pairs={{0,16},{16,0},{1,17},{17,1},{2,18},{18,2},{3,19},{19,3},{4,20},{20... | collective-permute-start | bytes 1376264 | tf_op jit(solution)/shard_map/ppermute | solution.py:197
  8.6 33.3 %copy-start.1 = (bf16[128,1792]{1,0:T(8,128)(2,1)}, bf16[128,1792]{1,0:T(8,128)(2,1)S(1)}, u32[]{:S(2)}) copy-start(bf16[128,1792]{1,0:T(8,128)(2,1)S(1)} %constant_dynamic-update-slice_fusion.2.refs_8_) | copy-start | bytes 1376260
  8.6 20.1 %collective-permute-start.8 = (bf16[128,1792]{1,0:T(8,128)(2,1)S(1)}, bf16[128,1792]{1,0:T(8,128)(2,1)S(1)}, u32[]{:S(2)}, u32[]{:S(2)}) collective-permute-start(bf16[128,1792]{1,0:T(8,128)(2,1)S(1)} %constant_dynamic-update-slice_fusion.2.refs_8_), channel_id=1, source_target_pairs={{0,2},{2,0},{1,3},{3,1},{4,6},{6,4},{5,7},{7,5},{8,10},{10,8},{9,1... | collective-permute-start | bytes 1376264 | tf_op jit(solution)/shard_map/ppermute | solution.py:197
  10.1 20.4 %collective-permute-start.7 = (bf16[128,1792]{1,0:T(8,128)(2,1)S(1)}, bf16[128,1792]{1,0:T(8,128)(2,1)S(1)}, u32[]{:S(2)}, u32[]{:S(2)}) collective-permute-start(bf16[128,1792]{1,0:T(8,128)(2,1)S(1)} %constant_dynamic-update-slice_fusion.2.refs_8_), channel_id=1, source_target_pairs={{0,8},{8,0},{1,9},{9,1},{2,10},{10,2},{3,11},{11,3},{4,12},{12,4},... | collective-permute-start | bytes 1376264 | tf_op jit(solution)/shard_map/ppermute | solution.py:197
  11.7 19.4 %collective-permute-start.1 = (bf16[128,1792]{1,0:T(8,128)(2,1)S(1)}, bf16[128,1792]{1,0:T(8,128)(2,1)S(1)}, u32[]{:S(2)}, u32[]{:S(2)}) collective-permute-start(bf16[128,1792]{1,0:T(8,128)(2,1)S(1)} %constant_dynamic-update-slice_fusion.refs_0_), channel_id=1, source_target_pairs={{0,4},{4,0},{1,5},{5,1},{2,6},{6,2},{3,7},{7,3},{8,12},{12,8},{9,1... | collective-permute-start | bytes 1376264 | tf_op jit(solution)/shard_map/ppermute | solution.py:197
  27.1 14.7 %copy-start.4 = (bf16[128,1792]{1,0:T(8,128)(2,1)}, bf16[128,1792]{1,0:T(8,128)(2,1)S(1)}, u32[]{:S(2)}) copy-start(bf16[128,1792]{1,0:T(8,128)(2,1)S(1)} %collective-permute-done.refs_1_) | copy-start | bytes 1376260
  27.1 11.6 %collective-permute-start.2 = (bf16[128,1792]{1,0:T(8,128)(2,1)S(1)}, bf16[128,1792]{1,0:T(8,128)(2,1)S(1)}, u32[]{:S(2)}, u32[]{:S(2)}) collective-permute-start(bf16[128,1792]{1,0:T(8,128)(2,1)S(1)} %collective-permute-done.refs_1_), channel_id=1, source_target_pairs={{0,4},{4,0},{1,5},{5,1},{2,6},{6,2},{3,7},{7,3},{8,12},{12,8},{9,1... | collective-permute-start | bytes 1376264 | tf_op jit(solution)/shard_map/ppermute | solution.py:197
  28.7 10.1 %collective-permute-start.3 = (bf16[128,1792]{1,0:T(8,128)(2,1)S(1)}, bf16[128,1792]{1,0:T(8,128)(2,1)}, u32[]{:S(2)}, u32[]{:S(2)}) collective-permute-start(bf16[128,1792]{1,0:T(8,128)(2,1)S(1)} %constant_dynamic-update-slice_fusion.refs_0_), channel_id=1, source_target_pairs={{0,1},{1,0},{2,3},{3,2},{4,5},{5,4},{6,7},{7,6},{8,9},{9,8},{10,11... | collective-permute-start | bytes 1376264 | tf_op jit(solution)/shard_map/ppermute | solution.py:197
  28.7 13.1 %collective-permute-start.4 = (bf16[128,1792]{1,0:T(8,128)(2,1)S(1)}, bf16[128,1792]{1,0:T(8,128)(2,1)}, u32[]{:S(2)}, u32[]{:S(2)}) collective-permute-start(bf16[128,1792]{1,0:T(8,128)(2,1)S(1)} %collective-permute-done.refs_1_), channel_id=1, source_target_pairs={{0,1},{1,0},{2,3},{3,2},{4,5},{5,4},{6,7},{7,6},{8,9},{9,8},{10,11... | collective-permute-start | bytes 1376264 | tf_op jit(solution)/shard_map/ppermute | solution.py:197
  30.5 11.3 %collective-permute-start.9 = (bf16[128,1792]{1,0:T(8,128)(2,1)S(1)}, bf16[128,1792]{1,0:T(8,128)(2,1)}, u32[]{:S(2)}, u32[]{:S(2)}) collective-permute-start(bf16[128,1792]{1,0:T(8,128)(2,1)S(1)} %collective-permute-done.7.refs_9_), channel_id=1, source_target_pairs={{0,2},{2,0},{1,3},{3,1},{4,6},{6,4},{5,7},{7,5},{8,10},{10,8},{9,1... | collective-permute-start | bytes 1376264 | tf_op jit(solution)/shard_map/ppermute | solution.py:197
  31.1 10.7 %collective-permute-start.5 = (bf16[128,1792]{1,0:T(8,128)(2,1)S(1)}, bf16[128,1792]{1,0:T(8,128)(2,1)}, u32[]{:S(2)}, u32[]{:S(2)}) collective-permute-start(bf16[128,1792]{1,0:T(8,128)(2,1)S(1)} %collective-permute-done.1.refs_2_), channel_id=1, source_target_pairs={{0,1},{1,0},{2,3},{3,2},{4,5},{5,4},{6,7},{7,6},{8,9},{9,8},{10,11... | collective-permute-start | bytes 1376264 | tf_op jit(solution)/shard_map/ppermute | solution.py:197
  38.8 3.1 %collective-permute-start.6 = (bf16[128,1792]{1,0:T(8,128)(2,1)S(1)}, bf16[128,1792]{1,0:T(8,128)(2,1)}, u32[]{:S(2)}, u32[]{:S(2)}) collective-permute-start(bf16[128,1792]{1,0:T(8,128)(2,1)S(1)} %collective-permute-done.2.refs_3_), channel_id=1, source_target_pairs={{0,1},{1,0},{2,3},{3,2},{4,5},{5,4},{6,7},{7,6},{8,9},{9,8},{10,11... | collective-permute-start | bytes 1376264 | tf_op jit(solution)/shard_map/ppermute | solution.py:197
  49.6 1.6 %collective-permute-start.10 = (f32[8,1024]{1,0:T(8,128)}, f32[8,1024]{1,0:T(8,128)S(1)}, u32[]{:S(2)}, u32[]{:S(2)}) collective-permute-start(f32[8,1024]{1,0:T(8,128)} %get-tuple-element.27), channel_id=1, source_target_pairs={{0,1},{1,0},{2,3},{3,2},{4,5},{5,4},{6,7},{7,6},{8,9},{9,8},{10,11... | collective-permute-start | bytes 98312 | tf_op jit(solution)/shard_map/ppermute | solution.py:197
  49.6 8.1 %collective-permute-start.16 = (f32[8,512]{1,0:T(8,128)}, f32[8,512]{1,0:T(8,128)S(1)}, u32[]{:S(2)}, u32[]{:S(2)}) collective-permute-start(f32[8,512]{1,0:T(8,128)} %get-tuple-element.28.refs_18_), channel_id=1, source_target_pairs={{0,10},{2,8},{8,2},{10,0},{1,11},{3,9},{9,3},{11,1},{4,14},{6,12},... | collective-permute-start | bytes 49160 | tf_op jit(solution)/shard_map/ppermute | solution.py:197
  52.0 9.7 %collective-permute-start.13 = (f32[8,1024]{1,0:T(8,128)S(1)}, f32[8,1024]{1,0:T(8,128)S(1)}, u32[]{:S(2)}, u32[]{:S(2)}) collective-permute-start(f32[8,1024]{1,0:T(8,128)S(1)} %add.40.refs_14_), channel_id=1, source_target_pairs={{0,20},{4,16},{16,4},{20,0},{1,21},{5,17},{17,5},{21,1},{2,22},{6,... | collective-permute-start | bytes 98312 | tf_op jit(solution)/shard_map/ppermute | solution.py:197
  56.1 5.6 %collective-permute-start.12 = (f32[8,1024]{1,0:T(8,128)S(1)}, f32[8,1024]{1,0:T(8,128)S(1)}, u32[]{:S(2)}, u32[]{:S(2)}) collective-permute-start(f32[8,1024]{1,0:T(8,128)S(1)} %add.40.refs_14_), channel_id=1, source_target_pairs={{0,4},{4,0},{1,5},{5,1},{2,6},{6,2},{3,7},{7,3},{8,12},{12,8},{9,1... | collective-permute-start | bytes 98312 | tf_op jit(solution)/shard_map/ppermute | solution.py:197
  56.9 5.1 %collective-permute-start.11 = (f32[8,1024]{1,0:T(8,128)S(1)}, f32[8,1024]{1,0:T(8,128)S(1)}, u32[]{:S(2)}, u32[]{:S(2)}) collective-permute-start(f32[8,1024]{1,0:T(8,128)S(1)} %add.40.refs_14_), channel_id=1, source_target_pairs={{0,16},{16,0},{1,17},{17,1},{2,18},{18,2},{3,19},{19,3},{4,20},{20... | collective-permute-start | bytes 98312 | tf_op jit(solution)/shard_map/ppermute | solution.py:197
  56.9 3.9 %collective-permute-start.15 = (f32[8,512]{1,0:T(8,128)}, f32[8,512]{1,0:T(8,128)S(1)}, u32[]{:S(2)}, u32[]{:S(2)}) collective-permute-start(f32[8,512]{1,0:T(8,128)} %get-tuple-element.28.refs_18_), channel_id=1, source_target_pairs={{0,2},{2,0},{1,3},{3,1},{4,6},{6,4},{5,7},{7,5},{8,10},{10,8},{9,1... | collective-permute-start | bytes 49160 | tf_op jit(solution)/shard_map/ppermute | solution.py:197
  57.7 4.0 %collective-permute-start.14 = (f32[8,512]{1,0:T(8,128)}, f32[8,512]{1,0:T(8,128)S(1)}, u32[]{:S(2)}, u32[]{:S(2)}) collective-permute-start(f32[8,512]{1,0:T(8,128)} %get-tuple-element.28.refs_18_), channel_id=1, source_target_pairs={{0,8},{8,0},{1,9},{9,1},{2,10},{10,2},{3,11},{11,3},{4,12},{12,4},... | collective-permute-start | bytes 49160 | tf_op jit(solution)/shard_map/ppermute | solution.py:197
  70.6 5.2 %collective-permute-start.18 = (f32[256,512]{1,0:T(8,128)}, f32[256,512]{1,0:T(8,128)S(1)}, u32[]{:S(2)}, u32[]{:S(2)}) collective-permute-start(f32[256,512]{1,0:T(8,128)} %get-tuple-element.32), channel_id=1, source_target_pairs={{0,1},{1,0},{2,3},{3,2},{4,5},{5,4},{6,7},{7,6},{8,9},{9,8},{10,11... | collective-permute-start | bytes 1572872 | tf_op jit(solution)/shard_map/ppermute | solution.py:197
  70.7 13.9 %collective-permute-start.17 = (f32[256,512]{1,0:T(8,128)}, f32[256,512]{1,0:T(8,128)S(1)}, u32[]{:S(2)}, u32[]{:S(2)}) collective-permute-start(f32[256,512]{1,0:T(8,128)} %get-tuple-element.30), channel_id=1, source_target_pairs={{0,1},{1,0},{2,3},{3,2},{4,5},{5,4},{6,7},{7,6},{8,9},{9,8},{10,11... | collective-permute-start | bytes 1572872 | tf_op jit(solution)/shard_map/ppermute | solution.py:197
  71.2 2.4 %collective-permute-start.19 = (f32[8,128]{1,0:T(8,128)}, f32[8,128]{1,0:T(8,128)S(1)}, u32[]{:S(2)}, u32[]{:S(2)}) collective-permute-start(f32[8,128]{1,0:T(8,128)} %get-tuple-element.33), channel_id=1, source_target_pairs={{0,1},{1,0},{2,3},{3,2},{4,5},{5,4},{6,7},{7,6},{8,9},{9,8},{10,11... | collective-permute-start | bytes 12296 | tf_op jit(solution)/shard_map/ppermute | solution.py:197
  71.3 3.8 %collective-permute-start.20 = (f32[8,128]{1,0:T(8,128)}, f32[8,128]{1,0:T(8,128)S(1)}, u32[]{:S(2)}, u32[]{:S(2)}) collective-permute-start(f32[8,128]{1,0:T(8,128)} %get-tuple-element.35), channel_id=1, source_target_pairs={{0,2},{2,0},{1,3},{3,1},{4,6},{6,4},{5,7},{7,5},{8,10},{10,8},{9,1... | collective-permute-start | bytes 12296 | tf_op jit(solution)/shard_map/ppermute | solution.py:197
  72.2 14.3 %copy-start.3 = (f32[256,512]{1,0:T(8,128)S(1)}, f32[256,512]{1,0:T(8,128)}, u32[]{:S(2)}) copy-start(f32[256,512]{1,0:T(8,128)} %get-tuple-element.38) | copy-start | bytes 1572868
  77.0 7.7 %collective-permute-start.21 = (f16[256,512]{1,0:T(8,128)(2,1)S(1)}, f16[256,512]{1,0:T(8,128)(2,1)S(1)}, u32[]{:S(2)}, u32[]{:S(2)}) collective-permute-start(f16[256,512]{1,0:T(8,128)(2,1)S(1)} %add_convert_fusion), channel_id=1, source_target_pairs={{0,4},{4,0},{1,5},{5,1},{2,6},{6,2},{3,7},{7,3},{8,12},{12,8},{9,1... | collective-permute-start | bytes 786440 | tf_op jit(solution)/shard_map/ppermute | solution.py:197
  78.1 6.5 %collective-permute-start.22 = (f32[8,128]{1,0:T(8,128)S(1)}, f32[8,128]{1,0:T(8,128)S(1)}, u32[]{:S(2)}, u32[]{:S(2)}) collective-permute-start(f32[8,128]{1,0:T(8,128)S(1)} %add.43), channel_id=1, source_target_pairs={{0,4},{4,0},{1,5},{5,1},{2,6},{6,2},{3,7},{7,3},{8,12},{12,8},{9,1... | collective-permute-start | bytes 12296 | tf_op jit(solution)/shard_map/ppermute | solution.py:197
  79.1 11.5 %collective-permute-start.25 = (f32[8,128]{1,0:T(8,128)S(1)}, f32[8,128]{1,0:T(8,128)S(1)}, u32[]{:S(2)}, u32[]{:S(2)}) collective-permute-start(f32[8,128]{1,0:T(8,128)S(1)} %add.44), channel_id=1, source_target_pairs={{0,8},{8,0},{1,9},{9,1},{2,10},{10,2},{3,11},{11,3},{4,12},{12,4},... | collective-permute-start | bytes 12296 | tf_op jit(solution)/shard_map/ppermute | solution.py:197
  79.9 6.7 %collective-permute-start.23 = (f16[256,512]{1,0:T(8,128)(2,1)S(1)}, f16[256,512]{1,0:T(8,128)(2,1)S(1)}, u32[]{:S(2)}, u32[]{:S(2)}) collective-permute-start(f16[256,512]{1,0:T(8,128)(2,1)S(1)} %convert_element_type.21), channel_id=1, source_target_pairs={{0,2},{2,0},{1,3},{3,1},{4,6},{6,4},{5,7},{7,5},{8,10},{10,8},{9,1... | collective-permute-start | bytes 786440 | tf_op jit(solution)/shard_map/ppermute | solution.py:197
  86.6 5.6 %collective-permute-start.24 = (f32[8,128]{1,0:T(8,128)S(1)}, f32[8,128]{1,0:T(8,128)S(1)}, u32[]{:S(2)}, u32[]{:S(2)}) collective-permute-start(f32[8,128]{1,0:T(8,128)S(1)} %add.46), channel_id=1, source_target_pairs={{0,16},{16,0},{1,17},{17,1},{2,18},{18,2},{3,19},{19,3},{4,20},{20... | collective-permute-start | bytes 12296 | tf_op jit(solution)/shard_map/ppermute | solution.py:197
  89.6 7.3 %collective-permute-start.26 = (f16[128,512]{1,0:T(8,128)(2,1)S(1)}, f16[128,512]{1,0:T(8,128)(2,1)S(1)}, u32[]{:S(2)}, u32[]{:S(2)}) collective-permute-start(f16[128,512]{1,0:T(8,128)(2,1)S(1)} %slice_convert_fusion.1), channel_id=1, source_target_pairs={{0,16},{16,0},{1,17},{17,1},{2,18},{18,2},{3,19},{19,3},{4,20},{20... | collective-permute-start | bytes 393224 | tf_op jit(solution)/shard_map/ppermute | solution.py:197
  91.0 6.6 %collective-permute-start.27 = (f16[128,512]{1,0:T(8,128)(2,1)S(1)}, f16[128,512]{1,0:T(8,128)(2,1)S(1)}, u32[]{:S(2)}, u32[]{:S(2)}) collective-permute-start(f16[128,512]{1,0:T(8,128)(2,1)S(1)} %slice_convert_fusion), channel_id=1, source_target_pairs={{0,8},{8,0},{1,9},{9,1},{2,10},{10,2},{3,11},{11,3},{4,12},{12,4},... | collective-permute-start | bytes 393224 | tf_op jit(solution)/shard_map/ppermute | solution.py:197
  (12 other events, 70.4 us)

commit v6 on v5

--- a/solution.py
+++ b/solution.py
@@ -1,4 +1,5 @@
 import functools
+import math
 
 import jax
 import jax.numpy as jnp
@@ -15,7 +16,9 @@
 LN2 = 0.6931471805599453
 LINES = 8
 KINDS = 3
-PARAMS = pltpu.CompilerParams(vmem_limit_bytes=56 * 2**20)
+EXTRA = 16
+DIGITS = (64.0, 2.0**-4, 2.0**-14, 2.0**-24, 2.0**-34)
+ROOM = 12 * 2**20
 VMEM = pl.BlockSpec(memory_space=pltpu.VMEM)
 SMEM = pl.BlockSpec(memory_space=pltpu.SMEM)
 
@@ -44,13 +47,15 @@
 
 def stats_kernel(nr, nc, b, tw, scale_t, scale_s, core, *refs):
     images, texts, refs = refs[:nr], refs[nr : nr + nc], refs[nr + nc :]
-    tl_ref, sl_ref, row_ref, swap_ref, col_ref, text_t, text_s = refs
+    tl_ref, sl_ref, row_ref, swap_ref, col_ref, image_s, text_s, text_t = refs
     for p in range(nc):
         text_t[block(p, b), :] = texts[p][:, :tw]
         text_s[block(p, b), :] = texts[p][:, tw:]
+    for p in range(nr):
+        image_s[block(p, b), :] = images[p][:, tw:]
     largest = [
-        functools.reduce(jnp.maximum, [jnp.max(jnp.abs(x[:, tw:].astype(F32)), 0, keepdims=True) for x in xs])
-        for xs in (images, texts)
+        functools.reduce(jnp.maximum, [jnp.max(jnp.abs(x[block(p, b), :].astype(F32)), 0, keepdims=True) for p in range(n)])
+        for x, n in ((image_s, nr), (text_s, nc))
     ]
     width = largest[0].shape[1]
 
@@ -65,7 +70,7 @@
     for p in range(0, nr, step):
         rows = slice(p * b, p * b + count)
         tl = matmul(jnp.concatenate([x[:, :tw] for x in images[p : p + step]], 0), text_t[...], 1, 1) * (scale_t * LOG2E)
-        sl = matmul(jnp.concatenate([x[:, tw:] for x in images[p : p + step]], 0), text_s[...], 1, 1) * (scale_s * LOG2E)
+        sl = matmul(image_s[rows, :], text_s[...], 1, 1) * (scale_s * LOG2E)
         tl_ref[rows, :] = tl
         sl_ref[rows, :] = sl
         top_t, top_s = jnp.max(tl, 0, keepdims=True), jnp.max(sl, 0, keepdims=True)
@@ -100,6 +105,24 @@
     col_ref[...] = stack_rows(lines + (most,), col_ref.shape, 0)
 
 
+def join_kernel(teacher_image, student_image, teacher_text, student_text, image, text):
+    tw = teacher_image.shape[1]
+    image[:, :tw] = teacher_image[...]
+    image[:, tw:] = student_image[...]
+    text[:, :tw] = teacher_text[...]
+    text[:, tw:] = student_text[...]
+
+
+def digits(share, rank, slots, width):
+    rows = []
+    for unit in DIGITS:
+        digit = jnp.floor(share * (1.0 / unit))
+        share = share - digit * unit
+        rows.append(digit)
+    lane = lax.broadcasted_iota(jnp.int32, (EXTRA, width), 1)
+    return jnp.where(lane // (width // slots) == rank, stack_rows(rows, (EXTRA, width), 0), 0.0)
+
+
 def combine(tiles, terms):
     lses = []
     for kind in (1, 0):
@@ -124,23 +147,19 @@
     return jnp.exp2(15.0 - power) * scale, jnp.exp2(power - 15.0)
 
 
-def gradient_kernel(nr, nc, b, tw, pairs, scale, *refs):
-    images, texts, refs = refs[:nr], refs[nr : nr + nc], refs[nr + nc :]
-    tl_ref, sl_ref, refs = refs[0], refs[1], refs[2:]
+def gradient_kernel(nr, nc, b, pairs, scale, place, *refs):
+    image, text, tl_ref, sl_ref, refs = *refs[:4], refs[4:]
     row_parts, refs = refs[: nr // 2], refs[nr // 2 :]
     col_parts, refs = refs[:nc], refs[nc:]
     image_parts, text_parts, refs = refs[:4], refs[4:6], refs[6:]
-    back, image_share, text_share, refs = *refs[:3], refs[3:]
-    width = back.shape[1]
+    image_back_ref, text_back_ref, refs = refs[0], refs[1], refs[2:]
+    width = image_back_ref.shape[1]
     lines = [x[2 * KINDS + core : 2 * KINDS + core + 1, :width] for x in row_parts for core in range(2)]
     image_scale, image_back = powers(lines, pairs, scale)
     text_scale, text_back = powers([x[KINDS : KINDS + 1, :width] for x in col_parts], pairs, scale)
-    back[...] = stack_rows((image_back, text_back), back.shape, 0)
-    text, image, high_ref, low_ref, row_terms, col_terms = refs
-    for p in range(nc):
-        text[block(p, b), :] = texts[p][:, tw:]
-    for p in range(nr):
-        image[block(p, b), :] = images[p][:, tw:]
+    image_back_ref[...] = image_back
+    text_back_ref[...] = text_back
+    high_ref, low_ref, row_terms, col_terms = refs
     tiles = []
     for q in range(nr // 2):
         x = jnp.concatenate([row_parts[q][:, block(p ^ q, b)] for p in range(nr)], 1)
@@ -164,30 +183,33 @@
         high = delta.astype(BF16)
         high_ref[block(p, b), :] = high
         low_ref[block(p, b), :] = (delta - high.astype(F32)).astype(BF16)
-    image_share[...] = jnp.broadcast_to(col_share, image_share.shape)
-    text_share[...] = jnp.broadcast_to(row_share, text_share.shape)
+    image_extra = digits(col_share * (1.0 / (nc * b)), place[1], nr, width)
+    text_extra = digits(row_share * (1.0 / (nr * b)), place[2], nc, width)
     quarter = nr // 4
     for n in (3, 2, 1, 0):
         rows = slice(n * quarter * b, (n + 1) * quarter * b)
         part = matmul(high_ref[rows, :], text[...], 1, 0) + matmul(low_ref[rows, :], text[...], 1, 0)
-        image_parts[n][...] = part * image_scale
+        image_parts[n][: quarter * b, :] = part * image_scale
+        image_parts[n][quarter * b :, :] = image_extra
     half = nc // 2
     for n in (1, 0):
         cols = slice(n * half * b, (n + 1) * half * b)
         part = matmul(high_ref[:, cols], image[...], 0, 0) + matmul(low_ref[:, cols], image[...], 0, 0)
-        text_parts[n][...] = part * text_scale
+        text_parts[n][: half * b, :] = part * text_scale
+        text_parts[n][half * b :, :] = text_extra
 
 
 def call(kernel, outs, args, scratch=(), flops=0, transcendentals=0):
     shapes = [jax.ShapeDtypeStruct(s, d) for s, d in outs]
     size = sum(x.size * x.dtype.itemsize for x in list(args) + shapes)
+    held = sum(math.prod(s) * jnp.dtype(d).itemsize for s, d in scratch)
     return pl.pallas_call(
         kernel,
         out_shape=shapes,
         in_specs=[SMEM if x.dtype == jnp.int32 else VMEM for x in args],
         out_specs=[VMEM] * len(shapes),
         scratch_shapes=[pltpu.VMEM(s, d) for s, d in scratch],
-        compiler_params=PARAMS,
+        compiler_params=pltpu.CompilerParams(vmem_limit_bytes=size + held + ROOM),
         cost_estimate=pl.CostEstimate(flops=flops, bytes_accessed=size, transcendentals=transcendentals),
     )(*args)
 
@@ -207,13 +229,16 @@
 
 def gather(bits, x):
     blocks = [x]
-    for bit in bits:
-        blocks = blocks + [swap((bit,), y) for y in blocks]
+    for k, bit in enumerate(bits):
+        own = together(x, blocks[2])[0] if k > 1 else x
+        blocks = blocks + [swap((bit,), y) for y in [own] + blocks[1:]]
     return blocks
 
 
-def halves(x):
-    return x[: x.shape[0] // 2], x[x.shape[0] // 2 :]
+def add_message(keep, come):
+    rows = keep[0].shape[0]
+    come = come.astype(F32)
+    return keep[0] + come[:rows], keep[1] + come[rows:]
 
 
 def local(image_bits, text_bits, teacher_image, teacher_text, student_image, student_text):
@@ -222,51 +247,49 @@
     nr, nc = 1 << len(image_bits), 1 << len(text_bits)
     r, c = nr * b, nc * b
     pair, others = image_bits[-1:], image_bits[:-1]
-    images = gather(image_bits, jnp.concatenate([teacher_image, student_image], 1))
-    texts = gather(text_bits, jnp.concatenate([teacher_text, student_text], 1))
-    core = lax.axis_index(pair).astype(jnp.int32).reshape(1)
-    tl, sl, rows, rows_swapped, cols = call(
+    whole = ((b, tw + sw), BF16)
+    image, text = call(join_kernel, [whole, whole], [teacher_image, student_image, teacher_text, student_text])
+    images, texts = gather(image_bits, image), gather(text_bits, text)
+    place = jnp.stack([lax.axis_index(x) for x in (pair, image_bits, text_bits)]).astype(jnp.int32)
+    tl, sl, rows, rows_swapped, cols, image, text = call(
         functools.partial(stats_kernel, nr, nc, b, tw, tw**-0.5, sw**-0.5),
-        [((r, c), F32), ((r, c), F32), ((LINES, r), F32), ((LINES, r), F32), ((LINES, c), F32)],
-        [core] + images + texts, [((c, tw), BF16), ((c, sw), BF16)], 2 * r * c * (tw + sw), 4 * r * c,
+        [((r, c), F32), ((r, c), F32), ((LINES, r), F32), ((LINES, r), F32), ((LINES, c), F32), ((r, sw), BF16), ((c, sw), BF16)],
+        [place] + images + texts, [((c, tw), BF16)], 2 * r * c * (tw + sw), 4 * r * c,
     )
     other = swap(pair, rows_swapped)
     col_parts = [cols] + [swap(subset(text_bits, q), cols) for q in range(1, nc)]
     rows = rows + other
     row_parts = [rows] + [swap(subset(others, q), rows) for q in range(1, nr // 2)]
     pairs = b << (len(image_bits) + len(text_bits))
-    lanes = ((8, 128), F32)
-    near, far, other_near, other_far, text_keep, text_send, back, image_share, text_share = call(
-        functools.partial(gradient_kernel, nr, nc, b, tw, pairs, sw**-0.5),
-        [((r // 4, sw), F32)] * 4 + [((c // 2, sw), F32)] * 2 + [((8, sw), F32), lanes, lanes],
-        images + texts + [tl, sl] + row_parts + col_parts,
-        [((c, sw), BF16), ((r, sw), BF16), ((r, c), BF16), ((r, c), BF16), ((nr, r), F32), ((max(nc, 8), c), F32)],
+    near, far, other_near, other_far, text_keep, text_send, image_back, text_back = call(
+        functools.partial(gradient_kernel, nr, nc, b, pairs, sw**-0.5),
+        [((r // 4 + EXTRA, sw), F32)] * 4 + [((c // 2 + EXTRA, sw), F32)] * 2 + [((1, sw), F32)] * 2,
+        [place, image, text, tl, sl] + row_parts + col_parts,
+        [((r, c), BF16), ((r, c), BF16), ((nr, r), F32), ((max(nc, 8), c), F32)],
         8 * r * c * sw, 4 * r * c,
     )
     image_send = far + swap(pair, other_far)
     image_keep = near + swap(pair, other_near)
-    image_share = image_share + swap(pair, image_share)
-    text_share = text_share + swap(text_bits[-1:], text_share)
+    image_keep, text_keep = [(x[:-EXTRA], x[-EXTRA:]) for x in (image_keep, text_keep)]
     for k in reversed(range(max(len(text_bits), len(others)))):
         todo = {}
         if k < len(text_bits):
-            todo["text"] = [text_send.astype(F16)]
-        if 0 < k < len(text_bits):
-            todo["text"].append(text_share)
+            todo["text"] = text_send.astype(F16)
         if k < len(others):
-            todo["image"] = [image_send.astype(F16), image_share]
+            todo["image"] = image_send.astype(F16)
         (todo,) = together(todo)
+        half = b << k >> 1
         if k < len(text_bits):
-            text_total = text_keep + swap(text_bits[k : k + 1], todo["text"][0]).astype(F32)
-            text_keep, text_send = halves(text_total)
-        if 0 < k < len(text_bits):
-            text_share = todo["text"][1] + swap(text_bits[k - 1 : k], todo["text"][1])
+            body, extra = text_keep = add_message(text_keep, swap(text_bits[k : k + 1], todo["text"]))
+            if k:
+                text_keep, text_send = (body[:half], extra), jnp.concatenate([body[half:], extra])
         if k < len(others):
-            image_total = image_keep + swap(others[k : k + 1], todo["image"][0]).astype(F32)
-            image_keep, image_send = halves(image_total)
-            image_share = todo["image"][1] + swap(others[k : k + 1], todo["image"][1])
-    loss = (image_share[0, 0] + text_share[0, 0]) / (2.0 * pairs)
-    return (loss, image_total * back[0:1], text_total * back[1:2])
+            body, extra = image_keep = add_message(image_keep, swap(others[k : k + 1], todo["image"]))
+            if k:
+                image_keep, image_send = (body[:half], extra), jnp.concatenate([body[half:], extra])
+    units = stack_rows(DIGITS, (EXTRA, sw), 0)
+    loss = jnp.sum((image_keep[1] + text_keep[1]) * units) * (0.5 / sw)
+    return (loss, image_keep[0] * image_back, text_keep[0] * text_back)
 
 
 def solution(mesh):

time: 100 us -> 89.3 us (0.89)
  Pallas kernels: 15.7 us -> 9.6 us
  waiting for transfers between devices: 38.5 us -> 44 us
  starting transfers between devices: 29.6 us -> 26.1 us
  other arithmetic: 6.15 us -> 3.01 us
  local copies, waits for them, and re-layouts: 6.3 us -> 3.75 us
    pallas_call x2 -> x3, Pallas kernels: 15.7 us -> 9.6 us  [call(): pl.pallas_call(kernel, out_shape=shapes, in_specs=[SMEM if x.dtype == jnp...]
    ppermute x28 -> x23, waiting for transfers between devices: 38.5 us -> 44 us  [swap(): return lax.ppermute(x, bits, perm)]
    ppermute x28 -> x23, starting transfers between devices: 29.6 us -> 26.1 us  [swap(): return lax.ppermute(x, bits, perm)]
    convert_element_type x2 -> x6, other arithmetic: 2.3 us -> 0.33 us  [the longest x4 0.16 us: add_message(): come = come.astype(F32)]
    concatenate x2 -> x0, local copies, waits for them, and re-layouts: 1.83 us -> none  [the longest x1 0.92 us: local(): jnp.concatenate([teacher_image, student_image], 1)]
    slice x3 -> x0, local copies, waits for them, and re-layouts: 1.82 us -> none  [the longest x2 1.03 us: local(): loss = (image_share[0, 0] + text_share[0, 0]) / (2.0 * pairs)]
    add x7 -> x3, other arithmetic: 1.56 us -> 0.27 us  [the longest x2 0.17 us: add_message(): return (keep[0] + come[:rows], keep[1] + come[rows:])]
    unnamed x34 -> x8, local copies, waits for them, and re-layouts: 2.64 us -> 3.75 us
  transfers between devices with their start and end apart: 28 -> 23, of which waited for: 12 -> 11; matrix products, arithmetic and copies ran while one was open for 9% -> 1% of each run, Pallas kernels for 0% -> 0%
where the time goes in v6:
time: 89.3 us; the launch traced here: 89 us
  waiting for transfers between devices  44 us (49%)
  starting transfers between devices  26.1 us (29%)
  Pallas kernels  9.6 us (11%)
  local copies, waits for them, and re-layouts  3.75 us (4%)
  other arithmetic  3.01 us (3%)
  between operations  2.56 us (3%)
    ppermute x23, waiting for transfers between devices, swap(): return lax.ppermute(x, bits, perm)  44 us
    ppermute x23, starting transfers between devices, swap(): return lax.ppermute(x, bits, perm)  26.1 us
    pallas_call x3, Pallas kernels, call(): pl.pallas_call(kernel, out_shape=shapes, in_specs=[SMEM if x.dtype == jnp...  9.6 us
    unnamed x8, local copies, waits for them, and re-layouts  3.75 us
  transfers between devices with their start and end apart: 23, of which 11 were waited for; matrix products, arithmetic and copies ran while one was open for 1% of the time, Pallas kernels for 0%

profile of v6, /device:TPU:0, one launch (start us, length us, event | category | flops | bytes accessed | tf_op | source)
XLA Modules:
  0.0 89.0 jit_solution(5862222874420922468)
XLA Ops:
  0.6 1.0 %copy-done = bf16[128,1280]{1,0:T(8,128)(2,1)S(1)} copy-done((bf16[128,1280]{1,0:T(8,128)(2,1)S(1)}, bf16[128,1280]{1,0:T(8,128)(2,1)}, u32[]{:S(2)}) %copy-start) | copy-done | bytes 327704
  1.6 1.0 %copy-done.1 = bf16[128,1280]{1,0:T(8,128)(2,1)S(1)} copy-done((bf16[128,1280]{1,0:T(8,128)(2,1)S(1)}, bf16[128,1280]{1,0:T(8,128)(2,1)}, u32[]{:S(2)}) %copy-start.1) | copy-done | bytes 327704
  2.6 0.9 %copy-done.2 = bf16[128,512]{1,0:T(8,128)(2,1)S(1)} copy-done((bf16[128,512]{1,0:T(8,128)(2,1)S(1)}, bf16[128,512]{1,0:T(8,128)(2,1)}, u32[]{:S(2)}) %copy-start.2) | copy-done | bytes 131096
  3.5 0.9 %copy-done.3 = bf16[128,512]{1,0:T(8,128)(2,1)S(1)} copy-done((bf16[128,512]{1,0:T(8,128)(2,1)S(1)}, bf16[128,512]{1,0:T(8,128)(2,1)}, u32[]{:S(2)}) %copy-start.3) | copy-done | bytes 131096
  4.5 4.1 %collective-permute-start = (bf16[128,1792]{1,0:T(8,128)(2,1)S(1)}, bf16[128,1792]{1,0:T(8,128)(2,1)S(1)}, u32[]{:S(2)}, u32[]{:S(2)}) collective-permute-start(bf16[128,1792]{1,0:T(8,128)(2,1)S(1)} %get-tuple-element.26.refs_0_), channel_id=1, source_target_pairs={{0,16},{16,0},{1,17},{17,1},{2,18},{18,2},{3,19},{19,3},{4,20},{20... | collective-permute-start | bytes 1376264 | tf_op jit(solution)/shard_map/ppermute | solution.py:219
  8.6 1.5 %collective-permute-start.1 = (bf16[128,1792]{1,0:T(8,128)(2,1)S(1)}, bf16[128,1792]{1,0:T(8,128)(2,1)S(1)}, u32[]{:S(2)}, u32[]{:S(2)}) collective-permute-start(bf16[128,1792]{1,0:T(8,128)(2,1)S(1)} %get-tuple-element.26.refs_0_), channel_id=1, source_target_pairs={{0,4},{4,0},{1,5},{5,1},{2,6},{6,2},{3,7},{7,3},{8,12},{12,8},{9,1... | collective-permute-start | bytes 1376264 | tf_op jit(solution)/shard_map/ppermute | solution.py:219
  10.1 1.6 %collective-permute-start.7 = (bf16[128,1792]{1,0:T(8,128)(2,1)S(1)}, bf16[128,1792]{1,0:T(8,128)(2,1)S(1)}, u32[]{:S(2)}, u32[]{:S(2)}) collective-permute-start(bf16[128,1792]{1,0:T(8,128)(2,1)S(1)} %get-tuple-element.27.refs_8_), channel_id=1, source_target_pairs={{0,8},{8,0},{1,9},{9,1},{2,10},{10,2},{3,11},{11,3},{4,12},{12,4},... | collective-permute-start | bytes 1376264 | tf_op jit(solution)/shard_map/ppermute | solution.py:219
  11.6 1.5 %collective-permute-start.8 = (bf16[128,1792]{1,0:T(8,128)(2,1)S(1)}, bf16[128,1792]{1,0:T(8,128)(2,1)S(1)}, u32[]{:S(2)}, u32[]{:S(2)}) collective-permute-start(bf16[128,1792]{1,0:T(8,128)(2,1)S(1)} %get-tuple-element.27.refs_8_), channel_id=1, source_target_pairs={{0,2},{2,0},{1,3},{3,1},{4,6},{6,4},{5,7},{7,5},{8,10},{10,8},{9,1... | collective-permute-start | bytes 1376264 | tf_op jit(solution)/shard_map/ppermute | solution.py:219
  13.1 15.9 %collective-permute-done.refs_1_ = bf16[128,1792]{1,0:T(8,128)(2,1)S(1)} collective-permute-done((bf16[128,1792]{1,0:T(8,128)(2,1)S(1)}, bf16[128,1792]{1,0:T(8,128)(2,1)S(1)}, u32[]{:S(2)}, u32[]{:S(2)}) %collective-permute-start) | collective-permute-done | bytes 458784 | tf_op jit(solution)/shard_map/ppermute | solution.py:219
  29.0 1.6 %collective-permute-start.2 = (bf16[128,1792]{1,0:T(8,128)(2,1)S(1)}, bf16[128,1792]{1,0:T(8,128)(2,1)S(1)}, u32[]{:S(2)}, u32[]{:S(2)}) collective-permute-start(bf16[128,1792]{1,0:T(8,128)(2,1)S(1)} %collective-permute-done.refs_1_), channel_id=1, source_target_pairs={{0,4},{4,0},{1,5},{5,1},{2,6},{6,2},{3,7},{7,3},{8,12},{12,8},{9,1... | collective-permute-start | bytes 1376264 | tf_op jit(solution)/shard_map/ppermute | solution.py:219
  31.1 1.6 %collective-permute-start.9 = (bf16[128,1792]{1,0:T(8,128)(2,1)S(1)}, bf16[128,1792]{1,0:T(8,128)(2,1)}, u32[]{:S(2)}, u32[]{:S(2)}) collective-permute-start(bf16[128,1792]{1,0:T(8,128)(2,1)S(1)} %collective-permute-done.7.refs_9_), channel_id=1, source_target_pairs={{0,2},{2,0},{1,3},{3,1},{4,6},{6,4},{5,7},{7,5},{8,10},{10,8},{9,1... | collective-permute-start | bytes 1376264 | tf_op jit(solution)/shard_map/ppermute | solution.py:219
  32.7 8.0 %collective-permute-done.2.refs_3_ = bf16[128,1792]{1,0:T(8,128)(2,1)S(1)} collective-permute-done((bf16[128,1792]{1,0:T(8,128)(2,1)S(1)}, bf16[128,1792]{1,0:T(8,128)(2,1)S(1)}, u32[]{:S(2)}, u32[]{:S(2)}) %collective-permute-start.2) | collective-permute-done | bytes 458784 | tf_op jit(solution)/shard_map/ppermute | solution.py:219
  40.7 3.4 %collective-permute-done.9.refs_11_ = bf16[128,1792]{1,0:T(8,128)(2,1)} collective-permute-done((bf16[128,1792]{1,0:T(8,128)(2,1)S(1)}, bf16[128,1792]{1,0:T(8,128)(2,1)}, u32[]{:S(2)}, u32[]{:S(2)}) %collective-permute-start.9) | collective-permute-done | bytes 458784 | tf_op jit(solution)/shard_map/ppermute | solution.py:219
  44.1 5.6 %shard_map.68 = (f32[1024,512]{1,0:T(8,128)S(1)}, f32[1024,512]{1,0:T(8,128)S(1)}, f32[8,1024]{1,0:T(8,128)S(1)}, f32[8,1024]{1,0:T(8,128)S(1)}, f32[8,512]{1,0:...) custom-call(s32[3]{0:T(128)S(1)} %pad_add_fusion.core.place, ...), custom_call_target="tpu_custom_call" | custom-call | flops 1879048192 | bytes 11354124 | tf_op jit(solution)/shard_map/pallas_call | solution.py:206
  49.8 0.6 collective-permute-start.14
  51.0 2.9 %collective-permute-start.11 = (f32[8,1024]{1,0:T(8,128)S(1)}, f32[8,1024]{1,0:T(8,128)S(1)}, u32[]{:S(2)}, u32[]{:S(2)}) collective-permute-start(f32[8,1024]{1,0:T(8,128)S(1)} %add.48.refs_4_), channel_id=1, source_target_pairs={{0,16},{16,0},{1,17},{17,1},{2,18},{18,2},{3,19},{19,3},{4,20},{20... | collective-permute-start | bytes 98312 | tf_op jit(solution)/shard_map/ppermute | solution.py:219
  53.9 0.9 %collective-permute-start.12 = (f32[8,1024]{1,0:T(8,128)S(1)}, f32[8,1024]{1,0:T(8,128)S(1)}, u32[]{:S(2)}, u32[]{:S(2)}) collective-permute-start(f32[8,1024]{1,0:T(8,128)S(1)} %add.48.refs_4_), channel_id=1, source_target_pairs={{0,4},{4,0},{1,5},{5,1},{2,6},{6,2},{3,7},{7,3},{8,12},{12,8},{9,1... | collective-permute-start | bytes 98312 | tf_op jit(solution)/shard_map/ppermute | solution.py:219
  54.8 0.6 collective-permute-start.13
  55.4 1.5 %collective-permute-start.15 = (f32[8,512]{1,0:T(8,128)S(1)}, f32[8,512]{1,0:T(8,128)S(1)}, u32[]{:S(2)}, u32[]{:S(2)}) collective-permute-start(f32[8,512]{1,0:T(8,128)S(1)} %get-tuple-element.34.refs_8_), channel_id=1, source_target_pairs={{0,2},{2,0},{1,3},{3,1},{4,6},{6,4},{5,7},{7,5},{8,10},{10,8},{9,1... | collective-permute-start | bytes 49160 | tf_op jit(solution)/shard_map/ppermute | solution.py:219
  56.9 1.0 %collective-permute-start.16 = (f32[8,512]{1,0:T(8,128)S(1)}, f32[8,512]{1,0:T(8,128)S(1)}, u32[]{:S(2)}, u32[]{:S(2)}) collective-permute-start(f32[8,512]{1,0:T(8,128)S(1)} %get-tuple-element.34.refs_8_), channel_id=1, source_target_pairs={{0,10},{2,8},{8,2},{10,0},{1,11},{3,9},{9,3},{11,1},{4,14},{6,12},... | collective-permute-start | bytes 49160 | tf_op jit(solution)/shard_map/ppermute | solution.py:219
  58.0 1.2 %collective-permute-done.15.refs_10_ = f32[8,512]{1,0:T(8,128)S(1)} collective-permute-done((f32[8,512]{1,0:T(8,128)S(1)}, f32[8,512]{1,0:T(8,128)S(1)}, u32[]{:S(2)}, u32[]{:S(2)}) %collective-permute-start.15) | collective-permute-done | bytes 16416 | tf_op jit(solution)/shard_map/ppermute | solution.py:219
  59.2 2.4 %collective-permute-done.16.refs_11_ = f32[8,512]{1,0:T(8,128)S(1)} collective-permute-done((f32[8,512]{1,0:T(8,128)S(1)}, f32[8,512]{1,0:T(8,128)S(1)}, u32[]{:S(2)}, u32[]{:S(2)}) %collective-permute-start.16) | collective-permute-done | bytes 16416 | tf_op jit(solution)/shard_map/ppermute | solution.py:219
  61.6 3.9 %shard_map.69 = (f32[272,512]{1,0:T(8,128)S(1)}, f32[272,512]{1,0:T(8,128)S(1)}, f32[272,512]{1,0:T(8,128)S(1)}, f32[272,512]{1,0:T(8,128)S(1)}, f32[272,512]{1,...) custom-call(s32[3]{0:T(128)S(1)} %pad_add_fusion.core.place, ...), custom_call_target="tpu_custom_call" | custom-call | flops 2147483648 | bytes 9310220 | tf_op jit(solution)/shard_map/pallas_call | solution.py:206
  66.1 1.4 %collective-permute-done.18 = f32[272,512]{1,0:T(8,128)S(1)} collective-permute-done((f32[272,512]{1,0:T(8,128)S(1)}, f32[272,512]{1,0:T(8,128)S(1)}, u32[]{:S(2)}, u32[]{:S(2)}) %collective-permute-start.18) | collective-permute-done | bytes 557088 | tf_op jit(solution)/shard_map/ppermute | solution.py:219
  68.3 1.0 %collective-permute-start.19 = (f16[272,512]{1,0:T(8,128)(2,1)S(1)}, f16[272,512]{1,0:T(8,128)(2,1)S(1)}, u32[]{:S(2)}, u32[]{:S(2)}) collective-permute-start(f16[272,512]{1,0:T(8,128)(2,1)S(1)} %add_convert_fusion), channel_id=1, source_target_pairs={{0,4},{4,0},{1,5},{5,1},{2,6},{6,2},{3,7},{7,3},{8,12},{12,8},{9,1... | collective-permute-start | bytes 835592 | tf_op jit(solution)/shard_map/ppermute | solution.py:219
  69.4 7.1 %collective-permute-done.20 = f16[272,512]{1,0:T(8,128)(2,1)S(1)} collective-permute-done((f16[272,512]{1,0:T(8,128)(2,1)S(1)}, f16[272,512]{1,0:T(8,128)(2,1)S(1)}, u32[]{:S(2)}, u32[]{:S(2)}) %collective-permute-start.20) | collective-permute-done | bytes 278560 | tf_op jit(solution)/shard_map/ppermute | solution.py:219
  77.0 1.1 %collective-permute-start.22 = (f16[144,512]{1,0:T(8,128)(2,1)S(1)}, f16[144,512]{1,0:T(8,128)(2,1)S(1)}, u32[]{:S(2)}, u32[]{:S(2)}) collective-permute-start(f16[144,512]{1,0:T(8,128)(2,1)S(1)} %get-tuple-element.44), channel_id=1, source_target_pairs={{0,8},{8,0},{1,9},{9,1},{2,10},{10,2},{3,11},{11,3},{4,12},{12,4},... | collective-permute-start | bytes 442376 | tf_op jit(solution)/shard_map/ppermute | solution.py:219
  78.1 2.9 %collective-permute-start.21 = (f16[144,512]{1,0:T(8,128)(2,1)S(1)}, f16[144,512]{1,0:T(8,128)(2,1)S(1)}, u32[]{:S(2)}, u32[]{:S(2)}) collective-permute-start(f16[144,512]{1,0:T(8,128)(2,1)S(1)} %get-tuple-element.43), channel_id=1, source_target_pairs={{0,16},{16,0},{1,17},{17,1},{2,18},{18,2},{3,19},{19,3},{4,20},{20... | collective-permute-start | bytes 442376 | tf_op jit(solution)/shard_map/ppermute | solution.py:219
  81.0 3.9 %collective-permute-done.22 = f16[144,512]{1,0:T(8,128)(2,1)S(1)} collective-permute-done((f16[144,512]{1,0:T(8,128)(2,1)S(1)}, f16[144,512]{1,0:T(8,128)(2,1)S(1)}, u32[]{:S(2)}, u32[]{:S(2)}) %collective-permute-start.22) | collective-permute-done | bytes 147488 | tf_op jit(solution)/shard_map/ppermute | solution.py:219
  84.9 0.7 fusion
  85.8 0.7 fusion.1
  86.5 0.7 fusion.4
  (47 shorter events, 3.4 us)
Async XLA Ops:
  0.6 1.0 %copy-start = (bf16[128,1280]{1,0:T(8,128)(2,1)S(1)}, bf16[128,1280]{1,0:T(8,128)(2,1)}, u32[]{:S(2)}) copy-start(bf16[128,1280]{1,0:T(8,128)(2,1)} %teacher_image.1) | copy-start | bytes 983044
  1.6 1.0 %copy-start.1 = (bf16[128,1280]{1,0:T(8,128)(2,1)S(1)}, bf16[128,1280]{1,0:T(8,128)(2,1)}, u32[]{:S(2)}) copy-start(bf16[128,1280]{1,0:T(8,128)(2,1)} %teacher_text.1) | copy-start | bytes 983044
  2.6 0.9 %copy-start.2 = (bf16[128,512]{1,0:T(8,128)(2,1)S(1)}, bf16[128,512]{1,0:T(8,128)(2,1)}, u32[]{:S(2)}) copy-start(bf16[128,512]{1,0:T(8,128)(2,1)} %student_image.1) | copy-start | bytes 393220
  3.5 0.9 %copy-start.3 = (bf16[128,512]{1,0:T(8,128)(2,1)S(1)}, bf16[128,512]{1,0:T(8,128)(2,1)}, u32[]{:S(2)}) copy-start(bf16[128,512]{1,0:T(8,128)(2,1)} %student_text.1) | copy-start | bytes 393220
  4.5 24.6 %collective-permute-start = (bf16[128,1792]{1,0:T(8,128)(2,1)S(1)}, bf16[128,1792]{1,0:T(8,128)(2,1)S(1)}, u32[]{:S(2)}, u32[]{:S(2)}) collective-permute-start(bf16[128,1792]{1,0:T(8,128)(2,1)S(1)} %get-tuple-element.26.refs_0_), channel_id=1, source_target_pairs={{0,16},{16,0},{1,17},{17,1},{2,18},{18,2},{3,19},{19,3},{4,20},{20... | collective-permute-start | bytes 1376264 | tf_op jit(solution)/shard_map/ppermute | solution.py:219
  8.6 22.0 %collective-permute-start.1 = (bf16[128,1792]{1,0:T(8,128)(2,1)S(1)}, bf16[128,1792]{1,0:T(8,128)(2,1)S(1)}, u32[]{:S(2)}, u32[]{:S(2)}) collective-permute-start(bf16[128,1792]{1,0:T(8,128)(2,1)S(1)} %get-tuple-element.26.refs_0_), channel_id=1, source_target_pairs={{0,4},{4,0},{1,5},{5,1},{2,6},{6,2},{3,7},{7,3},{8,12},{12,8},{9,1... | collective-permute-start | bytes 1376264 | tf_op jit(solution)/shard_map/ppermute | solution.py:219
  10.1 21.0 %collective-permute-start.7 = (bf16[128,1792]{1,0:T(8,128)(2,1)S(1)}, bf16[128,1792]{1,0:T(8,128)(2,1)S(1)}, u32[]{:S(2)}, u32[]{:S(2)}) collective-permute-start(bf16[128,1792]{1,0:T(8,128)(2,1)S(1)} %get-tuple-element.27.refs_8_), channel_id=1, source_target_pairs={{0,8},{8,0},{1,9},{9,1},{2,10},{10,2},{3,11},{11,3},{4,12},{12,4},... | collective-permute-start | bytes 1376264 | tf_op jit(solution)/shard_map/ppermute | solution.py:219
  11.6 19.5 %collective-permute-start.8 = (bf16[128,1792]{1,0:T(8,128)(2,1)S(1)}, bf16[128,1792]{1,0:T(8,128)(2,1)S(1)}, u32[]{:S(2)}, u32[]{:S(2)}) collective-permute-start(bf16[128,1792]{1,0:T(8,128)(2,1)S(1)} %get-tuple-element.27.refs_8_), channel_id=1, source_target_pairs={{0,2},{2,0},{1,3},{3,1},{4,6},{6,4},{5,7},{7,5},{8,10},{10,8},{9,1... | collective-permute-start | bytes 1376264 | tf_op jit(solution)/shard_map/ppermute | solution.py:219
  29.0 11.6 %collective-permute-start.2 = (bf16[128,1792]{1,0:T(8,128)(2,1)S(1)}, bf16[128,1792]{1,0:T(8,128)(2,1)S(1)}, u32[]{:S(2)}, u32[]{:S(2)}) collective-permute-start(bf16[128,1792]{1,0:T(8,128)(2,1)S(1)} %collective-permute-done.refs_1_), channel_id=1, source_target_pairs={{0,4},{4,0},{1,5},{5,1},{2,6},{6,2},{3,7},{7,3},{8,12},{12,8},{9,1... | collective-permute-start | bytes 1376264 | tf_op jit(solution)/shard_map/ppermute | solution.py:219
  30.6 10.2 %collective-permute-start.3 = (bf16[128,1792]{1,0:T(8,128)(2,1)S(1)}, bf16[128,1792]{1,0:T(8,128)(2,1)}, u32[]{:S(2)}, u32[]{:S(2)}) collective-permute-start(bf16[128,1792]{1,0:T(8,128)(2,1)S(1)} %get-tuple-element.26.refs_0_), channel_id=1, source_target_pairs={{0,1},{1,0},{2,3},{3,2},{4,5},{5,4},{6,7},{7,6},{8,9},{9,8},{10,11... | collective-permute-start | bytes 1376264 | tf_op jit(solution)/shard_map/ppermute | solution.py:219
  30.6 10.2 %collective-permute-start.4 = (bf16[128,1792]{1,0:T(8,128)(2,1)S(1)}, bf16[128,1792]{1,0:T(8,128)(2,1)}, u32[]{:S(2)}, u32[]{:S(2)}) collective-permute-start(bf16[128,1792]{1,0:T(8,128)(2,1)S(1)} %collective-permute-done.refs_1_), channel_id=1, source_target_pairs={{0,1},{1,0},{2,3},{3,2},{4,5},{5,4},{6,7},{7,6},{8,9},{9,8},{10,11... | collective-permute-start | bytes 1376264 | tf_op jit(solution)/shard_map/ppermute | solution.py:219
  31.1 9.6 %collective-permute-start.5 = (bf16[128,1792]{1,0:T(8,128)(2,1)S(1)}, bf16[128,1792]{1,0:T(8,128)(2,1)}, u32[]{:S(2)}, u32[]{:S(2)}) collective-permute-start(bf16[128,1792]{1,0:T(8,128)(2,1)S(1)} %collective-permute-done.1.refs_2_), channel_id=1, source_target_pairs={{0,1},{1,0},{2,3},{3,2},{4,5},{5,4},{6,7},{7,6},{8,9},{9,8},{10,11... | collective-permute-start | bytes 1376264 | tf_op jit(solution)/shard_map/ppermute | solution.py:219
  31.1 13.0 %collective-permute-start.9 = (bf16[128,1792]{1,0:T(8,128)(2,1)S(1)}, bf16[128,1792]{1,0:T(8,128)(2,1)}, u32[]{:S(2)}, u32[]{:S(2)}) collective-permute-start(bf16[128,1792]{1,0:T(8,128)(2,1)S(1)} %collective-permute-done.7.refs_9_), channel_id=1, source_target_pairs={{0,2},{2,0},{1,3},{3,1},{4,6},{6,4},{5,7},{7,5},{8,10},{10,8},{9,1... | collective-permute-start | bytes 1376264 | tf_op jit(solution)/shard_map/ppermute | solution.py:219
  40.7 3.5 %collective-permute-start.6 = (bf16[128,1792]{1,0:T(8,128)(2,1)S(1)}, bf16[128,1792]{1,0:T(8,128)(2,1)}, u32[]{:S(2)}, u32[]{:S(2)}) collective-permute-start(bf16[128,1792]{1,0:T(8,128)(2,1)S(1)} %collective-permute-done.2.refs_3_), channel_id=1, source_target_pairs={{0,1},{1,0},{2,3},{3,2},{4,5},{5,4},{6,7},{7,6},{8,9},{9,8},{10,11... | collective-permute-start | bytes 1376264 | tf_op jit(solution)/shard_map/ppermute | solution.py:219
  49.8 1.2 %collective-permute-start.10 = (f32[8,1024]{1,0:T(8,128)S(1)}, f32[8,1024]{1,0:T(8,128)S(1)}, u32[]{:S(2)}, u32[]{:S(2)}) collective-permute-start(f32[8,1024]{1,0:T(8,128)S(1)} %get-tuple-element.33), channel_id=1, source_target_pairs={{0,1},{1,0},{2,3},{3,2},{4,5},{5,4},{6,7},{7,6},{8,9},{9,8},{10,11... | collective-permute-start | bytes 98312 | tf_op jit(solution)/shard_map/ppermute | solution.py:219
  49.8 7.1 %collective-permute-start.14 = (f32[8,512]{1,0:T(8,128)S(1)}, f32[8,512]{1,0:T(8,128)S(1)}, u32[]{:S(2)}, u32[]{:S(2)}) collective-permute-start(f32[8,512]{1,0:T(8,128)S(1)} %get-tuple-element.34.refs_8_), channel_id=1, source_target_pairs={{0,8},{8,0},{1,9},{9,1},{2,10},{10,2},{3,11},{11,3},{4,12},{12,4},... | collective-permute-start | bytes 49160 | tf_op jit(solution)/shard_map/ppermute | solution.py:219
  51.0 10.6 %collective-permute-start.11 = (f32[8,1024]{1,0:T(8,128)S(1)}, f32[8,1024]{1,0:T(8,128)S(1)}, u32[]{:S(2)}, u32[]{:S(2)}) collective-permute-start(f32[8,1024]{1,0:T(8,128)S(1)} %add.48.refs_4_), channel_id=1, source_target_pairs={{0,16},{16,0},{1,17},{17,1},{2,18},{18,2},{3,19},{19,3},{4,20},{20... | collective-permute-start | bytes 98312 | tf_op jit(solution)/shard_map/ppermute | solution.py:219
  53.9 7.7 %collective-permute-start.12 = (f32[8,1024]{1,0:T(8,128)S(1)}, f32[8,1024]{1,0:T(8,128)S(1)}, u32[]{:S(2)}, u32[]{:S(2)}) collective-permute-start(f32[8,1024]{1,0:T(8,128)S(1)} %add.48.refs_4_), channel_id=1, source_target_pairs={{0,4},{4,0},{1,5},{5,1},{2,6},{6,2},{3,7},{7,3},{8,12},{12,8},{9,1... | collective-permute-start | bytes 98312 | tf_op jit(solution)/shard_map/ppermute | solution.py:219
  54.8 6.8 %collective-permute-start.13 = (f32[8,1024]{1,0:T(8,128)S(1)}, f32[8,1024]{1,0:T(8,128)S(1)}, u32[]{:S(2)}, u32[]{:S(2)}) collective-permute-start(f32[8,1024]{1,0:T(8,128)S(1)} %add.48.refs_4_), channel_id=1, source_target_pairs={{0,20},{4,16},{16,4},{20,0},{1,21},{5,17},{17,5},{21,1},{2,22},{6,... | collective-permute-start | bytes 98312 | tf_op jit(solution)/shard_map/ppermute | solution.py:219
  55.4 3.7 %collective-permute-start.15 = (f32[8,512]{1,0:T(8,128)S(1)}, f32[8,512]{1,0:T(8,128)S(1)}, u32[]{:S(2)}, u32[]{:S(2)}) collective-permute-start(f32[8,512]{1,0:T(8,128)S(1)} %get-tuple-element.34.refs_8_), channel_id=1, source_target_pairs={{0,2},{2,0},{1,3},{3,1},{4,6},{6,4},{5,7},{7,5},{8,10},{10,8},{9,1... | collective-permute-start | bytes 49160 | tf_op jit(solution)/shard_map/ppermute | solution.py:219
  56.9 4.6 %collective-permute-start.16 = (f32[8,512]{1,0:T(8,128)S(1)}, f32[8,512]{1,0:T(8,128)S(1)}, u32[]{:S(2)}, u32[]{:S(2)}) collective-permute-start(f32[8,512]{1,0:T(8,128)S(1)} %get-tuple-element.34.refs_8_), channel_id=1, source_target_pairs={{0,10},{2,8},{8,2},{10,0},{1,11},{3,9},{9,3},{11,1},{4,14},{6,12},... | collective-permute-start | bytes 49160 | tf_op jit(solution)/shard_map/ppermute | solution.py:219
  65.5 2.0 %collective-permute-start.18 = (f32[272,512]{1,0:T(8,128)S(1)}, f32[272,512]{1,0:T(8,128)S(1)}, u32[]{:S(2)}, u32[]{:S(2)}) collective-permute-start(f32[272,512]{1,0:T(8,128)S(1)} %get-tuple-element.38), channel_id=1, source_target_pairs={{0,1},{1,0},{2,3},{3,2},{4,5},{5,4},{6,7},{7,6},{8,9},{9,8},{10,11... | collective-permute-start | bytes 1671176 | tf_op jit(solution)/shard_map/ppermute | solution.py:219
  65.6 3.7 %collective-permute-start.17 = (f32[272,512]{1,0:T(8,128)S(1)}, f32[272,512]{1,0:T(8,128)S(1)}, u32[]{:S(2)}, u32[]{:S(2)}) collective-permute-start(f32[272,512]{1,0:T(8,128)S(1)} %get-tuple-element.36), channel_id=1, source_target_pairs={{0,1},{1,0},{2,3},{3,2},{4,5},{5,4},{6,7},{7,6},{8,9},{9,8},{10,11... | collective-permute-start | bytes 1671176 | tf_op jit(solution)/shard_map/ppermute | solution.py:219
  67.7 8.8 %collective-permute-start.20 = (f16[272,512]{1,0:T(8,128)(2,1)S(1)}, f16[272,512]{1,0:T(8,128)(2,1)S(1)}, u32[]{:S(2)}, u32[]{:S(2)}) collective-permute-start(f16[272,512]{1,0:T(8,128)(2,1)S(1)} %convert_element_type.21), channel_id=1, source_target_pairs={{0,2},{2,0},{1,3},{3,1},{4,6},{6,4},{5,7},{7,5},{8,10},{10,8},{9,1... | collective-permute-start | bytes 835592 | tf_op jit(solution)/shard_map/ppermute | solution.py:219
  68.3 8.4 %collective-permute-start.19 = (f16[272,512]{1,0:T(8,128)(2,1)S(1)}, f16[272,512]{1,0:T(8,128)(2,1)S(1)}, u32[]{:S(2)}, u32[]{:S(2)}) collective-permute-start(f16[272,512]{1,0:T(8,128)(2,1)S(1)} %add_convert_fusion), channel_id=1, source_target_pairs={{0,4},{4,0},{1,5},{5,1},{2,6},{6,2},{3,7},{7,3},{8,12},{12,8},{9,1... | collective-permute-start | bytes 835592 | tf_op jit(solution)/shard_map/ppermute | solution.py:219
  77.0 7.9 %collective-permute-start.22 = (f16[144,512]{1,0:T(8,128)(2,1)S(1)}, f16[144,512]{1,0:T(8,128)(2,1)S(1)}, u32[]{:S(2)}, u32[]{:S(2)}) collective-permute-start(f16[144,512]{1,0:T(8,128)(2,1)S(1)} %get-tuple-element.44), channel_id=1, source_target_pairs={{0,8},{8,0},{1,9},{9,1},{2,10},{10,2},{3,11},{11,3},{4,12},{12,4},... | collective-permute-start | bytes 442376 | tf_op jit(solution)/shard_map/ppermute | solution.py:219
  78.1 7.6 %collective-permute-start.21 = (f16[144,512]{1,0:T(8,128)(2,1)S(1)}, f16[144,512]{1,0:T(8,128)(2,1)S(1)}, u32[]{:S(2)}, u32[]{:S(2)}) collective-permute-start(f16[144,512]{1,0:T(8,128)(2,1)S(1)} %get-tuple-element.43), channel_id=1, source_target_pairs={{0,16},{16,0},{1,17},{17,1},{2,18},{18,2},{3,19},{19,3},{4,20},{20... | collective-permute-start | bytes 442376 | tf_op jit(solution)/shard_map/ppermute | solution.py:219

commit v7 on v6

--- a/solution.py
+++ b/solution.py
@@ -18,6 +18,7 @@
 KINDS = 3
 EXTRA = 16
 DIGITS = (64.0, 2.0**-4, 2.0**-14, 2.0**-24, 2.0**-34)
+MOST = 60 * 2**20
 ROOM = 12 * 2**20
 VMEM = pl.BlockSpec(memory_space=pltpu.VMEM)
 SMEM = pl.BlockSpec(memory_space=pltpu.SMEM)
@@ -105,12 +106,18 @@
     col_ref[...] = stack_rows(lines + (most,), col_ref.shape, 0)
 
 
-def join_kernel(teacher_image, student_image, teacher_text, student_text, image, text):
+def join_kernel(teacher_image, student_image, teacher_text, student_text, image, text, sems):
     tw = teacher_image.shape[1]
-    image[:, :tw] = teacher_image[...]
-    image[:, tw:] = student_image[...]
-    text[:, :tw] = teacher_text[...]
-    text[:, tw:] = student_text[...]
+    copies = [
+        pltpu.make_async_copy(teacher_image, image.at[:, :tw], sems.at[0]),
+        pltpu.make_async_copy(student_image, image.at[:, tw:], sems.at[1]),
+        pltpu.make_async_copy(teacher_text, text.at[:, :tw], sems.at[2]),
+        pltpu.make_async_copy(student_text, text.at[:, tw:], sems.at[3]),
+    ]
+    for copy in copies:
+        copy.start()
+    for copy in copies:
+        copy.wait()
 
 
 def digits(share, rank, slots, width):
@@ -147,10 +154,18 @@
     return jnp.exp2(15.0 - power) * scale, jnp.exp2(power - 15.0)
 
 
+def split_lines(refs, n):
+    views = []
+    while len(views) < n:
+        views += [refs[0].at[block(k, LINES), :] for k in range(refs[0].shape[0] // LINES)]
+        refs = refs[1:]
+    return views, refs
+
+
 def gradient_kernel(nr, nc, b, pairs, scale, place, *refs):
     image, text, tl_ref, sl_ref, refs = *refs[:4], refs[4:]
-    row_parts, refs = refs[: nr // 2], refs[nr // 2 :]
-    col_parts, refs = refs[:nc], refs[nc:]
+    row_parts, refs = split_lines(refs, nr // 2)
+    col_parts, refs = split_lines(refs, nc)
     image_parts, text_parts, refs = refs[:4], refs[4:6], refs[6:]
     image_back_ref, text_back_ref, refs = refs[0], refs[1], refs[2:]
     width = image_back_ref.shape[1]
@@ -235,10 +250,27 @@
     return blocks
 
 
-def add_message(keep, come):
-    rows = keep[0].shape[0]
-    come = come.astype(F32)
-    return keep[0] + come[:rows], keep[1] + come[rows:]
+def exchange(bits, x):
+    parts = [x]
+    for bit in bits:
+        parts.append(swap((bit,), jnp.concatenate(parts) if len(parts) > 1 else x))
+    return parts
+
+
+def start_step(send, b, gate):
+    half = 0 if send.shape[0] - EXTRA == b else (send.shape[0] - EXTRA) // 2
+    if not half:
+        return [send.astype(F16)]
+    return [send[half:].astype(F16), together(send[:half].astype(F16), gate)[0]]
+
+
+def end_step(keep, come, b):
+    if len(come) == 1:
+        return (keep[0] + come[0][:b].astype(F32), keep[1] + come[0][b:].astype(F32)), None
+    half = come[1].shape[0]
+    on = keep[half:] + come[0].astype(F32)
+    keep = keep[:half] + come[1].astype(F32), on[half:]
+    return keep if half == b else jnp.concatenate(keep), on
 
 
 def local(image_bits, text_bits, teacher_image, teacher_text, student_image, student_text):
@@ -247,8 +279,15 @@
     nr, nc = 1 << len(image_bits), 1 << len(text_bits)
     r, c = nr * b, nc * b
     pair, others = image_bits[-1:], image_bits[:-1]
-    whole = ((b, tw + sw), BF16)
-    image, text = call(join_kernel, [whole, whole], [teacher_image, student_image, teacher_text, student_text])
+    whole = jax.ShapeDtypeStruct((b, tw + sw), BF16)
+    image, text = pl.pallas_call(
+        join_kernel,
+        out_shape=[whole, whole],
+        in_specs=[pl.BlockSpec(memory_space=pltpu.HBM)] * 4,
+        out_specs=[VMEM] * 2,
+        scratch_shapes=[pltpu.SemaphoreType.DMA((4,))],
+        compiler_params=pltpu.CompilerParams(vmem_limit_bytes=MOST),
+    )(teacher_image, student_image, teacher_text, student_text)
     images, texts = gather(image_bits, image), gather(text_bits, text)
     place = jnp.stack([lax.axis_index(x) for x in (pair, image_bits, text_bits)]).astype(jnp.int32)
     tl, sl, rows, rows_swapped, cols, image, text = call(
@@ -257,9 +296,7 @@
         [place] + images + texts, [((c, tw), BF16)], 2 * r * c * (tw + sw), 4 * r * c,
     )
     other = swap(pair, rows_swapped)
-    col_parts = [cols] + [swap(subset(text_bits, q), cols) for q in range(1, nc)]
-    rows = rows + other
-    row_parts = [rows] + [swap(subset(others, q), rows) for q in range(1, nr // 2)]
+    row_parts, col_parts = exchange(others, rows + other), exchange(text_bits, cols)
     pairs = b << (len(image_bits) + len(text_bits))
     near, far, other_near, other_far, text_keep, text_send, image_back, text_back = call(
         functools.partial(gradient_kernel, nr, nc, b, pairs, sw**-0.5),
@@ -270,23 +307,19 @@
     )
     image_send = far + swap(pair, other_far)
     image_keep = near + swap(pair, other_near)
-    image_keep, text_keep = [(x[:-EXTRA], x[-EXTRA:]) for x in (image_keep, text_keep)]
     for k in reversed(range(max(len(text_bits), len(others)))):
         todo = {}
         if k < len(text_bits):
-            todo["text"] = text_send.astype(F16)
+            todo["text"] = start_step(text_send, b, image_keep)
         if k < len(others):
-            todo["image"] = image_send.astype(F16)
-        (todo,) = together(todo)
-        half = b << k >> 1
+            todo["image"] = start_step(image_send, b, image_keep)
+        first = {name: x[0] for name, x in todo.items()}
+        (first,) = together(first)
+        todo = {name: [first[name]] + x[1:] for name, x in todo.items()}
         if k < len(text_bits):
-            body, extra = text_keep = add_message(text_keep, swap(text_bits[k : k + 1], todo["text"]))
-            if k:
-                text_keep, text_send = (body[:half], extra), jnp.concatenate([body[half:], extra])
+            text_keep, text_send = end_step(text_keep, [swap(text_bits[k : k + 1], x) for x in todo["text"]], b)
         if k < len(others):
-            body, extra = image_keep = add_message(image_keep, swap(others[k : k + 1], todo["image"]))
-            if k:
-                image_keep, image_send = (body[:half], extra), jnp.concatenate([body[half:], extra])
+            image_keep, image_send = end_step(image_keep, [swap(others[k : k + 1], x) for x in todo["image"]], b)
     units = stack_rows(DIGITS, (EXTRA, sw), 0)
     loss = jnp.sum((image_keep[1] + text_keep[1]) * units) * (0.5 / sw)
     return (loss, image_keep[0] * image_back, text_keep[0] * text_back)

time: 89.3 us -> 88.4 us (0.990)
  waiting for transfers between devices: 44 us -> 42 us
  Pallas kernels: 9.6 us -> 11.4 us
  local copies, waits for them, and re-layouts: 3.75 us -> 2.14 us
  starting transfers between devices: 26.1 us -> 27.5 us
    pallas_call x0 -> x1, Pallas kernels: none -> 2.14 us  [local(): pl.pallas_call(join_kernel, out_shape=[whole, whole], in_specs=[pl.BlockS...]
    ppermute x23, waiting for transfers between devices: 44 us -> 42 us  [swap(): return lax.ppermute(x, bits, perm)]
    unnamed x8 -> x4, local copies, waits for them, and re-layouts: 3.75 us -> 2.04 us
    ppermute x23, starting transfers between devices: 26.1 us -> 27.5 us  [swap(): return lax.ppermute(x, bits, perm)]
    pallas_call x3 -> x2, Pallas kernels: 9.6 us -> 9.23 us  [call(): pl.pallas_call(kernel, out_shape=shapes, in_specs=[SMEM if x.dtype == jnp...]
  transfers between devices with their start and end apart: 23 -> 23, of which waited for: 11 -> 13; matrix products, arithmetic and copies ran while one was open for 1% -> 2% of each run, Pallas kernels for 0% -> 0%
where the time goes in v7:
time: 88.4 us; the launch traced here: 88.2 us
  waiting for transfers between devices  42 us (48%)
  starting transfers between devices  27.5 us (31%)
  Pallas kernels  11.4 us (13%)
  other arithmetic  2.69 us (3%)
  between operations  2.54 us (3%)
  local copies, waits for them, and re-layouts  2.14 us (2%)
    ppermute x23, waiting for transfers between devices, swap(): return lax.ppermute(x, bits, perm)  42 us
    ppermute x23, starting transfers between devices, swap(): return lax.ppermute(x, bits, perm)  27.5 us
    pallas_call x2, Pallas kernels, call(): pl.pallas_call(kernel, out_shape=shapes, in_specs=[SMEM if x.dtype == jnp...  9.23 us
    pallas_call x1, Pallas kernels, local(): pl.pallas_call(join_kernel, out_shape=[whole, whole], in_specs=[pl.BlockS...  2.14 us
    unnamed x4, local copies, waits for them, and re-layouts  2.04 us
  transfers between devices with their start and end apart: 23, of which 13 were waited for; matrix products, arithmetic and copies ran while one was open for 2% of the time, Pallas kernels for 0%

profile of v7, /device:TPU:0, one launch (start us, length us, event | category | flops | bytes accessed | tf_op | source)
XLA Modules:
  0.0 88.2 jit_solution(2708943167591451087)
XLA Ops:
  0.6 2.1 %shard_map.67 = (bf16[128,1792]{1,0:T(8,128)(2,1)}, bf16[128,1792]{1,0:T(8,128)(2,1)}) custom-call(bf16[128,1280]{1,0:T(8,128)(2,1)} %teacher_image.1, bf16[128,512]{1,0:T(8,128)(2,1)} %student_image.1, bf16[128,1280]{1,0:T(8,128)(2,1)} %teacher_text.1, bf16[128,512]{1,0:T(8,128)(2,1)} %student_text.1), custom_call_target="tpu_custom_call" | custom-call | tf_op jit(solution)/shard_map/pallas_call | solution.py:283
  2.8 4.1 %collective-permute-start = (bf16[128,1792]{1,0:T(8,128)(2,1)}, bf16[128,1792]{1,0:T(8,128)(2,1)S(1)}, u32[]{:S(2)}, u32[]{:S(2)}) collective-permute-start(bf16[128,1792]{1,0:T(8,128)(2,1)} %get-tuple-element.28.refs_0_), channel_id=1, source_target_pairs={{0,16},{16,0},{1,17},{17,1},{2,18},{18,2},{3,19},{19,3},{4,20},{20... | collective-permute-start | bytes 1376264 | tf_op jit(solution)/shard_map/ppermute | solution.py:234
  6.9 1.5 %collective-permute-start.1 = (bf16[128,1792]{1,0:T(8,128)(2,1)}, bf16[128,1792]{1,0:T(8,128)(2,1)S(1)}, u32[]{:S(2)}, u32[]{:S(2)}) collective-permute-start(bf16[128,1792]{1,0:T(8,128)(2,1)} %get-tuple-element.28.refs_0_), channel_id=1, source_target_pairs={{0,4},{4,0},{1,5},{5,1},{2,6},{6,2},{3,7},{7,3},{8,12},{12,8},{9,1... | collective-permute-start | bytes 1376264 | tf_op jit(solution)/shard_map/ppermute | solution.py:234
  8.4 1.6 %collective-permute-start.7 = (bf16[128,1792]{1,0:T(8,128)(2,1)}, bf16[128,1792]{1,0:T(8,128)(2,1)S(1)}, u32[]{:S(2)}, u32[]{:S(2)}) collective-permute-start(bf16[128,1792]{1,0:T(8,128)(2,1)} %get-tuple-element.29.refs_8_), channel_id=1, source_target_pairs={{0,8},{8,0},{1,9},{9,1},{2,10},{10,2},{3,11},{11,3},{4,12},{12,4},... | collective-permute-start | bytes 1376264 | tf_op jit(solution)/shard_map/ppermute | solution.py:234
  10.0 1.5 %collective-permute-start.8 = (bf16[128,1792]{1,0:T(8,128)(2,1)}, bf16[128,1792]{1,0:T(8,128)(2,1)S(1)}, u32[]{:S(2)}, u32[]{:S(2)}) collective-permute-start(bf16[128,1792]{1,0:T(8,128)(2,1)} %get-tuple-element.29.refs_8_), channel_id=1, source_target_pairs={{0,2},{2,0},{1,3},{3,1},{4,6},{6,4},{5,7},{7,5},{8,10},{10,8},{9,1... | collective-permute-start | bytes 1376264 | tf_op jit(solution)/shard_map/ppermute | solution.py:234
  11.5 16.1 %collective-permute-done.refs_1_ = bf16[128,1792]{1,0:T(8,128)(2,1)S(1)} collective-permute-done((bf16[128,1792]{1,0:T(8,128)(2,1)}, bf16[128,1792]{1,0:T(8,128)(2,1)S(1)}, u32[]{:S(2)}, u32[]{:S(2)}) %collective-permute-start) | collective-permute-done | bytes 458784 | tf_op jit(solution)/shard_map/ppermute | solution.py:234
  27.5 1.6 %collective-permute-start.2 = (bf16[128,1792]{1,0:T(8,128)(2,1)S(1)}, bf16[128,1792]{1,0:T(8,128)(2,1)S(1)}, u32[]{:S(2)}, u32[]{:S(2)}) collective-permute-start(bf16[128,1792]{1,0:T(8,128)(2,1)S(1)} %collective-permute-done.refs_1_), channel_id=1, source_target_pairs={{0,4},{4,0},{1,5},{5,1},{2,6},{6,2},{3,7},{7,3},{8,12},{12,8},{9,1... | collective-permute-start | bytes 1376264 | tf_op jit(solution)/shard_map/ppermute | solution.py:234
  29.6 1.6 %collective-permute-start.9 = (bf16[128,1792]{1,0:T(8,128)(2,1)S(1)}, bf16[128,1792]{1,0:T(8,128)(2,1)}, u32[]{:S(2)}, u32[]{:S(2)}) collective-permute-start(bf16[128,1792]{1,0:T(8,128)(2,1)S(1)} %collective-permute-done.7.refs_9_), channel_id=1, source_target_pairs={{0,2},{2,0},{1,3},{3,1},{4,6},{6,4},{5,7},{7,5},{8,10},{10,8},{9,1... | collective-permute-start | bytes 1376264 | tf_op jit(solution)/shard_map/ppermute | solution.py:234
  31.2 8.0 %collective-permute-done.2.refs_3_ = bf16[128,1792]{1,0:T(8,128)(2,1)S(1)} collective-permute-done((bf16[128,1792]{1,0:T(8,128)(2,1)S(1)}, bf16[128,1792]{1,0:T(8,128)(2,1)S(1)}, u32[]{:S(2)}, u32[]{:S(2)}) %collective-permute-start.2) | collective-permute-done | bytes 458784 | tf_op jit(solution)/shard_map/ppermute | solution.py:234
  39.3 3.4 %collective-permute-done.9.refs_11_ = bf16[128,1792]{1,0:T(8,128)(2,1)} collective-permute-done((bf16[128,1792]{1,0:T(8,128)(2,1)S(1)}, bf16[128,1792]{1,0:T(8,128)(2,1)}, u32[]{:S(2)}, u32[]{:S(2)}) %collective-permute-start.9) | collective-permute-done | bytes 458784 | tf_op jit(solution)/shard_map/ppermute | solution.py:234
  42.7 1.0 %copy-done = bf16[128,1792]{1,0:T(8,128)(2,1)S(1)} copy-done((bf16[128,1792]{1,0:T(8,128)(2,1)S(1)}, bf16[128,1792]{1,0:T(8,128)(2,1)}, u32[]{:S(2)}) %copy-start) | copy-done | bytes 458776
  43.7 1.0 %copy-done.1 = bf16[128,1792]{1,0:T(8,128)(2,1)S(1)} copy-done((bf16[128,1792]{1,0:T(8,128)(2,1)S(1)}, bf16[128,1792]{1,0:T(8,128)(2,1)}, u32[]{:S(2)}) %copy-start.1) | copy-done | bytes 458776
  44.7 5.2 %shard_map.68 = (f32[1024,512]{1,0:T(8,128)S(1)}, f32[1024,512]{1,0:T(8,128)S(1)}, f32[8,1024]{1,0:T(8,128)S(1)}, f32[8,1024]{1,0:T(8,128)S(1)}, f32[8,512]{1,0:...) custom-call(s32[3]{0:T(128)S(1)} %pad_add_fusion.core.place, bf16[128,1792]{1,0:T(8,128)(2,1)S(1)} %copy-done, ...), custom_call_target="tpu_custom_call" | custom-call | flops 1879048192 | bytes 11354124 | tf_op jit(solution)/shard_map/pallas_call | solution.py:221
  50.0 1.2 %collective-permute-done.10 = f32[8,1024]{1,0:T(8,128)S(1)} collective-permute-done((f32[8,1024]{1,0:T(8,128)S(1)}, f32[8,1024]{1,0:T(8,128)S(1)}, u32[]{:S(2)}, u32[]{:S(2)}) %collective-permute-start.10) | collective-permute-done | bytes 32800 | tf_op jit(solution)/shard_map/ppermute | solution.py:234
  51.3 3.9 %collective-permute-start.13 = (f32[8,512]{1,0:T(8,128)S(1)}, f32[8,512]{1,0:T(8,128)S(1)}, u32[]{:S(2)}, u32[]{:S(2)}) collective-permute-start(f32[8,512]{1,0:T(8,128)S(1)} %get-tuple-element.36.refs_7_), channel_id=1, source_target_pairs={{0,8},{8,0},{1,9},{9,1},{2,10},{10,2},{3,11},{11,3},{4,12},{12,4},... | collective-permute-start | bytes 49160 | tf_op jit(solution)/shard_map/ppermute | solution.py:234
  55.2 1.5 %collective-permute-done.11.refs_5_ = f32[8,1024]{1,0:T(8,128)S(1)} collective-permute-done((f32[8,1024]{1,0:T(8,128)S(1)}, f32[8,1024]{1,0:T(8,128)S(1)}, u32[]{:S(2)}, u32[]{:S(2)}) %collective-permute-start.11) | collective-permute-done | bytes 32800 | tf_op jit(solution)/shard_map/ppermute | solution.py:234
  56.9 1.5 %collective-permute-start.14 = (f32[16,512]{1,0:T(8,128)S(1)}, f32[16,512]{1,0:T(8,128)S(1)}, u32[]{:S(2)}, u32[]{:S(2)}) collective-permute-start(f32[16,512]{1,0:T(8,128)S(1)} %pad_maximum_fusion.1), channel_id=1, source_target_pairs={{0,2},{2,0},{1,3},{3,1},{4,6},{6,4},{5,7},{7,5},{8,10},{10,8},{9,1... | collective-permute-start | bytes 98312 | tf_op jit(solution)/shard_map/ppermute | solution.py:234
  58.4 2.4 %collective-permute-done.14.refs_9_ = f32[16,512]{1,0:T(8,128)S(1)} collective-permute-done((f32[16,512]{1,0:T(8,128)S(1)}, f32[16,512]{1,0:T(8,128)S(1)}, u32[]{:S(2)}, u32[]{:S(2)}) %collective-permute-start.14) | collective-permute-done | bytes 32800 | tf_op jit(solution)/shard_map/ppermute | solution.py:234
  60.9 4.0 %shard_map.69 = (f32[272,512]{1,0:T(8,128)S(1)}, f32[272,512]{1,0:T(8,128)S(1)}, f32[272,512]{1,0:T(8,128)S(1)}, f32[272,512]{1,0:T(8,128)S(1)}, f32[272,512]{1,...) custom-call(s32[3]{0:T(128)S(1)} %pad_add_fusion.core.place, ...), custom_call_target="tpu_custom_call" | custom-call | flops 2147483648 | bytes 9310220 | tf_op jit(solution)/shard_map/pallas_call | solution.py:221
  65.6 1.4 %collective-permute-done.16 = f32[272,512]{1,0:T(8,128)S(1)} collective-permute-done((f32[272,512]{1,0:T(8,128)S(1)}, f32[272,512]{1,0:T(8,128)S(1)}, u32[]{:S(2)}, u32[]{:S(2)}) %collective-permute-start.16) | collective-permute-done | bytes 557088 | tf_op jit(solution)/shard_map/ppermute | solution.py:234
  67.1 1.8 %collective-permute-start.17 = (f16[144,512]{1,0:T(8,128)(2,1)S(1)}, f16[144,512]{1,0:T(8,128)(2,1)S(1)}, u32[]{:S(2)}, u32[]{:S(2)}) collective-permute-start(f16[144,512]{1,0:T(8,128)(2,1)S(1)} %slice.61), channel_id=1, source_target_pairs={{0,4},{4,0},{1,5},{5,1},{2,6},{6,2},{3,7},{7,3},{8,12},{12,8},{9,1... | collective-permute-start | bytes 442376 | tf_op jit(solution)/shard_map/ppermute | solution.py:234
  68.9 1.5 %collective-permute-start.18 = (f16[144,512]{1,0:T(8,128)(2,1)S(1)}, f16[144,512]{1,0:T(8,128)(2,1)S(1)}, u32[]{:S(2)}, u32[]{:S(2)}) collective-permute-start(f16[144,512]{1,0:T(8,128)(2,1)S(1)} %slice.62), channel_id=1, source_target_pairs={{0,2},{2,0},{1,3},{3,1},{4,6},{6,4},{5,7},{7,5},{8,10},{10,8},{9,1... | collective-permute-start | bytes 442376 | tf_op jit(solution)/shard_map/ppermute | solution.py:234
  70.5 2.6 %collective-permute-done.17 = f16[144,512]{1,0:T(8,128)(2,1)S(1)} collective-permute-done((f16[144,512]{1,0:T(8,128)(2,1)S(1)}, f16[144,512]{1,0:T(8,128)(2,1)S(1)}, u32[]{:S(2)}, u32[]{:S(2)}) %collective-permute-start.17) | collective-permute-done | bytes 147488 | tf_op jit(solution)/shard_map/ppermute | solution.py:234
  73.1 1.4 %collective-permute-done.18 = f16[144,512]{1,0:T(8,128)(2,1)S(1)} collective-permute-done((f16[144,512]{1,0:T(8,128)(2,1)S(1)}, f16[144,512]{1,0:T(8,128)(2,1)S(1)}, u32[]{:S(2)}, u32[]{:S(2)}) %collective-permute-start.18) | collective-permute-done | bytes 147488 | tf_op jit(solution)/shard_map/ppermute | solution.py:234
  74.5 1.1 %collective-permute-start.20 = (f16[144,512]{1,0:T(8,128)(2,1)S(1)}, f16[144,512]{1,0:T(8,128)(2,1)S(1)}, u32[]{:S(2)}, u32[]{:S(2)}) collective-permute-start(f16[144,512]{1,0:T(8,128)(2,1)S(1)} %get-tuple-element.46), channel_id=1, source_target_pairs={{0,8},{8,0},{1,9},{9,1},{2,10},{10,2},{3,11},{11,3},{4,12},{12,4},... | collective-permute-start | bytes 442376 | tf_op jit(solution)/shard_map/ppermute | solution.py:234
  75.6 2.3 %collective-permute-start.19 = (f16[144,512]{1,0:T(8,128)(2,1)S(1)}, f16[144,512]{1,0:T(8,128)(2,1)S(1)}, u32[]{:S(2)}, u32[]{:S(2)}) collective-permute-start(f16[144,512]{1,0:T(8,128)(2,1)S(1)} %get-tuple-element.45), channel_id=1, source_target_pairs={{0,16},{16,0},{1,17},{17,1},{2,18},{18,2},{3,19},{19,3},{4,20},{20... | collective-permute-start | bytes 442376 | tf_op jit(solution)/shard_map/ppermute | solution.py:234
  78.0 1.6 %collective-permute-start.22 = (f16[128,512]{1,0:T(8,128)(2,1)S(1)}, f16[128,512]{1,0:T(8,128)(2,1)S(1)}, u32[]{:S(2)}, u32[]{:S(2)}) collective-permute-start(f16[128,512]{1,0:T(8,128)(2,1)S(1)} %slice.70), channel_id=1, source_target_pairs={{0,2},{2,0},{1,3},{3,1},{4,6},{6,4},{5,7},{7,5},{8,10},{10,8},{9,1... | collective-permute-start | bytes 393224 | tf_op jit(solution)/shard_map/ppermute | solution.py:234
  79.5 0.9 %collective-permute-start.21 = (f16[128,512]{1,0:T(8,128)(2,1)S(1)}, f16[128,512]{1,0:T(8,128)(2,1)S(1)}, u32[]{:S(2)}, u32[]{:S(2)}) collective-permute-start(f16[128,512]{1,0:T(8,128)(2,1)S(1)} %slice.68), channel_id=1, source_target_pairs={{0,4},{4,0},{1,5},{5,1},{2,6},{6,2},{3,7},{7,3},{8,12},{12,8},{9,1... | collective-permute-start | bytes 393224 | tf_op jit(solution)/shard_map/ppermute | solution.py:234
  80.4 1.3 %collective-permute-done.20 = f16[144,512]{1,0:T(8,128)(2,1)S(1)} collective-permute-done((f16[144,512]{1,0:T(8,128)(2,1)S(1)}, f16[144,512]{1,0:T(8,128)(2,1)S(1)}, u32[]{:S(2)}, u32[]{:S(2)}) %collective-permute-start.20) | collective-permute-done | bytes 147488 | tf_op jit(solution)/shard_map/ppermute | solution.py:234
  81.8 2.4 %collective-permute-done.19 = f16[144,512]{1,0:T(8,128)(2,1)S(1)} collective-permute-done((f16[144,512]{1,0:T(8,128)(2,1)S(1)}, f16[144,512]{1,0:T(8,128)(2,1)S(1)}, u32[]{:S(2)}, u32[]{:S(2)}) %collective-permute-start.19) | collective-permute-done | bytes 147488 | tf_op jit(solution)/shard_map/ppermute | solution.py:234
  85.5 0.8 add_multiply_fusion
  86.3 0.8 fusion.1
  (40 shorter events, 2.8 us)
Async XLA Ops:
  2.8 24.8 %collective-permute-start = (bf16[128,1792]{1,0:T(8,128)(2,1)}, bf16[128,1792]{1,0:T(8,128)(2,1)S(1)}, u32[]{:S(2)}, u32[]{:S(2)}) collective-permute-start(bf16[128,1792]{1,0:T(8,128)(2,1)} %get-tuple-element.28.refs_0_), channel_id=1, source_target_pairs={{0,16},{16,0},{1,17},{17,1},{2,18},{18,2},{3,19},{19,3},{4,20},{20... | collective-permute-start | bytes 1376264 | tf_op jit(solution)/shard_map/ppermute | solution.py:234
  6.9 22.2 %collective-permute-start.1 = (bf16[128,1792]{1,0:T(8,128)(2,1)}, bf16[128,1792]{1,0:T(8,128)(2,1)S(1)}, u32[]{:S(2)}, u32[]{:S(2)}) collective-permute-start(bf16[128,1792]{1,0:T(8,128)(2,1)} %get-tuple-element.28.refs_0_), channel_id=1, source_target_pairs={{0,4},{4,0},{1,5},{5,1},{2,6},{6,2},{3,7},{7,3},{8,12},{12,8},{9,1... | collective-permute-start | bytes 1376264 | tf_op jit(solution)/shard_map/ppermute | solution.py:234
  8.4 21.2 %collective-permute-start.7 = (bf16[128,1792]{1,0:T(8,128)(2,1)}, bf16[128,1792]{1,0:T(8,128)(2,1)S(1)}, u32[]{:S(2)}, u32[]{:S(2)}) collective-permute-start(bf16[128,1792]{1,0:T(8,128)(2,1)} %get-tuple-element.29.refs_8_), channel_id=1, source_target_pairs={{0,8},{8,0},{1,9},{9,1},{2,10},{10,2},{3,11},{11,3},{4,12},{12,4},... | collective-permute-start | bytes 1376264 | tf_op jit(solution)/shard_map/ppermute | solution.py:234
  10.0 19.7 %collective-permute-start.8 = (bf16[128,1792]{1,0:T(8,128)(2,1)}, bf16[128,1792]{1,0:T(8,128)(2,1)S(1)}, u32[]{:S(2)}, u32[]{:S(2)}) collective-permute-start(bf16[128,1792]{1,0:T(8,128)(2,1)} %get-tuple-element.29.refs_8_), channel_id=1, source_target_pairs={{0,2},{2,0},{1,3},{3,1},{4,6},{6,4},{5,7},{7,5},{8,10},{10,8},{9,1... | collective-permute-start | bytes 1376264 | tf_op jit(solution)/shard_map/ppermute | solution.py:234
  27.5 11.6 %collective-permute-start.2 = (bf16[128,1792]{1,0:T(8,128)(2,1)S(1)}, bf16[128,1792]{1,0:T(8,128)(2,1)S(1)}, u32[]{:S(2)}, u32[]{:S(2)}) collective-permute-start(bf16[128,1792]{1,0:T(8,128)(2,1)S(1)} %collective-permute-done.refs_1_), channel_id=1, source_target_pairs={{0,4},{4,0},{1,5},{5,1},{2,6},{6,2},{3,7},{7,3},{8,12},{12,8},{9,1... | collective-permute-start | bytes 1376264 | tf_op jit(solution)/shard_map/ppermute | solution.py:234
  29.1 10.2 %collective-permute-start.3 = (bf16[128,1792]{1,0:T(8,128)(2,1)}, bf16[128,1792]{1,0:T(8,128)(2,1)S(1)}, u32[]{:S(2)}, u32[]{:S(2)}) collective-permute-start(bf16[128,1792]{1,0:T(8,128)(2,1)} %get-tuple-element.28.refs_0_), channel_id=1, source_target_pairs={{0,1},{1,0},{2,3},{3,2},{4,5},{5,4},{6,7},{7,6},{8,9},{9,8},{10,11... | collective-permute-start | bytes 1376264 | tf_op jit(solution)/shard_map/ppermute | solution.py:234
  29.1 10.2 %collective-permute-start.4 = (bf16[128,1792]{1,0:T(8,128)(2,1)S(1)}, bf16[128,1792]{1,0:T(8,128)(2,1)S(1)}, u32[]{:S(2)}, u32[]{:S(2)}) collective-permute-start(bf16[128,1792]{1,0:T(8,128)(2,1)S(1)} %collective-permute-done.refs_1_), channel_id=1, source_target_pairs={{0,1},{1,0},{2,3},{3,2},{4,5},{5,4},{6,7},{7,6},{8,9},{9,8},{10,11... | collective-permute-start | bytes 1376264 | tf_op jit(solution)/shard_map/ppermute | solution.py:234
  29.6 9.6 %collective-permute-start.5 = (bf16[128,1792]{1,0:T(8,128)(2,1)S(1)}, bf16[128,1792]{1,0:T(8,128)(2,1)}, u32[]{:S(2)}, u32[]{:S(2)}) collective-permute-start(bf16[128,1792]{1,0:T(8,128)(2,1)S(1)} %collective-permute-done.1.refs_2_), channel_id=1, source_target_pairs={{0,1},{1,0},{2,3},{3,2},{4,5},{5,4},{6,7},{7,6},{8,9},{9,8},{10,11... | collective-permute-start | bytes 1376264 | tf_op jit(solution)/shard_map/ppermute | solution.py:234
  29.6 13.0 %collective-permute-start.9 = (bf16[128,1792]{1,0:T(8,128)(2,1)S(1)}, bf16[128,1792]{1,0:T(8,128)(2,1)}, u32[]{:S(2)}, u32[]{:S(2)}) collective-permute-start(bf16[128,1792]{1,0:T(8,128)(2,1)S(1)} %collective-permute-done.7.refs_9_), channel_id=1, source_target_pairs={{0,2},{2,0},{1,3},{3,1},{4,6},{6,4},{5,7},{7,5},{8,10},{10,8},{9,1... | collective-permute-start | bytes 1376264 | tf_op jit(solution)/shard_map/ppermute | solution.py:234
  39.2 3.5 %collective-permute-start.6 = (bf16[128,1792]{1,0:T(8,128)(2,1)S(1)}, bf16[128,1792]{1,0:T(8,128)(2,1)}, u32[]{:S(2)}, u32[]{:S(2)}) collective-permute-start(bf16[128,1792]{1,0:T(8,128)(2,1)S(1)} %collective-permute-done.2.refs_3_), channel_id=1, source_target_pairs={{0,1},{1,0},{2,3},{3,2},{4,5},{5,4},{6,7},{7,6},{8,9},{9,8},{10,11... | collective-permute-start | bytes 1376264 | tf_op jit(solution)/shard_map/ppermute | solution.py:234
  42.7 1.0 %copy-start = (bf16[128,1792]{1,0:T(8,128)(2,1)S(1)}, bf16[128,1792]{1,0:T(8,128)(2,1)}, u32[]{:S(2)}) copy-start(bf16[128,1792]{1,0:T(8,128)(2,1)} %get-tuple-element.28.refs_0_) | copy-start | bytes 1376260
  43.7 1.0 %copy-start.1 = (bf16[128,1792]{1,0:T(8,128)(2,1)S(1)}, bf16[128,1792]{1,0:T(8,128)(2,1)}, u32[]{:S(2)}) copy-start(bf16[128,1792]{1,0:T(8,128)(2,1)} %get-tuple-element.29.refs_8_) | copy-start | bytes 1376260
  50.0 1.2 %collective-permute-start.10 = (f32[8,1024]{1,0:T(8,128)S(1)}, f32[8,1024]{1,0:T(8,128)S(1)}, u32[]{:S(2)}, u32[]{:S(2)}) collective-permute-start(f32[8,1024]{1,0:T(8,128)S(1)} %get-tuple-element.35), channel_id=1, source_target_pairs={{0,1},{1,0},{2,3},{3,2},{4,5},{5,4},{6,7},{7,6},{8,9},{9,8},{10,11... | collective-permute-start | bytes 98312 | tf_op jit(solution)/shard_map/ppermute | solution.py:234
  51.2 5.5 %collective-permute-start.11 = (f32[8,1024]{1,0:T(8,128)S(1)}, f32[8,1024]{1,0:T(8,128)S(1)}, u32[]{:S(2)}, u32[]{:S(2)}) collective-permute-start(f32[8,1024]{1,0:T(8,128)S(1)} %add.48.refs_4_), channel_id=1, source_target_pairs={{0,16},{16,0},{1,17},{17,1},{2,18},{18,2},{3,19},{19,3},{4,20},{20... | collective-permute-start | bytes 98312 | tf_op jit(solution)/shard_map/ppermute | solution.py:234
  51.3 5.6 %collective-permute-start.13 = (f32[8,512]{1,0:T(8,128)S(1)}, f32[8,512]{1,0:T(8,128)S(1)}, u32[]{:S(2)}, u32[]{:S(2)}) collective-permute-start(f32[8,512]{1,0:T(8,128)S(1)} %get-tuple-element.36.refs_7_), channel_id=1, source_target_pairs={{0,8},{8,0},{1,9},{9,1},{2,10},{10,2},{3,11},{11,3},{4,12},{12,4},... | collective-permute-start | bytes 49160 | tf_op jit(solution)/shard_map/ppermute | solution.py:234
  56.7 4.3 %collective-permute-start.12 = (f32[16,1024]{1,0:T(8,128)S(1)}, f32[16,1024]{1,0:T(8,128)S(1)}, u32[]{:S(2)}, u32[]{:S(2)}) collective-permute-start(f32[16,1024]{1,0:T(8,128)S(1)} %pad_maximum_fusion), channel_id=1, source_target_pairs={{0,4},{4,0},{1,5},{5,1},{2,6},{6,2},{3,7},{7,3},{8,12},{12,8},{9,1... | collective-permute-start | bytes 196616 | tf_op jit(solution)/shard_map/ppermute | solution.py:234
  56.9 3.9 %collective-permute-start.14 = (f32[16,512]{1,0:T(8,128)S(1)}, f32[16,512]{1,0:T(8,128)S(1)}, u32[]{:S(2)}, u32[]{:S(2)}) collective-permute-start(f32[16,512]{1,0:T(8,128)S(1)} %pad_maximum_fusion.1), channel_id=1, source_target_pairs={{0,2},{2,0},{1,3},{3,1},{4,6},{6,4},{5,7},{7,5},{8,10},{10,8},{9,1... | collective-permute-start | bytes 98312 | tf_op jit(solution)/shard_map/ppermute | solution.py:234
  64.9 2.0 %collective-permute-start.16 = (f32[272,512]{1,0:T(8,128)S(1)}, f32[272,512]{1,0:T(8,128)S(1)}, u32[]{:S(2)}, u32[]{:S(2)}) collective-permute-start(f32[272,512]{1,0:T(8,128)S(1)} %get-tuple-element.40), channel_id=1, source_target_pairs={{0,1},{1,0},{2,3},{3,2},{4,5},{5,4},{6,7},{7,6},{8,9},{9,8},{10,11... | collective-permute-start | bytes 1671176 | tf_op jit(solution)/shard_map/ppermute | solution.py:234
  65.0 5.4 %collective-permute-start.15 = (f32[272,512]{1,0:T(8,128)S(1)}, f32[272,512]{1,0:T(8,128)S(1)}, u32[]{:S(2)}, u32[]{:S(2)}) collective-permute-start(f32[272,512]{1,0:T(8,128)S(1)} %get-tuple-element.38), channel_id=1, source_target_pairs={{0,1},{1,0},{2,3},{3,2},{4,5},{5,4},{6,7},{7,6},{8,9},{9,8},{10,11... | collective-permute-start | bytes 1671176 | tf_op jit(solution)/shard_map/ppermute | solution.py:234
  67.1 6.0 %collective-permute-start.17 = (f16[144,512]{1,0:T(8,128)(2,1)S(1)}, f16[144,512]{1,0:T(8,128)(2,1)S(1)}, u32[]{:S(2)}, u32[]{:S(2)}) collective-permute-start(f16[144,512]{1,0:T(8,128)(2,1)S(1)} %slice.61), channel_id=1, source_target_pairs={{0,4},{4,0},{1,5},{5,1},{2,6},{6,2},{3,7},{7,3},{8,12},{12,8},{9,1... | collective-permute-start | bytes 442376 | tf_op jit(solution)/shard_map/ppermute | solution.py:234
  68.9 5.6 %collective-permute-start.18 = (f16[144,512]{1,0:T(8,128)(2,1)S(1)}, f16[144,512]{1,0:T(8,128)(2,1)S(1)}, u32[]{:S(2)}, u32[]{:S(2)}) collective-permute-start(f16[144,512]{1,0:T(8,128)(2,1)S(1)} %slice.62), channel_id=1, source_target_pairs={{0,2},{2,0},{1,3},{3,1},{4,6},{6,4},{5,7},{7,5},{8,10},{10,8},{9,1... | collective-permute-start | bytes 442376 | tf_op jit(solution)/shard_map/ppermute | solution.py:234
  74.5 7.2 %collective-permute-start.20 = (f16[144,512]{1,0:T(8,128)(2,1)S(1)}, f16[144,512]{1,0:T(8,128)(2,1)S(1)}, u32[]{:S(2)}, u32[]{:S(2)}) collective-permute-start(f16[144,512]{1,0:T(8,128)(2,1)S(1)} %get-tuple-element.46), channel_id=1, source_target_pairs={{0,8},{8,0},{1,9},{9,1},{2,10},{10,2},{3,11},{11,3},{4,12},{12,4},... | collective-permute-start | bytes 442376 | tf_op jit(solution)/shard_map/ppermute | solution.py:234
  75.6 8.5 %collective-permute-start.19 = (f16[144,512]{1,0:T(8,128)(2,1)S(1)}, f16[144,512]{1,0:T(8,128)(2,1)S(1)}, u32[]{:S(2)}, u32[]{:S(2)}) collective-permute-start(f16[144,512]{1,0:T(8,128)(2,1)S(1)} %get-tuple-element.45), channel_id=1, source_target_pairs={{0,16},{16,0},{1,17},{17,1},{2,18},{18,2},{3,19},{19,3},{4,20},{20... | collective-permute-start | bytes 442376 | tf_op jit(solution)/shard_map/ppermute | solution.py:234
  78.0 7.5 %collective-permute-start.22 = (f16[128,512]{1,0:T(8,128)(2,1)S(1)}, f16[128,512]{1,0:T(8,128)(2,1)S(1)}, u32[]{:S(2)}, u32[]{:S(2)}) collective-permute-start(f16[128,512]{1,0:T(8,128)(2,1)S(1)} %slice.70), channel_id=1, source_target_pairs={{0,2},{2,0},{1,3},{3,1},{4,6},{6,4},{5,7},{7,5},{8,10},{10,8},{9,1... | collective-permute-start | bytes 393224 | tf_op jit(solution)/shard_map/ppermute | solution.py:234
  79.5 6.7 %collective-permute-start.21 = (f16[128,512]{1,0:T(8,128)(2,1)S(1)}, f16[128,512]{1,0:T(8,128)(2,1)S(1)}, u32[]{:S(2)}, u32[]{:S(2)}) collective-permute-start(f16[128,512]{1,0:T(8,128)(2,1)S(1)} %slice.68), channel_id=1, source_target_pairs={{0,4},{4,0},{1,5},{5,1},{2,6},{6,2},{3,7},{7,3},{8,12},{12,8},{9,1... | collective-permute-start | bytes 393224 | tf_op jit(solution)/shard_map/ppermute | solution.py:234

commit v8 on v6

--- a/solution.py
+++ b/solution.py
@@ -47,22 +47,19 @@
 
 def stats_kernel(nr, nc, b, tw, scale_t, scale_s, core, *refs):
     images, texts, refs = refs[:nr], refs[nr : nr + nc], refs[nr + nc :]
-    tl_ref, sl_ref, row_ref, swap_ref, col_ref, image_s, text_s, text_t = refs
+    tl_ref, sl_ref, row_ref, swap_ref, peak_ref, image_s, text_s, text_t = refs
     for p in range(nc):
         text_t[block(p, b), :] = texts[p][:, :tw]
         text_s[block(p, b), :] = texts[p][:, tw:]
     for p in range(nr):
         image_s[block(p, b), :] = images[p][:, tw:]
-    largest = [
-        functools.reduce(jnp.maximum, [jnp.max(jnp.abs(x[block(p, b), :].astype(F32)), 0, keepdims=True) for p in range(n)])
-        for x, n in ((image_s, nr), (text_s, nc))
-    ]
-    width = largest[0].shape[1]
+    largest = jnp.max(jnp.abs(text_s[...].astype(F32)), 0, keepdims=True)
+    width = largest.shape[1]
 
     def with_largest(flat, k):
         if (k + 1) * b > width:
             return flat
-        return flat + stack_rows((largest[1][:, block(k, b)],), flat.shape, 0, 2 * KINDS + core[0])
+        return flat + stack_rows((largest[:, block(k, b)],), flat.shape, 0, 2 * KINDS + core[0])
 
     step = 2 if nr % 2 == 0 else 1
     count = step * b
@@ -88,29 +85,28 @@
             other = (p + k) ^ (nr // 2)
             row_ref[:, block(p + k, b)] = with_largest(flat, p + k)
             swap_ref[:, block(other, b)] = with_largest(flat, other)
-    sum_t = sum_s = gap = None
-    for p in range(0, nr, step):
-        tl, sl = tl_ref[p * b : p * b + count, :], sl_ref[p * b : p * b + count, :]
+    peak_ref[...] = stack_rows((peak_t, peak_s), peak_ref.shape, 0)
+
+
+def column_kernel(step, tl_ref, sl_ref, peaks, image, col_ref):
+    peak_t, peak_s = peaks[0:1, :], peaks[1:2, :]
+    sums = None
+    for k in range(0, tl_ref.shape[0], step):
+        tl, sl = tl_ref[k : k + step, :], sl_ref[k : k + step, :]
         et = jnp.exp2(tl - peak_t)
-        parts = [
-            jnp.sum(et, 0, keepdims=True),
-            jnp.sum(jnp.exp2(sl - peak_s), 0, keepdims=True),
-            jnp.sum(et * (tl - sl), 0, keepdims=True),
-        ]
-        sum_t, sum_s, gap = parts if p == 0 else [x + y for x, y in zip((sum_t, sum_s, gap), parts)]
-    lines = (peak_t + jnp.log2(sum_t), peak_s + jnp.log2(sum_s), gap / sum_t)
-    most = largest[0]
-    if col_ref.shape[1] > width:
-        most = jnp.concatenate([most, jnp.zeros((1, col_ref.shape[1] - width), F32)], 1)
-    col_ref[...] = stack_rows(lines + (most,), col_ref.shape, 0)
-
-
-def join_kernel(teacher_image, student_image, teacher_text, student_text, image, text):
-    tw = teacher_image.shape[1]
-    image[:, :tw] = teacher_image[...]
-    image[:, tw:] = student_image[...]
-    text[:, :tw] = teacher_text[...]
-    text[:, tw:] = student_text[...]
+        parts = [jnp.sum(x, 0, keepdims=True) for x in (et, jnp.exp2(sl - peak_s), et * (tl - sl))]
+        sums = parts if sums is None else [x + y for x, y in zip(sums, parts)]
+    most = jnp.max(jnp.abs(image[...].astype(F32)), 0, keepdims=True)
+    if col_ref.shape[1] > most.shape[1]:
+        most = jnp.concatenate([most, jnp.zeros((1, col_ref.shape[1] - most.shape[1]), F32)], 1)
+    lines = (peak_t + jnp.log2(sums[0]), peak_s + jnp.log2(sums[1]), sums[2] / sums[0], most)
+    col_ref[...] = stack_rows(lines, col_ref.shape, 0)
+
+
+def join_kernel(teacher, student, both):
+    tw = teacher.shape[1]
+    both[:, :tw] = teacher[...]
+    both[:, tw:] = student[...]
 
 
 def digits(share, rank, slots, width):
@@ -147,19 +143,27 @@
     return jnp.exp2(15.0 - power) * scale, jnp.exp2(power - 15.0)
 
 
-def gradient_kernel(nr, nc, b, pairs, scale, place, *refs):
-    image, text, tl_ref, sl_ref, refs = *refs[:4], refs[4:]
-    row_parts, refs = refs[: nr // 2], refs[nr // 2 :]
-    col_parts, refs = refs[:nc], refs[nc:]
-    image_parts, text_parts, refs = refs[:4], refs[4:6], refs[6:]
-    image_back_ref, text_back_ref, refs = refs[0], refs[1], refs[2:]
+def split_lines(refs, n):
+    views = []
+    while len(views) < n:
+        views += [refs[0].at[block(k, LINES), :] for k in range(refs[0].shape[0] // LINES)]
+        refs = refs[1:]
+    return views, refs
+
+
+def delta_kernel(nr, nc, b, pairs, scale, place, *refs):
+    text, tl_ref, sl_ref, refs = *refs[:3], refs[3:]
+    row_parts, refs = split_lines(refs, nr // 2)
+    col_parts, refs = split_lines(refs, nc)
+    other_near, other_far, high_ref, low_ref, refs = *refs[:4], refs[4:]
+    image_back_ref, text_back_ref, scale_ref, image_extra, text_extra, row_terms, col_terms = refs
     width = image_back_ref.shape[1]
     lines = [x[2 * KINDS + core : 2 * KINDS + core + 1, :width] for x in row_parts for core in range(2)]
     image_scale, image_back = powers(lines, pairs, scale)
     text_scale, text_back = powers([x[KINDS : KINDS + 1, :width] for x in col_parts], pairs, scale)
     image_back_ref[...] = image_back
     text_back_ref[...] = text_back
-    high_ref, low_ref, row_terms, col_terms = refs
+    scale_ref[...] = stack_rows((image_scale, text_scale), scale_ref.shape, 0)
     tiles = []
     for q in range(nr // 2):
         x = jnp.concatenate([row_parts[q][:, block(p ^ q, b)] for p in range(nr)], 1)
@@ -183,20 +187,26 @@
         high = delta.astype(BF16)
         high_ref[block(p, b), :] = high
         low_ref[block(p, b), :] = (delta - high.astype(F32)).astype(BF16)
-    image_extra = digits(col_share * (1.0 / (nc * b)), place[1], nr, width)
-    text_extra = digits(row_share * (1.0 / (nr * b)), place[2], nc, width)
-    quarter = nr // 4
-    for n in (3, 2, 1, 0):
-        rows = slice(n * quarter * b, (n + 1) * quarter * b)
-        part = matmul(high_ref[rows, :], text[...], 1, 0) + matmul(low_ref[rows, :], text[...], 1, 0)
-        image_parts[n][: quarter * b, :] = part * image_scale
-        image_parts[n][quarter * b :, :] = image_extra
-    half = nc // 2
-    for n in (1, 0):
-        cols = slice(n * half * b, (n + 1) * half * b)
-        part = matmul(high_ref[:, cols], image[...], 0, 0) + matmul(low_ref[:, cols], image[...], 0, 0)
-        text_parts[n][: half * b, :] = part * text_scale
-        text_parts[n][half * b :, :] = text_extra
+    image_extra[...] = digits(col_share * (1.0 / (nc * b)), place[1], nr, width)
+    text_extra[...] = digits(row_share * (1.0 / (nr * b)), place[2], nc, width)
+    rows = nr * b // 4
+    for n, ref in ((3, other_far), (2, other_near)):
+        ref[:rows, :] = product(high_ref, low_ref, (block(n, rows), slice(None)), text, 1) * image_scale
+        ref[rows:, :] = image_extra[...]
+
+
+def product(high_ref, low_ref, place, other, dim):
+    return matmul(high_ref[place], other[...], dim, 0) + matmul(low_ref[place], other[...], dim, 0)
+
+
+def gradient_kernel(image, text, high_ref, low_ref, scale_ref, image_extra, text_extra, near, far, keep, send):
+    rows, cols = near.shape[0] - EXTRA, keep.shape[0] - EXTRA
+    for n, ref in ((1, far), (0, near)):
+        ref[:rows, :] = product(high_ref, low_ref, (block(n, rows), slice(None)), text, 1) * scale_ref[0:1, :]
+        ref[rows:, :] = image_extra[...]
+    for n, ref in ((1, send), (0, keep)):
+        ref[:cols, :] = product(high_ref, low_ref, (slice(None), block(n, cols)), image, 0) * scale_ref[1:2, :]
+        ref[cols:, :] = text_extra[...]
 
 
 def call(kernel, outs, args, scratch=(), flops=0, transcendentals=0):
@@ -235,6 +245,13 @@
     return blocks
 
 
+def exchange(bits, x):
+    parts = [x]
+    for bit in bits:
+        parts.append(swap((bit,), jnp.concatenate(parts) if len(parts) > 1 else x))
+    return parts
+
+
 def add_message(keep, come):
     rows = keep[0].shape[0]
     come = come.astype(F32)
@@ -247,29 +264,35 @@
     nr, nc = 1 << len(image_bits), 1 << len(text_bits)
     r, c = nr * b, nc * b
     pair, others = image_bits[-1:], image_bits[:-1]
-    whole = ((b, tw + sw), BF16)
-    image, text = call(join_kernel, [whole, whole], [teacher_image, student_image, teacher_text, student_text])
+    (image,) = call(join_kernel, [((b, tw + sw), BF16)], [teacher_image, student_image])
+    (text,) = call(join_kernel, [((b, tw + sw), BF16)], [teacher_text, student_text])
     images, texts = gather(image_bits, image), gather(text_bits, text)
     place = jnp.stack([lax.axis_index(x) for x in (pair, image_bits, text_bits)]).astype(jnp.int32)
-    tl, sl, rows, rows_swapped, cols, image, text = call(
+    tl, sl, rows, rows_swapped, peaks, image, text = call(
         functools.partial(stats_kernel, nr, nc, b, tw, tw**-0.5, sw**-0.5),
         [((r, c), F32), ((r, c), F32), ((LINES, r), F32), ((LINES, r), F32), ((LINES, c), F32), ((r, sw), BF16), ((c, sw), BF16)],
         [place] + images + texts, [((c, tw), BF16)], 2 * r * c * (tw + sw), 4 * r * c,
     )
     other = swap(pair, rows_swapped)
-    col_parts = [cols] + [swap(subset(text_bits, q), cols) for q in range(1, nc)]
-    rows = rows + other
-    row_parts = [rows] + [swap(subset(others, q), rows) for q in range(1, nr // 2)]
+    (cols,) = call(
+        functools.partial(column_kernel, 2 * b), [((LINES, c), F32)], [tl, sl, peaks, image], (), 0, 2 * r * c
+    )
+    row_parts, col_parts = exchange(others, rows + other), exchange(text_bits, cols)
     pairs = b << (len(image_bits) + len(text_bits))
-    near, far, other_near, other_far, text_keep, text_send, image_back, text_back = call(
-        functools.partial(gradient_kernel, nr, nc, b, pairs, sw**-0.5),
-        [((r // 4 + EXTRA, sw), F32)] * 4 + [((c // 2 + EXTRA, sw), F32)] * 2 + [((1, sw), F32)] * 2,
-        [place, image, text, tl, sl] + row_parts + col_parts,
-        [((r, c), BF16), ((r, c), BF16), ((nr, r), F32), ((max(nc, 8), c), F32)],
-        8 * r * c * sw, 4 * r * c,
-    )
-    image_send = far + swap(pair, other_far)
-    image_keep = near + swap(pair, other_near)
+    row, extra = ((1, sw), F32), ((EXTRA, sw), F32)
+    near_shape, keep_shape = ((r // 4 + EXTRA, sw), F32), ((c // 2 + EXTRA, sw), F32)
+    other_near, other_far, high, low, image_back, text_back, *more = call(
+        functools.partial(delta_kernel, nr, nc, b, pairs, sw**-0.5),
+        [near_shape, near_shape, ((r, c), BF16), ((r, c), BF16), row, row, ((8, sw), F32), extra, extra],
+        [place, text, tl, sl] + row_parts + col_parts,
+        [((nr, r), F32), ((max(nc, 8), c), F32)], 2 * r * c * sw, 4 * r * c,
+    )
+    other_far, other_near = swap(pair, other_far), swap(pair, other_near)
+    near, far, text_keep, text_send = call(
+        gradient_kernel, [near_shape, near_shape, keep_shape, keep_shape], [image, text, high, low] + more, (), 6 * r * c * sw
+    )
+    image_send = far + other_far
+    image_keep = near + other_near
     image_keep, text_keep = [(x[:-EXTRA], x[-EXTRA:]) for x in (image_keep, text_keep)]
     for k in reversed(range(max(len(text_bits), len(others)))):
         todo = {}

time: 89.3 us -> 88.5 us (level)
  starting transfers between devices: 26.1 us -> 22.6 us
  waiting for transfers between devices: 44 us -> 46.3 us
    ppermute x23 -> x21, starting transfers between devices: 26.1 us -> 22.6 us  [swap(): return lax.ppermute(x, bits, perm)]
    ppermute x23 -> x21, waiting for transfers between devices: 44 us -> 46.3 us  [swap(): return lax.ppermute(x, bits, perm)]
    pallas_call x3 -> x6, Pallas kernels: 9.6 us -> 10 us  [call(): pl.pallas_call(kernel, out_shape=shapes, in_specs=[SMEM if x.dtype == jnp...]
  transfers between devices with their start and end apart: 23 -> 21, of which waited for: 11 -> 12; matrix products, arithmetic and copies ran while one was open for 1% -> 1% of each run, Pallas kernels for 0% -> 4%
where the time goes in v8:
time: 88.5 us; the launch traced here: 88.3 us
  waiting for transfers between devices  46.3 us (52%)
  starting transfers between devices  22.6 us (26%)
  Pallas kernels  10 us (11%)
  local copies, waits for them, and re-layouts  3.75 us (4%)
  other arithmetic  2.99 us (3%)
  between operations  2.59 us (3%)
    ppermute x21, waiting for transfers between devices, swap(): return lax.ppermute(x, bits, perm)  46.3 us
    ppermute x21, starting transfers between devices, swap(): return lax.ppermute(x, bits, perm)  22.6 us
    pallas_call x6, Pallas kernels, call(): pl.pallas_call(kernel, out_shape=shapes, in_specs=[SMEM if x.dtype == jnp...  10 us
    unnamed x8, local copies, waits for them, and re-layouts  3.75 us
  transfers between devices with their start and end apart: 21, of which 12 were waited for; matrix products, arithmetic and copies ran while one was open for 1% of the time, Pallas kernels for 4%

profile of v8, /device:TPU:0, one launch (start us, length us, event | category | flops | bytes accessed | tf_op | source)
XLA Modules:
  0.0 88.3 jit_solution(993381940135227773)
XLA Ops:
  0.6 1.0 %copy-done = bf16[128,1280]{1,0:T(8,128)(2,1)S(1)} copy-done((bf16[128,1280]{1,0:T(8,128)(2,1)S(1)}, bf16[128,1280]{1,0:T(8,128)(2,1)}, u32[]{:S(2)}) %copy-start) | copy-done | bytes 327704
  1.6 0.9 %copy-done.2 = bf16[128,512]{1,0:T(8,128)(2,1)S(1)} copy-done((bf16[128,512]{1,0:T(8,128)(2,1)S(1)}, bf16[128,512]{1,0:T(8,128)(2,1)}, u32[]{:S(2)}) %copy-start.2) | copy-done | bytes 131096
  2.5 4.1 %collective-permute-start = (bf16[128,1792]{1,0:T(8,128)(2,1)S(1)}, bf16[128,1792]{1,0:T(8,128)(2,1)S(1)}, u32[]{:S(2)}, u32[]{:S(2)}) collective-permute-start(bf16[128,1792]{1,0:T(8,128)(2,1)S(1)} %shard_map.67.refs_0_), channel_id=1, source_target_pairs={{0,16},{16,0},{1,17},{17,1},{2,18},{18,2},{3,19},{19,3},{4,20},{20... | collective-permute-start | bytes 1376264 | tf_op jit(solution)/shard_map/ppermute | solution.py:229
  6.6 1.5 %collective-permute-start.1 = (bf16[128,1792]{1,0:T(8,128)(2,1)S(1)}, bf16[128,1792]{1,0:T(8,128)(2,1)S(1)}, u32[]{:S(2)}, u32[]{:S(2)}) collective-permute-start(bf16[128,1792]{1,0:T(8,128)(2,1)S(1)} %shard_map.67.refs_0_), channel_id=1, source_target_pairs={{0,4},{4,0},{1,5},{5,1},{2,6},{6,2},{3,7},{7,3},{8,12},{12,8},{9,1... | collective-permute-start | bytes 1376264 | tf_op jit(solution)/shard_map/ppermute | solution.py:229
  8.2 1.0 %copy-done.1 = bf16[128,1280]{1,0:T(8,128)(2,1)S(1)} copy-done((bf16[128,1280]{1,0:T(8,128)(2,1)S(1)}, bf16[128,1280]{1,0:T(8,128)(2,1)}, u32[]{:S(2)}) %copy-start.1) | copy-done | bytes 327704
  9.1 0.9 %copy-done.3 = bf16[128,512]{1,0:T(8,128)(2,1)S(1)} copy-done((bf16[128,512]{1,0:T(8,128)(2,1)S(1)}, bf16[128,512]{1,0:T(8,128)(2,1)}, u32[]{:S(2)}) %copy-start.3) | copy-done | bytes 131096
  10.1 1.6 %collective-permute-start.7 = (bf16[128,1792]{1,0:T(8,128)(2,1)S(1)}, bf16[128,1792]{1,0:T(8,128)(2,1)S(1)}, u32[]{:S(2)}, u32[]{:S(2)}) collective-permute-start(bf16[128,1792]{1,0:T(8,128)(2,1)S(1)} %shard_map.68.refs_8_), channel_id=1, source_target_pairs={{0,8},{8,0},{1,9},{9,1},{2,10},{10,2},{3,11},{11,3},{4,12},{12,4},... | collective-permute-start | bytes 1376264 | tf_op jit(solution)/shard_map/ppermute | solution.py:229
  11.7 1.5 %collective-permute-start.8 = (bf16[128,1792]{1,0:T(8,128)(2,1)S(1)}, bf16[128,1792]{1,0:T(8,128)(2,1)S(1)}, u32[]{:S(2)}, u32[]{:S(2)}) collective-permute-start(bf16[128,1792]{1,0:T(8,128)(2,1)S(1)} %shard_map.68.refs_8_), channel_id=1, source_target_pairs={{0,2},{2,0},{1,3},{3,1},{4,6},{6,4},{5,7},{7,5},{8,10},{10,8},{9,1... | collective-permute-start | bytes 1376264 | tf_op jit(solution)/shard_map/ppermute | solution.py:229
  13.2 13.9 %collective-permute-done.refs_1_ = bf16[128,1792]{1,0:T(8,128)(2,1)S(1)} collective-permute-done((bf16[128,1792]{1,0:T(8,128)(2,1)S(1)}, bf16[128,1792]{1,0:T(8,128)(2,1)S(1)}, u32[]{:S(2)}, u32[]{:S(2)}) %collective-permute-start) | collective-permute-done | bytes 458784 | tf_op jit(solution)/shard_map/ppermute | solution.py:229
  27.1 1.6 %collective-permute-start.2 = (bf16[128,1792]{1,0:T(8,128)(2,1)S(1)}, bf16[128,1792]{1,0:T(8,128)(2,1)S(1)}, u32[]{:S(2)}, u32[]{:S(2)}) collective-permute-start(bf16[128,1792]{1,0:T(8,128)(2,1)S(1)} %collective-permute-done.refs_1_), channel_id=1, source_target_pairs={{0,4},{4,0},{1,5},{5,1},{2,6},{6,2},{3,7},{7,3},{8,12},{12,8},{9,1... | collective-permute-start | bytes 1376264 | tf_op jit(solution)/shard_map/ppermute | solution.py:229
  29.2 1.3 %collective-permute-done.7.refs_9_ = bf16[128,1792]{1,0:T(8,128)(2,1)S(1)} collective-permute-done((bf16[128,1792]{1,0:T(8,128)(2,1)S(1)}, bf16[128,1792]{1,0:T(8,128)(2,1)S(1)}, u32[]{:S(2)}, u32[]{:S(2)}) %collective-permute-start.7) | collective-permute-done | bytes 458784 | tf_op jit(solution)/shard_map/ppermute | solution.py:229
  30.5 1.5 %collective-permute-start.9 = (bf16[128,1792]{1,0:T(8,128)(2,1)S(1)}, bf16[128,1792]{1,0:T(8,128)(2,1)}, u32[]{:S(2)}, u32[]{:S(2)}) collective-permute-start(bf16[128,1792]{1,0:T(8,128)(2,1)S(1)} %collective-permute-done.7.refs_9_), channel_id=1, source_target_pairs={{0,2},{2,0},{1,3},{3,1},{4,6},{6,4},{5,7},{7,5},{8,10},{10,8},{9,1... | collective-permute-start | bytes 1376264 | tf_op jit(solution)/shard_map/ppermute | solution.py:229
  32.1 6.7 %collective-permute-done.2.refs_3_ = bf16[128,1792]{1,0:T(8,128)(2,1)S(1)} collective-permute-done((bf16[128,1792]{1,0:T(8,128)(2,1)S(1)}, bf16[128,1792]{1,0:T(8,128)(2,1)S(1)}, u32[]{:S(2)}, u32[]{:S(2)}) %collective-permute-start.2) | collective-permute-done | bytes 458784 | tf_op jit(solution)/shard_map/ppermute | solution.py:229
  38.8 4.7 %collective-permute-done.9.refs_11_ = bf16[128,1792]{1,0:T(8,128)(2,1)} collective-permute-done((bf16[128,1792]{1,0:T(8,128)(2,1)S(1)}, bf16[128,1792]{1,0:T(8,128)(2,1)}, u32[]{:S(2)}, u32[]{:S(2)}) %collective-permute-start.9) | collective-permute-done | bytes 458784 | tf_op jit(solution)/shard_map/ppermute | solution.py:229
  43.6 4.5 %shard_map.69 = (f32[1024,512]{1,0:T(8,128)S(1)}, f32[1024,512]{1,0:T(8,128)S(1)}, f32[8,1024]{1,0:T(8,128)S(1)}, f32[8,1024]{1,0:T(8,128)S(1)}, f32[8,512]{1,0:...) custom-call(s32[3]{0:T(128)S(1)} %pad_add_fusion.core.place, ...), custom_call_target="tpu_custom_call" | custom-call | flops 1879048192 | bytes 11354124 | tf_op jit(solution)/shard_map/pallas_call | solution.py:216
  48.1 1.2 %collective-permute-done.10 = f32[8,1024]{1,0:T(8,128)S(1)} collective-permute-done((f32[8,1024]{1,0:T(8,128)S(1)}, f32[8,1024]{1,0:T(8,128)S(1)}, u32[]{:S(2)}, u32[]{:S(2)}) %collective-permute-start.10) | collective-permute-done | bytes 32800 | tf_op jit(solution)/shard_map/ppermute | solution.py:229
  49.8 1.4 %shard_map.70.refs_6_ = f32[8,512]{1,0:T(8,128)S(1)} custom-call(f32[1024,512]{1,0:T(8,128)S(1)} %get-tuple-element.31.tl_ref.refs_1_, f32[1024,512]{1,0:T(8,128)S(1)} %get-tuple-element.32.sl_ref.refs_2_, f32[8,512]{1,0:T(8,128)S(1)} %get-tuple-element.35.peaks, bf16[1024,512]{1,0:T(8,128)(2,1)S(1)} %get-tuple-element.29.image), custom_call_target="tpu_custom_call" | custom-call | bytes 5275648 | tf_op jit(solution)/shard_map/pallas_call | solution.py:216
  51.2 2.5 %collective-permute-start.13 = (f32[8,512]{1,0:T(8,128)S(1)}, f32[8,512]{1,0:T(8,128)S(1)}, u32[]{:S(2)}, u32[]{:S(2)}) collective-permute-start(f32[8,512]{1,0:T(8,128)S(1)} %shard_map.70.refs_6_), channel_id=1, source_target_pairs={{0,8},{8,0},{1,9},{9,1},{2,10},{10,2},{3,11},{11,3},{4,12},{12,4},... | collective-permute-start | bytes 49160 | tf_op jit(solution)/shard_map/ppermute | solution.py:229
  54.7 0.8 collective-permute-done.13.refs_7_
  55.4 1.5 %collective-permute-start.14 = (f32[16,512]{1,0:T(8,128)S(1)}, f32[16,512]{1,0:T(8,128)S(1)}, u32[]{:S(2)}, u32[]{:S(2)}) collective-permute-start(f32[16,512]{1,0:T(8,128)S(1)} %pad_maximum_fusion.3), channel_id=1, source_target_pairs={{0,2},{2,0},{1,3},{3,1},{4,6},{6,4},{5,7},{7,5},{8,10},{10,8},{9,1... | collective-permute-start | bytes 98312 | tf_op jit(solution)/shard_map/ppermute | solution.py:229
  56.9 2.4 %collective-permute-done.14.refs_8_ = f32[16,512]{1,0:T(8,128)S(1)} collective-permute-done((f32[16,512]{1,0:T(8,128)S(1)}, f32[16,512]{1,0:T(8,128)S(1)}, u32[]{:S(2)}, u32[]{:S(2)}) %collective-permute-start.14) | collective-permute-done | bytes 32800 | tf_op jit(solution)/shard_map/ppermute | solution.py:229
  59.4 2.3 %shard_map.71 = (f32[272,512]{1,0:T(8,128)S(1)}, f32[272,512]{1,0:T(8,128)S(1)}, bf16[1024,512]{1,0:T(8,128)(2,1)S(1)}, bf16[1024,512]{1,0:T(8,128)(2,1)S(1)}, f...) custom-call(s32[3]{0:T(128)S(1)} %pad_add_fusion.core.place, ...), custom_call_target="tpu_custom_call" | custom-call | flops 536870912 | bytes 8212492 | tf_op jit(solution)/shard_map/pallas_call | solution.py:216
  62.2 1.8 %shard_map.72 = (f32[272,512]{1,0:T(8,128)S(1)}, f32[272,512]{1,0:T(8,128)S(1)}, f32[272,512]{1,0:T(8,128)S(1)}, f32[272,512]{1,0:T(8,128)S(1)}) custom-call(bf16[1024,512]{1,0:T(8,128)(2,1)S(1)} %get-tuple-element.29.image, bf16[512,512]{1,0:T(8,128)(2,1)S(1)} %get-tuple-element.30.refs_0_.text, bf16[1024,512]{1,0:T(8,128)(2,1)S(1)} %get-tuple-element.36.high_ref, ...), custom_call_target="tpu_custom_call" | custom-call | flops 1610612736 | bytes 5980160 | tf_op jit(solution)/shard_map/pallas_call | solution.py:216
  64.3 1.6 %collective-permute-start.18 = (f16[272,512]{1,0:T(8,128)(2,1)S(1)}, f16[272,512]{1,0:T(8,128)(2,1)S(1)}, u32[]{:S(2)}, u32[]{:S(2)}) collective-permute-start(f16[272,512]{1,0:T(8,128)(2,1)S(1)} %convert_element_type.21), channel_id=1, source_target_pairs={{0,2},{2,0},{1,3},{3,1},{4,6},{6,4},{5,7},{7,5},{8,10},{10,8},{9,1... | collective-permute-start | bytes 835592 | tf_op jit(solution)/shard_map/ppermute | solution.py:229
  65.8 0.7 collective-permute-start.17
  66.6 6.3 %collective-permute-done.18 = f16[272,512]{1,0:T(8,128)(2,1)S(1)} collective-permute-done((f16[272,512]{1,0:T(8,128)(2,1)S(1)}, f16[272,512]{1,0:T(8,128)(2,1)S(1)}, u32[]{:S(2)}, u32[]{:S(2)}) %collective-permute-start.18) | collective-permute-done | bytes 278560 | tf_op jit(solution)/shard_map/ppermute | solution.py:229
  73.1 1.0 %collective-permute-done.17 = f16[272,512]{1,0:T(8,128)(2,1)S(1)} collective-permute-done((f16[272,512]{1,0:T(8,128)(2,1)S(1)}, f16[272,512]{1,0:T(8,128)(2,1)S(1)}, u32[]{:S(2)}, u32[]{:S(2)}) %collective-permute-start.17) | collective-permute-done | bytes 278560 | tf_op jit(solution)/shard_map/ppermute | solution.py:229
  74.5 2.1 %collective-permute-start.20 = (f16[144,512]{1,0:T(8,128)(2,1)S(1)}, f16[144,512]{1,0:T(8,128)(2,1)S(1)}, u32[]{:S(2)}, u32[]{:S(2)}) collective-permute-start(f16[144,512]{1,0:T(8,128)(2,1)S(1)} %get-tuple-element.50), channel_id=1, source_target_pairs={{0,8},{8,0},{1,9},{9,1},{2,10},{10,2},{3,11},{11,3},{4,12},{12,4},... | collective-permute-start | bytes 442376 | tf_op jit(solution)/shard_map/ppermute | solution.py:229
  76.7 3.8 %collective-permute-done.20 = f16[144,512]{1,0:T(8,128)(2,1)S(1)} collective-permute-done((f16[144,512]{1,0:T(8,128)(2,1)S(1)}, f16[144,512]{1,0:T(8,128)(2,1)S(1)}, u32[]{:S(2)}, u32[]{:S(2)}) %collective-permute-start.20) | collective-permute-done | bytes 147488 | tf_op jit(solution)/shard_map/ppermute | solution.py:229
  80.5 0.7 fusion
  81.3 3.8 %collective-permute-done.19 = f16[144,512]{1,0:T(8,128)(2,1)S(1)} collective-permute-done((f16[144,512]{1,0:T(8,128)(2,1)S(1)}, f16[144,512]{1,0:T(8,128)(2,1)S(1)}, u32[]{:S(2)}, u32[]{:S(2)}) %collective-permute-start.19) | collective-permute-done | bytes 147488 | tf_op jit(solution)/shard_map/ppermute | solution.py:229
  85.1 0.7 fusion.1
  (48 shorter events, 4.3 us)
Async XLA Ops:
  0.6 1.0 %copy-start = (bf16[128,1280]{1,0:T(8,128)(2,1)S(1)}, bf16[128,1280]{1,0:T(8,128)(2,1)}, u32[]{:S(2)}) copy-start(bf16[128,1280]{1,0:T(8,128)(2,1)} %teacher.2) | copy-start | bytes 983044
  1.6 0.9 %copy-start.2 = (bf16[128,512]{1,0:T(8,128)(2,1)S(1)}, bf16[128,512]{1,0:T(8,128)(2,1)}, u32[]{:S(2)}) copy-start(bf16[128,512]{1,0:T(8,128)(2,1)} %student.2) | copy-start | bytes 393220
  2.5 24.6 %collective-permute-start = (bf16[128,1792]{1,0:T(8,128)(2,1)S(1)}, bf16[128,1792]{1,0:T(8,128)(2,1)S(1)}, u32[]{:S(2)}, u32[]{:S(2)}) collective-permute-start(bf16[128,1792]{1,0:T(8,128)(2,1)S(1)} %shard_map.67.refs_0_), channel_id=1, source_target_pairs={{0,16},{16,0},{1,17},{17,1},{2,18},{18,2},{3,19},{19,3},{4,20},{20... | collective-permute-start | bytes 1376264 | tf_op jit(solution)/shard_map/ppermute | solution.py:229
  6.6 22.0 %collective-permute-start.1 = (bf16[128,1792]{1,0:T(8,128)(2,1)S(1)}, bf16[128,1792]{1,0:T(8,128)(2,1)S(1)}, u32[]{:S(2)}, u32[]{:S(2)}) collective-permute-start(bf16[128,1792]{1,0:T(8,128)(2,1)S(1)} %shard_map.67.refs_0_), channel_id=1, source_target_pairs={{0,4},{4,0},{1,5},{5,1},{2,6},{6,2},{3,7},{7,3},{8,12},{12,8},{9,1... | collective-permute-start | bytes 1376264 | tf_op jit(solution)/shard_map/ppermute | solution.py:229
  8.2 1.0 %copy-start.1 = (bf16[128,1280]{1,0:T(8,128)(2,1)S(1)}, bf16[128,1280]{1,0:T(8,128)(2,1)}, u32[]{:S(2)}) copy-start(bf16[128,1280]{1,0:T(8,128)(2,1)} %teacher.3) | copy-start | bytes 983044
  9.1 0.9 %copy-start.3 = (bf16[128,512]{1,0:T(8,128)(2,1)S(1)}, bf16[128,512]{1,0:T(8,128)(2,1)}, u32[]{:S(2)}) copy-start(bf16[128,512]{1,0:T(8,128)(2,1)} %student.3) | copy-start | bytes 393220
  10.1 20.4 %collective-permute-start.7 = (bf16[128,1792]{1,0:T(8,128)(2,1)S(1)}, bf16[128,1792]{1,0:T(8,128)(2,1)S(1)}, u32[]{:S(2)}, u32[]{:S(2)}) collective-permute-start(bf16[128,1792]{1,0:T(8,128)(2,1)S(1)} %shard_map.68.refs_8_), channel_id=1, source_target_pairs={{0,8},{8,0},{1,9},{9,1},{2,10},{10,2},{3,11},{11,3},{4,12},{12,4},... | collective-permute-start | bytes 1376264 | tf_op jit(solution)/shard_map/ppermute | solution.py:229
  11.7 18.8 %collective-permute-start.8 = (bf16[128,1792]{1,0:T(8,128)(2,1)S(1)}, bf16[128,1792]{1,0:T(8,128)(2,1)S(1)}, u32[]{:S(2)}, u32[]{:S(2)}) collective-permute-start(bf16[128,1792]{1,0:T(8,128)(2,1)S(1)} %shard_map.68.refs_8_), channel_id=1, source_target_pairs={{0,2},{2,0},{1,3},{3,1},{4,6},{6,4},{5,7},{7,5},{8,10},{10,8},{9,1... | collective-permute-start | bytes 1376264 | tf_op jit(solution)/shard_map/ppermute | solution.py:229
  27.1 11.6 %collective-permute-start.2 = (bf16[128,1792]{1,0:T(8,128)(2,1)S(1)}, bf16[128,1792]{1,0:T(8,128)(2,1)S(1)}, u32[]{:S(2)}, u32[]{:S(2)}) collective-permute-start(bf16[128,1792]{1,0:T(8,128)(2,1)S(1)} %collective-permute-done.refs_1_), channel_id=1, source_target_pairs={{0,4},{4,0},{1,5},{5,1},{2,6},{6,2},{3,7},{7,3},{8,12},{12,8},{9,1... | collective-permute-start | bytes 1376264 | tf_op jit(solution)/shard_map/ppermute | solution.py:229
  28.7 10.2 %collective-permute-start.3 = (bf16[128,1792]{1,0:T(8,128)(2,1)S(1)}, bf16[128,1792]{1,0:T(8,128)(2,1)}, u32[]{:S(2)}, u32[]{:S(2)}) collective-permute-start(bf16[128,1792]{1,0:T(8,128)(2,1)S(1)} %shard_map.67.refs_0_), channel_id=1, source_target_pairs={{0,1},{1,0},{2,3},{3,2},{4,5},{5,4},{6,7},{7,6},{8,9},{9,8},{10,11... | collective-permute-start | bytes 1376264 | tf_op jit(solution)/shard_map/ppermute | solution.py:229
  28.7 10.2 %collective-permute-start.4 = (bf16[128,1792]{1,0:T(8,128)(2,1)S(1)}, bf16[128,1792]{1,0:T(8,128)(2,1)}, u32[]{:S(2)}, u32[]{:S(2)}) collective-permute-start(bf16[128,1792]{1,0:T(8,128)(2,1)S(1)} %collective-permute-done.refs_1_), channel_id=1, source_target_pairs={{0,1},{1,0},{2,3},{3,2},{4,5},{5,4},{6,7},{7,6},{8,9},{9,8},{10,11... | collective-permute-start | bytes 1376264 | tf_op jit(solution)/shard_map/ppermute | solution.py:229
  30.5 8.3 %collective-permute-start.5 = (bf16[128,1792]{1,0:T(8,128)(2,1)S(1)}, bf16[128,1792]{1,0:T(8,128)(2,1)}, u32[]{:S(2)}, u32[]{:S(2)}) collective-permute-start(bf16[128,1792]{1,0:T(8,128)(2,1)S(1)} %collective-permute-done.1.refs_2_), channel_id=1, source_target_pairs={{0,1},{1,0},{2,3},{3,2},{4,5},{5,4},{6,7},{7,6},{8,9},{9,8},{10,11... | collective-permute-start | bytes 1376264 | tf_op jit(solution)/shard_map/ppermute | solution.py:229
  30.5 13.0 %collective-permute-start.9 = (bf16[128,1792]{1,0:T(8,128)(2,1)S(1)}, bf16[128,1792]{1,0:T(8,128)(2,1)}, u32[]{:S(2)}, u32[]{:S(2)}) collective-permute-start(bf16[128,1792]{1,0:T(8,128)(2,1)S(1)} %collective-permute-done.7.refs_9_), channel_id=1, source_target_pairs={{0,2},{2,0},{1,3},{3,1},{4,6},{6,4},{5,7},{7,5},{8,10},{10,8},{9,1... | collective-permute-start | bytes 1376264 | tf_op jit(solution)/shard_map/ppermute | solution.py:229
  38.7 4.8 %collective-permute-start.6 = (bf16[128,1792]{1,0:T(8,128)(2,1)S(1)}, bf16[128,1792]{1,0:T(8,128)(2,1)}, u32[]{:S(2)}, u32[]{:S(2)}) collective-permute-start(bf16[128,1792]{1,0:T(8,128)(2,1)S(1)} %collective-permute-done.2.refs_3_), channel_id=1, source_target_pairs={{0,1},{1,0},{2,3},{3,2},{4,5},{5,4},{6,7},{7,6},{8,9},{9,8},{10,11... | collective-permute-start | bytes 1376264 | tf_op jit(solution)/shard_map/ppermute | solution.py:229
  48.0 1.2 %collective-permute-start.10 = (f32[8,1024]{1,0:T(8,128)S(1)}, f32[8,1024]{1,0:T(8,128)S(1)}, u32[]{:S(2)}, u32[]{:S(2)}) collective-permute-start(f32[8,1024]{1,0:T(8,128)S(1)} %get-tuple-element.34), channel_id=1, source_target_pairs={{0,1},{1,0},{2,3},{3,2},{4,5},{5,4},{6,7},{7,6},{8,9},{9,8},{10,11... | collective-permute-start | bytes 98312 | tf_op jit(solution)/shard_map/ppermute | solution.py:229
  49.3 4.8 %collective-permute-start.11 = (f32[8,1024]{1,0:T(8,128)S(1)}, f32[8,1024]{1,0:T(8,128)S(1)}, u32[]{:S(2)}, u32[]{:S(2)}) collective-permute-start(f32[8,1024]{1,0:T(8,128)S(1)} %add.48.refs_3_), channel_id=1, source_target_pairs={{0,16},{16,0},{1,17},{17,1},{2,18},{18,2},{3,19},{19,3},{4,20},{20... | collective-permute-start | bytes 98312 | tf_op jit(solution)/shard_map/ppermute | solution.py:229
  51.2 4.3 %collective-permute-start.13 = (f32[8,512]{1,0:T(8,128)S(1)}, f32[8,512]{1,0:T(8,128)S(1)}, u32[]{:S(2)}, u32[]{:S(2)}) collective-permute-start(f32[8,512]{1,0:T(8,128)S(1)} %shard_map.70.refs_6_), channel_id=1, source_target_pairs={{0,8},{8,0},{1,9},{9,1},{2,10},{10,2},{3,11},{11,3},{4,12},{12,4},... | collective-permute-start | bytes 49160 | tf_op jit(solution)/shard_map/ppermute | solution.py:229
  54.1 5.2 %collective-permute-start.12 = (f32[16,1024]{1,0:T(8,128)S(1)}, f32[16,1024]{1,0:T(8,128)S(1)}, u32[]{:S(2)}, u32[]{:S(2)}) collective-permute-start(f32[16,1024]{1,0:T(8,128)S(1)} %pad_maximum_fusion.2), channel_id=1, source_target_pairs={{0,4},{4,0},{1,5},{5,1},{2,6},{6,2},{3,7},{7,3},{8,12},{12,8},{9,1... | collective-permute-start | bytes 196616 | tf_op jit(solution)/shard_map/ppermute | solution.py:229
  55.4 3.9 %collective-permute-start.14 = (f32[16,512]{1,0:T(8,128)S(1)}, f32[16,512]{1,0:T(8,128)S(1)}, u32[]{:S(2)}, u32[]{:S(2)}) collective-permute-start(f32[16,512]{1,0:T(8,128)S(1)} %pad_maximum_fusion.3), channel_id=1, source_target_pairs={{0,2},{2,0},{1,3},{3,1},{4,6},{6,4},{5,7},{7,5},{8,10},{10,8},{9,1... | collective-permute-start | bytes 98312 | tf_op jit(solution)/shard_map/ppermute | solution.py:229
  61.7 2.4 %collective-permute-start.16 = (f32[272,512]{1,0:T(8,128)S(1)}, f32[272,512]{1,0:T(8,128)S(1)}, u32[]{:S(2)}, u32[]{:S(2)}) collective-permute-start(f32[272,512]{1,0:T(8,128)S(1)} %get-tuple-element.44), channel_id=1, source_target_pairs={{0,1},{1,0},{2,3},{3,2},{4,5},{5,4},{6,7},{7,6},{8,9},{9,8},{10,11... | collective-permute-start | bytes 1671176 | tf_op jit(solution)/shard_map/ppermute | solution.py:229
  61.7 4.8 %collective-permute-start.15 = (f32[272,512]{1,0:T(8,128)S(1)}, f32[272,512]{1,0:T(8,128)S(1)}, u32[]{:S(2)}, u32[]{:S(2)}) collective-permute-start(f32[272,512]{1,0:T(8,128)S(1)} %get-tuple-element.42), channel_id=1, source_target_pairs={{0,1},{1,0},{2,3},{3,2},{4,5},{5,4},{6,7},{7,6},{8,9},{9,8},{10,11... | collective-permute-start | bytes 1671176 | tf_op jit(solution)/shard_map/ppermute | solution.py:229
  64.3 8.7 %collective-permute-start.18 = (f16[272,512]{1,0:T(8,128)(2,1)S(1)}, f16[272,512]{1,0:T(8,128)(2,1)S(1)}, u32[]{:S(2)}, u32[]{:S(2)}) collective-permute-start(f16[272,512]{1,0:T(8,128)(2,1)S(1)} %convert_element_type.21), channel_id=1, source_target_pairs={{0,2},{2,0},{1,3},{3,1},{4,6},{6,4},{5,7},{7,5},{8,10},{10,8},{9,1... | collective-permute-start | bytes 835592 | tf_op jit(solution)/shard_map/ppermute | solution.py:229
  65.8 8.4 %collective-permute-start.17 = (f16[272,512]{1,0:T(8,128)(2,1)S(1)}, f16[272,512]{1,0:T(8,128)(2,1)S(1)}, u32[]{:S(2)}, u32[]{:S(2)}) collective-permute-start(f16[272,512]{1,0:T(8,128)(2,1)S(1)} %add_convert_fusion), channel_id=1, source_target_pairs={{0,4},{4,0},{1,5},{5,1},{2,6},{6,2},{3,7},{7,3},{8,12},{12,8},{9,1... | collective-permute-start | bytes 835592 | tf_op jit(solution)/shard_map/ppermute | solution.py:229
  74.5 6.0 %collective-permute-start.20 = (f16[144,512]{1,0:T(8,128)(2,1)S(1)}, f16[144,512]{1,0:T(8,128)(2,1)S(1)}, u32[]{:S(2)}, u32[]{:S(2)}) collective-permute-start(f16[144,512]{1,0:T(8,128)(2,1)S(1)} %get-tuple-element.50), channel_id=1, source_target_pairs={{0,8},{8,0},{1,9},{9,1},{2,10},{10,2},{3,11},{11,3},{4,12},{12,4},... | collective-permute-start | bytes 442376 | tf_op jit(solution)/shard_map/ppermute | solution.py:229
  76.6 8.5 %collective-permute-start.19 = (f16[144,512]{1,0:T(8,128)(2,1)S(1)}, f16[144,512]{1,0:T(8,128)(2,1)S(1)}, u32[]{:S(2)}, u32[]{:S(2)}) collective-permute-start(f16[144,512]{1,0:T(8,128)(2,1)S(1)} %get-tuple-element.49), channel_id=1, source_target_pairs={{0,16},{16,0},{1,17},{17,1},{2,18},{18,2},{3,19},{19,3},{4,20},{20... | collective-permute-start | bytes 442376 | tf_op jit(solution)/shard_map/ppermute | solution.py:229

commit v9 on v8

--- a/solution.py
+++ b/solution.py
@@ -45,14 +45,22 @@
     return items[0]
 
 
-def stats_kernel(nr, nc, b, tw, scale_t, scale_s, core, *refs):
-    images, texts, refs = refs[:nr], refs[nr : nr + nc], refs[nr + nc :]
+def stats_kernel(image_forms, text_forms, b, tw, scale_t, scale_s, core, *refs):
+    nr, nc = len(image_forms), len(text_forms)
+    images, texts = [], []
+    for forms, blocks in ((image_forms, images), (text_forms, texts)):
+        for form in forms:
+            blocks.append(refs[:form])
+            refs = refs[form:]
     tl_ref, sl_ref, row_ref, swap_ref, peak_ref, image_s, text_s, text_t = refs
     for p in range(nc):
-        text_t[block(p, b), :] = texts[p][:, :tw]
-        text_s[block(p, b), :] = texts[p][:, tw:]
+        for k, x in enumerate(texts[p]):
+            rows = slice(p * b + k * x.shape[0], p * b + (k + 1) * x.shape[0])
+            text_t[rows, :] = x[:, :tw]
+            text_s[rows, :] = x[:, tw:]
     for p in range(nr):
-        image_s[block(p, b), :] = images[p][:, tw:]
+        for k, x in enumerate(images[p]):
+            image_s[p * b + k * x.shape[0] : p * b + (k + 1) * x.shape[0], :] = x[:, tw:]
     largest = jnp.max(jnp.abs(text_s[...].astype(F32)), 0, keepdims=True)
     width = largest.shape[1]
 
@@ -66,7 +74,7 @@
     peak_t = peak_s = None
     for p in range(0, nr, step):
         rows = slice(p * b, p * b + count)
-        tl = matmul(jnp.concatenate([x[:, :tw] for x in images[p : p + step]], 0), text_t[...], 1, 1) * (scale_t * LOG2E)
+        tl = matmul(jnp.concatenate([x[:, :tw] for pieces in images[p : p + step] for x in pieces], 0), text_t[...], 1, 1) * (scale_t * LOG2E)
         sl = matmul(image_s[rows, :], text_s[...], 1, 1) * (scale_s * LOG2E)
         tl_ref[rows, :] = tl
         sl_ref[rows, :] = sl
@@ -237,12 +245,20 @@
     return lax.optimization_barrier(groups)
 
 
-def gather(bits, x):
-    blocks = [x]
-    for k, bit in enumerate(bits):
-        own = together(x, blocks[2])[0] if k > 1 else x
-        blocks = blocks + [swap((bit,), y) for y in [own] + blocks[1:]]
-    return blocks
+def gather(image_bits, text_bits, image, text):
+    groups = [(image_bits, image), (text_bits, text)]
+    own = [[swap(bits[k : k + 1], x) for k in range(1, len(bits))] for bits, x in groups]
+    half = image.shape[0] // 2
+    first = [swap(bits[:1], x[:half]) for bits, x in groups]
+    second = [swap(bits[:1], together(x[half:], own[0][-1])[0]) for bits, x in groups]
+    result = []
+    for n, (bits, x) in enumerate(groups):
+        blocks = [[x], [first[n], second[n]]]
+        for k in range(1, len(bits)):
+            ways = [[swap(bits[k : k + 1], together(y, own[n][k - 1])[0]) for y in pieces] for pieces in blocks[1:]]
+            blocks = blocks + [[own[n][k - 1]]] + ways
+        result.append(blocks)
+    return result
 
 
 def exchange(bits, x):
@@ -266,18 +282,19 @@
     pair, others = image_bits[-1:], image_bits[:-1]
     (image,) = call(join_kernel, [((b, tw + sw), BF16)], [teacher_image, student_image])
     (text,) = call(join_kernel, [((b, tw + sw), BF16)], [teacher_text, student_text])
-    images, texts = gather(image_bits, image), gather(text_bits, text)
+    images, texts = gather(image_bits, text_bits, image, text)
+    forms = [[len(x) for x in blocks] for blocks in (images, texts)]
     place = jnp.stack([lax.axis_index(x) for x in (pair, image_bits, text_bits)]).astype(jnp.int32)
     tl, sl, rows, rows_swapped, peaks, image, text = call(
-        functools.partial(stats_kernel, nr, nc, b, tw, tw**-0.5, sw**-0.5),
+        functools.partial(stats_kernel, *forms, b, tw, tw**-0.5, sw**-0.5),
         [((r, c), F32), ((r, c), F32), ((LINES, r), F32), ((LINES, r), F32), ((LINES, c), F32), ((r, sw), BF16), ((c, sw), BF16)],
-        [place] + images + texts, [((c, tw), BF16)], 2 * r * c * (tw + sw), 4 * r * c,
+        [place] + [x for pieces in images + texts for x in pieces], [((c, tw), BF16)], 2 * r * c * (tw + sw), 4 * r * c,
     )
     other = swap(pair, rows_swapped)
     (cols,) = call(
         functools.partial(column_kernel, 2 * b), [((LINES, c), F32)], [tl, sl, peaks, image], (), 0, 2 * r * c
     )
-    row_parts, col_parts = exchange(others, rows + other), exchange(text_bits, cols)
+    row_parts, col_parts = exchange(others, together(rows, cols)[0] + other), exchange(text_bits, cols)
     pairs = b << (len(image_bits) + len(text_bits))
     row, extra = ((1, sw), F32), ((EXTRA, sw), F32)
     near_shape, keep_shape = ((r // 4 + EXTRA, sw), F32), ((c // 2 + EXTRA, sw), F32)

time: 88.5 us -> 92.5 us (1.045)
  starting transfers between devices: 22.6 us -> 27.1 us
  waiting for transfers between devices: 46.3 us -> 42.5 us
  local copies, waits for them, and re-layouts: 3.75 us -> 7.06 us
    ppermute x21 -> x27, starting transfers between devices: 22.6 us -> 27.1 us  [swap(): return lax.ppermute(x, bits, perm)]
    ppermute x21 -> x27, waiting for transfers between devices: 46.3 us -> 42.5 us  [swap(): return lax.ppermute(x, bits, perm)]
    unnamed x8 -> x16, local copies, waits for them, and re-layouts: 3.75 us -> 7 us
  transfers between devices with their start and end apart: 21 -> 27, of which waited for: 12 -> 11; matrix products, arithmetic and copies ran while one was open for 1% -> 1% of each run, Pallas kernels for 4% -> 4%
where the time goes in v9:
time: 92.5 us; the launch traced here: 92.2 us
  waiting for transfers between devices  42.5 us (46%)
  starting transfers between devices  27.1 us (29%)
  Pallas kernels  9.93 us (11%)
  local copies, waits for them, and re-layouts  7.06 us (8%)
  other arithmetic  2.99 us (3%)
  between operations  2.63 us (3%)
    ppermute x27, waiting for transfers between devices, swap(): return lax.ppermute(x, bits, perm)  42.5 us
    ppermute x27, starting transfers between devices, swap(): return lax.ppermute(x, bits, perm)  27.1 us
    pallas_call x6, Pallas kernels, call(): pl.pallas_call(kernel, out_shape=shapes, in_specs=[SMEM if x.dtype == jnp...  9.93 us
    unnamed x16, local copies, waits for them, and re-layouts  7 us
  transfers between devices with their start and end apart: 27, of which 11 were waited for; matrix products, arithmetic and copies ran while one was open for 1% of the time, Pallas kernels for 4%

profile of v9, /device:TPU:0, one launch (start us, length us, event | category | flops | bytes accessed | tf_op | source)
XLA Modules:
  0.0 92.2 jit_solution(8040729230025020596)
XLA Ops:
  0.6 1.0 %copy-done = bf16[128,1280]{1,0:T(8,128)(2,1)S(1)} copy-done((bf16[128,1280]{1,0:T(8,128)(2,1)S(1)}, bf16[128,1280]{1,0:T(8,128)(2,1)}, u32[]{:S(2)}) %copy-start) | copy-done | bytes 327704
  1.6 0.9 copy-done.2
  3.1 2.6 %collective-permute-start.3 = (bf16[128,1792]{1,0:T(8,128)(2,1)S(1)}, bf16[128,1792]{1,0:T(8,128)(2,1)S(1)}, u32[]{:S(2)}, u32[]{:S(2)}) collective-permute-start(bf16[128,1792]{1,0:T(8,128)(2,1)S(1)} %shard_map.67.refs_0_), channel_id=1, source_target_pairs={{0,4},{4,0},{1,5},{5,1},{2,6},{6,2},{3,7},{7,3},{8,12},{12,8},{9,1... | collective-permute-start | bytes 1376264 | tf_op jit(solution)/shard_map/ppermute | solution.py:237
  5.7 2.7 %collective-permute-start = (bf16[64,1792]{1,0:T(8,128)(2,1)S(1)}, bf16[64,1792]{1,0:T(8,128)(2,1)S(1)}, u32[]{:S(2)}, u32[]{:S(2)}) collective-permute-start(bf16[64,1792]{1,0:T(8,128)(2,1)S(1)} %get-tuple-element.78), channel_id=1, source_target_pairs={{0,16},{16,0},{1,17},{17,1},{2,18},{18,2},{3,19},{19,3},{4,20},{20... | collective-permute-start | bytes 688136 | tf_op jit(solution)/shard_map/ppermute | solution.py:237
  8.3 1.0 %copy-done.1 = bf16[128,1280]{1,0:T(8,128)(2,1)S(1)} copy-done((bf16[128,1280]{1,0:T(8,128)(2,1)S(1)}, bf16[128,1280]{1,0:T(8,128)(2,1)}, u32[]{:S(2)}) %copy-start.1) | copy-done | bytes 327704
  9.3 0.9 copy-done.3
  10.3 1.6 %collective-permute-start.13 = (bf16[128,1792]{1,0:T(8,128)(2,1)S(1)}, bf16[128,1792]{1,0:T(8,128)(2,1)S(1)}, u32[]{:S(2)}, u32[]{:S(2)}) collective-permute-start(bf16[128,1792]{1,0:T(8,128)(2,1)S(1)} %shard_map.68.refs_12_), channel_id=1, source_target_pairs={{0,2},{2,0},{1,3},{3,1},{4,6},{6,4},{5,7},{7,5},{8,10},{10,8},{9,1... | collective-permute-start | bytes 1376264 | tf_op jit(solution)/shard_map/ppermute | solution.py:237
  12.2 1.6 %collective-permute-start.11 = (bf16[64,1792]{1,0:T(8,128)(2,1)S(1)}, bf16[64,1792]{1,0:T(8,128)(2,1)S(1)}, u32[]{:S(2)}, u32[]{:S(2)}) collective-permute-start(bf16[64,1792]{1,0:T(8,128)(2,1)S(1)} %get-tuple-element.76), channel_id=1, source_target_pairs={{0,8},{8,0},{1,9},{9,1},{2,10},{10,2},{3,11},{11,3},{4,12},{12,4},... | collective-permute-start | bytes 688136 | tf_op jit(solution)/shard_map/ppermute | solution.py:237
  13.8 11.1 %collective-permute-done.refs_1_ = bf16[64,1792]{1,0:T(8,128)(2,1)S(1)} collective-permute-done((bf16[64,1792]{1,0:T(8,128)(2,1)S(1)}, bf16[64,1792]{1,0:T(8,128)(2,1)S(1)}, u32[]{:S(2)}, u32[]{:S(2)}) %collective-permute-start) | collective-permute-done | bytes 229408 | tf_op jit(solution)/shard_map/ppermute | solution.py:237
  25.4 3.8 %collective-permute-done.2.refs_2_ = bf16[64,1792]{1,0:T(8,128)(2,1)S(1)} collective-permute-done((bf16[64,1792]{1,0:T(8,128)(2,1)S(1)}, bf16[64,1792]{1,0:T(8,128)(2,1)S(1)}, u32[]{:S(2)}, u32[]{:S(2)}) %collective-permute-start.2) | collective-permute-done | bytes 229408 | tf_op jit(solution)/shard_map/ppermute | solution.py:237
  29.6 1.6 %collective-permute-start.14 = (bf16[64,1792]{1,0:T(8,128)(2,1)S(1)}, bf16[64,1792]{1,0:T(8,128)(2,1)S(1)}, u32[]{:S(2)}, u32[]{:S(2)}) collective-permute-start(bf16[64,1792]{1,0:T(8,128)(2,1)S(1)} %collective-permute-done.11.refs_13_), channel_id=1, source_target_pairs={{0,2},{2,0},{1,3},{3,1},{4,6},{6,4},{5,7},{7,5},{8,10},{10,8},{9,1... | collective-permute-start | bytes 688136 | tf_op jit(solution)/shard_map/ppermute | solution.py:237
  31.4 2.7 %collective-permute-done.12.refs_14_ = bf16[64,1792]{1,0:T(8,128)(2,1)} collective-permute-done((bf16[64,1792]{1,0:T(8,128)(2,1)S(1)}, bf16[64,1792]{1,0:T(8,128)(2,1)}, u32[]{:S(2)}, u32[]{:S(2)}) %collective-permute-start.12) | collective-permute-done | bytes 229408 | tf_op jit(solution)/shard_map/ppermute | solution.py:237
  34.1 1.9 %collective-permute-done.5.refs_5_ = bf16[64,1792]{1,0:T(8,128)(2,1)} collective-permute-done((bf16[64,1792]{1,0:T(8,128)(2,1)S(1)}, bf16[64,1792]{1,0:T(8,128)(2,1)}, u32[]{:S(2)}, u32[]{:S(2)}) %collective-permute-start.5) | collective-permute-done | bytes 229408 | tf_op jit(solution)/shard_map/ppermute | solution.py:237
  36.7 1.5 %collective-permute-start.15 = (bf16[64,1792]{1,0:T(8,128)(2,1)}, bf16[64,1792]{1,0:T(8,128)(2,1)}, u32[]{:S(2)}, u32[]{:S(2)}) collective-permute-start(bf16[64,1792]{1,0:T(8,128)(2,1)} %collective-permute-done.12.refs_14_), channel_id=1, source_target_pairs={{0,2},{2,0},{1,3},{3,1},{4,6},{6,4},{5,7},{7,5},{8,10},{10,8},{9,1... | collective-permute-start | bytes 688136 | tf_op jit(solution)/shard_map/ppermute | solution.py:237
  39.3 5.8 %collective-permute-done.15.refs_17_ = bf16[64,1792]{1,0:T(8,128)(2,1)} collective-permute-done((bf16[64,1792]{1,0:T(8,128)(2,1)}, bf16[64,1792]{1,0:T(8,128)(2,1)}, u32[]{:S(2)}, u32[]{:S(2)}) %collective-permute-start.15) | collective-permute-done | bytes 229408 | tf_op jit(solution)/shard_map/ppermute | solution.py:237
  45.1 0.9 %copy-done.5 = bf16[64,1792]{1,0:T(8,128)(2,1)S(1)} copy-done((bf16[64,1792]{1,0:T(8,128)(2,1)S(1)}, bf16[64,1792]{1,0:T(8,128)(2,1)}, u32[]{:S(2)}) %copy-start.5) | copy-done | bytes 229400
  46.0 0.9 %copy-done.7 = bf16[64,1792]{1,0:T(8,128)(2,1)S(1)} copy-done((bf16[64,1792]{1,0:T(8,128)(2,1)S(1)}, bf16[64,1792]{1,0:T(8,128)(2,1)}, u32[]{:S(2)}) %copy-start.7) | copy-done | bytes 229400
  47.0 4.4 %shard_map.69 = (f32[1024,512]{1,0:T(8,128)S(1)}, f32[1024,512]{1,0:T(8,128)S(1)}, f32[8,1024]{1,0:T(8,128)S(1)}, f32[8,1024]{1,0:T(8,128)S(1)}, f32[8,512]{1,0:...) custom-call(s32[3]{0:T(128)S(1)} %pad_add_fusion.core.place, ...), custom_call_target="tpu_custom_call" | custom-call | flops 1879048192 | bytes 11354124 | tf_op jit(solution)/shard_map/pallas_call | solution.py:224
  51.4 1.4 %shard_map.70.refs_6_ = f32[8,512]{1,0:T(8,128)S(1)} custom-call(f32[1024,512]{1,0:T(8,128)S(1)} %get-tuple-element.52.tl_ref.refs_1_, f32[1024,512]{1,0:T(8,128)S(1)} %get-tuple-element.53.sl_ref.refs_2_, f32[8,512]{1,0:T(8,128)S(1)} %get-tuple-element.55.peaks, bf16[1024,512]{1,0:T(8,128)(2,1)S(1)} %get-tuple-element.50.image), custom_call_target="tpu_custom_call" | custom-call | bytes 5275648 | tf_op jit(solution)/shard_map/pallas_call | solution.py:224
  52.9 4.8 %collective-permute-start.19 = (f32[8,512]{1,0:T(8,128)S(1)}, f32[8,512]{1,0:T(8,128)S(1)}, u32[]{:S(2)}, u32[]{:S(2)}) collective-permute-start(f32[8,512]{1,0:T(8,128)S(1)} %shard_map.70.refs_6_), channel_id=1, source_target_pairs={{0,8},{8,0},{1,9},{9,1},{2,10},{10,2},{3,11},{11,3},{4,12},{12,4},... | collective-permute-start | bytes 49160 | tf_op jit(solution)/shard_map/ppermute | solution.py:237
  58.4 0.9 collective-permute-done.19.refs_7_
  59.4 1.5 %collective-permute-start.20 = (f32[16,512]{1,0:T(8,128)S(1)}, f32[16,512]{1,0:T(8,128)S(1)}, u32[]{:S(2)}, u32[]{:S(2)}) collective-permute-start(f32[16,512]{1,0:T(8,128)S(1)} %pad_maximum_fusion.3), channel_id=1, source_target_pairs={{0,2},{2,0},{1,3},{3,1},{4,6},{6,4},{5,7},{7,5},{8,10},{10,8},{9,1... | collective-permute-start | bytes 98312 | tf_op jit(solution)/shard_map/ppermute | solution.py:237
  60.8 2.4 %collective-permute-done.20.refs_8_ = f32[16,512]{1,0:T(8,128)S(1)} collective-permute-done((f32[16,512]{1,0:T(8,128)S(1)}, f32[16,512]{1,0:T(8,128)S(1)}, u32[]{:S(2)}, u32[]{:S(2)}) %collective-permute-start.20) | collective-permute-done | bytes 32800 | tf_op jit(solution)/shard_map/ppermute | solution.py:237
  63.3 2.3 %shard_map.71 = (f32[272,512]{1,0:T(8,128)S(1)}, f32[272,512]{1,0:T(8,128)S(1)}, bf16[1024,512]{1,0:T(8,128)(2,1)S(1)}, bf16[1024,512]{1,0:T(8,128)(2,1)S(1)}, f...) custom-call(s32[3]{0:T(128)S(1)} %pad_add_fusion.core.place, ...), custom_call_target="tpu_custom_call" | custom-call | flops 536870912 | bytes 8212492 | tf_op jit(solution)/shard_map/pallas_call | solution.py:224
  66.2 1.8 %shard_map.72 = (f32[272,512]{1,0:T(8,128)S(1)}, f32[272,512]{1,0:T(8,128)S(1)}, f32[272,512]{1,0:T(8,128)S(1)}, f32[272,512]{1,0:T(8,128)S(1)}) custom-call(bf16[1024,512]{1,0:T(8,128)(2,1)S(1)} %get-tuple-element.50.image, bf16[512,512]{1,0:T(8,128)(2,1)S(1)} %get-tuple-element.51.refs_0_.text, bf16[1024,512]{1,0:T(8,128)(2,1)S(1)} %get-tuple-element.58.high_ref, ...), custom_call_target="tpu_custom_call" | custom-call | flops 1610612736 | bytes 5980160 | tf_op jit(solution)/shard_map/pallas_call | solution.py:224
  68.2 1.6 %collective-permute-start.24 = (f16[272,512]{1,0:T(8,128)(2,1)S(1)}, f16[272,512]{1,0:T(8,128)(2,1)S(1)}, u32[]{:S(2)}, u32[]{:S(2)}) collective-permute-start(f16[272,512]{1,0:T(8,128)(2,1)S(1)} %convert_element_type.21), channel_id=1, source_target_pairs={{0,2},{2,0},{1,3},{3,1},{4,6},{6,4},{5,7},{7,5},{8,10},{10,8},{9,1... | collective-permute-start | bytes 835592 | tf_op jit(solution)/shard_map/ppermute | solution.py:237
  70.3 6.6 %collective-permute-done.24 = f16[272,512]{1,0:T(8,128)(2,1)S(1)} collective-permute-done((f16[272,512]{1,0:T(8,128)(2,1)S(1)}, f16[272,512]{1,0:T(8,128)(2,1)S(1)}, u32[]{:S(2)}, u32[]{:S(2)}) %collective-permute-start.24) | collective-permute-done | bytes 278560 | tf_op jit(solution)/shard_map/ppermute | solution.py:237
  77.0 1.0 %collective-permute-done.23 = f16[272,512]{1,0:T(8,128)(2,1)S(1)} collective-permute-done((f16[272,512]{1,0:T(8,128)(2,1)S(1)}, f16[272,512]{1,0:T(8,128)(2,1)S(1)}, u32[]{:S(2)}, u32[]{:S(2)}) %collective-permute-start.23) | collective-permute-done | bytes 278560 | tf_op jit(solution)/shard_map/ppermute | solution.py:237
  78.4 2.1 %collective-permute-start.26 = (f16[144,512]{1,0:T(8,128)(2,1)S(1)}, f16[144,512]{1,0:T(8,128)(2,1)S(1)}, u32[]{:S(2)}, u32[]{:S(2)}) collective-permute-start(f16[144,512]{1,0:T(8,128)(2,1)S(1)} %get-tuple-element.72), channel_id=1, source_target_pairs={{0,8},{8,0},{1,9},{9,1},{2,10},{10,2},{3,11},{11,3},{4,12},{12,4},... | collective-permute-start | bytes 442376 | tf_op jit(solution)/shard_map/ppermute | solution.py:237
  80.5 1.6 %collective-permute-start.25 = (f16[144,512]{1,0:T(8,128)(2,1)S(1)}, f16[144,512]{1,0:T(8,128)(2,1)S(1)}, u32[]{:S(2)}, u32[]{:S(2)}) collective-permute-start(f16[144,512]{1,0:T(8,128)(2,1)S(1)} %get-tuple-element.71), channel_id=1, source_target_pairs={{0,16},{16,0},{1,17},{17,1},{2,18},{18,2},{3,19},{19,3},{4,20},{20... | collective-permute-start | bytes 442376 | tf_op jit(solution)/shard_map/ppermute | solution.py:237
  82.0 2.5 %collective-permute-done.26 = f16[144,512]{1,0:T(8,128)(2,1)S(1)} collective-permute-done((f16[144,512]{1,0:T(8,128)(2,1)S(1)}, f16[144,512]{1,0:T(8,128)(2,1)S(1)}, u32[]{:S(2)}, u32[]{:S(2)}) %collective-permute-start.26) | collective-permute-done | bytes 147488 | tf_op jit(solution)/shard_map/ppermute | solution.py:237
  85.3 3.6 %collective-permute-done.25 = f16[144,512]{1,0:T(8,128)(2,1)S(1)} collective-permute-done((f16[144,512]{1,0:T(8,128)(2,1)S(1)}, f16[144,512]{1,0:T(8,128)(2,1)S(1)}, u32[]{:S(2)}, u32[]{:S(2)}) %collective-permute-start.25) | collective-permute-done | bytes 147488 | tf_op jit(solution)/shard_map/ppermute | solution.py:237
  (70 shorter events, 8.7 us)
Async XLA Ops:
  0.6 1.0 %copy-start = (bf16[128,1280]{1,0:T(8,128)(2,1)S(1)}, bf16[128,1280]{1,0:T(8,128)(2,1)}, u32[]{:S(2)}) copy-start(bf16[128,1280]{1,0:T(8,128)(2,1)} %teacher.2) | copy-start | bytes 983044
  1.6 0.9 copy-start.2
  2.5 9.3 %collective-permute-start.1 = (bf16[128,1792]{1,0:T(8,128)(2,1)S(1)}, bf16[128,1792]{1,0:T(8,128)(2,1)S(1)}, u32[]{:S(2)}, u32[]{:S(2)}) collective-permute-start(bf16[128,1792]{1,0:T(8,128)(2,1)S(1)} %shard_map.67.refs_0_), channel_id=1, source_target_pairs={{0,1},{1,0},{2,3},{3,2},{4,5},{5,4},{6,7},{7,6},{8,9},{9,8},{10,11... | collective-permute-start | bytes 1376264 | tf_op jit(solution)/shard_map/ppermute | solution.py:237
  3.1 21.9 %collective-permute-start.3 = (bf16[128,1792]{1,0:T(8,128)(2,1)S(1)}, bf16[128,1792]{1,0:T(8,128)(2,1)S(1)}, u32[]{:S(2)}, u32[]{:S(2)}) collective-permute-start(bf16[128,1792]{1,0:T(8,128)(2,1)S(1)} %shard_map.67.refs_0_), channel_id=1, source_target_pairs={{0,4},{4,0},{1,5},{5,1},{2,6},{6,2},{3,7},{7,3},{8,12},{12,8},{9,1... | collective-permute-start | bytes 1376264 | tf_op jit(solution)/shard_map/ppermute | solution.py:237
  5.7 19.2 %collective-permute-start = (bf16[64,1792]{1,0:T(8,128)(2,1)S(1)}, bf16[64,1792]{1,0:T(8,128)(2,1)S(1)}, u32[]{:S(2)}, u32[]{:S(2)}) collective-permute-start(bf16[64,1792]{1,0:T(8,128)(2,1)S(1)} %get-tuple-element.78), channel_id=1, source_target_pairs={{0,16},{16,0},{1,17},{17,1},{2,18},{18,2},{3,19},{19,3},{4,20},{20... | collective-permute-start | bytes 688136 | tf_op jit(solution)/shard_map/ppermute | solution.py:237
  8.3 1.0 %copy-start.1 = (bf16[128,1280]{1,0:T(8,128)(2,1)S(1)}, bf16[128,1280]{1,0:T(8,128)(2,1)}, u32[]{:S(2)}) copy-start(bf16[128,1280]{1,0:T(8,128)(2,1)} %teacher.3) | copy-start | bytes 983044
  10.3 19.4 %collective-permute-start.13 = (bf16[128,1792]{1,0:T(8,128)(2,1)S(1)}, bf16[128,1792]{1,0:T(8,128)(2,1)S(1)}, u32[]{:S(2)}, u32[]{:S(2)}) collective-permute-start(bf16[128,1792]{1,0:T(8,128)(2,1)S(1)} %shard_map.68.refs_12_), channel_id=1, source_target_pairs={{0,2},{2,0},{1,3},{3,1},{4,6},{6,4},{5,7},{7,5},{8,10},{10,8},{9,1... | collective-permute-start | bytes 1376264 | tf_op jit(solution)/shard_map/ppermute | solution.py:237
  11.8 17.4 %collective-permute-start.2 = (bf16[64,1792]{1,0:T(8,128)(2,1)S(1)}, bf16[64,1792]{1,0:T(8,128)(2,1)S(1)}, u32[]{:S(2)}, u32[]{:S(2)}) collective-permute-start(bf16[64,1792]{1,0:T(8,128)(2,1)S(1)} %get-tuple-element.39), channel_id=1, source_target_pairs={{0,16},{16,0},{1,17},{17,1},{2,18},{18,2},{3,19},{19,3},{4,20},{20... | collective-permute-start | bytes 688136 | tf_op jit(solution)/shard_map/ppermute | solution.py:237
  12.2 17.5 %collective-permute-start.11 = (bf16[64,1792]{1,0:T(8,128)(2,1)S(1)}, bf16[64,1792]{1,0:T(8,128)(2,1)S(1)}, u32[]{:S(2)}, u32[]{:S(2)}) collective-permute-start(bf16[64,1792]{1,0:T(8,128)(2,1)S(1)} %get-tuple-element.76), channel_id=1, source_target_pairs={{0,8},{8,0},{1,9},{9,1},{2,10},{10,2},{3,11},{11,3},{4,12},{12,4},... | collective-permute-start | bytes 688136 | tf_op jit(solution)/shard_map/ppermute | solution.py:237
  24.9 6.3 %collective-permute-start.4 = (bf16[64,1792]{1,0:T(8,128)(2,1)S(1)}, bf16[64,1792]{1,0:T(8,128)(2,1)}, u32[]{:S(2)}, u32[]{:S(2)}) collective-permute-start(bf16[64,1792]{1,0:T(8,128)(2,1)S(1)} %collective-permute-done.refs_1_), channel_id=1, source_target_pairs={{0,4},{4,0},{1,5},{5,1},{2,6},{6,2},{3,7},{7,3},{8,12},{12,8},{9,1... | collective-permute-start | bytes 688136 | tf_op jit(solution)/shard_map/ppermute | solution.py:237
  25.1 9.0 %collective-permute-start.12 = (bf16[64,1792]{1,0:T(8,128)(2,1)S(1)}, bf16[64,1792]{1,0:T(8,128)(2,1)}, u32[]{:S(2)}, u32[]{:S(2)}) collective-permute-start(bf16[64,1792]{1,0:T(8,128)(2,1)S(1)} %get-tuple-element.47), channel_id=1, source_target_pairs={{0,8},{8,0},{1,9},{9,1},{2,10},{10,2},{3,11},{11,3},{4,12},{12,4},... | collective-permute-start | bytes 688136 | tf_op jit(solution)/shard_map/ppermute | solution.py:237
  29.2 6.9 %collective-permute-start.5 = (bf16[64,1792]{1,0:T(8,128)(2,1)S(1)}, bf16[64,1792]{1,0:T(8,128)(2,1)}, u32[]{:S(2)}, u32[]{:S(2)}) collective-permute-start(bf16[64,1792]{1,0:T(8,128)(2,1)S(1)} %collective-permute-done.2.refs_2_), channel_id=1, source_target_pairs={{0,4},{4,0},{1,5},{5,1},{2,6},{6,2},{3,7},{7,3},{8,12},{12,8},{9,1... | collective-permute-start | bytes 688136 | tf_op jit(solution)/shard_map/ppermute | solution.py:237
  29.6 6.4 %collective-permute-start.6 = (bf16[64,1792]{1,0:T(8,128)(2,1)S(1)}, bf16[64,1792]{1,0:T(8,128)(2,1)S(1)}, u32[]{:S(2)}, u32[]{:S(2)}) collective-permute-start(bf16[64,1792]{1,0:T(8,128)(2,1)S(1)} %collective-permute-done.refs_1_), channel_id=1, source_target_pairs={{0,1},{1,0},{2,3},{3,2},{4,5},{5,4},{6,7},{7,6},{8,9},{9,8},{10,11... | collective-permute-start | bytes 688136 | tf_op jit(solution)/shard_map/ppermute | solution.py:237
  29.6 8.6 %collective-permute-start.14 = (bf16[64,1792]{1,0:T(8,128)(2,1)S(1)}, bf16[64,1792]{1,0:T(8,128)(2,1)S(1)}, u32[]{:S(2)}, u32[]{:S(2)}) collective-permute-start(bf16[64,1792]{1,0:T(8,128)(2,1)S(1)} %collective-permute-done.11.refs_13_), channel_id=1, source_target_pairs={{0,2},{2,0},{1,3},{3,1},{4,6},{6,4},{5,7},{7,5},{8,10},{10,8},{9,1... | collective-permute-start | bytes 688136 | tf_op jit(solution)/shard_map/ppermute | solution.py:237
  31.3 13.8 %collective-permute-start.8 = (bf16[128,1792]{1,0:T(8,128)(2,1)S(1)}, bf16[128,1792]{1,0:T(8,128)(2,1)S(1)}, u32[]{:S(2)}, u32[]{:S(2)}) collective-permute-start(bf16[128,1792]{1,0:T(8,128)(2,1)S(1)} %collective-permute-done.3.refs_3_), channel_id=1, source_target_pairs={{0,1},{1,0},{2,3},{3,2},{4,5},{5,4},{6,7},{7,6},{8,9},{9,8},{10,11... | collective-permute-start | bytes 1376264 | tf_op jit(solution)/shard_map/ppermute | solution.py:237
  34.1 5.2 %collective-permute-start.7 = (bf16[64,1792]{1,0:T(8,128)(2,1)S(1)}, bf16[64,1792]{1,0:T(8,128)(2,1)}, u32[]{:S(2)}, u32[]{:S(2)}) collective-permute-start(bf16[64,1792]{1,0:T(8,128)(2,1)S(1)} %collective-permute-done.2.refs_2_), channel_id=1, source_target_pairs={{0,1},{1,0},{2,3},{3,2},{4,5},{5,4},{6,7},{7,6},{8,9},{9,8},{10,11... | collective-permute-start | bytes 688136 | tf_op jit(solution)/shard_map/ppermute | solution.py:237
  36.0 3.2 %collective-permute-start.9 = (bf16[64,1792]{1,0:T(8,128)(2,1)}, bf16[64,1792]{1,0:T(8,128)(2,1)}, u32[]{:S(2)}, u32[]{:S(2)}) collective-permute-start(bf16[64,1792]{1,0:T(8,128)(2,1)} %collective-permute-done.4.refs_4_), channel_id=1, source_target_pairs={{0,1},{1,0},{2,3},{3,2},{4,5},{5,4},{6,7},{7,6},{8,9},{9,8},{10,11... | collective-permute-start | bytes 688136 | tf_op jit(solution)/shard_map/ppermute | solution.py:237
  36.7 8.3 %collective-permute-start.15 = (bf16[64,1792]{1,0:T(8,128)(2,1)}, bf16[64,1792]{1,0:T(8,128)(2,1)}, u32[]{:S(2)}, u32[]{:S(2)}) collective-permute-start(bf16[64,1792]{1,0:T(8,128)(2,1)} %collective-permute-done.12.refs_14_), channel_id=1, source_target_pairs={{0,2},{2,0},{1,3},{3,1},{4,6},{6,4},{5,7},{7,5},{8,10},{10,8},{9,1... | collective-permute-start | bytes 688136 | tf_op jit(solution)/shard_map/ppermute | solution.py:237
  38.9 6.1 %collective-permute-start.10 = (bf16[64,1792]{1,0:T(8,128)(2,1)}, bf16[64,1792]{1,0:T(8,128)(2,1)}, u32[]{:S(2)}, u32[]{:S(2)}) collective-permute-start(bf16[64,1792]{1,0:T(8,128)(2,1)} %collective-permute-done.5.refs_5_), channel_id=1, source_target_pairs={{0,1},{1,0},{2,3},{3,2},{4,5},{5,4},{6,7},{7,6},{8,9},{9,8},{10,11... | collective-permute-start | bytes 688136 | tf_op jit(solution)/shard_map/ppermute | solution.py:237
  45.1 0.9 %copy-start.5 = (bf16[64,1792]{1,0:T(8,128)(2,1)S(1)}, bf16[64,1792]{1,0:T(8,128)(2,1)}, u32[]{:S(2)}) copy-start(bf16[64,1792]{1,0:T(8,128)(2,1)} %copy-done.4) | copy-start | bytes 688132
  46.0 0.9 %copy-start.7 = (bf16[64,1792]{1,0:T(8,128)(2,1)S(1)}, bf16[64,1792]{1,0:T(8,128)(2,1)}, u32[]{:S(2)}) copy-start(bf16[64,1792]{1,0:T(8,128)(2,1)} %copy-done.6) | copy-start | bytes 688132
  51.3 1.4 %collective-permute-start.16 = (f32[8,1024]{1,0:T(8,128)S(1)}, f32[8,1024]{1,0:T(8,128)S(1)}, u32[]{:S(2)}, u32[]{:S(2)}) collective-permute-start(f32[8,1024]{1,0:T(8,128)S(1)} %get-tuple-element.57), channel_id=1, source_target_pairs={{0,1},{1,0},{2,3},{3,2},{4,5},{5,4},{6,7},{7,6},{8,9},{9,8},{10,11... | collective-permute-start | bytes 98312 | tf_op jit(solution)/shard_map/ppermute | solution.py:237
  52.8 4.9 %collective-permute-start.17 = (f32[8,1024]{1,0:T(8,128)S(1)}, f32[8,1024]{1,0:T(8,128)S(1)}, u32[]{:S(2)}, u32[]{:S(2)}) collective-permute-start(f32[8,1024]{1,0:T(8,128)S(1)} %add.48.refs_3_), channel_id=1, source_target_pairs={{0,16},{16,0},{1,17},{17,1},{2,18},{18,2},{3,19},{19,3},{4,20},{20... | collective-permute-start | bytes 98312 | tf_op jit(solution)/shard_map/ppermute | solution.py:237
  52.9 6.5 %collective-permute-start.19 = (f32[8,512]{1,0:T(8,128)S(1)}, f32[8,512]{1,0:T(8,128)S(1)}, u32[]{:S(2)}, u32[]{:S(2)}) collective-permute-start(f32[8,512]{1,0:T(8,128)S(1)} %shard_map.70.refs_6_), channel_id=1, source_target_pairs={{0,8},{8,0},{1,9},{9,1},{2,10},{10,2},{3,11},{11,3},{4,12},{12,4},... | collective-permute-start | bytes 49160 | tf_op jit(solution)/shard_map/ppermute | solution.py:237
  57.7 5.6 %collective-permute-start.18 = (f32[16,1024]{1,0:T(8,128)S(1)}, f32[16,1024]{1,0:T(8,128)S(1)}, u32[]{:S(2)}, u32[]{:S(2)}) collective-permute-start(f32[16,1024]{1,0:T(8,128)S(1)} %pad_maximum_fusion.2), channel_id=1, source_target_pairs={{0,4},{4,0},{1,5},{5,1},{2,6},{6,2},{3,7},{7,3},{8,12},{12,8},{9,1... | collective-permute-start | bytes 196616 | tf_op jit(solution)/shard_map/ppermute | solution.py:237
  59.4 3.9 %collective-permute-start.20 = (f32[16,512]{1,0:T(8,128)S(1)}, f32[16,512]{1,0:T(8,128)S(1)}, u32[]{:S(2)}, u32[]{:S(2)}) collective-permute-start(f32[16,512]{1,0:T(8,128)S(1)} %pad_maximum_fusion.3), channel_id=1, source_target_pairs={{0,2},{2,0},{1,3},{3,1},{4,6},{6,4},{5,7},{7,5},{8,10},{10,8},{9,1... | collective-permute-start | bytes 98312 | tf_op jit(solution)/shard_map/ppermute | solution.py:237
  65.6 2.4 %collective-permute-start.22 = (f32[272,512]{1,0:T(8,128)S(1)}, f32[272,512]{1,0:T(8,128)S(1)}, u32[]{:S(2)}, u32[]{:S(2)}) collective-permute-start(f32[272,512]{1,0:T(8,128)S(1)} %get-tuple-element.66), channel_id=1, source_target_pairs={{0,1},{1,0},{2,3},{3,2},{4,5},{5,4},{6,7},{7,6},{8,9},{9,8},{10,11... | collective-permute-start | bytes 1671176 | tf_op jit(solution)/shard_map/ppermute | solution.py:237
  65.7 4.5 %collective-permute-start.21 = (f32[272,512]{1,0:T(8,128)S(1)}, f32[272,512]{1,0:T(8,128)S(1)}, u32[]{:S(2)}, u32[]{:S(2)}) collective-permute-start(f32[272,512]{1,0:T(8,128)S(1)} %get-tuple-element.64), channel_id=1, source_target_pairs={{0,1},{1,0},{2,3},{3,2},{4,5},{5,4},{6,7},{7,6},{8,9},{9,8},{10,11... | collective-permute-start | bytes 1671176 | tf_op jit(solution)/shard_map/ppermute | solution.py:237
  68.2 8.7 %collective-permute-start.24 = (f16[272,512]{1,0:T(8,128)(2,1)S(1)}, f16[272,512]{1,0:T(8,128)(2,1)S(1)}, u32[]{:S(2)}, u32[]{:S(2)}) collective-permute-start(f16[272,512]{1,0:T(8,128)(2,1)S(1)} %convert_element_type.21), channel_id=1, source_target_pairs={{0,2},{2,0},{1,3},{3,1},{4,6},{6,4},{5,7},{7,5},{8,10},{10,8},{9,1... | collective-permute-start | bytes 835592 | tf_op jit(solution)/shard_map/ppermute | solution.py:237
  69.7 8.4 %collective-permute-start.23 = (f16[272,512]{1,0:T(8,128)(2,1)S(1)}, f16[272,512]{1,0:T(8,128)(2,1)S(1)}, u32[]{:S(2)}, u32[]{:S(2)}) collective-permute-start(f16[272,512]{1,0:T(8,128)(2,1)S(1)} %add_convert_fusion), channel_id=1, source_target_pairs={{0,4},{4,0},{1,5},{5,1},{2,6},{6,2},{3,7},{7,3},{8,12},{12,8},{9,1... | collective-permute-start | bytes 835592 | tf_op jit(solution)/shard_map/ppermute | solution.py:237
  78.4 6.1 %collective-permute-start.26 = (f16[144,512]{1,0:T(8,128)(2,1)S(1)}, f16[144,512]{1,0:T(8,128)(2,1)S(1)}, u32[]{:S(2)}, u32[]{:S(2)}) collective-permute-start(f16[144,512]{1,0:T(8,128)(2,1)S(1)} %get-tuple-element.72), channel_id=1, source_target_pairs={{0,8},{8,0},{1,9},{9,1},{2,10},{10,2},{3,11},{11,3},{4,12},{12,4},... | collective-permute-start | bytes 442376 | tf_op jit(solution)/shard_map/ppermute | solution.py:237
  80.5 8.5 %collective-permute-start.25 = (f16[144,512]{1,0:T(8,128)(2,1)S(1)}, f16[144,512]{1,0:T(8,128)(2,1)S(1)}, u32[]{:S(2)}, u32[]{:S(2)}) collective-permute-start(f16[144,512]{1,0:T(8,128)(2,1)S(1)} %get-tuple-element.71), channel_id=1, source_target_pairs={{0,16},{16,0},{1,17},{17,1},{2,18},{18,2},{3,19},{19,3},{4,20},{20... | collective-permute-start | bytes 442376 | tf_op jit(solution)/shard_map/ppermute | solution.py:237
  (3 other events, 2.3 us)

commit v10 on v8

--- a/solution.py
+++ b/solution.py
@@ -45,14 +45,25 @@
     return items[0]
 
 
-def stats_kernel(nr, nc, b, tw, scale_t, scale_s, core, *refs):
-    images, texts, refs = refs[:nr], refs[nr : nr + nc], refs[nr + nc :]
+def views(refs, forms, tw):
+    teachers, students = [], []
+    for form in forms:
+        teachers.append(refs[0].at[:, :tw] if form == 1 else refs[0])
+        students.append(refs[0].at[:, tw:] if form == 1 else refs[1])
+        refs = refs[form:]
+    return teachers, students, refs
+
+
+def stats_kernel(image_forms, text_forms, b, tw, scale_t, scale_s, core, *refs):
+    nr, nc = len(image_forms), len(text_forms)
+    ti, si, refs = views(refs, image_forms, tw)
+    tt, st, refs = views(refs, text_forms, tw)
     tl_ref, sl_ref, row_ref, swap_ref, peak_ref, image_s, text_s, text_t = refs
     for p in range(nc):
-        text_t[block(p, b), :] = texts[p][:, :tw]
-        text_s[block(p, b), :] = texts[p][:, tw:]
+        text_t[block(p, b), :] = tt[p][...]
+        text_s[block(p, b), :] = st[p][...]
     for p in range(nr):
-        image_s[block(p, b), :] = images[p][:, tw:]
+        image_s[block(p, b), :] = si[p][...]
     largest = jnp.max(jnp.abs(text_s[...].astype(F32)), 0, keepdims=True)
     width = largest.shape[1]
 
@@ -66,7 +77,7 @@
     peak_t = peak_s = None
     for p in range(0, nr, step):
         rows = slice(p * b, p * b + count)
-        tl = matmul(jnp.concatenate([x[:, :tw] for x in images[p : p + step]], 0), text_t[...], 1, 1) * (scale_t * LOG2E)
+        tl = matmul(jnp.concatenate([x[...] for x in ti[p : p + step]], 0), text_t[...], 1, 1) * (scale_t * LOG2E)
         sl = matmul(image_s[rows, :], text_s[...], 1, 1) * (scale_s * LOG2E)
         tl_ref[rows, :] = tl
         sl_ref[rows, :] = sl
@@ -237,11 +248,18 @@
     return lax.optimization_barrier(groups)
 
 
-def gather(bits, x):
-    blocks = [x]
+def gather(bits, both, apart=None, gates=(None, None)):
+    blocks = [(both,)]
     for k, bit in enumerate(bits):
-        own = together(x, blocks[2])[0] if k > 1 else x
-        blocks = blocks + [swap((bit,), y) for y in [own] + blocks[1:]]
+        own = apart if k == 0 and apart else (both,)
+        if k > 1:
+            own = together(own, blocks[2])[0]
+        if k == 1 and gates[0] is not None:
+            own = together(own, gates[0])[0]
+        ways = blocks[1:]
+        if k and gates[1] is not None:
+            ways = together(ways, gates[1])[0]
+        blocks = blocks + [tuple(swap((bit,), y) for y in parts) for parts in [own] + list(ways)]
     return blocks
 
 
@@ -266,12 +284,14 @@
     pair, others = image_bits[-1:], image_bits[:-1]
     (image,) = call(join_kernel, [((b, tw + sw), BF16)], [teacher_image, student_image])
     (text,) = call(join_kernel, [((b, tw + sw), BF16)], [teacher_text, student_text])
-    images, texts = gather(image_bits, image), gather(text_bits, text)
+    texts = gather(text_bits, text)
+    images = gather(image_bits, image, None, (text, texts[1:3]))
+    forms = [[len(x) for x in blocks] for blocks in (images, texts)]
     place = jnp.stack([lax.axis_index(x) for x in (pair, image_bits, text_bits)]).astype(jnp.int32)
     tl, sl, rows, rows_swapped, peaks, image, text = call(
-        functools.partial(stats_kernel, nr, nc, b, tw, tw**-0.5, sw**-0.5),
+        functools.partial(stats_kernel, *forms, b, tw, tw**-0.5, sw**-0.5),
         [((r, c), F32), ((r, c), F32), ((LINES, r), F32), ((LINES, r), F32), ((LINES, c), F32), ((r, sw), BF16), ((c, sw), BF16)],
-        [place] + images + texts, [((c, tw), BF16)], 2 * r * c * (tw + sw), 4 * r * c,
+        [place] + [x for parts in images + texts for x in parts], [((c, tw), BF16)], 2 * r * c * (tw + sw), 4 * r * c,
     )
     other = swap(pair, rows_swapped)
     (cols,) = call(

time: 88.5 us -> 90 us (1.017)
  starting transfers between devices: 22.6 us -> 24.7 us
    ppermute x21, starting transfers between devices: 22.6 us -> 24.7 us  [swap(): return lax.ppermute(x, bits, perm)]
  transfers between devices with their start and end apart: 21 -> 21, of which waited for: 12 -> 11; matrix products, arithmetic and copies ran while one was open for 1% -> 1% of each run, Pallas kernels for 4% -> 4%
where the time goes in v10:
time: 90 us; the launch traced here: 89.7 us
  waiting for transfers between devices  45.7 us (51%)
  starting transfers between devices  24.7 us (27%)
  Pallas kernels  10 us (11%)
  local copies, waits for them, and re-layouts  3.75 us (4%)
  other arithmetic  2.99 us (3%)
  between operations  2.6 us (3%)
    ppermute x21, waiting for transfers between devices, swap(): return lax.ppermute(x, bits, perm)  45.7 us
    ppermute x21, starting transfers between devices, swap(): return lax.ppermute(x, bits, perm)  24.7 us
    pallas_call x6, Pallas kernels, call(): pl.pallas_call(kernel, out_shape=shapes, in_specs=[SMEM if x.dtype == jnp...  10 us
    unnamed x8, local copies, waits for them, and re-layouts  3.75 us
  transfers between devices with their start and end apart: 21, of which 11 were waited for; matrix products, arithmetic and copies ran while one was open for 1% of the time, Pallas kernels for 4%

profile of v10, /device:TPU:0, one launch (start us, length us, event | category | flops | bytes accessed | tf_op | source)
XLA Modules:
  0.0 89.7 jit_solution(9212734925446472341)
XLA Ops:
  0.6 1.0 %copy-done = bf16[128,1280]{1,0:T(8,128)(2,1)S(1)} copy-done((bf16[128,1280]{1,0:T(8,128)(2,1)S(1)}, bf16[128,1280]{1,0:T(8,128)(2,1)}, u32[]{:S(2)}) %copy-start) | copy-done | bytes 327704
  1.6 0.9 %copy-done.2 = bf16[128,512]{1,0:T(8,128)(2,1)S(1)} copy-done((bf16[128,512]{1,0:T(8,128)(2,1)S(1)}, bf16[128,512]{1,0:T(8,128)(2,1)}, u32[]{:S(2)}) %copy-start.2) | copy-done | bytes 131096
  2.5 3.1 %collective-permute-start.2 = (bf16[128,1792]{1,0:T(8,128)(2,1)S(1)}, bf16[128,1792]{1,0:T(8,128)(2,1)S(1)}, u32[]{:S(2)}, u32[]{:S(2)}) collective-permute-start(bf16[128,1792]{1,0:T(8,128)(2,1)S(1)} %shard_map.68.refs_8_), channel_id=1, source_target_pairs={{0,8},{8,0},{1,9},{9,1},{2,10},{10,2},{3,11},{11,3},{4,12},{12,4},... | collective-permute-start | bytes 1376264 | tf_op jit(solution)/shard_map/ppermute | solution.py:240
  5.6 1.0 %copy-done.1 = bf16[128,1280]{1,0:T(8,128)(2,1)S(1)} copy-done((bf16[128,1280]{1,0:T(8,128)(2,1)S(1)}, bf16[128,1280]{1,0:T(8,128)(2,1)}, u32[]{:S(2)}) %copy-start.1) | copy-done | bytes 327704
  6.6 0.9 %copy-done.3 = bf16[128,512]{1,0:T(8,128)(2,1)S(1)} copy-done((bf16[128,512]{1,0:T(8,128)(2,1)S(1)}, bf16[128,512]{1,0:T(8,128)(2,1)}, u32[]{:S(2)}) %copy-start.3) | copy-done | bytes 131096
  7.5 2.7 %collective-permute-start = (bf16[128,1792]{1,0:T(8,128)(2,1)S(1)}, bf16[128,1792]{1,0:T(8,128)(2,1)S(1)}, u32[]{:S(2)}, u32[]{:S(2)}) collective-permute-start(bf16[128,1792]{1,0:T(8,128)(2,1)S(1)} %shard_map.67.refs_0_), channel_id=1, source_target_pairs={{0,16},{16,0},{1,17},{17,1},{2,18},{18,2},{3,19},{19,3},{4,20},{20... | collective-permute-start | bytes 1376264 | tf_op jit(solution)/shard_map/ppermute | solution.py:240
  10.2 1.5 %collective-permute-start.3 = (bf16[128,1792]{1,0:T(8,128)(2,1)S(1)}, bf16[128,1792]{1,0:T(8,128)(2,1)S(1)}, u32[]{:S(2)}, u32[]{:S(2)}) collective-permute-start(bf16[128,1792]{1,0:T(8,128)(2,1)S(1)} %shard_map.68.refs_8_), channel_id=1, source_target_pairs={{0,2},{2,0},{1,3},{3,1},{4,6},{6,4},{5,7},{7,5},{8,10},{10,8},{9,1... | collective-permute-start | bytes 1376264 | tf_op jit(solution)/shard_map/ppermute | solution.py:240
  11.7 1.5 %collective-permute-start.1 = (bf16[128,1792]{1,0:T(8,128)(2,1)S(1)}, bf16[128,1792]{1,0:T(8,128)(2,1)S(1)}, u32[]{:S(2)}, u32[]{:S(2)}) collective-permute-start(bf16[128,1792]{1,0:T(8,128)(2,1)S(1)} %shard_map.67.refs_0_), channel_id=1, source_target_pairs={{0,4},{4,0},{1,5},{5,1},{2,6},{6,2},{3,7},{7,3},{8,12},{12,8},{9,1... | collective-permute-start | bytes 1376264 | tf_op jit(solution)/shard_map/ppermute | solution.py:240
  13.2 10.7 %collective-permute-done.2.refs_9_ = bf16[128,1792]{1,0:T(8,128)(2,1)S(1)} collective-permute-done((bf16[128,1792]{1,0:T(8,128)(2,1)S(1)}, bf16[128,1792]{1,0:T(8,128)(2,1)S(1)}, u32[]{:S(2)}, u32[]{:S(2)}) %collective-permute-start.2) | collective-permute-done | bytes 458784 | tf_op jit(solution)/shard_map/ppermute | solution.py:240
  23.9 6.5 %collective-permute-done.refs_1_ = bf16[128,1792]{1,0:T(8,128)(2,1)S(1)} collective-permute-done((bf16[128,1792]{1,0:T(8,128)(2,1)S(1)}, bf16[128,1792]{1,0:T(8,128)(2,1)S(1)}, u32[]{:S(2)}, u32[]{:S(2)}) %collective-permute-start) | collective-permute-done | bytes 458784 | tf_op jit(solution)/shard_map/ppermute | solution.py:240
  30.4 1.5 %collective-permute-start.4 = (bf16[128,1792]{1,0:T(8,128)(2,1)S(1)}, bf16[128,1792]{1,0:T(8,128)(2,1)S(1)}, u32[]{:S(2)}, u32[]{:S(2)}) collective-permute-start(bf16[128,1792]{1,0:T(8,128)(2,1)S(1)} %collective-permute-done.refs_1_), channel_id=1, source_target_pairs={{0,4},{4,0},{1,5},{5,1},{2,6},{6,2},{3,7},{7,3},{8,12},{12,8},{9,1... | collective-permute-start | bytes 1376264 | tf_op jit(solution)/shard_map/ppermute | solution.py:240
  31.9 1.5 %collective-permute-start.9 = (bf16[128,1792]{1,0:T(8,128)(2,1)S(1)}, bf16[128,1792]{1,0:T(8,128)(2,1)}, u32[]{:S(2)}, u32[]{:S(2)}) collective-permute-start(bf16[128,1792]{1,0:T(8,128)(2,1)S(1)} %collective-permute-done.2.refs_9_), channel_id=1, source_target_pairs={{0,2},{2,0},{1,3},{3,1},{4,6},{6,4},{5,7},{7,5},{8,10},{10,8},{9,1... | collective-permute-start | bytes 1376264 | tf_op jit(solution)/shard_map/ppermute | solution.py:240
  33.4 8.1 %collective-permute-done.4.refs_3_ = bf16[128,1792]{1,0:T(8,128)(2,1)S(1)} collective-permute-done((bf16[128,1792]{1,0:T(8,128)(2,1)S(1)}, bf16[128,1792]{1,0:T(8,128)(2,1)S(1)}, u32[]{:S(2)}, u32[]{:S(2)}) %collective-permute-start.4) | collective-permute-done | bytes 458784 | tf_op jit(solution)/shard_map/ppermute | solution.py:240
  42.1 2.9 %collective-permute-done.9.refs_11_ = bf16[128,1792]{1,0:T(8,128)(2,1)} collective-permute-done((bf16[128,1792]{1,0:T(8,128)(2,1)S(1)}, bf16[128,1792]{1,0:T(8,128)(2,1)}, u32[]{:S(2)}, u32[]{:S(2)}) %collective-permute-start.9) | collective-permute-done | bytes 458784 | tf_op jit(solution)/shard_map/ppermute | solution.py:240
  44.9 4.5 %shard_map.69 = (f32[1024,512]{1,0:T(8,128)S(1)}, f32[1024,512]{1,0:T(8,128)S(1)}, f32[8,1024]{1,0:T(8,128)S(1)}, f32[8,1024]{1,0:T(8,128)S(1)}, f32[8,512]{1,0:...) custom-call(s32[3]{0:T(128)S(1)} %pad_add_fusion.core.place, ...), custom_call_target="tpu_custom_call" | custom-call | flops 1879048192 | bytes 11354124 | tf_op jit(solution)/shard_map/pallas_call | solution.py:227
  49.5 1.2 %collective-permute-done.10 = f32[8,1024]{1,0:T(8,128)S(1)} collective-permute-done((f32[8,1024]{1,0:T(8,128)S(1)}, f32[8,1024]{1,0:T(8,128)S(1)}, u32[]{:S(2)}, u32[]{:S(2)}) %collective-permute-start.10) | collective-permute-done | bytes 32800 | tf_op jit(solution)/shard_map/ppermute | solution.py:240
  50.7 1.4 %shard_map.70.refs_6_ = f32[8,512]{1,0:T(8,128)S(1)} custom-call(f32[1024,512]{1,0:T(8,128)S(1)} %get-tuple-element.41.tl_ref.refs_1_, f32[1024,512]{1,0:T(8,128)S(1)} %get-tuple-element.42.sl_ref.refs_2_, f32[8,512]{1,0:T(8,128)S(1)} %get-tuple-element.45.peaks, bf16[1024,512]{1,0:T(8,128)(2,1)S(1)} %get-tuple-element.39.image), custom_call_target="tpu_custom_call" | custom-call | bytes 5275648 | tf_op jit(solution)/shard_map/pallas_call | solution.py:227
  52.1 3.1 %collective-permute-start.13 = (f32[8,512]{1,0:T(8,128)S(1)}, f32[8,512]{1,0:T(8,128)S(1)}, u32[]{:S(2)}, u32[]{:S(2)}) collective-permute-start(f32[8,512]{1,0:T(8,128)S(1)} %shard_map.70.refs_6_), channel_id=1, source_target_pairs={{0,8},{8,0},{1,9},{9,1},{2,10},{10,2},{3,11},{11,3},{4,12},{12,4},... | collective-permute-start | bytes 49160 | tf_op jit(solution)/shard_map/ppermute | solution.py:240
  55.6 1.3 %collective-permute-start.12 = (f32[16,1024]{1,0:T(8,128)S(1)}, f32[16,1024]{1,0:T(8,128)S(1)}, u32[]{:S(2)}, u32[]{:S(2)}) collective-permute-start(f32[16,1024]{1,0:T(8,128)S(1)} %pad_maximum_fusion.2), channel_id=1, source_target_pairs={{0,4},{4,0},{1,5},{5,1},{2,6},{6,2},{3,7},{7,3},{8,12},{12,8},{9,1... | collective-permute-start | bytes 196616 | tf_op jit(solution)/shard_map/ppermute | solution.py:240
  56.9 1.5 %collective-permute-start.14 = (f32[16,512]{1,0:T(8,128)S(1)}, f32[16,512]{1,0:T(8,128)S(1)}, u32[]{:S(2)}, u32[]{:S(2)}) collective-permute-start(f32[16,512]{1,0:T(8,128)S(1)} %pad_maximum_fusion.3), channel_id=1, source_target_pairs={{0,2},{2,0},{1,3},{3,1},{4,6},{6,4},{5,7},{7,5},{8,10},{10,8},{9,1... | collective-permute-start | bytes 98312 | tf_op jit(solution)/shard_map/ppermute | solution.py:240
  58.4 2.4 %collective-permute-done.14.refs_8_ = f32[16,512]{1,0:T(8,128)S(1)} collective-permute-done((f32[16,512]{1,0:T(8,128)S(1)}, f32[16,512]{1,0:T(8,128)S(1)}, u32[]{:S(2)}, u32[]{:S(2)}) %collective-permute-start.14) | collective-permute-done | bytes 32800 | tf_op jit(solution)/shard_map/ppermute | solution.py:240
  60.8 2.3 %shard_map.71 = (f32[272,512]{1,0:T(8,128)S(1)}, f32[272,512]{1,0:T(8,128)S(1)}, bf16[1024,512]{1,0:T(8,128)(2,1)S(1)}, bf16[1024,512]{1,0:T(8,128)(2,1)S(1)}, f...) custom-call(s32[3]{0:T(128)S(1)} %pad_add_fusion.core.place, ...), custom_call_target="tpu_custom_call" | custom-call | flops 536870912 | bytes 8212492 | tf_op jit(solution)/shard_map/pallas_call | solution.py:227
  63.7 1.8 %shard_map.72 = (f32[272,512]{1,0:T(8,128)S(1)}, f32[272,512]{1,0:T(8,128)S(1)}, f32[272,512]{1,0:T(8,128)S(1)}, f32[272,512]{1,0:T(8,128)S(1)}) custom-call(bf16[1024,512]{1,0:T(8,128)(2,1)S(1)} %get-tuple-element.39.image, bf16[512,512]{1,0:T(8,128)(2,1)S(1)} %get-tuple-element.40.refs_0_.text, bf16[1024,512]{1,0:T(8,128)(2,1)S(1)} %get-tuple-element.46.high_ref, ...), custom_call_target="tpu_custom_call" | custom-call | flops 1610612736 | bytes 5980160 | tf_op jit(solution)/shard_map/pallas_call | solution.py:227
  65.7 1.6 %collective-permute-start.18 = (f16[272,512]{1,0:T(8,128)(2,1)S(1)}, f16[272,512]{1,0:T(8,128)(2,1)S(1)}, u32[]{:S(2)}, u32[]{:S(2)}) collective-permute-start(f16[272,512]{1,0:T(8,128)(2,1)S(1)} %convert_element_type.21), channel_id=1, source_target_pairs={{0,2},{2,0},{1,3},{3,1},{4,6},{6,4},{5,7},{7,5},{8,10},{10,8},{9,1... | collective-permute-start | bytes 835592 | tf_op jit(solution)/shard_map/ppermute | solution.py:240
  67.3 1.3 %collective-permute-start.17 = (f16[272,512]{1,0:T(8,128)(2,1)S(1)}, f16[272,512]{1,0:T(8,128)(2,1)S(1)}, u32[]{:S(2)}, u32[]{:S(2)}) collective-permute-start(f16[272,512]{1,0:T(8,128)(2,1)S(1)} %add_convert_fusion), channel_id=1, source_target_pairs={{0,4},{4,0},{1,5},{5,1},{2,6},{6,2},{3,7},{7,3},{8,12},{12,8},{9,1... | collective-permute-start | bytes 835592 | tf_op jit(solution)/shard_map/ppermute | solution.py:240
  68.7 5.7 %collective-permute-done.18 = f16[272,512]{1,0:T(8,128)(2,1)S(1)} collective-permute-done((f16[272,512]{1,0:T(8,128)(2,1)S(1)}, f16[272,512]{1,0:T(8,128)(2,1)S(1)}, u32[]{:S(2)}, u32[]{:S(2)}) %collective-permute-start.18) | collective-permute-done | bytes 278560 | tf_op jit(solution)/shard_map/ppermute | solution.py:240
  74.6 1.1 %collective-permute-done.17 = f16[272,512]{1,0:T(8,128)(2,1)S(1)} collective-permute-done((f16[272,512]{1,0:T(8,128)(2,1)S(1)}, f16[272,512]{1,0:T(8,128)(2,1)S(1)}, u32[]{:S(2)}, u32[]{:S(2)}) %collective-permute-start.17) | collective-permute-done | bytes 278560 | tf_op jit(solution)/shard_map/ppermute | solution.py:240
  75.9 2.1 %collective-permute-start.20 = (f16[144,512]{1,0:T(8,128)(2,1)S(1)}, f16[144,512]{1,0:T(8,128)(2,1)S(1)}, u32[]{:S(2)}, u32[]{:S(2)}) collective-permute-start(f16[144,512]{1,0:T(8,128)(2,1)S(1)} %get-tuple-element.60), channel_id=1, source_target_pairs={{0,8},{8,0},{1,9},{9,1},{2,10},{10,2},{3,11},{11,3},{4,12},{12,4},... | collective-permute-start | bytes 442376 | tf_op jit(solution)/shard_map/ppermute | solution.py:240
  78.0 0.9 %collective-permute-start.19 = (f16[144,512]{1,0:T(8,128)(2,1)S(1)}, f16[144,512]{1,0:T(8,128)(2,1)S(1)}, u32[]{:S(2)}, u32[]{:S(2)}) collective-permute-start(f16[144,512]{1,0:T(8,128)(2,1)S(1)} %get-tuple-element.59), channel_id=1, source_target_pairs={{0,16},{16,0},{1,17},{17,1},{2,18},{18,2},{3,19},{19,3},{4,20},{20... | collective-permute-start | bytes 442376 | tf_op jit(solution)/shard_map/ppermute | solution.py:240
  79.0 2.9 %collective-permute-done.20 = f16[144,512]{1,0:T(8,128)(2,1)S(1)} collective-permute-done((f16[144,512]{1,0:T(8,128)(2,1)S(1)}, f16[144,512]{1,0:T(8,128)(2,1)S(1)}, u32[]{:S(2)}, u32[]{:S(2)}) %collective-permute-start.20) | collective-permute-done | bytes 147488 | tf_op jit(solution)/shard_map/ppermute | solution.py:240
  82.6 3.9 %collective-permute-done.19 = f16[144,512]{1,0:T(8,128)(2,1)S(1)} collective-permute-done((f16[144,512]{1,0:T(8,128)(2,1)S(1)}, f16[144,512]{1,0:T(8,128)(2,1)S(1)}, u32[]{:S(2)}, u32[]{:S(2)}) %collective-permute-start.19) | collective-permute-done | bytes 147488 | tf_op jit(solution)/shard_map/ppermute | solution.py:240
  86.5 0.7 fusion.1
  (48 shorter events, 3.9 us)
Async XLA Ops:
  0.6 1.0 %copy-start = (bf16[128,1280]{1,0:T(8,128)(2,1)S(1)}, bf16[128,1280]{1,0:T(8,128)(2,1)}, u32[]{:S(2)}) copy-start(bf16[128,1280]{1,0:T(8,128)(2,1)} %teacher.3) | copy-start | bytes 983044
  1.6 0.9 %copy-start.2 = (bf16[128,512]{1,0:T(8,128)(2,1)S(1)}, bf16[128,512]{1,0:T(8,128)(2,1)}, u32[]{:S(2)}) copy-start(bf16[128,512]{1,0:T(8,128)(2,1)} %student.3) | copy-start | bytes 393220
  2.5 21.3 %collective-permute-start.2 = (bf16[128,1792]{1,0:T(8,128)(2,1)S(1)}, bf16[128,1792]{1,0:T(8,128)(2,1)S(1)}, u32[]{:S(2)}, u32[]{:S(2)}) collective-permute-start(bf16[128,1792]{1,0:T(8,128)(2,1)S(1)} %shard_map.68.refs_8_), channel_id=1, source_target_pairs={{0,8},{8,0},{1,9},{9,1},{2,10},{10,2},{3,11},{11,3},{4,12},{12,4},... | collective-permute-start | bytes 1376264 | tf_op jit(solution)/shard_map/ppermute | solution.py:240
  5.6 1.0 %copy-start.1 = (bf16[128,1280]{1,0:T(8,128)(2,1)S(1)}, bf16[128,1280]{1,0:T(8,128)(2,1)}, u32[]{:S(2)}) copy-start(bf16[128,1280]{1,0:T(8,128)(2,1)} %teacher.2) | copy-start | bytes 983044
  6.6 0.9 %copy-start.3 = (bf16[128,512]{1,0:T(8,128)(2,1)S(1)}, bf16[128,512]{1,0:T(8,128)(2,1)}, u32[]{:S(2)}) copy-start(bf16[128,512]{1,0:T(8,128)(2,1)} %student.2) | copy-start | bytes 393220
  7.5 22.8 %collective-permute-start = (bf16[128,1792]{1,0:T(8,128)(2,1)S(1)}, bf16[128,1792]{1,0:T(8,128)(2,1)S(1)}, u32[]{:S(2)}, u32[]{:S(2)}) collective-permute-start(bf16[128,1792]{1,0:T(8,128)(2,1)S(1)} %shard_map.67.refs_0_), channel_id=1, source_target_pairs={{0,16},{16,0},{1,17},{17,1},{2,18},{18,2},{3,19},{19,3},{4,20},{20... | collective-permute-start | bytes 1376264 | tf_op jit(solution)/shard_map/ppermute | solution.py:240
  10.2 20.2 %collective-permute-start.3 = (bf16[128,1792]{1,0:T(8,128)(2,1)S(1)}, bf16[128,1792]{1,0:T(8,128)(2,1)S(1)}, u32[]{:S(2)}, u32[]{:S(2)}) collective-permute-start(bf16[128,1792]{1,0:T(8,128)(2,1)S(1)} %shard_map.68.refs_8_), channel_id=1, source_target_pairs={{0,2},{2,0},{1,3},{3,1},{4,6},{6,4},{5,7},{7,5},{8,10},{10,8},{9,1... | collective-permute-start | bytes 1376264 | tf_op jit(solution)/shard_map/ppermute | solution.py:240
  11.7 20.2 %collective-permute-start.1 = (bf16[128,1792]{1,0:T(8,128)(2,1)S(1)}, bf16[128,1792]{1,0:T(8,128)(2,1)S(1)}, u32[]{:S(2)}, u32[]{:S(2)}) collective-permute-start(bf16[128,1792]{1,0:T(8,128)(2,1)S(1)} %shard_map.67.refs_0_), channel_id=1, source_target_pairs={{0,4},{4,0},{1,5},{5,1},{2,6},{6,2},{3,7},{7,3},{8,12},{12,8},{9,1... | collective-permute-start | bytes 1376264 | tf_op jit(solution)/shard_map/ppermute | solution.py:240
  30.4 11.1 %collective-permute-start.4 = (bf16[128,1792]{1,0:T(8,128)(2,1)S(1)}, bf16[128,1792]{1,0:T(8,128)(2,1)S(1)}, u32[]{:S(2)}, u32[]{:S(2)}) collective-permute-start(bf16[128,1792]{1,0:T(8,128)(2,1)S(1)} %collective-permute-done.refs_1_), channel_id=1, source_target_pairs={{0,4},{4,0},{1,5},{5,1},{2,6},{6,2},{3,7},{7,3},{8,12},{12,8},{9,1... | collective-permute-start | bytes 1376264 | tf_op jit(solution)/shard_map/ppermute | solution.py:240
  31.9 10.2 %collective-permute-start.5 = (bf16[128,1792]{1,0:T(8,128)(2,1)S(1)}, bf16[128,1792]{1,0:T(8,128)(2,1)}, u32[]{:S(2)}, u32[]{:S(2)}) collective-permute-start(bf16[128,1792]{1,0:T(8,128)(2,1)S(1)} %shard_map.67.refs_0_), channel_id=1, source_target_pairs={{0,1},{1,0},{2,3},{3,2},{4,5},{5,4},{6,7},{7,6},{8,9},{9,8},{10,11... | collective-permute-start | bytes 1376264 | tf_op jit(solution)/shard_map/ppermute | solution.py:240
  31.9 13.0 %collective-permute-start.9 = (bf16[128,1792]{1,0:T(8,128)(2,1)S(1)}, bf16[128,1792]{1,0:T(8,128)(2,1)}, u32[]{:S(2)}, u32[]{:S(2)}) collective-permute-start(bf16[128,1792]{1,0:T(8,128)(2,1)S(1)} %collective-permute-done.2.refs_9_), channel_id=1, source_target_pairs={{0,2},{2,0},{1,3},{3,1},{4,6},{6,4},{5,7},{7,5},{8,10},{10,8},{9,1... | collective-permute-start | bytes 1376264 | tf_op jit(solution)/shard_map/ppermute | solution.py:240
  41.5 3.5 %collective-permute-start.6 = (bf16[128,1792]{1,0:T(8,128)(2,1)S(1)}, bf16[128,1792]{1,0:T(8,128)(2,1)}, u32[]{:S(2)}, u32[]{:S(2)}) collective-permute-start(bf16[128,1792]{1,0:T(8,128)(2,1)S(1)} %collective-permute-done.refs_1_), channel_id=1, source_target_pairs={{0,1},{1,0},{2,3},{3,2},{4,5},{5,4},{6,7},{7,6},{8,9},{9,8},{10,11... | collective-permute-start | bytes 1376264 | tf_op jit(solution)/shard_map/ppermute | solution.py:240
  41.5 3.5 %collective-permute-start.7 = (bf16[128,1792]{1,0:T(8,128)(2,1)S(1)}, bf16[128,1792]{1,0:T(8,128)(2,1)}, u32[]{:S(2)}, u32[]{:S(2)}) collective-permute-start(bf16[128,1792]{1,0:T(8,128)(2,1)S(1)} %collective-permute-done.1.refs_2_), channel_id=1, source_target_pairs={{0,1},{1,0},{2,3},{3,2},{4,5},{5,4},{6,7},{7,6},{8,9},{9,8},{10,11... | collective-permute-start | bytes 1376264 | tf_op jit(solution)/shard_map/ppermute | solution.py:240
  42.0 2.9 %collective-permute-start.8 = (bf16[128,1792]{1,0:T(8,128)(2,1)S(1)}, bf16[128,1792]{1,0:T(8,128)(2,1)}, u32[]{:S(2)}, u32[]{:S(2)}) collective-permute-start(bf16[128,1792]{1,0:T(8,128)(2,1)S(1)} %collective-permute-done.4.refs_3_), channel_id=1, source_target_pairs={{0,1},{1,0},{2,3},{3,2},{4,5},{5,4},{6,7},{7,6},{8,9},{9,8},{10,11... | collective-permute-start | bytes 1376264 | tf_op jit(solution)/shard_map/ppermute | solution.py:240
  49.4 1.2 %collective-permute-start.10 = (f32[8,1024]{1,0:T(8,128)S(1)}, f32[8,1024]{1,0:T(8,128)S(1)}, u32[]{:S(2)}, u32[]{:S(2)}) collective-permute-start(f32[8,1024]{1,0:T(8,128)S(1)} %get-tuple-element.44), channel_id=1, source_target_pairs={{0,1},{1,0},{2,3},{3,2},{4,5},{5,4},{6,7},{7,6},{8,9},{9,8},{10,11... | collective-permute-start | bytes 98312 | tf_op jit(solution)/shard_map/ppermute | solution.py:240
  50.7 4.9 %collective-permute-start.11 = (f32[8,1024]{1,0:T(8,128)S(1)}, f32[8,1024]{1,0:T(8,128)S(1)}, u32[]{:S(2)}, u32[]{:S(2)}) collective-permute-start(f32[8,1024]{1,0:T(8,128)S(1)} %add.48.refs_3_), channel_id=1, source_target_pairs={{0,16},{16,0},{1,17},{17,1},{2,18},{18,2},{3,19},{19,3},{4,20},{20... | collective-permute-start | bytes 98312 | tf_op jit(solution)/shard_map/ppermute | solution.py:240
  52.1 4.8 %collective-permute-start.13 = (f32[8,512]{1,0:T(8,128)S(1)}, f32[8,512]{1,0:T(8,128)S(1)}, u32[]{:S(2)}, u32[]{:S(2)}) collective-permute-start(f32[8,512]{1,0:T(8,128)S(1)} %shard_map.70.refs_6_), channel_id=1, source_target_pairs={{0,8},{8,0},{1,9},{9,1},{2,10},{10,2},{3,11},{11,3},{4,12},{12,4},... | collective-permute-start | bytes 49160 | tf_op jit(solution)/shard_map/ppermute | solution.py:240
  55.6 5.2 %collective-permute-start.12 = (f32[16,1024]{1,0:T(8,128)S(1)}, f32[16,1024]{1,0:T(8,128)S(1)}, u32[]{:S(2)}, u32[]{:S(2)}) collective-permute-start(f32[16,1024]{1,0:T(8,128)S(1)} %pad_maximum_fusion.2), channel_id=1, source_target_pairs={{0,4},{4,0},{1,5},{5,1},{2,6},{6,2},{3,7},{7,3},{8,12},{12,8},{9,1... | collective-permute-start | bytes 196616 | tf_op jit(solution)/shard_map/ppermute | solution.py:240
  56.9 3.9 %collective-permute-start.14 = (f32[16,512]{1,0:T(8,128)S(1)}, f32[16,512]{1,0:T(8,128)S(1)}, u32[]{:S(2)}, u32[]{:S(2)}) collective-permute-start(f32[16,512]{1,0:T(8,128)S(1)} %pad_maximum_fusion.3), channel_id=1, source_target_pairs={{0,2},{2,0},{1,3},{3,1},{4,6},{6,4},{5,7},{7,5},{8,10},{10,8},{9,1... | collective-permute-start | bytes 98312 | tf_op jit(solution)/shard_map/ppermute | solution.py:240
  63.1 2.4 %collective-permute-start.16 = (f32[272,512]{1,0:T(8,128)S(1)}, f32[272,512]{1,0:T(8,128)S(1)}, u32[]{:S(2)}, u32[]{:S(2)}) collective-permute-start(f32[272,512]{1,0:T(8,128)S(1)} %get-tuple-element.54), channel_id=1, source_target_pairs={{0,1},{1,0},{2,3},{3,2},{4,5},{5,4},{6,7},{7,6},{8,9},{9,8},{10,11... | collective-permute-start | bytes 1671176 | tf_op jit(solution)/shard_map/ppermute | solution.py:240
  63.2 5.4 %collective-permute-start.15 = (f32[272,512]{1,0:T(8,128)S(1)}, f32[272,512]{1,0:T(8,128)S(1)}, u32[]{:S(2)}, u32[]{:S(2)}) collective-permute-start(f32[272,512]{1,0:T(8,128)S(1)} %get-tuple-element.52), channel_id=1, source_target_pairs={{0,1},{1,0},{2,3},{3,2},{4,5},{5,4},{6,7},{7,6},{8,9},{9,8},{10,11... | collective-permute-start | bytes 1671176 | tf_op jit(solution)/shard_map/ppermute | solution.py:240
  65.7 8.7 %collective-permute-start.18 = (f16[272,512]{1,0:T(8,128)(2,1)S(1)}, f16[272,512]{1,0:T(8,128)(2,1)S(1)}, u32[]{:S(2)}, u32[]{:S(2)}) collective-permute-start(f16[272,512]{1,0:T(8,128)(2,1)S(1)} %convert_element_type.21), channel_id=1, source_target_pairs={{0,2},{2,0},{1,3},{3,1},{4,6},{6,4},{5,7},{7,5},{8,10},{10,8},{9,1... | collective-permute-start | bytes 835592 | tf_op jit(solution)/shard_map/ppermute | solution.py:240
  67.3 8.4 %collective-permute-start.17 = (f16[272,512]{1,0:T(8,128)(2,1)S(1)}, f16[272,512]{1,0:T(8,128)(2,1)S(1)}, u32[]{:S(2)}, u32[]{:S(2)}) collective-permute-start(f16[272,512]{1,0:T(8,128)(2,1)S(1)} %add_convert_fusion), channel_id=1, source_target_pairs={{0,4},{4,0},{1,5},{5,1},{2,6},{6,2},{3,7},{7,3},{8,12},{12,8},{9,1... | collective-permute-start | bytes 835592 | tf_op jit(solution)/shard_map/ppermute | solution.py:240
  75.9 5.9 %collective-permute-start.20 = (f16[144,512]{1,0:T(8,128)(2,1)S(1)}, f16[144,512]{1,0:T(8,128)(2,1)S(1)}, u32[]{:S(2)}, u32[]{:S(2)}) collective-permute-start(f16[144,512]{1,0:T(8,128)(2,1)S(1)} %get-tuple-element.60), channel_id=1, source_target_pairs={{0,8},{8,0},{1,9},{9,1},{2,10},{10,2},{3,11},{11,3},{4,12},{12,4},... | collective-permute-start | bytes 442376 | tf_op jit(solution)/shard_map/ppermute | solution.py:240
  78.0 8.5 %collective-permute-start.19 = (f16[144,512]{1,0:T(8,128)(2,1)S(1)}, f16[144,512]{1,0:T(8,128)(2,1)S(1)}, u32[]{:S(2)}, u32[]{:S(2)}) collective-permute-start(f16[144,512]{1,0:T(8,128)(2,1)S(1)} %get-tuple-element.59), channel_id=1, source_target_pairs={{0,16},{16,0},{1,17},{17,1},{2,18},{18,2},{3,19},{19,3},{4,20},{20... | collective-permute-start | bytes 442376 | tf_op jit(solution)/shard_map/ppermute | solution.py:240

commit v11 on v10

--- a/solution.py
+++ b/solution.py
@@ -248,18 +248,24 @@
     return lax.optimization_barrier(groups)
 
 
-def gather(bits, both, apart=None, gates=(None, None)):
-    blocks = [(both,)]
-    for k, bit in enumerate(bits):
-        own = apart if k == 0 and apart else (both,)
-        if k > 1:
-            own = together(own, blocks[2])[0]
-        if k == 1 and gates[0] is not None:
-            own = together(own, gates[0])[0]
-        ways = blocks[1:]
-        if k and gates[1] is not None:
-            ways = together(ways, gates[1])[0]
-        blocks = blocks + [tuple(swap((bit,), y) for y in parts) for parts in [own] + list(ways)]
+def gather(groups):
+    blocks, own = [], []
+    for bits, both, apart in groups:
+        first = swap(bits[:1], apart[0])
+        own.append(swap(bits[1:2], both))
+        second = swap(bits[:1], together(apart[1], first)[0])
+        blocks.append([(both,), (first, second)])
+    late = [x[1][1] for x in blocks]
+    for n, (bits, both, _) in enumerate(groups):
+        for k in range(1, len(bits)):
+            if k == 1:
+                first, second = blocks[n][1]
+                ways = [(together(first, own[n])[0], second)]
+                new = [(own[n],)]
+            else:
+                ways = together(blocks[n][1:], late)[0]
+                new = [(swap(bits[k : k + 1], together(both, own[n])[0]),)]
+            blocks[n] = blocks[n] + new + [tuple(swap(bits[k : k + 1], y) for y in parts) for parts in ways]
     return blocks
 
 
@@ -284,8 +290,9 @@
     pair, others = image_bits[-1:], image_bits[:-1]
     (image,) = call(join_kernel, [((b, tw + sw), BF16)], [teacher_image, student_image])
     (text,) = call(join_kernel, [((b, tw + sw), BF16)], [teacher_text, student_text])
-    texts = gather(text_bits, text)
-    images = gather(image_bits, image, None, (text, texts[1:3]))
+    images, texts = gather(
+        [(image_bits, image, (teacher_image, student_image)), (text_bits, text, (teacher_text, student_text))]
+    )
     forms = [[len(x) for x in blocks] for blocks in (images, texts)]
     place = jnp.stack([lax.axis_index(x) for x in (pair, image_bits, text_bits)]).astype(jnp.int32)
     tl, sl, rows, rows_swapped, peaks, image, text = call(

time: 90 us -> 92.8 us (1.031)
  local copies, waits for them, and re-layouts: 3.75 us -> 10.7 us
  waiting for transfers between devices: 45.7 us -> 39.2 us
  starting transfers between devices: 24.7 us -> 26.3 us
    unnamed x8 -> x26, local copies, waits for them, and re-layouts: 3.75 us -> 10.7 us
    ppermute x21 -> x27, waiting for transfers between devices: 45.7 us -> 39.2 us  [swap(): return lax.ppermute(x, bits, perm)]
    ppermute x21 -> x27, starting transfers between devices: 24.7 us -> 26.3 us  [swap(): return lax.ppermute(x, bits, perm)]
  transfers between devices with their start and end apart: 21 -> 27, of which waited for: 11 -> 14; matrix products, arithmetic and copies ran while one was open for 1% -> 1% of each run, Pallas kernels for 4% -> 4%
where the time goes in v11:
time: 92.8 us; the launch traced here: 92.4 us
  waiting for transfers between devices  39.2 us (42%)
  starting transfers between devices  26.3 us (28%)
  local copies, waits for them, and re-layouts  10.7 us (12%)
  Pallas kernels  10.6 us (11%)
  other arithmetic  3.01 us (3%)
  between operations  2.61 us (3%)
    ppermute x27, waiting for transfers between devices, swap(): return lax.ppermute(x, bits, perm)  39.2 us
    ppermute x27, starting transfers between devices, swap(): return lax.ppermute(x, bits, perm)  26.3 us
    unnamed x26, local copies, waits for them, and re-layouts  10.7 us
    pallas_call x6, Pallas kernels, call(): pl.pallas_call(kernel, out_shape=shapes, in_specs=[SMEM if x.dtype == jnp...  10.6 us
  transfers between devices with their start and end apart: 27, of which 14 were waited for; matrix products, arithmetic and copies ran while one was open for 1% of the time, Pallas kernels for 4%

profile of v11, /device:TPU:0, one launch (start us, length us, event | category | flops | bytes accessed | tf_op | source)
XLA Modules:
  0.0 92.4 jit_solution(11298734125141939475)
XLA Ops:
  1.5 1.0 %shard_map.67.refs_0_ = bf16[128,1792]{1,0:T(8,128)(2,1)S(1)} custom-call(bf16[128,1280]{1,0:T(8,128)(2,1)} %teacher.2, bf16[128,512]{1,0:T(8,128)(2,1)S(1)} %copy-done.1), custom_call_target="tpu_custom_call" | custom-call | bytes 917504 | tf_op jit(solution)/shard_map/pallas_call | solution.py:227
  2.5 3.0 %collective-permute-start.2 = (bf16[128,1792]{1,0:T(8,128)(2,1)S(1)}, bf16[128,1792]{1,0:T(8,128)(2,1)S(1)}, u32[]{:S(2)}, u32[]{:S(2)}) collective-permute-start(bf16[128,1792]{1,0:T(8,128)(2,1)S(1)} %shard_map.67.refs_0_), channel_id=1, source_target_pairs={{0,4},{4,0},{1,5},{5,1},{2,6},{6,2},{3,7},{7,3},{8,12},{12,8},{9,1... | collective-permute-start | bytes 1376264 | tf_op jit(solution)/shard_map/ppermute | solution.py:240
  5.6 2.6 %collective-permute-start = (bf16[128,1280]{1,0:T(8,128)(2,1)}, bf16[128,1280]{1,0:T(8,128)(2,1)S(1)}, u32[]{:S(2)}, u32[]{:S(2)}) collective-permute-start(bf16[128,1280]{1,0:T(8,128)(2,1)} %teacher.2), channel_id=1, source_target_pairs={{0,16},{16,0},{1,17},{17,1},{2,18},{18,2},{3,19},{19,3},{4,20},{20... | collective-permute-start | bytes 983048 | tf_op jit(solution)/shard_map/ppermute | solution.py:240
  8.2 1.0 %copy-done = bf16[128,1280]{1,0:T(8,128)(2,1)S(1)} copy-done((bf16[128,1280]{1,0:T(8,128)(2,1)S(1)}, bf16[128,1280]{1,0:T(8,128)(2,1)}, u32[]{:S(2)}) %copy-start) | copy-done | bytes 327704
  10.1 1.6 %collective-permute-start.13 = (bf16[128,1792]{1,0:T(8,128)(2,1)S(1)}, bf16[128,1792]{1,0:T(8,128)(2,1)S(1)}, u32[]{:S(2)}, u32[]{:S(2)}) collective-permute-start(bf16[128,1792]{1,0:T(8,128)(2,1)S(1)} %shard_map.68.refs_12_), channel_id=1, source_target_pairs={{0,2},{2,0},{1,3},{3,1},{4,6},{6,4},{5,7},{7,5},{8,10},{10,8},{9,1... | collective-permute-start | bytes 1376264 | tf_op jit(solution)/shard_map/ppermute | solution.py:240
  11.6 1.6 %collective-permute-start.6 = (bf16[128,1280]{1,0:T(8,128)(2,1)S(1)}, bf16[128,1280]{1,0:T(8,128)(2,1)S(1)}, u32[]{:S(2)}, u32[]{:S(2)}) collective-permute-start(bf16[128,1280]{1,0:T(8,128)(2,1)S(1)} %copy-done), channel_id=1, source_target_pairs={{0,8},{8,0},{1,9},{9,1},{2,10},{10,2},{3,11},{11,3},{4,12},{12,4},... | collective-permute-start | bytes 983048 | tf_op jit(solution)/shard_map/ppermute | solution.py:240
  13.2 9.8 %collective-permute-done.refs_1_ = bf16[128,1280]{1,0:T(8,128)(2,1)S(1)} collective-permute-done((bf16[128,1280]{1,0:T(8,128)(2,1)}, bf16[128,1280]{1,0:T(8,128)(2,1)S(1)}, u32[]{:S(2)}, u32[]{:S(2)}) %collective-permute-start) | collective-permute-done | bytes 327712 | tf_op jit(solution)/shard_map/ppermute | solution.py:240
  23.4 4.1 %collective-permute-done.6.refs_13_ = bf16[128,1280]{1,0:T(8,128)(2,1)S(1)} collective-permute-done((bf16[128,1280]{1,0:T(8,128)(2,1)S(1)}, bf16[128,1280]{1,0:T(8,128)(2,1)S(1)}, u32[]{:S(2)}, u32[]{:S(2)}) %collective-permute-start.6) | collective-permute-done | bytes 327712 | tf_op jit(solution)/shard_map/ppermute | solution.py:240
  27.6 1.5 %collective-permute-start.7 = (bf16[128,512]{1,0:T(8,128)(2,1)S(1)}, bf16[128,512]{1,0:T(8,128)(2,1)S(1)}, u32[]{:S(2)}, u32[]{:S(2)}) collective-permute-start(bf16[128,512]{1,0:T(8,128)(2,1)S(1)} %copy-done.2), channel_id=1, source_target_pairs={{0,8},{8,0},{1,9},{9,1},{2,10},{10,2},{3,11},{11,3},{4,12},{12,4},... | collective-permute-start | bytes 393224 | tf_op jit(solution)/shard_map/ppermute | solution.py:240
  29.0 3.0 %collective-permute-done.1.refs_2_ = bf16[128,512]{1,0:T(8,128)(2,1)S(1)} collective-permute-done((bf16[128,512]{1,0:T(8,128)(2,1)}, bf16[128,512]{1,0:T(8,128)(2,1)S(1)}, u32[]{:S(2)}, u32[]{:S(2)}) %collective-permute-start.1) | collective-permute-done | bytes 131104 | tf_op jit(solution)/shard_map/ppermute | solution.py:240
  32.0 1.5 %collective-permute-start.4 = (bf16[128,512]{1,0:T(8,128)(2,1)S(1)}, bf16[128,512]{1,0:T(8,128)(2,1)S(1)}, u32[]{:S(2)}, u32[]{:S(2)}) collective-permute-start(bf16[128,512]{1,0:T(8,128)(2,1)S(1)} %collective-permute-done.1.refs_2_), channel_id=1, source_target_pairs={{0,4},{4,0},{1,5},{5,1},{2,6},{6,2},{3,7},{7,3},{8,12},{12,8},{9,1... | collective-permute-start | bytes 393224 | tf_op jit(solution)/shard_map/ppermute | solution.py:240
  33.6 1.5 %collective-permute-start.15 = (bf16[128,512]{1,0:T(8,128)(2,1)S(1)}, bf16[128,512]{1,0:T(8,128)(2,1)S(1)}, u32[]{:S(2)}, u32[]{:S(2)}) collective-permute-start(bf16[128,512]{1,0:T(8,128)(2,1)S(1)} %collective-permute-done.7.refs_14_), channel_id=1, source_target_pairs={{0,2},{2,0},{1,3},{3,1},{4,6},{6,4},{5,7},{7,5},{8,10},{10,8},{9,1... | collective-permute-start | bytes 393224 | tf_op jit(solution)/shard_map/ppermute | solution.py:240
  35.7 1.3 %collective-permute-done.4.refs_5_ = bf16[128,512]{1,0:T(8,128)(2,1)S(1)} collective-permute-done((bf16[128,512]{1,0:T(8,128)(2,1)S(1)}, bf16[128,512]{1,0:T(8,128)(2,1)S(1)}, u32[]{:S(2)}, u32[]{:S(2)}) %collective-permute-start.4) | collective-permute-done | bytes 131104 | tf_op jit(solution)/shard_map/ppermute | solution.py:240
  37.5 2.0 %collective-permute-done.15.refs_17_ = bf16[128,512]{1,0:T(8,128)(2,1)S(1)} collective-permute-done((bf16[128,512]{1,0:T(8,128)(2,1)S(1)}, bf16[128,512]{1,0:T(8,128)(2,1)S(1)}, u32[]{:S(2)}, u32[]{:S(2)}) %collective-permute-start.15) | collective-permute-done | bytes 131104 | tf_op jit(solution)/shard_map/ppermute | solution.py:240
  43.4 1.0 %collective-permute-done.9.refs_8_ = bf16[128,512]{1,0:T(8,128)(2,1)} collective-permute-done((bf16[128,512]{1,0:T(8,128)(2,1)S(1)}, bf16[128,512]{1,0:T(8,128)(2,1)}, u32[]{:S(2)}, u32[]{:S(2)}) %collective-permute-start.9) | collective-permute-done | bytes 131104 | tf_op jit(solution)/shard_map/ppermute | solution.py:240
  44.5 1.0 %copy-done.4 = bf16[128,1280]{1,0:T(8,128)(2,1)S(1)} copy-done((bf16[128,1280]{1,0:T(8,128)(2,1)S(1)}, bf16[128,1280]{1,0:T(8,128)(2,1)}, u32[]{:S(2)}) %copy-start.4) | copy-done | bytes 327704
  49.1 4.1 %shard_map.69 = (f32[1024,512]{1,0:T(8,128)S(1)}, f32[1024,512]{1,0:T(8,128)S(1)}, f32[8,1024]{1,0:T(8,128)S(1)}, f32[8,1024]{1,0:T(8,128)S(1)}, f32[8,512]{1,0:...) custom-call(s32[3]{0:T(128)S(1)} %pad_add_fusion.core.place, ...), custom_call_target="tpu_custom_call" | custom-call | flops 1879048192 | bytes 11354124 | tf_op jit(solution)/shard_map/pallas_call | solution.py:227
  54.5 1.4 %shard_map.70.refs_6_ = f32[8,512]{1,0:T(8,128)S(1)} custom-call(f32[1024,512]{1,0:T(8,128)S(1)} %get-tuple-element.49.tl_ref.refs_1_, f32[1024,512]{1,0:T(8,128)S(1)} %get-tuple-element.50.sl_ref.refs_2_, f32[8,512]{1,0:T(8,128)S(1)} %get-tuple-element.53.peaks, bf16[1024,512]{1,0:T(8,128)(2,1)S(1)} %get-tuple-element.47.image), custom_call_target="tpu_custom_call" | custom-call | bytes 5275648 | tf_op jit(solution)/shard_map/pallas_call | solution.py:227
  55.9 2.6 %collective-permute-start.19 = (f32[8,512]{1,0:T(8,128)S(1)}, f32[8,512]{1,0:T(8,128)S(1)}, u32[]{:S(2)}, u32[]{:S(2)}) collective-permute-start(f32[8,512]{1,0:T(8,128)S(1)} %shard_map.70.refs_6_), channel_id=1, source_target_pairs={{0,8},{8,0},{1,9},{9,1},{2,10},{10,2},{3,11},{11,3},{4,12},{12,4},... | collective-permute-start | bytes 49160 | tf_op jit(solution)/shard_map/ppermute | solution.py:240
  59.3 0.9 collective-permute-start.18
  60.3 1.4 %collective-permute-start.20 = (f32[16,512]{1,0:T(8,128)S(1)}, f32[16,512]{1,0:T(8,128)S(1)}, u32[]{:S(2)}, u32[]{:S(2)}) collective-permute-start(f32[16,512]{1,0:T(8,128)S(1)} %pad_maximum_fusion.3), channel_id=1, source_target_pairs={{0,2},{2,0},{1,3},{3,1},{4,6},{6,4},{5,7},{7,5},{8,10},{10,8},{9,1... | collective-permute-start | bytes 98312 | tf_op jit(solution)/shard_map/ppermute | solution.py:240
  61.7 2.5 %collective-permute-done.20.refs_8_ = f32[16,512]{1,0:T(8,128)S(1)} collective-permute-done((f32[16,512]{1,0:T(8,128)S(1)}, f32[16,512]{1,0:T(8,128)S(1)}, u32[]{:S(2)}, u32[]{:S(2)}) %collective-permute-start.20) | collective-permute-done | bytes 32800 | tf_op jit(solution)/shard_map/ppermute | solution.py:240
  64.2 2.3 %shard_map.71 = (f32[272,512]{1,0:T(8,128)S(1)}, f32[272,512]{1,0:T(8,128)S(1)}, bf16[1024,512]{1,0:T(8,128)(2,1)S(1)}, bf16[1024,512]{1,0:T(8,128)(2,1)S(1)}, f...) custom-call(s32[3]{0:T(128)S(1)} %pad_add_fusion.core.place, ...), custom_call_target="tpu_custom_call" | custom-call | flops 536870912 | bytes 8212492 | tf_op jit(solution)/shard_map/pallas_call | solution.py:227
  67.1 1.8 %shard_map.72 = (f32[272,512]{1,0:T(8,128)S(1)}, f32[272,512]{1,0:T(8,128)S(1)}, f32[272,512]{1,0:T(8,128)S(1)}, f32[272,512]{1,0:T(8,128)S(1)}) custom-call(bf16[1024,512]{1,0:T(8,128)(2,1)S(1)} %get-tuple-element.47.image, bf16[512,512]{1,0:T(8,128)(2,1)S(1)} %get-tuple-element.48.refs_0_.text, bf16[1024,512]{1,0:T(8,128)(2,1)S(1)} %get-tuple-element.54.high_ref, ...), custom_call_target="tpu_custom_call" | custom-call | flops 1610612736 | bytes 5980160 | tf_op jit(solution)/shard_map/pallas_call | solution.py:227
  69.1 1.5 %collective-permute-start.24 = (f16[272,512]{1,0:T(8,128)(2,1)S(1)}, f16[272,512]{1,0:T(8,128)(2,1)S(1)}, u32[]{:S(2)}, u32[]{:S(2)}) collective-permute-start(f16[272,512]{1,0:T(8,128)(2,1)S(1)} %convert_element_type.21), channel_id=1, source_target_pairs={{0,2},{2,0},{1,3},{3,1},{4,6},{6,4},{5,7},{7,5},{8,10},{10,8},{9,1... | collective-permute-start | bytes 835592 | tf_op jit(solution)/shard_map/ppermute | solution.py:240
  70.5 1.2 %collective-permute-start.23 = (f16[272,512]{1,0:T(8,128)(2,1)S(1)}, f16[272,512]{1,0:T(8,128)(2,1)S(1)}, u32[]{:S(2)}, u32[]{:S(2)}) collective-permute-start(f16[272,512]{1,0:T(8,128)(2,1)S(1)} %add_convert_fusion), channel_id=1, source_target_pairs={{0,4},{4,0},{1,5},{5,1},{2,6},{6,2},{3,7},{7,3},{8,12},{12,8},{9,1... | collective-permute-start | bytes 835592 | tf_op jit(solution)/shard_map/ppermute | solution.py:240
  71.8 5.9 %collective-permute-done.24 = f16[272,512]{1,0:T(8,128)(2,1)S(1)} collective-permute-done((f16[272,512]{1,0:T(8,128)(2,1)S(1)}, f16[272,512]{1,0:T(8,128)(2,1)S(1)}, u32[]{:S(2)}, u32[]{:S(2)}) %collective-permute-start.24) | collective-permute-done | bytes 278560 | tf_op jit(solution)/shard_map/ppermute | solution.py:240
  78.0 0.9 %collective-permute-done.23 = f16[272,512]{1,0:T(8,128)(2,1)S(1)} collective-permute-done((f16[272,512]{1,0:T(8,128)(2,1)S(1)}, f16[272,512]{1,0:T(8,128)(2,1)S(1)}, u32[]{:S(2)}, u32[]{:S(2)}) %collective-permute-start.23) | collective-permute-done | bytes 278560 | tf_op jit(solution)/shard_map/ppermute | solution.py:240
  79.2 1.4 %collective-permute-start.26 = (f16[144,512]{1,0:T(8,128)(2,1)S(1)}, f16[144,512]{1,0:T(8,128)(2,1)S(1)}, u32[]{:S(2)}, u32[]{:S(2)}) collective-permute-start(f16[144,512]{1,0:T(8,128)(2,1)S(1)} %get-tuple-element.68), channel_id=1, source_target_pairs={{0,8},{8,0},{1,9},{9,1},{2,10},{10,2},{3,11},{11,3},{4,12},{12,4},... | collective-permute-start | bytes 442376 | tf_op jit(solution)/shard_map/ppermute | solution.py:240
  80.7 1.1 %collective-permute-start.25 = (f16[144,512]{1,0:T(8,128)(2,1)S(1)}, f16[144,512]{1,0:T(8,128)(2,1)S(1)}, u32[]{:S(2)}, u32[]{:S(2)}) collective-permute-start(f16[144,512]{1,0:T(8,128)(2,1)S(1)} %get-tuple-element.67), channel_id=1, source_target_pairs={{0,16},{16,0},{1,17},{17,1},{2,18},{18,2},{3,19},{19,3},{4,20},{20... | collective-permute-start | bytes 442376 | tf_op jit(solution)/shard_map/ppermute | solution.py:240
  81.8 5.0 %collective-permute-done.26 = f16[144,512]{1,0:T(8,128)(2,1)S(1)} collective-permute-done((f16[144,512]{1,0:T(8,128)(2,1)S(1)}, f16[144,512]{1,0:T(8,128)(2,1)S(1)}, u32[]{:S(2)}, u32[]{:S(2)}) %collective-permute-start.26) | collective-permute-done | bytes 147488 | tf_op jit(solution)/shard_map/ppermute | solution.py:240
  87.6 1.5 %collective-permute-done.25 = f16[144,512]{1,0:T(8,128)(2,1)S(1)} collective-permute-done((f16[144,512]{1,0:T(8,128)(2,1)S(1)}, f16[144,512]{1,0:T(8,128)(2,1)S(1)}, u32[]{:S(2)}, u32[]{:S(2)}) %collective-permute-start.25) | collective-permute-done | bytes 147488 | tf_op jit(solution)/shard_map/ppermute | solution.py:240
  (78 shorter events, 16.7 us)
Async XLA Ops:
  0.6 0.9 copy-start.1
  2.5 20.4 %collective-permute-start.2 = (bf16[128,1792]{1,0:T(8,128)(2,1)S(1)}, bf16[128,1792]{1,0:T(8,128)(2,1)S(1)}, u32[]{:S(2)}, u32[]{:S(2)}) collective-permute-start(bf16[128,1792]{1,0:T(8,128)(2,1)S(1)} %shard_map.67.refs_0_), channel_id=1, source_target_pairs={{0,4},{4,0},{1,5},{5,1},{2,6},{6,2},{3,7},{7,3},{8,12},{12,8},{9,1... | collective-permute-start | bytes 1376264 | tf_op jit(solution)/shard_map/ppermute | solution.py:240
  5.6 17.4 %collective-permute-start = (bf16[128,1280]{1,0:T(8,128)(2,1)}, bf16[128,1280]{1,0:T(8,128)(2,1)S(1)}, u32[]{:S(2)}, u32[]{:S(2)}) collective-permute-start(bf16[128,1280]{1,0:T(8,128)(2,1)} %teacher.2), channel_id=1, source_target_pairs={{0,16},{16,0},{1,17},{17,1},{2,18},{18,2},{3,19},{19,3},{4,20},{20... | collective-permute-start | bytes 983048 | tf_op jit(solution)/shard_map/ppermute | solution.py:240
  8.2 1.0 %copy-start = (bf16[128,1280]{1,0:T(8,128)(2,1)S(1)}, bf16[128,1280]{1,0:T(8,128)(2,1)}, u32[]{:S(2)}) copy-start(bf16[128,1280]{1,0:T(8,128)(2,1)} %teacher.3) | copy-start | bytes 983044
  9.1 0.9 copy-start.2
  10.1 17.5 %collective-permute-start.13 = (bf16[128,1792]{1,0:T(8,128)(2,1)S(1)}, bf16[128,1792]{1,0:T(8,128)(2,1)S(1)}, u32[]{:S(2)}, u32[]{:S(2)}) collective-permute-start(bf16[128,1792]{1,0:T(8,128)(2,1)S(1)} %shard_map.68.refs_12_), channel_id=1, source_target_pairs={{0,2},{2,0},{1,3},{3,1},{4,6},{6,4},{5,7},{7,5},{8,10},{10,8},{9,1... | collective-permute-start | bytes 1376264 | tf_op jit(solution)/shard_map/ppermute | solution.py:240
  11.6 15.9 %collective-permute-start.6 = (bf16[128,1280]{1,0:T(8,128)(2,1)S(1)}, bf16[128,1280]{1,0:T(8,128)(2,1)S(1)}, u32[]{:S(2)}, u32[]{:S(2)}) collective-permute-start(bf16[128,1280]{1,0:T(8,128)(2,1)S(1)} %copy-done), channel_id=1, source_target_pairs={{0,8},{8,0},{1,9},{9,1},{2,10},{10,2},{3,11},{11,3},{4,12},{12,4},... | collective-permute-start | bytes 983048 | tf_op jit(solution)/shard_map/ppermute | solution.py:240
  23.0 14.0 %collective-permute-start.3 = (bf16[128,1280]{1,0:T(8,128)(2,1)S(1)}, bf16[128,1280]{1,0:T(8,128)(2,1)}, u32[]{:S(2)}, u32[]{:S(2)}) collective-permute-start(bf16[128,1280]{1,0:T(8,128)(2,1)S(1)} %collective-permute-done.refs_1_), channel_id=1, source_target_pairs={{0,4},{4,0},{1,5},{5,1},{2,6},{6,2},{3,7},{7,3},{8,12},{12,8},{9,1... | collective-permute-start | bytes 983048 | tf_op jit(solution)/shard_map/ppermute | solution.py:240
  23.4 8.6 %collective-permute-start.1 = (bf16[128,512]{1,0:T(8,128)(2,1)}, bf16[128,512]{1,0:T(8,128)(2,1)S(1)}, u32[]{:S(2)}, u32[]{:S(2)}) collective-permute-start(bf16[128,512]{1,0:T(8,128)(2,1)} %student.2), channel_id=1, source_target_pairs={{0,16},{16,0},{1,17},{17,1},{2,18},{18,2},{3,19},{19,3},{4,20},{20... | collective-permute-start | bytes 393224 | tf_op jit(solution)/shard_map/ppermute | solution.py:240
  27.6 12.6 %collective-permute-start.14 = (bf16[128,1280]{1,0:T(8,128)(2,1)S(1)}, bf16[128,1280]{1,0:T(8,128)(2,1)S(1)}, u32[]{:S(2)}, u32[]{:S(2)}) collective-permute-start(bf16[128,1280]{1,0:T(8,128)(2,1)S(1)} %collective-permute-done.6.refs_13_), channel_id=1, source_target_pairs={{0,2},{2,0},{1,3},{3,1},{4,6},{6,4},{5,7},{7,5},{8,10},{10,8},{9,1... | collective-permute-start | bytes 983048 | tf_op jit(solution)/shard_map/ppermute | solution.py:240
  27.6 6.0 %collective-permute-start.7 = (bf16[128,512]{1,0:T(8,128)(2,1)S(1)}, bf16[128,512]{1,0:T(8,128)(2,1)S(1)}, u32[]{:S(2)}, u32[]{:S(2)}) collective-permute-start(bf16[128,512]{1,0:T(8,128)(2,1)S(1)} %copy-done.2), channel_id=1, source_target_pairs={{0,8},{8,0},{1,9},{9,1},{2,10},{10,2},{3,11},{11,3},{4,12},{12,4},... | collective-permute-start | bytes 393224 | tf_op jit(solution)/shard_map/ppermute | solution.py:240
  32.0 5.0 %collective-permute-start.4 = (bf16[128,512]{1,0:T(8,128)(2,1)S(1)}, bf16[128,512]{1,0:T(8,128)(2,1)S(1)}, u32[]{:S(2)}, u32[]{:S(2)}) collective-permute-start(bf16[128,512]{1,0:T(8,128)(2,1)S(1)} %collective-permute-done.1.refs_2_), channel_id=1, source_target_pairs={{0,4},{4,0},{1,5},{5,1},{2,6},{6,2},{3,7},{7,3},{8,12},{12,8},{9,1... | collective-permute-start | bytes 393224 | tf_op jit(solution)/shard_map/ppermute | solution.py:240
  33.6 10.9 %collective-permute-start.5 = (bf16[128,1792]{1,0:T(8,128)(2,1)S(1)}, bf16[128,1792]{1,0:T(8,128)(2,1)S(1)}, u32[]{:S(2)}, u32[]{:S(2)}) collective-permute-start(bf16[128,1792]{1,0:T(8,128)(2,1)S(1)} %shard_map.67.refs_0_), channel_id=1, source_target_pairs={{0,1},{1,0},{2,3},{3,2},{4,5},{5,4},{6,7},{7,6},{8,9},{9,8},{10,11... | collective-permute-start | bytes 1376264 | tf_op jit(solution)/shard_map/ppermute | solution.py:240
  33.6 5.9 %collective-permute-start.15 = (bf16[128,512]{1,0:T(8,128)(2,1)S(1)}, bf16[128,512]{1,0:T(8,128)(2,1)S(1)}, u32[]{:S(2)}, u32[]{:S(2)}) collective-permute-start(bf16[128,512]{1,0:T(8,128)(2,1)S(1)} %collective-permute-done.7.refs_14_), channel_id=1, source_target_pairs={{0,2},{2,0},{1,3},{3,1},{4,6},{6,4},{5,7},{7,5},{8,10},{10,8},{9,1... | collective-permute-start | bytes 393224 | tf_op jit(solution)/shard_map/ppermute | solution.py:240
  37.0 7.5 %collective-permute-start.10 = (bf16[128,1792]{1,0:T(8,128)(2,1)S(1)}, bf16[128,1792]{1,0:T(8,128)(2,1)S(1)}, u32[]{:S(2)}, u32[]{:S(2)}) collective-permute-start(bf16[128,1792]{1,0:T(8,128)(2,1)S(1)} %collective-permute-done.2.refs_3_), channel_id=1, source_target_pairs={{0,1},{1,0},{2,3},{3,2},{4,5},{5,4},{6,7},{7,6},{8,9},{9,8},{10,11... | collective-permute-start | bytes 1376264 | tf_op jit(solution)/shard_map/ppermute | solution.py:240
  37.0 7.5 %collective-permute-start.11 = (bf16[128,1280]{1,0:T(8,128)(2,1)}, bf16[128,1280]{1,0:T(8,128)(2,1)}, u32[]{:S(2)}, u32[]{:S(2)}) collective-permute-start(bf16[128,1280]{1,0:T(8,128)(2,1)} %collective-permute-done.3.refs_4_), channel_id=1, source_target_pairs={{0,1},{1,0},{2,3},{3,2},{4,5},{5,4},{6,7},{7,6},{8,9},{9,8},{10,11... | collective-permute-start | bytes 983048 | tf_op jit(solution)/shard_map/ppermute | solution.py:240
  40.1 4.4 %collective-permute-start.8 = (bf16[128,1280]{1,0:T(8,128)(2,1)S(1)}, bf16[128,1280]{1,0:T(8,128)(2,1)}, u32[]{:S(2)}, u32[]{:S(2)}) collective-permute-start(bf16[128,1280]{1,0:T(8,128)(2,1)S(1)} %collective-permute-done.refs_1_), channel_id=1, source_target_pairs={{0,1},{1,0},{2,3},{3,2},{4,5},{5,4},{6,7},{7,6},{8,9},{9,8},{10,11... | collective-permute-start | bytes 983048 | tf_op jit(solution)/shard_map/ppermute | solution.py:240
  40.9 1.5 %collective-permute-start.12 = (bf16[128,512]{1,0:T(8,128)(2,1)S(1)}, bf16[128,512]{1,0:T(8,128)(2,1)S(1)}, u32[]{:S(2)}, u32[]{:S(2)}) collective-permute-start(bf16[128,512]{1,0:T(8,128)(2,1)S(1)} %collective-permute-done.4.refs_5_), channel_id=1, source_target_pairs={{0,1},{1,0},{2,3},{3,2},{4,5},{5,4},{6,7},{7,6},{8,9},{9,8},{10,11... | collective-permute-start | bytes 393224 | tf_op jit(solution)/shard_map/ppermute | solution.py:240
  43.0 1.5 %collective-permute-start.9 = (bf16[128,512]{1,0:T(8,128)(2,1)S(1)}, bf16[128,512]{1,0:T(8,128)(2,1)}, u32[]{:S(2)}, u32[]{:S(2)}) collective-permute-start(bf16[128,512]{1,0:T(8,128)(2,1)S(1)} %collective-permute-done.1.refs_2_), channel_id=1, source_target_pairs={{0,1},{1,0},{2,3},{3,2},{4,5},{5,4},{6,7},{7,6},{8,9},{9,8},{10,11... | collective-permute-start | bytes 393224 | tf_op jit(solution)/shard_map/ppermute | solution.py:240
  44.5 1.0 %copy-start.4 = (bf16[128,1280]{1,0:T(8,128)(2,1)S(1)}, bf16[128,1280]{1,0:T(8,128)(2,1)}, u32[]{:S(2)}) copy-start(bf16[128,1280]{1,0:T(8,128)(2,1)} %copy-done.3) | copy-start | bytes 983044
  45.5 0.9 copy-start.6
  53.2 1.3 %collective-permute-start.16 = (f32[8,1024]{1,0:T(8,128)S(1)}, f32[8,1024]{1,0:T(8,128)S(1)}, u32[]{:S(2)}, u32[]{:S(2)}) collective-permute-start(f32[8,1024]{1,0:T(8,128)S(1)} %get-tuple-element.52), channel_id=1, source_target_pairs={{0,1},{1,0},{2,3},{3,2},{4,5},{5,4},{6,7},{7,6},{8,9},{9,8},{10,11... | collective-permute-start | bytes 98312 | tf_op jit(solution)/shard_map/ppermute | solution.py:240
  54.4 4.9 %collective-permute-start.17 = (f32[8,1024]{1,0:T(8,128)S(1)}, f32[8,1024]{1,0:T(8,128)S(1)}, u32[]{:S(2)}, u32[]{:S(2)}) collective-permute-start(f32[8,1024]{1,0:T(8,128)S(1)} %add.48.refs_3_), channel_id=1, source_target_pairs={{0,16},{16,0},{1,17},{17,1},{2,18},{18,2},{3,19},{19,3},{4,20},{20... | collective-permute-start | bytes 98312 | tf_op jit(solution)/shard_map/ppermute | solution.py:240
  55.9 4.4 %collective-permute-start.19 = (f32[8,512]{1,0:T(8,128)S(1)}, f32[8,512]{1,0:T(8,128)S(1)}, u32[]{:S(2)}, u32[]{:S(2)}) collective-permute-start(f32[8,512]{1,0:T(8,128)S(1)} %shard_map.70.refs_6_), channel_id=1, source_target_pairs={{0,8},{8,0},{1,9},{9,1},{2,10},{10,2},{3,11},{11,3},{4,12},{12,4},... | collective-permute-start | bytes 49160 | tf_op jit(solution)/shard_map/ppermute | solution.py:240
  59.3 4.9 %collective-permute-start.18 = (f32[16,1024]{1,0:T(8,128)S(1)}, f32[16,1024]{1,0:T(8,128)S(1)}, u32[]{:S(2)}, u32[]{:S(2)}) collective-permute-start(f32[16,1024]{1,0:T(8,128)S(1)} %pad_maximum_fusion.2), channel_id=1, source_target_pairs={{0,4},{4,0},{1,5},{5,1},{2,6},{6,2},{3,7},{7,3},{8,12},{12,8},{9,1... | collective-permute-start | bytes 196616 | tf_op jit(solution)/shard_map/ppermute | solution.py:240
  60.3 3.9 %collective-permute-start.20 = (f32[16,512]{1,0:T(8,128)S(1)}, f32[16,512]{1,0:T(8,128)S(1)}, u32[]{:S(2)}, u32[]{:S(2)}) collective-permute-start(f32[16,512]{1,0:T(8,128)S(1)} %pad_maximum_fusion.3), channel_id=1, source_target_pairs={{0,2},{2,0},{1,3},{3,1},{4,6},{6,4},{5,7},{7,5},{8,10},{10,8},{9,1... | collective-permute-start | bytes 98312 | tf_op jit(solution)/shard_map/ppermute | solution.py:240
  66.5 2.4 %collective-permute-start.22 = (f32[272,512]{1,0:T(8,128)S(1)}, f32[272,512]{1,0:T(8,128)S(1)}, u32[]{:S(2)}, u32[]{:S(2)}) collective-permute-start(f32[272,512]{1,0:T(8,128)S(1)} %get-tuple-element.62), channel_id=1, source_target_pairs={{0,1},{1,0},{2,3},{3,2},{4,5},{5,4},{6,7},{7,6},{8,9},{9,8},{10,11... | collective-permute-start | bytes 1671176 | tf_op jit(solution)/shard_map/ppermute | solution.py:240
  66.6 5.2 %collective-permute-start.21 = (f32[272,512]{1,0:T(8,128)S(1)}, f32[272,512]{1,0:T(8,128)S(1)}, u32[]{:S(2)}, u32[]{:S(2)}) collective-permute-start(f32[272,512]{1,0:T(8,128)S(1)} %get-tuple-element.60), channel_id=1, source_target_pairs={{0,1},{1,0},{2,3},{3,2},{4,5},{5,4},{6,7},{7,6},{8,9},{9,8},{10,11... | collective-permute-start | bytes 1671176 | tf_op jit(solution)/shard_map/ppermute | solution.py:240
  69.1 8.7 %collective-permute-start.24 = (f16[272,512]{1,0:T(8,128)(2,1)S(1)}, f16[272,512]{1,0:T(8,128)(2,1)S(1)}, u32[]{:S(2)}, u32[]{:S(2)}) collective-permute-start(f16[272,512]{1,0:T(8,128)(2,1)S(1)} %convert_element_type.21), channel_id=1, source_target_pairs={{0,2},{2,0},{1,3},{3,1},{4,6},{6,4},{5,7},{7,5},{8,10},{10,8},{9,1... | collective-permute-start | bytes 835592 | tf_op jit(solution)/shard_map/ppermute | solution.py:240
  70.5 8.4 %collective-permute-start.23 = (f16[272,512]{1,0:T(8,128)(2,1)S(1)}, f16[272,512]{1,0:T(8,128)(2,1)S(1)}, u32[]{:S(2)}, u32[]{:S(2)}) collective-permute-start(f16[272,512]{1,0:T(8,128)(2,1)S(1)} %add_convert_fusion), channel_id=1, source_target_pairs={{0,4},{4,0},{1,5},{5,1},{2,6},{6,2},{3,7},{7,3},{8,12},{12,8},{9,1... | collective-permute-start | bytes 835592 | tf_op jit(solution)/shard_map/ppermute | solution.py:240
  79.2 7.6 %collective-permute-start.26 = (f16[144,512]{1,0:T(8,128)(2,1)S(1)}, f16[144,512]{1,0:T(8,128)(2,1)S(1)}, u32[]{:S(2)}, u32[]{:S(2)}) collective-permute-start(f16[144,512]{1,0:T(8,128)(2,1)S(1)} %get-tuple-element.68), channel_id=1, source_target_pairs={{0,8},{8,0},{1,9},{9,1},{2,10},{10,2},{3,11},{11,3},{4,12},{12,4},... | collective-permute-start | bytes 442376 | tf_op jit(solution)/shard_map/ppermute | solution.py:240
  80.7 8.5 %collective-permute-start.25 = (f16[144,512]{1,0:T(8,128)(2,1)S(1)}, f16[144,512]{1,0:T(8,128)(2,1)S(1)}, u32[]{:S(2)}, u32[]{:S(2)}) collective-permute-start(f16[144,512]{1,0:T(8,128)(2,1)S(1)} %get-tuple-element.67), channel_id=1, source_target_pairs={{0,16},{16,0},{1,17},{17,1},{2,18},{18,2},{3,19},{19,3},{4,20},{20... | collective-permute-start | bytes 442376 | tf_op jit(solution)/shard_map/ppermute | solution.py:240
  (8 other events, 6.0 us)

commit v12 on v8

--- a/solution.py
+++ b/solution.py
@@ -18,6 +18,7 @@
 KINDS = 3
 EXTRA = 16
 DIGITS = (64.0, 2.0**-4, 2.0**-14, 2.0**-24, 2.0**-34)
+MOST = 60 * 2**20
 ROOM = 12 * 2**20
 VMEM = pl.BlockSpec(memory_space=pltpu.VMEM)
 SMEM = pl.BlockSpec(memory_space=pltpu.SMEM)
@@ -107,6 +108,20 @@
     tw = teacher.shape[1]
     both[:, :tw] = teacher[...]
     both[:, tw:] = student[...]
+
+
+def send_kernel(teacher_image, student_image, teacher_text, student_text, image, text, sems):
+    tw = teacher_image.shape[1]
+    copies = [
+        pltpu.make_async_copy(teacher_image, image.at[:, :tw], sems.at[0]),
+        pltpu.make_async_copy(student_image, image.at[:, tw:], sems.at[1]),
+        pltpu.make_async_copy(teacher_text, text.at[:, :tw], sems.at[2]),
+        pltpu.make_async_copy(student_text, text.at[:, tw:], sems.at[3]),
+    ]
+    for copy in copies:
+        copy.start()
+    for copy in copies:
+        copy.wait()
 
 
 def digits(share, rank, slots, width):
@@ -209,6 +224,17 @@
         ref[cols:, :] = text_extra[...]
 
 
+def last_kernel(*refs):
+    (image, image_extra, image_come, image_back), (text, text_extra, text_come, text_back) = refs[:4], refs[4:8]
+    image_grad, text_grad, loss = refs[8:]
+    rows, width = image.shape
+    image_grad[...] = (image[...] + image_come[:rows, :]) * image_back[...]
+    text_grad[...] = (text[...] + text_come[:rows, :]) * text_back[...]
+    counts = (image_extra[...] + image_come[rows:, :]) + (text_extra[...] + text_come[rows:, :])
+    counts = counts * stack_rows(DIGITS, counts.shape, 0)
+    loss[...] = jnp.sum(counts, axis=(0, 1), keepdims=True) * (0.5 / width)
+
+
 def call(kernel, outs, args, scratch=(), flops=0, transcendentals=0):
     shapes = [jax.ShapeDtypeStruct(s, d) for s, d in outs]
     size = sum(x.size * x.dtype.itemsize for x in list(args) + shapes)
@@ -264,9 +290,19 @@
     nr, nc = 1 << len(image_bits), 1 << len(text_bits)
     r, c = nr * b, nc * b
     pair, others = image_bits[-1:], image_bits[:-1]
-    (image,) = call(join_kernel, [((b, tw + sw), BF16)], [teacher_image, student_image])
-    (text,) = call(join_kernel, [((b, tw + sw), BF16)], [teacher_text, student_text])
+    whole = jax.ShapeDtypeStruct((b, tw + sw), BF16)
+    image, text = pl.pallas_call(
+        send_kernel,
+        out_shape=[whole, whole],
+        in_specs=[pl.BlockSpec(memory_space=pltpu.HBM)] * 4,
+        out_specs=[VMEM] * 2,
+        scratch_shapes=[pltpu.SemaphoreType.DMA((4,))],
+        compiler_params=pltpu.CompilerParams(vmem_limit_bytes=MOST),
+    )(teacher_image, student_image, teacher_text, student_text)
     images, texts = gather(image_bits, image), gather(text_bits, text)
+    own = together([teacher_image, student_image, teacher_text, student_text], [images[2], texts[2]])[0]
+    (images[0],) = call(join_kernel, [((b, tw + sw), BF16)], own[:2])
+    (texts[0],) = call(join_kernel, [((b, tw + sw), BF16)], own[2:])
     place = jnp.stack([lax.axis_index(x) for x in (pair, image_bits, text_bits)]).astype(jnp.int32)
     tl, sl, rows, rows_swapped, peaks, image, text = call(
         functools.partial(stats_kernel, nr, nc, b, tw, tw**-0.5, sw**-0.5),
@@ -303,16 +339,20 @@
         (todo,) = together(todo)
         half = b << k >> 1
         if k < len(text_bits):
-            body, extra = text_keep = add_message(text_keep, swap(text_bits[k : k + 1], todo["text"]))
+            text_come = swap(text_bits[k : k + 1], todo["text"])
             if k:
+                body, extra = add_message(text_keep, text_come)
                 text_keep, text_send = (body[:half], extra), jnp.concatenate([body[half:], extra])
         if k < len(others):
-            body, extra = image_keep = add_message(image_keep, swap(others[k : k + 1], todo["image"]))
+            image_come = swap(others[k : k + 1], todo["image"])
             if k:
+                body, extra = add_message(image_keep, image_come)
                 image_keep, image_send = (body[:half], extra), jnp.concatenate([body[half:], extra])
-    units = stack_rows(DIGITS, (EXTRA, sw), 0)
-    loss = jnp.sum((image_keep[1] + text_keep[1]) * units) * (0.5 / sw)
-    return (loss, image_keep[0] * image_back, text_keep[0] * text_back)
+    image_grad, text_grad, loss = call(
+        last_kernel, [((b, sw), F32), ((b, sw), F32), ((1, 1), F32)],
+        [*image_keep, image_come.astype(F32), image_back, *text_keep, text_come.astype(F32), text_back],
+    )
+    return (loss.reshape(()), image_grad, text_grad)
 
 
 def solution(mesh):

time: 88.5 us -> 84.9 us (0.959)
  waiting for transfers between devices: 46.3 us -> 40.7 us
  starting transfers between devices: 22.6 us -> 26.7 us
  Pallas kernels: 10 us -> 12.8 us
  other arithmetic: 2.99 us -> 0.84 us
  between operations: 2.59 us -> 0.84 us
  local copies, waits for them, and re-layouts: 3.75 us -> 2.78 us
    ppermute x21, waiting for transfers between devices: 46.3 us -> 40.7 us  [swap(): return lax.ppermute(x, bits, perm)]
    ppermute x21, starting transfers between devices: 22.6 us -> 26.7 us  [swap(): return lax.ppermute(x, bits, perm)]
    pallas_call x0 -> x1, Pallas kernels: none -> 2.18 us  [local(): pl.pallas_call(send_kernel, out_shape=[whole, whole], in_specs=[pl.BlockS...]
    mul x2 -> x0, other arithmetic: 1.49 us -> none  [local(): return (loss, image_keep[0] * image_back, text_keep[0] * text_back)]
    unnamed x8, local copies, waits for them, and re-layouts: 3.75 us -> 2.78 us
    pallas_call x6 -> x7, Pallas kernels: 10 us -> 10.6 us  [call(): pl.pallas_call(kernel, out_shape=shapes, in_specs=[SMEM if x.dtype == jnp...]
  transfers between devices with their start and end apart: 21 -> 21, of which waited for: 12 -> 8; matrix products, arithmetic and copies ran while one was open for 1% -> 1% of each run, Pallas kernels for 4% -> 4%
where the time goes in v12:
time: 84.9 us; the launch traced here: 84.7 us
  waiting for transfers between devices  40.7 us (48%)
  starting transfers between devices  26.7 us (31%)
  Pallas kernels  12.8 us (15%)
  local copies, waits for them, and re-layouts  2.78 us (3%)
    ppermute x21, waiting for transfers between devices, swap(): return lax.ppermute(x, bits, perm)  40.7 us
    ppermute x21, starting transfers between devices, swap(): return lax.ppermute(x, bits, perm)  26.7 us
    pallas_call x7, Pallas kernels, call(): pl.pallas_call(kernel, out_shape=shapes, in_specs=[SMEM if x.dtype == jnp...  10.6 us
    unnamed x8, local copies, waits for them, and re-layouts  2.78 us
    pallas_call x1, Pallas kernels, local(): pl.pallas_call(send_kernel, out_shape=[whole, whole], in_specs=[pl.BlockS...  2.18 us
  transfers between devices with their start and end apart: 21, of which 8 were waited for; matrix products, arithmetic and copies ran while one was open for 1% of the time, Pallas kernels for 4%

profile of v12, /device:TPU:0, one launch (start us, length us, event | category | flops | bytes accessed | tf_op | source)
XLA Modules:
  0.0 84.7 jit_solution(16974277192021402893)
XLA Ops:
  0.6 2.2 %shard_map.67 = (bf16[128,1792]{1,0:T(8,128)(2,1)}, bf16[128,1792]{1,0:T(8,128)(2,1)}) custom-call(bf16[128,1280]{1,0:T(8,128)(2,1)} %teacher, bf16[128,512]{1,0:T(8,128)(2,1)} %student, bf16[128,1280]{1,0:T(8,128)(2,1)} %teacher.1, bf16[128,512]{1,0:T(8,128)(2,1)} %student.1), custom_call_target="tpu_custom_call" | custom-call | tf_op jit(solution)/shard_map/pallas_call | solution.py:294
  2.8 4.1 %collective-permute-start.2 = (bf16[128,1792]{1,0:T(8,128)(2,1)}, bf16[128,1792]{1,0:T(8,128)(2,1)S(1)}, u32[]{:S(2)}, u32[]{:S(2)}) collective-permute-start(bf16[128,1792]{1,0:T(8,128)(2,1)} %get-tuple-element.41), channel_id=1, source_target_pairs={{0,16},{16,0},{1,17},{17,1},{2,18},{18,2},{3,19},{19,3},{4,20},{20... | collective-permute-start | bytes 1376264 | tf_op jit(solution)/shard_map/ppermute | solution.py:255
  6.9 1.5 %collective-permute-start = (bf16[128,1792]{1,0:T(8,128)(2,1)}, bf16[128,1792]{1,0:T(8,128)(2,1)S(1)}, u32[]{:S(2)}, u32[]{:S(2)}) collective-permute-start(bf16[128,1792]{1,0:T(8,128)(2,1)} %get-tuple-element.41), channel_id=1, source_target_pairs={{0,4},{4,0},{1,5},{5,1},{2,6},{6,2},{3,7},{7,3},{8,12},{12,8},{9,1... | collective-permute-start | bytes 1376264 | tf_op jit(solution)/shard_map/ppermute | solution.py:255
  8.4 1.6 %collective-permute-start.8 = (bf16[128,1792]{1,0:T(8,128)(2,1)}, bf16[128,1792]{1,0:T(8,128)(2,1)S(1)}, u32[]{:S(2)}, u32[]{:S(2)}) collective-permute-start(bf16[128,1792]{1,0:T(8,128)(2,1)} %get-tuple-element.38), channel_id=1, source_target_pairs={{0,8},{8,0},{1,9},{9,1},{2,10},{10,2},{3,11},{11,3},{4,12},{12,4},... | collective-permute-start | bytes 1376264 | tf_op jit(solution)/shard_map/ppermute | solution.py:255
  10.0 1.5 %collective-permute-start.1 = (bf16[128,1792]{1,0:T(8,128)(2,1)}, bf16[128,1792]{1,0:T(8,128)(2,1)S(1)}, u32[]{:S(2)}, u32[]{:S(2)}) collective-permute-start(bf16[128,1792]{1,0:T(8,128)(2,1)} %get-tuple-element.38), channel_id=1, source_target_pairs={{0,2},{2,0},{1,3},{3,1},{4,6},{6,4},{5,7},{7,5},{8,10},{10,8},{9,1... | collective-permute-start | bytes 1376264 | tf_op jit(solution)/shard_map/ppermute | solution.py:255
  11.5 16.1 %collective-permute-done.2.refs_1_ = bf16[128,1792]{1,0:T(8,128)(2,1)S(1)} collective-permute-done((bf16[128,1792]{1,0:T(8,128)(2,1)}, bf16[128,1792]{1,0:T(8,128)(2,1)S(1)}, u32[]{:S(2)}, u32[]{:S(2)}) %collective-permute-start.2) | collective-permute-done | bytes 458784 | tf_op jit(solution)/shard_map/ppermute | solution.py:255
  27.6 1.6 %collective-permute-start.3 = (bf16[128,1792]{1,0:T(8,128)(2,1)S(1)}, bf16[128,1792]{1,0:T(8,128)(2,1)S(1)}, u32[]{:S(2)}, u32[]{:S(2)}) collective-permute-start(bf16[128,1792]{1,0:T(8,128)(2,1)S(1)} %collective-permute-done.2.refs_1_), channel_id=1, source_target_pairs={{0,4},{4,0},{1,5},{5,1},{2,6},{6,2},{3,7},{7,3},{8,12},{12,8},{9,1... | collective-permute-start | bytes 1376264 | tf_op jit(solution)/shard_map/ppermute | solution.py:255
  29.2 0.5 collective-permute-start.5
  29.7 1.5 %collective-permute-start.9 = (bf16[128,1792]{1,0:T(8,128)(2,1)S(1)}, bf16[128,1792]{1,0:T(8,128)(2,1)}, u32[]{:S(2)}, u32[]{:S(2)}) collective-permute-start(bf16[128,1792]{1,0:T(8,128)(2,1)S(1)} %collective-permute-done.8.refs_9_), channel_id=1, source_target_pairs={{0,2},{2,0},{1,3},{3,1},{4,6},{6,4},{5,7},{7,5},{8,10},{10,8},{9,1... | collective-permute-start | bytes 1376264 | tf_op jit(solution)/shard_map/ppermute | solution.py:255
  31.2 8.1 %collective-permute-done.3.refs_3_ = bf16[128,1792]{1,0:T(8,128)(2,1)S(1)} collective-permute-done((bf16[128,1792]{1,0:T(8,128)(2,1)S(1)}, bf16[128,1792]{1,0:T(8,128)(2,1)S(1)}, u32[]{:S(2)}, u32[]{:S(2)}) %collective-permute-start.3) | collective-permute-done | bytes 458784 | tf_op jit(solution)/shard_map/ppermute | solution.py:255
  39.3 1.0 %copy-done = bf16[128,1280]{1,0:T(8,128)(2,1)S(1)} copy-done((bf16[128,1280]{1,0:T(8,128)(2,1)S(1)}, bf16[128,1280]{1,0:T(8,128)(2,1)}, u32[]{:S(2)}) %copy-start) | copy-done | bytes 327704
  40.3 0.9 %copy-done.2 = bf16[128,512]{1,0:T(8,128)(2,1)S(1)} copy-done((bf16[128,512]{1,0:T(8,128)(2,1)S(1)}, bf16[128,512]{1,0:T(8,128)(2,1)}, u32[]{:S(2)}) %copy-start.2) | copy-done | bytes 131096
  41.3 0.9 %copy-done.3 = bf16[128,512]{1,0:T(8,128)(2,1)S(1)} copy-done((bf16[128,512]{1,0:T(8,128)(2,1)S(1)}, bf16[128,512]{1,0:T(8,128)(2,1)}, u32[]{:S(2)}) %copy-start.3) | copy-done | bytes 131096
  42.2 4.2 %shard_map.70 = (f32[1024,512]{1,0:T(8,128)S(1)}, f32[1024,512]{1,0:T(8,128)S(1)}, f32[8,1024]{1,0:T(8,128)S(1)}, f32[8,1024]{1,0:T(8,128)S(1)}, f32[8,512]{1,0:...) custom-call(s32[3]{0:T(128)S(1)} %pad_add_fusion.core.place, ...), custom_call_target="tpu_custom_call" | custom-call | flops 1879048192 | bytes 11354124 | tf_op jit(solution)/shard_map/pallas_call | solution.py:242
  46.4 0.5 collective-permute-start.10
  47.0 0.9 %collective-permute-done.10 = f32[8,1024]{1,0:T(8,128)S(1)} collective-permute-done((f32[8,1024]{1,0:T(8,128)S(1)}, f32[8,1024]{1,0:T(8,128)S(1)}, u32[]{:S(2)}, u32[]{:S(2)}) %collective-permute-start.10) | collective-permute-done | bytes 32800 | tf_op jit(solution)/shard_map/ppermute | solution.py:255
  47.8 1.4 %shard_map.71.refs_6_ = f32[8,512]{1,0:T(8,128)S(1)} custom-call(f32[1024,512]{1,0:T(8,128)S(1)} %get-tuple-element.46.tl_ref.refs_1_, f32[1024,512]{1,0:T(8,128)S(1)} %get-tuple-element.47.sl_ref.refs_2_, f32[8,512]{1,0:T(8,128)S(1)} %get-tuple-element.50.peaks, bf16[1024,512]{1,0:T(8,128)(2,1)S(1)} %get-tuple-element.44.image), custom_call_target="tpu_custom_call" | custom-call | bytes 5275648 | tf_op jit(solution)/shard_map/pallas_call | solution.py:242
  49.2 4.9 %collective-permute-start.13 = (f32[8,512]{1,0:T(8,128)S(1)}, f32[8,512]{1,0:T(8,128)S(1)}, u32[]{:S(2)}, u32[]{:S(2)}) collective-permute-start(f32[8,512]{1,0:T(8,128)S(1)} %shard_map.71.refs_6_), channel_id=1, source_target_pairs={{0,8},{8,0},{1,9},{9,1},{2,10},{10,2},{3,11},{11,3},{4,12},{12,4},... | collective-permute-start | bytes 49160 | tf_op jit(solution)/shard_map/ppermute | solution.py:255
  54.1 1.5 %collective-permute-start.12 = (f32[16,1024]{1,0:T(8,128)S(1)}, f32[16,1024]{1,0:T(8,128)S(1)}, u32[]{:S(2)}, u32[]{:S(2)}) collective-permute-start(f32[16,1024]{1,0:T(8,128)S(1)} %pad_maximum_fusion.2), channel_id=1, source_target_pairs={{0,4},{4,0},{1,5},{5,1},{2,6},{6,2},{3,7},{7,3},{8,12},{12,8},{9,1... | collective-permute-start | bytes 196616 | tf_op jit(solution)/shard_map/ppermute | solution.py:255
  55.7 0.2 collective-permute-done.13.refs_7_
  55.8 1.5 %collective-permute-start.14 = (f32[16,512]{1,0:T(8,128)S(1)}, f32[16,512]{1,0:T(8,128)S(1)}, u32[]{:S(2)}, u32[]{:S(2)}) collective-permute-start(f32[16,512]{1,0:T(8,128)S(1)} %pad_maximum_fusion.3), channel_id=1, source_target_pairs={{0,2},{2,0},{1,3},{3,1},{4,6},{6,4},{5,7},{7,5},{8,10},{10,8},{9,1... | collective-permute-start | bytes 98312 | tf_op jit(solution)/shard_map/ppermute | solution.py:255
  57.3 2.4 %collective-permute-done.14.refs_8_ = f32[16,512]{1,0:T(8,128)S(1)} collective-permute-done((f32[16,512]{1,0:T(8,128)S(1)}, f32[16,512]{1,0:T(8,128)S(1)}, u32[]{:S(2)}, u32[]{:S(2)}) %collective-permute-start.14) | collective-permute-done | bytes 32800 | tf_op jit(solution)/shard_map/ppermute | solution.py:255
  59.8 2.3 %shard_map.72 = (f32[272,512]{1,0:T(8,128)S(1)}, f32[272,512]{1,0:T(8,128)S(1)}, bf16[1024,512]{1,0:T(8,128)(2,1)S(1)}, bf16[1024,512]{1,0:T(8,128)(2,1)S(1)}, f...) custom-call(s32[3]{0:T(128)S(1)} %pad_add_fusion.core.place, ...), custom_call_target="tpu_custom_call" | custom-call | flops 536870912 | bytes 8212492 | tf_op jit(solution)/shard_map/pallas_call | solution.py:242
  62.2 0.5 collective-permute-start.15
  62.7 1.8 %shard_map.73 = (f32[272,512]{1,0:T(8,128)S(1)}, f32[272,512]{1,0:T(8,128)S(1)}, f32[272,512]{1,0:T(8,128)S(1)}, f32[272,512]{1,0:T(8,128)S(1)}) custom-call(bf16[1024,512]{1,0:T(8,128)(2,1)S(1)} %get-tuple-element.44.image, bf16[512,512]{1,0:T(8,128)(2,1)S(1)} %get-tuple-element.45.refs_0_.text, bf16[1024,512]{1,0:T(8,128)(2,1)S(1)} %get-tuple-element.51.high_ref, ...), custom_call_target="tpu_custom_call" | custom-call | flops 1610612736 | bytes 5980160 | tf_op jit(solution)/shard_map/pallas_call | solution.py:242
  64.7 1.5 %collective-permute-start.17 = (f16[272,512]{1,0:T(8,128)(2,1)S(1)}, f16[272,512]{1,0:T(8,128)(2,1)S(1)}, u32[]{:S(2)}, u32[]{:S(2)}) collective-permute-start(f16[272,512]{1,0:T(8,128)(2,1)S(1)} %add_convert_fusion), channel_id=1, source_target_pairs={{0,4},{4,0},{1,5},{5,1},{2,6},{6,2},{3,7},{7,3},{8,12},{12,8},{9,1... | collective-permute-start | bytes 835592 | tf_op jit(solution)/shard_map/ppermute | solution.py:255
  66.2 1.5 %collective-permute-start.18 = (f16[272,512]{1,0:T(8,128)(2,1)S(1)}, f16[272,512]{1,0:T(8,128)(2,1)S(1)}, u32[]{:S(2)}, u32[]{:S(2)}) collective-permute-start(f16[272,512]{1,0:T(8,128)(2,1)S(1)} %convert_element_type.21), channel_id=1, source_target_pairs={{0,2},{2,0},{1,3},{3,1},{4,6},{6,4},{5,7},{7,5},{8,10},{10,8},{9,1... | collective-permute-start | bytes 835592 | tf_op jit(solution)/shard_map/ppermute | solution.py:255
  67.8 5.6 %collective-permute-done.17 = f16[272,512]{1,0:T(8,128)(2,1)S(1)} collective-permute-done((f16[272,512]{1,0:T(8,128)(2,1)S(1)}, f16[272,512]{1,0:T(8,128)(2,1)S(1)}, u32[]{:S(2)}, u32[]{:S(2)}) %collective-permute-start.17) | collective-permute-done | bytes 278560 | tf_op jit(solution)/shard_map/ppermute | solution.py:255
  73.5 1.0 %collective-permute-done.18 = f16[272,512]{1,0:T(8,128)(2,1)S(1)} collective-permute-done((f16[272,512]{1,0:T(8,128)(2,1)S(1)}, f16[272,512]{1,0:T(8,128)(2,1)S(1)}, u32[]{:S(2)}, u32[]{:S(2)}) %collective-permute-start.18) | collective-permute-done | bytes 278560 | tf_op jit(solution)/shard_map/ppermute | solution.py:255
  75.0 2.3 %collective-permute-start.20 = (f16[144,512]{1,0:T(8,128)(2,1)S(1)}, f16[144,512]{1,0:T(8,128)(2,1)S(1)}, u32[]{:S(2)}, u32[]{:S(2)}) collective-permute-start(f16[144,512]{1,0:T(8,128)(2,1)S(1)} %get-tuple-element.66), channel_id=1, source_target_pairs={{0,8},{8,0},{1,9},{9,1},{2,10},{10,2},{3,11},{11,3},{4,12},{12,4},... | collective-permute-start | bytes 442376 | tf_op jit(solution)/shard_map/ppermute | solution.py:255
  77.3 6.5 %collective-permute-done.19 = f16[144,512]{1,0:T(8,128)(2,1)S(1)} collective-permute-done((f16[144,512]{1,0:T(8,128)(2,1)S(1)}, f16[144,512]{1,0:T(8,128)(2,1)S(1)}, u32[]{:S(2)}, u32[]{:S(2)}) %collective-permute-start.19) | collective-permute-done | bytes 147488 | tf_op jit(solution)/shard_map/ppermute | solution.py:255
  83.8 0.9 %shard_map.74 = (f32[128,512]{1,0:T(8,128)}, f32[128,512]{1,0:T(8,128)}, f32[1,1]{1,0:T(1,128)}) custom-call(f32[128,512]{1,0:T(8,128)S(1)} %get-tuple-element.78.refs_0_, f32[16,512]{1,0:T(8,128)S(1)} %get-tuple-element.74.refs_1_, f32[144,512]{1,0:T(8,128)S(1)} %convert_element_type.24.refs_2_, f32[1,512]{1,0:T(1,128)S(1)} %get-tuple-element.65.refs_3_, ...), custom_call_target="tpu_custom_call" | custom-call | bytes 1708036 | tf_op jit(solution)/shard_map/pallas_call | solution.py:242
  (44 shorter events, 1.1 us)
Async XLA Ops:
  0.6 40.6 %copy-start.1 = (bf16[128,1280]{1,0:T(8,128)(2,1)S(1)}, bf16[128,1280]{1,0:T(8,128)(2,1)}, u32[]{:S(2)}) copy-start(bf16[128,1280]{1,0:T(8,128)(2,1)} %teacher.1) | copy-start | bytes 983044
  2.8 24.8 %collective-permute-start.2 = (bf16[128,1792]{1,0:T(8,128)(2,1)}, bf16[128,1792]{1,0:T(8,128)(2,1)S(1)}, u32[]{:S(2)}, u32[]{:S(2)}) collective-permute-start(bf16[128,1792]{1,0:T(8,128)(2,1)} %get-tuple-element.41), channel_id=1, source_target_pairs={{0,16},{16,0},{1,17},{17,1},{2,18},{18,2},{3,19},{19,3},{4,20},{20... | collective-permute-start | bytes 1376264 | tf_op jit(solution)/shard_map/ppermute | solution.py:255
  6.9 22.2 %collective-permute-start = (bf16[128,1792]{1,0:T(8,128)(2,1)}, bf16[128,1792]{1,0:T(8,128)(2,1)S(1)}, u32[]{:S(2)}, u32[]{:S(2)}) collective-permute-start(bf16[128,1792]{1,0:T(8,128)(2,1)} %get-tuple-element.41), channel_id=1, source_target_pairs={{0,4},{4,0},{1,5},{5,1},{2,6},{6,2},{3,7},{7,3},{8,12},{12,8},{9,1... | collective-permute-start | bytes 1376264 | tf_op jit(solution)/shard_map/ppermute | solution.py:255
  8.4 21.2 %collective-permute-start.8 = (bf16[128,1792]{1,0:T(8,128)(2,1)}, bf16[128,1792]{1,0:T(8,128)(2,1)S(1)}, u32[]{:S(2)}, u32[]{:S(2)}) collective-permute-start(bf16[128,1792]{1,0:T(8,128)(2,1)} %get-tuple-element.38), channel_id=1, source_target_pairs={{0,8},{8,0},{1,9},{9,1},{2,10},{10,2},{3,11},{11,3},{4,12},{12,4},... | collective-permute-start | bytes 1376264 | tf_op jit(solution)/shard_map/ppermute | solution.py:255
  10.0 21.2 %collective-permute-start.1 = (bf16[128,1792]{1,0:T(8,128)(2,1)}, bf16[128,1792]{1,0:T(8,128)(2,1)S(1)}, u32[]{:S(2)}, u32[]{:S(2)}) collective-permute-start(bf16[128,1792]{1,0:T(8,128)(2,1)} %get-tuple-element.38), channel_id=1, source_target_pairs={{0,2},{2,0},{1,3},{3,1},{4,6},{6,4},{5,7},{7,5},{8,10},{10,8},{9,1... | collective-permute-start | bytes 1376264 | tf_op jit(solution)/shard_map/ppermute | solution.py:255
  27.6 11.6 %collective-permute-start.3 = (bf16[128,1792]{1,0:T(8,128)(2,1)S(1)}, bf16[128,1792]{1,0:T(8,128)(2,1)S(1)}, u32[]{:S(2)}, u32[]{:S(2)}) collective-permute-start(bf16[128,1792]{1,0:T(8,128)(2,1)S(1)} %collective-permute-done.2.refs_1_), channel_id=1, source_target_pairs={{0,4},{4,0},{1,5},{5,1},{2,6},{6,2},{3,7},{7,3},{8,12},{12,8},{9,1... | collective-permute-start | bytes 1376264 | tf_op jit(solution)/shard_map/ppermute | solution.py:255
  29.2 13.1 %collective-permute-start.4 = (bf16[128,1792]{1,0:T(8,128)(2,1)}, bf16[128,1792]{1,0:T(8,128)(2,1)S(1)}, u32[]{:S(2)}, u32[]{:S(2)}) collective-permute-start(bf16[128,1792]{1,0:T(8,128)(2,1)} %get-tuple-element.41), channel_id=1, source_target_pairs={{0,1},{1,0},{2,3},{3,2},{4,5},{5,4},{6,7},{7,6},{8,9},{9,8},{10,11... | collective-permute-start | bytes 1376264 | tf_op jit(solution)/shard_map/ppermute | solution.py:255
  29.2 13.0 %collective-permute-start.5 = (bf16[128,1792]{1,0:T(8,128)(2,1)S(1)}, bf16[128,1792]{1,0:T(8,128)(2,1)S(1)}, u32[]{:S(2)}, u32[]{:S(2)}) collective-permute-start(bf16[128,1792]{1,0:T(8,128)(2,1)S(1)} %collective-permute-done.2.refs_1_), channel_id=1, source_target_pairs={{0,1},{1,0},{2,3},{3,2},{4,5},{5,4},{6,7},{7,6},{8,9},{9,8},{10,11... | collective-permute-start | bytes 1376264 | tf_op jit(solution)/shard_map/ppermute | solution.py:255
  29.7 12.5 %collective-permute-start.9 = (bf16[128,1792]{1,0:T(8,128)(2,1)S(1)}, bf16[128,1792]{1,0:T(8,128)(2,1)}, u32[]{:S(2)}, u32[]{:S(2)}) collective-permute-start(bf16[128,1792]{1,0:T(8,128)(2,1)S(1)} %collective-permute-done.8.refs_9_), channel_id=1, source_target_pairs={{0,2},{2,0},{1,3},{3,1},{4,6},{6,4},{5,7},{7,5},{8,10},{10,8},{9,1... | collective-permute-start | bytes 1376264 | tf_op jit(solution)/shard_map/ppermute | solution.py:255
  31.2 11.0 %collective-permute-start.6 = (bf16[128,1792]{1,0:T(8,128)(2,1)S(1)}, bf16[128,1792]{1,0:T(8,128)(2,1)}, u32[]{:S(2)}, u32[]{:S(2)}) collective-permute-start(bf16[128,1792]{1,0:T(8,128)(2,1)S(1)} %collective-permute-done.refs_2_), channel_id=1, source_target_pairs={{0,1},{1,0},{2,3},{3,2},{4,5},{5,4},{6,7},{7,6},{8,9},{9,8},{10,11... | collective-permute-start | bytes 1376264 | tf_op jit(solution)/shard_map/ppermute | solution.py:255
  39.2 3.0 %collective-permute-start.7 = (bf16[128,1792]{1,0:T(8,128)(2,1)S(1)}, bf16[128,1792]{1,0:T(8,128)(2,1)}, u32[]{:S(2)}, u32[]{:S(2)}) collective-permute-start(bf16[128,1792]{1,0:T(8,128)(2,1)S(1)} %collective-permute-done.3.refs_3_), channel_id=1, source_target_pairs={{0,1},{1,0},{2,3},{3,2},{4,5},{5,4},{6,7},{7,6},{8,9},{9,8},{10,11... | collective-permute-start | bytes 1376264 | tf_op jit(solution)/shard_map/ppermute | solution.py:255
  39.3 1.0 %copy-start = (bf16[128,1280]{1,0:T(8,128)(2,1)S(1)}, bf16[128,1280]{1,0:T(8,128)(2,1)}, u32[]{:S(2)}) copy-start(bf16[128,1280]{1,0:T(8,128)(2,1)} %teacher) | copy-start | bytes 983044
  40.3 0.9 %copy-start.2 = (bf16[128,512]{1,0:T(8,128)(2,1)S(1)}, bf16[128,512]{1,0:T(8,128)(2,1)}, u32[]{:S(2)}) copy-start(bf16[128,512]{1,0:T(8,128)(2,1)} %student) | copy-start | bytes 393220
  41.2 0.9 %copy-start.3 = (bf16[128,512]{1,0:T(8,128)(2,1)S(1)}, bf16[128,512]{1,0:T(8,128)(2,1)}, u32[]{:S(2)}) copy-start(bf16[128,512]{1,0:T(8,128)(2,1)} %student.1) | copy-start | bytes 393220
  46.4 1.4 %collective-permute-start.10 = (f32[8,1024]{1,0:T(8,128)S(1)}, f32[8,1024]{1,0:T(8,128)S(1)}, u32[]{:S(2)}, u32[]{:S(2)}) collective-permute-start(f32[8,1024]{1,0:T(8,128)S(1)} %get-tuple-element.49), channel_id=1, source_target_pairs={{0,1},{1,0},{2,3},{3,2},{4,5},{5,4},{6,7},{7,6},{8,9},{9,8},{10,11... | collective-permute-start | bytes 98312 | tf_op jit(solution)/shard_map/ppermute | solution.py:255
  47.8 6.3 %collective-permute-start.11 = (f32[8,1024]{1,0:T(8,128)S(1)}, f32[8,1024]{1,0:T(8,128)S(1)}, u32[]{:S(2)}, u32[]{:S(2)}) collective-permute-start(f32[8,1024]{1,0:T(8,128)S(1)} %add.33.refs_3_), channel_id=1, source_target_pairs={{0,16},{16,0},{1,17},{17,1},{2,18},{18,2},{3,19},{19,3},{4,20},{20... | collective-permute-start | bytes 98312 | tf_op jit(solution)/shard_map/ppermute | solution.py:255
  49.2 6.6 %collective-permute-start.13 = (f32[8,512]{1,0:T(8,128)S(1)}, f32[8,512]{1,0:T(8,128)S(1)}, u32[]{:S(2)}, u32[]{:S(2)}) collective-permute-start(f32[8,512]{1,0:T(8,128)S(1)} %shard_map.71.refs_6_), channel_id=1, source_target_pairs={{0,8},{8,0},{1,9},{9,1},{2,10},{10,2},{3,11},{11,3},{4,12},{12,4},... | collective-permute-start | bytes 49160 | tf_op jit(solution)/shard_map/ppermute | solution.py:255
  54.1 5.6 %collective-permute-start.12 = (f32[16,1024]{1,0:T(8,128)S(1)}, f32[16,1024]{1,0:T(8,128)S(1)}, u32[]{:S(2)}, u32[]{:S(2)}) collective-permute-start(f32[16,1024]{1,0:T(8,128)S(1)} %pad_maximum_fusion.2), channel_id=1, source_target_pairs={{0,4},{4,0},{1,5},{5,1},{2,6},{6,2},{3,7},{7,3},{8,12},{12,8},{9,1... | collective-permute-start | bytes 196616 | tf_op jit(solution)/shard_map/ppermute | solution.py:255
  55.8 3.9 %collective-permute-start.14 = (f32[16,512]{1,0:T(8,128)S(1)}, f32[16,512]{1,0:T(8,128)S(1)}, u32[]{:S(2)}, u32[]{:S(2)}) collective-permute-start(f32[16,512]{1,0:T(8,128)S(1)} %pad_maximum_fusion.3), channel_id=1, source_target_pairs={{0,2},{2,0},{1,3},{3,1},{4,6},{6,4},{5,7},{7,5},{8,10},{10,8},{9,1... | collective-permute-start | bytes 98312 | tf_op jit(solution)/shard_map/ppermute | solution.py:255
  62.1 2.4 %collective-permute-start.16 = (f32[272,512]{1,0:T(8,128)S(1)}, f32[272,512]{1,0:T(8,128)S(1)}, u32[]{:S(2)}, u32[]{:S(2)}) collective-permute-start(f32[272,512]{1,0:T(8,128)S(1)} %get-tuple-element.59), channel_id=1, source_target_pairs={{0,1},{1,0},{2,3},{3,2},{4,5},{5,4},{6,7},{7,6},{8,9},{9,8},{10,11... | collective-permute-start | bytes 1671176 | tf_op jit(solution)/shard_map/ppermute | solution.py:255
  62.2 5.5 %collective-permute-start.15 = (f32[272,512]{1,0:T(8,128)S(1)}, f32[272,512]{1,0:T(8,128)S(1)}, u32[]{:S(2)}, u32[]{:S(2)}) collective-permute-start(f32[272,512]{1,0:T(8,128)S(1)} %get-tuple-element.57), channel_id=1, source_target_pairs={{0,1},{1,0},{2,3},{3,2},{4,5},{5,4},{6,7},{7,6},{8,9},{9,8},{10,11... | collective-permute-start | bytes 1671176 | tf_op jit(solution)/shard_map/ppermute | solution.py:255
  64.7 8.7 %collective-permute-start.17 = (f16[272,512]{1,0:T(8,128)(2,1)S(1)}, f16[272,512]{1,0:T(8,128)(2,1)S(1)}, u32[]{:S(2)}, u32[]{:S(2)}) collective-permute-start(f16[272,512]{1,0:T(8,128)(2,1)S(1)} %add_convert_fusion), channel_id=1, source_target_pairs={{0,4},{4,0},{1,5},{5,1},{2,6},{6,2},{3,7},{7,3},{8,12},{12,8},{9,1... | collective-permute-start | bytes 835592 | tf_op jit(solution)/shard_map/ppermute | solution.py:255
  66.2 8.4 %collective-permute-start.18 = (f16[272,512]{1,0:T(8,128)(2,1)S(1)}, f16[272,512]{1,0:T(8,128)(2,1)S(1)}, u32[]{:S(2)}, u32[]{:S(2)}) collective-permute-start(f16[272,512]{1,0:T(8,128)(2,1)S(1)} %convert_element_type.21), channel_id=1, source_target_pairs={{0,2},{2,0},{1,3},{3,1},{4,6},{6,4},{5,7},{7,5},{8,10},{10,8},{9,1... | collective-permute-start | bytes 835592 | tf_op jit(solution)/shard_map/ppermute | solution.py:255
  74.9 8.8 %collective-permute-start.19 = (f16[144,512]{1,0:T(8,128)(2,1)S(1)}, f16[144,512]{1,0:T(8,128)(2,1)S(1)}, u32[]{:S(2)}, u32[]{:S(2)}) collective-permute-start(f16[144,512]{1,0:T(8,128)(2,1)S(1)} %get-tuple-element.64), channel_id=1, source_target_pairs={{0,16},{16,0},{1,17},{17,1},{2,18},{18,2},{3,19},{19,3},{4,20},{20... | collective-permute-start | bytes 442376 | tf_op jit(solution)/shard_map/ppermute | solution.py:255
  75.0 8.8 %collective-permute-start.20 = (f16[144,512]{1,0:T(8,128)(2,1)S(1)}, f16[144,512]{1,0:T(8,128)(2,1)S(1)}, u32[]{:S(2)}, u32[]{:S(2)}) collective-permute-start(f16[144,512]{1,0:T(8,128)(2,1)S(1)} %get-tuple-element.66), channel_id=1, source_target_pairs={{0,8},{8,0},{1,9},{9,1},{2,10},{10,2},{3,11},{11,3},{4,12},{12,4},... | collective-permute-start | bytes 442376 | tf_op jit(solution)/shard_map/ppermute | solution.py:255

commit v13 on v12

--- a/solution.py
+++ b/solution.py
@@ -62,7 +62,7 @@
             return flat
         return flat + stack_rows((largest[:, block(k, b)],), flat.shape, 0, 2 * KINDS + core[0])
 
-    step = 2 if nr % 2 == 0 else 1
+    step = math.gcd(nr, 4)
     count = step * b
     peak_t = peak_s = None
     for p in range(0, nr, step):

time: 84.9 us -> 85.1 us (level)
  no operation moved by 1% of the time
where the time goes in v13:
time: 85.1 us; the launch traced here: 84.8 us
  waiting for transfers between devices  40.7 us (48%)
  starting transfers between devices  26.7 us (31%)
  Pallas kernels  12.9 us (15%)
  local copies, waits for them, and re-layouts  2.78 us (3%)
    ppermute x21, waiting for transfers between devices, swap(): return lax.ppermute(x, bits, perm)  40.7 us
    ppermute x21, starting transfers between devices, swap(): return lax.ppermute(x, bits, perm)  26.7 us
    pallas_call x7, Pallas kernels, call(): pl.pallas_call(kernel, out_shape=shapes, in_specs=[SMEM if x.dtype == jnp...  10.8 us
    unnamed x8, local copies, waits for them, and re-layouts  2.78 us
    pallas_call x1, Pallas kernels, local(): pl.pallas_call(send_kernel, out_shape=[whole, whole], in_specs=[pl.BlockS...  2.18 us
  transfers between devices with their start and end apart: 21, of which 8 were waited for; matrix products, arithmetic and copies ran while one was open for 1% of the time, Pallas kernels for 4%

profile of v13, /device:TPU:0, one launch (start us, length us, event | category | flops | bytes accessed | tf_op | source)
XLA Modules:
  0.0 84.8 jit_solution(396074233897690894)
XLA Ops:
  0.6 2.2 %shard_map.67 = (bf16[128,1792]{1,0:T(8,128)(2,1)}, bf16[128,1792]{1,0:T(8,128)(2,1)}) custom-call(bf16[128,1280]{1,0:T(8,128)(2,1)} %teacher, bf16[128,512]{1,0:T(8,128)(2,1)} %student, bf16[128,1280]{1,0:T(8,128)(2,1)} %teacher.1, bf16[128,512]{1,0:T(8,128)(2,1)} %student.1), custom_call_target="tpu_custom_call" | custom-call | tf_op jit(solution)/shard_map/pallas_call | solution.py:294
  2.8 4.1 %collective-permute-start.2 = (bf16[128,1792]{1,0:T(8,128)(2,1)}, bf16[128,1792]{1,0:T(8,128)(2,1)S(1)}, u32[]{:S(2)}, u32[]{:S(2)}) collective-permute-start(bf16[128,1792]{1,0:T(8,128)(2,1)} %get-tuple-element.41), channel_id=1, source_target_pairs={{0,16},{16,0},{1,17},{17,1},{2,18},{18,2},{3,19},{19,3},{4,20},{20... | collective-permute-start | bytes 1376264 | tf_op jit(solution)/shard_map/ppermute | solution.py:255
  6.9 1.5 %collective-permute-start = (bf16[128,1792]{1,0:T(8,128)(2,1)}, bf16[128,1792]{1,0:T(8,128)(2,1)S(1)}, u32[]{:S(2)}, u32[]{:S(2)}) collective-permute-start(bf16[128,1792]{1,0:T(8,128)(2,1)} %get-tuple-element.41), channel_id=1, source_target_pairs={{0,4},{4,0},{1,5},{5,1},{2,6},{6,2},{3,7},{7,3},{8,12},{12,8},{9,1... | collective-permute-start | bytes 1376264 | tf_op jit(solution)/shard_map/ppermute | solution.py:255
  8.4 1.6 %collective-permute-start.8 = (bf16[128,1792]{1,0:T(8,128)(2,1)}, bf16[128,1792]{1,0:T(8,128)(2,1)S(1)}, u32[]{:S(2)}, u32[]{:S(2)}) collective-permute-start(bf16[128,1792]{1,0:T(8,128)(2,1)} %get-tuple-element.38), channel_id=1, source_target_pairs={{0,8},{8,0},{1,9},{9,1},{2,10},{10,2},{3,11},{11,3},{4,12},{12,4},... | collective-permute-start | bytes 1376264 | tf_op jit(solution)/shard_map/ppermute | solution.py:255
  10.0 1.5 %collective-permute-start.1 = (bf16[128,1792]{1,0:T(8,128)(2,1)}, bf16[128,1792]{1,0:T(8,128)(2,1)S(1)}, u32[]{:S(2)}, u32[]{:S(2)}) collective-permute-start(bf16[128,1792]{1,0:T(8,128)(2,1)} %get-tuple-element.38), channel_id=1, source_target_pairs={{0,2},{2,0},{1,3},{3,1},{4,6},{6,4},{5,7},{7,5},{8,10},{10,8},{9,1... | collective-permute-start | bytes 1376264 | tf_op jit(solution)/shard_map/ppermute | solution.py:255
  11.5 16.1 %collective-permute-done.2.refs_1_ = bf16[128,1792]{1,0:T(8,128)(2,1)S(1)} collective-permute-done((bf16[128,1792]{1,0:T(8,128)(2,1)}, bf16[128,1792]{1,0:T(8,128)(2,1)S(1)}, u32[]{:S(2)}, u32[]{:S(2)}) %collective-permute-start.2) | collective-permute-done | bytes 458784 | tf_op jit(solution)/shard_map/ppermute | solution.py:255
  27.6 1.6 %collective-permute-start.3 = (bf16[128,1792]{1,0:T(8,128)(2,1)S(1)}, bf16[128,1792]{1,0:T(8,128)(2,1)S(1)}, u32[]{:S(2)}, u32[]{:S(2)}) collective-permute-start(bf16[128,1792]{1,0:T(8,128)(2,1)S(1)} %collective-permute-done.2.refs_1_), channel_id=1, source_target_pairs={{0,4},{4,0},{1,5},{5,1},{2,6},{6,2},{3,7},{7,3},{8,12},{12,8},{9,1... | collective-permute-start | bytes 1376264 | tf_op jit(solution)/shard_map/ppermute | solution.py:255
  29.2 0.5 collective-permute-start.5
  29.7 1.5 %collective-permute-start.9 = (bf16[128,1792]{1,0:T(8,128)(2,1)S(1)}, bf16[128,1792]{1,0:T(8,128)(2,1)}, u32[]{:S(2)}, u32[]{:S(2)}) collective-permute-start(bf16[128,1792]{1,0:T(8,128)(2,1)S(1)} %collective-permute-done.8.refs_9_), channel_id=1, source_target_pairs={{0,2},{2,0},{1,3},{3,1},{4,6},{6,4},{5,7},{7,5},{8,10},{10,8},{9,1... | collective-permute-start | bytes 1376264 | tf_op jit(solution)/shard_map/ppermute | solution.py:255
  31.2 8.1 %collective-permute-done.3.refs_3_ = bf16[128,1792]{1,0:T(8,128)(2,1)S(1)} collective-permute-done((bf16[128,1792]{1,0:T(8,128)(2,1)S(1)}, bf16[128,1792]{1,0:T(8,128)(2,1)S(1)}, u32[]{:S(2)}, u32[]{:S(2)}) %collective-permute-start.3) | collective-permute-done | bytes 458784 | tf_op jit(solution)/shard_map/ppermute | solution.py:255
  39.3 1.0 %copy-done = bf16[128,1280]{1,0:T(8,128)(2,1)S(1)} copy-done((bf16[128,1280]{1,0:T(8,128)(2,1)S(1)}, bf16[128,1280]{1,0:T(8,128)(2,1)}, u32[]{:S(2)}) %copy-start) | copy-done | bytes 327704
  40.3 0.9 %copy-done.2 = bf16[128,512]{1,0:T(8,128)(2,1)S(1)} copy-done((bf16[128,512]{1,0:T(8,128)(2,1)S(1)}, bf16[128,512]{1,0:T(8,128)(2,1)}, u32[]{:S(2)}) %copy-start.2) | copy-done | bytes 131096
  41.3 0.9 %copy-done.3 = bf16[128,512]{1,0:T(8,128)(2,1)S(1)} copy-done((bf16[128,512]{1,0:T(8,128)(2,1)S(1)}, bf16[128,512]{1,0:T(8,128)(2,1)}, u32[]{:S(2)}) %copy-start.3) | copy-done | bytes 131096
  42.2 4.3 %shard_map.70 = (f32[1024,512]{1,0:T(8,128)S(1)}, f32[1024,512]{1,0:T(8,128)S(1)}, f32[8,1024]{1,0:T(8,128)S(1)}, f32[8,1024]{1,0:T(8,128)S(1)}, f32[8,512]{1,0:...) custom-call(s32[3]{0:T(128)S(1)} %pad_add_fusion.core.place, ...), custom_call_target="tpu_custom_call" | custom-call | flops 1879048192 | bytes 11354124 | tf_op jit(solution)/shard_map/pallas_call | solution.py:242
  46.6 0.5 collective-permute-start.10
  47.1 0.9 %collective-permute-done.10 = f32[8,1024]{1,0:T(8,128)S(1)} collective-permute-done((f32[8,1024]{1,0:T(8,128)S(1)}, f32[8,1024]{1,0:T(8,128)S(1)}, u32[]{:S(2)}, u32[]{:S(2)}) %collective-permute-start.10) | collective-permute-done | bytes 32800 | tf_op jit(solution)/shard_map/ppermute | solution.py:255
  48.0 1.4 %shard_map.71.refs_6_ = f32[8,512]{1,0:T(8,128)S(1)} custom-call(f32[1024,512]{1,0:T(8,128)S(1)} %get-tuple-element.46.tl_ref.refs_1_, f32[1024,512]{1,0:T(8,128)S(1)} %get-tuple-element.47.sl_ref.refs_2_, f32[8,512]{1,0:T(8,128)S(1)} %get-tuple-element.50.peaks, bf16[1024,512]{1,0:T(8,128)(2,1)S(1)} %get-tuple-element.44.image), custom_call_target="tpu_custom_call" | custom-call | bytes 5275648 | tf_op jit(solution)/shard_map/pallas_call | solution.py:242
  49.4 4.9 %collective-permute-start.13 = (f32[8,512]{1,0:T(8,128)S(1)}, f32[8,512]{1,0:T(8,128)S(1)}, u32[]{:S(2)}, u32[]{:S(2)}) collective-permute-start(f32[8,512]{1,0:T(8,128)S(1)} %shard_map.71.refs_6_), channel_id=1, source_target_pairs={{0,8},{8,0},{1,9},{9,1},{2,10},{10,2},{3,11},{11,3},{4,12},{12,4},... | collective-permute-start | bytes 49160 | tf_op jit(solution)/shard_map/ppermute | solution.py:255
  54.3 1.5 %collective-permute-start.12 = (f32[16,1024]{1,0:T(8,128)S(1)}, f32[16,1024]{1,0:T(8,128)S(1)}, u32[]{:S(2)}, u32[]{:S(2)}) collective-permute-start(f32[16,1024]{1,0:T(8,128)S(1)} %pad_maximum_fusion.2), channel_id=1, source_target_pairs={{0,4},{4,0},{1,5},{5,1},{2,6},{6,2},{3,7},{7,3},{8,12},{12,8},{9,1... | collective-permute-start | bytes 196616 | tf_op jit(solution)/shard_map/ppermute | solution.py:255
  55.8 0.2 collective-permute-done.13.refs_7_
  56.0 1.5 %collective-permute-start.14 = (f32[16,512]{1,0:T(8,128)S(1)}, f32[16,512]{1,0:T(8,128)S(1)}, u32[]{:S(2)}, u32[]{:S(2)}) collective-permute-start(f32[16,512]{1,0:T(8,128)S(1)} %pad_maximum_fusion.3), channel_id=1, source_target_pairs={{0,2},{2,0},{1,3},{3,1},{4,6},{6,4},{5,7},{7,5},{8,10},{10,8},{9,1... | collective-permute-start | bytes 98312 | tf_op jit(solution)/shard_map/ppermute | solution.py:255
  57.5 2.4 %collective-permute-done.14.refs_8_ = f32[16,512]{1,0:T(8,128)S(1)} collective-permute-done((f32[16,512]{1,0:T(8,128)S(1)}, f32[16,512]{1,0:T(8,128)S(1)}, u32[]{:S(2)}, u32[]{:S(2)}) %collective-permute-start.14) | collective-permute-done | bytes 32800 | tf_op jit(solution)/shard_map/ppermute | solution.py:255
  59.9 2.3 %shard_map.72 = (f32[272,512]{1,0:T(8,128)S(1)}, f32[272,512]{1,0:T(8,128)S(1)}, bf16[1024,512]{1,0:T(8,128)(2,1)S(1)}, bf16[1024,512]{1,0:T(8,128)(2,1)S(1)}, f...) custom-call(s32[3]{0:T(128)S(1)} %pad_add_fusion.core.place, ...), custom_call_target="tpu_custom_call" | custom-call | flops 536870912 | bytes 8212492 | tf_op jit(solution)/shard_map/pallas_call | solution.py:242
  62.3 0.5 collective-permute-start.15
  62.8 1.8 %shard_map.73 = (f32[272,512]{1,0:T(8,128)S(1)}, f32[272,512]{1,0:T(8,128)S(1)}, f32[272,512]{1,0:T(8,128)S(1)}, f32[272,512]{1,0:T(8,128)S(1)}) custom-call(bf16[1024,512]{1,0:T(8,128)(2,1)S(1)} %get-tuple-element.44.image, bf16[512,512]{1,0:T(8,128)(2,1)S(1)} %get-tuple-element.45.refs_0_.text, bf16[1024,512]{1,0:T(8,128)(2,1)S(1)} %get-tuple-element.51.high_ref, ...), custom_call_target="tpu_custom_call" | custom-call | flops 1610612736 | bytes 5980160 | tf_op jit(solution)/shard_map/pallas_call | solution.py:242
  64.8 1.5 %collective-permute-start.17 = (f16[272,512]{1,0:T(8,128)(2,1)S(1)}, f16[272,512]{1,0:T(8,128)(2,1)S(1)}, u32[]{:S(2)}, u32[]{:S(2)}) collective-permute-start(f16[272,512]{1,0:T(8,128)(2,1)S(1)} %add_convert_fusion), channel_id=1, source_target_pairs={{0,4},{4,0},{1,5},{5,1},{2,6},{6,2},{3,7},{7,3},{8,12},{12,8},{9,1... | collective-permute-start | bytes 835592 | tf_op jit(solution)/shard_map/ppermute | solution.py:255
  66.4 1.5 %collective-permute-start.18 = (f16[272,512]{1,0:T(8,128)(2,1)S(1)}, f16[272,512]{1,0:T(8,128)(2,1)S(1)}, u32[]{:S(2)}, u32[]{:S(2)}) collective-permute-start(f16[272,512]{1,0:T(8,128)(2,1)S(1)} %convert_element_type.21), channel_id=1, source_target_pairs={{0,2},{2,0},{1,3},{3,1},{4,6},{6,4},{5,7},{7,5},{8,10},{10,8},{9,1... | collective-permute-start | bytes 835592 | tf_op jit(solution)/shard_map/ppermute | solution.py:255
  67.9 5.6 %collective-permute-done.17 = f16[272,512]{1,0:T(8,128)(2,1)S(1)} collective-permute-done((f16[272,512]{1,0:T(8,128)(2,1)S(1)}, f16[272,512]{1,0:T(8,128)(2,1)S(1)}, u32[]{:S(2)}, u32[]{:S(2)}) %collective-permute-start.17) | collective-permute-done | bytes 278560 | tf_op jit(solution)/shard_map/ppermute | solution.py:255
  73.7 1.0 %collective-permute-done.18 = f16[272,512]{1,0:T(8,128)(2,1)S(1)} collective-permute-done((f16[272,512]{1,0:T(8,128)(2,1)S(1)}, f16[272,512]{1,0:T(8,128)(2,1)S(1)}, u32[]{:S(2)}, u32[]{:S(2)}) %collective-permute-start.18) | collective-permute-done | bytes 278560 | tf_op jit(solution)/shard_map/ppermute | solution.py:255
  75.1 2.3 %collective-permute-start.20 = (f16[144,512]{1,0:T(8,128)(2,1)S(1)}, f16[144,512]{1,0:T(8,128)(2,1)S(1)}, u32[]{:S(2)}, u32[]{:S(2)}) collective-permute-start(f16[144,512]{1,0:T(8,128)(2,1)S(1)} %get-tuple-element.66), channel_id=1, source_target_pairs={{0,8},{8,0},{1,9},{9,1},{2,10},{10,2},{3,11},{11,3},{4,12},{12,4},... | collective-permute-start | bytes 442376 | tf_op jit(solution)/shard_map/ppermute | solution.py:255
  77.4 6.5 %collective-permute-done.19 = f16[144,512]{1,0:T(8,128)(2,1)S(1)} collective-permute-done((f16[144,512]{1,0:T(8,128)(2,1)S(1)}, f16[144,512]{1,0:T(8,128)(2,1)S(1)}, u32[]{:S(2)}, u32[]{:S(2)}) %collective-permute-start.19) | collective-permute-done | bytes 147488 | tf_op jit(solution)/shard_map/ppermute | solution.py:255
  84.0 0.9 %shard_map.74 = (f32[128,512]{1,0:T(8,128)}, f32[128,512]{1,0:T(8,128)}, f32[1,1]{1,0:T(1,128)}) custom-call(f32[128,512]{1,0:T(8,128)S(1)} %get-tuple-element.78.refs_0_, f32[16,512]{1,0:T(8,128)S(1)} %get-tuple-element.74.refs_1_, f32[144,512]{1,0:T(8,128)S(1)} %convert_element_type.24.refs_2_, f32[1,512]{1,0:T(1,128)S(1)} %get-tuple-element.65.refs_3_, ...), custom_call_target="tpu_custom_call" | custom-call | bytes 1708036 | tf_op jit(solution)/shard_map/pallas_call | solution.py:242
  (44 shorter events, 1.1 us)
Async XLA Ops:
  0.6 40.6 %copy-start.1 = (bf16[128,1280]{1,0:T(8,128)(2,1)S(1)}, bf16[128,1280]{1,0:T(8,128)(2,1)}, u32[]{:S(2)}) copy-start(bf16[128,1280]{1,0:T(8,128)(2,1)} %teacher.1) | copy-start | bytes 983044
  2.8 24.8 %collective-permute-start.2 = (bf16[128,1792]{1,0:T(8,128)(2,1)}, bf16[128,1792]{1,0:T(8,128)(2,1)S(1)}, u32[]{:S(2)}, u32[]{:S(2)}) collective-permute-start(bf16[128,1792]{1,0:T(8,128)(2,1)} %get-tuple-element.41), channel_id=1, source_target_pairs={{0,16},{16,0},{1,17},{17,1},{2,18},{18,2},{3,19},{19,3},{4,20},{20... | collective-permute-start | bytes 1376264 | tf_op jit(solution)/shard_map/ppermute | solution.py:255
  6.9 22.2 %collective-permute-start = (bf16[128,1792]{1,0:T(8,128)(2,1)}, bf16[128,1792]{1,0:T(8,128)(2,1)S(1)}, u32[]{:S(2)}, u32[]{:S(2)}) collective-permute-start(bf16[128,1792]{1,0:T(8,128)(2,1)} %get-tuple-element.41), channel_id=1, source_target_pairs={{0,4},{4,0},{1,5},{5,1},{2,6},{6,2},{3,7},{7,3},{8,12},{12,8},{9,1... | collective-permute-start | bytes 1376264 | tf_op jit(solution)/shard_map/ppermute | solution.py:255
  8.4 21.2 %collective-permute-start.8 = (bf16[128,1792]{1,0:T(8,128)(2,1)}, bf16[128,1792]{1,0:T(8,128)(2,1)S(1)}, u32[]{:S(2)}, u32[]{:S(2)}) collective-permute-start(bf16[128,1792]{1,0:T(8,128)(2,1)} %get-tuple-element.38), channel_id=1, source_target_pairs={{0,8},{8,0},{1,9},{9,1},{2,10},{10,2},{3,11},{11,3},{4,12},{12,4},... | collective-permute-start | bytes 1376264 | tf_op jit(solution)/shard_map/ppermute | solution.py:255
  10.0 21.2 %collective-permute-start.1 = (bf16[128,1792]{1,0:T(8,128)(2,1)}, bf16[128,1792]{1,0:T(8,128)(2,1)S(1)}, u32[]{:S(2)}, u32[]{:S(2)}) collective-permute-start(bf16[128,1792]{1,0:T(8,128)(2,1)} %get-tuple-element.38), channel_id=1, source_target_pairs={{0,2},{2,0},{1,3},{3,1},{4,6},{6,4},{5,7},{7,5},{8,10},{10,8},{9,1... | collective-permute-start | bytes 1376264 | tf_op jit(solution)/shard_map/ppermute | solution.py:255
  27.6 11.6 %collective-permute-start.3 = (bf16[128,1792]{1,0:T(8,128)(2,1)S(1)}, bf16[128,1792]{1,0:T(8,128)(2,1)S(1)}, u32[]{:S(2)}, u32[]{:S(2)}) collective-permute-start(bf16[128,1792]{1,0:T(8,128)(2,1)S(1)} %collective-permute-done.2.refs_1_), channel_id=1, source_target_pairs={{0,4},{4,0},{1,5},{5,1},{2,6},{6,2},{3,7},{7,3},{8,12},{12,8},{9,1... | collective-permute-start | bytes 1376264 | tf_op jit(solution)/shard_map/ppermute | solution.py:255
  29.2 13.1 %collective-permute-start.4 = (bf16[128,1792]{1,0:T(8,128)(2,1)}, bf16[128,1792]{1,0:T(8,128)(2,1)S(1)}, u32[]{:S(2)}, u32[]{:S(2)}) collective-permute-start(bf16[128,1792]{1,0:T(8,128)(2,1)} %get-tuple-element.41), channel_id=1, source_target_pairs={{0,1},{1,0},{2,3},{3,2},{4,5},{5,4},{6,7},{7,6},{8,9},{9,8},{10,11... | collective-permute-start | bytes 1376264 | tf_op jit(solution)/shard_map/ppermute | solution.py:255
  29.2 13.0 %collective-permute-start.5 = (bf16[128,1792]{1,0:T(8,128)(2,1)S(1)}, bf16[128,1792]{1,0:T(8,128)(2,1)S(1)}, u32[]{:S(2)}, u32[]{:S(2)}) collective-permute-start(bf16[128,1792]{1,0:T(8,128)(2,1)S(1)} %collective-permute-done.2.refs_1_), channel_id=1, source_target_pairs={{0,1},{1,0},{2,3},{3,2},{4,5},{5,4},{6,7},{7,6},{8,9},{9,8},{10,11... | collective-permute-start | bytes 1376264 | tf_op jit(solution)/shard_map/ppermute | solution.py:255
  29.7 12.5 %collective-permute-start.9 = (bf16[128,1792]{1,0:T(8,128)(2,1)S(1)}, bf16[128,1792]{1,0:T(8,128)(2,1)}, u32[]{:S(2)}, u32[]{:S(2)}) collective-permute-start(bf16[128,1792]{1,0:T(8,128)(2,1)S(1)} %collective-permute-done.8.refs_9_), channel_id=1, source_target_pairs={{0,2},{2,0},{1,3},{3,1},{4,6},{6,4},{5,7},{7,5},{8,10},{10,8},{9,1... | collective-permute-start | bytes 1376264 | tf_op jit(solution)/shard_map/ppermute | solution.py:255
  31.2 11.0 %collective-permute-start.6 = (bf16[128,1792]{1,0:T(8,128)(2,1)S(1)}, bf16[128,1792]{1,0:T(8,128)(2,1)}, u32[]{:S(2)}, u32[]{:S(2)}) collective-permute-start(bf16[128,1792]{1,0:T(8,128)(2,1)S(1)} %collective-permute-done.refs_2_), channel_id=1, source_target_pairs={{0,1},{1,0},{2,3},{3,2},{4,5},{5,4},{6,7},{7,6},{8,9},{9,8},{10,11... | collective-permute-start | bytes 1376264 | tf_op jit(solution)/shard_map/ppermute | solution.py:255
  39.2 3.0 %collective-permute-start.7 = (bf16[128,1792]{1,0:T(8,128)(2,1)S(1)}, bf16[128,1792]{1,0:T(8,128)(2,1)}, u32[]{:S(2)}, u32[]{:S(2)}) collective-permute-start(bf16[128,1792]{1,0:T(8,128)(2,1)S(1)} %collective-permute-done.3.refs_3_), channel_id=1, source_target_pairs={{0,1},{1,0},{2,3},{3,2},{4,5},{5,4},{6,7},{7,6},{8,9},{9,8},{10,11... | collective-permute-start | bytes 1376264 | tf_op jit(solution)/shard_map/ppermute | solution.py:255
  39.3 1.0 %copy-start = (bf16[128,1280]{1,0:T(8,128)(2,1)S(1)}, bf16[128,1280]{1,0:T(8,128)(2,1)}, u32[]{:S(2)}) copy-start(bf16[128,1280]{1,0:T(8,128)(2,1)} %teacher) | copy-start | bytes 983044
  40.3 0.9 %copy-start.2 = (bf16[128,512]{1,0:T(8,128)(2,1)S(1)}, bf16[128,512]{1,0:T(8,128)(2,1)}, u32[]{:S(2)}) copy-start(bf16[128,512]{1,0:T(8,128)(2,1)} %student) | copy-start | bytes 393220
  41.2 0.9 %copy-start.3 = (bf16[128,512]{1,0:T(8,128)(2,1)S(1)}, bf16[128,512]{1,0:T(8,128)(2,1)}, u32[]{:S(2)}) copy-start(bf16[128,512]{1,0:T(8,128)(2,1)} %student.1) | copy-start | bytes 393220
  46.6 1.4 %collective-permute-start.10 = (f32[8,1024]{1,0:T(8,128)S(1)}, f32[8,1024]{1,0:T(8,128)S(1)}, u32[]{:S(2)}, u32[]{:S(2)}) collective-permute-start(f32[8,1024]{1,0:T(8,128)S(1)} %get-tuple-element.49), channel_id=1, source_target_pairs={{0,1},{1,0},{2,3},{3,2},{4,5},{5,4},{6,7},{7,6},{8,9},{9,8},{10,11... | collective-permute-start | bytes 98312 | tf_op jit(solution)/shard_map/ppermute | solution.py:255
  48.0 6.3 %collective-permute-start.11 = (f32[8,1024]{1,0:T(8,128)S(1)}, f32[8,1024]{1,0:T(8,128)S(1)}, u32[]{:S(2)}, u32[]{:S(2)}) collective-permute-start(f32[8,1024]{1,0:T(8,128)S(1)} %add.33.refs_3_), channel_id=1, source_target_pairs={{0,16},{16,0},{1,17},{17,1},{2,18},{18,2},{3,19},{19,3},{4,20},{20... | collective-permute-start | bytes 98312 | tf_op jit(solution)/shard_map/ppermute | solution.py:255
  49.4 6.6 %collective-permute-start.13 = (f32[8,512]{1,0:T(8,128)S(1)}, f32[8,512]{1,0:T(8,128)S(1)}, u32[]{:S(2)}, u32[]{:S(2)}) collective-permute-start(f32[8,512]{1,0:T(8,128)S(1)} %shard_map.71.refs_6_), channel_id=1, source_target_pairs={{0,8},{8,0},{1,9},{9,1},{2,10},{10,2},{3,11},{11,3},{4,12},{12,4},... | collective-permute-start | bytes 49160 | tf_op jit(solution)/shard_map/ppermute | solution.py:255
  54.3 5.6 %collective-permute-start.12 = (f32[16,1024]{1,0:T(8,128)S(1)}, f32[16,1024]{1,0:T(8,128)S(1)}, u32[]{:S(2)}, u32[]{:S(2)}) collective-permute-start(f32[16,1024]{1,0:T(8,128)S(1)} %pad_maximum_fusion.2), channel_id=1, source_target_pairs={{0,4},{4,0},{1,5},{5,1},{2,6},{6,2},{3,7},{7,3},{8,12},{12,8},{9,1... | collective-permute-start | bytes 196616 | tf_op jit(solution)/shard_map/ppermute | solution.py:255
  56.0 3.9 %collective-permute-start.14 = (f32[16,512]{1,0:T(8,128)S(1)}, f32[16,512]{1,0:T(8,128)S(1)}, u32[]{:S(2)}, u32[]{:S(2)}) collective-permute-start(f32[16,512]{1,0:T(8,128)S(1)} %pad_maximum_fusion.3), channel_id=1, source_target_pairs={{0,2},{2,0},{1,3},{3,1},{4,6},{6,4},{5,7},{7,5},{8,10},{10,8},{9,1... | collective-permute-start | bytes 98312 | tf_op jit(solution)/shard_map/ppermute | solution.py:255
  62.2 2.4 %collective-permute-start.16 = (f32[272,512]{1,0:T(8,128)S(1)}, f32[272,512]{1,0:T(8,128)S(1)}, u32[]{:S(2)}, u32[]{:S(2)}) collective-permute-start(f32[272,512]{1,0:T(8,128)S(1)} %get-tuple-element.59), channel_id=1, source_target_pairs={{0,1},{1,0},{2,3},{3,2},{4,5},{5,4},{6,7},{7,6},{8,9},{9,8},{10,11... | collective-permute-start | bytes 1671176 | tf_op jit(solution)/shard_map/ppermute | solution.py:255
  62.3 5.5 %collective-permute-start.15 = (f32[272,512]{1,0:T(8,128)S(1)}, f32[272,512]{1,0:T(8,128)S(1)}, u32[]{:S(2)}, u32[]{:S(2)}) collective-permute-start(f32[272,512]{1,0:T(8,128)S(1)} %get-tuple-element.57), channel_id=1, source_target_pairs={{0,1},{1,0},{2,3},{3,2},{4,5},{5,4},{6,7},{7,6},{8,9},{9,8},{10,11... | collective-permute-start | bytes 1671176 | tf_op jit(solution)/shard_map/ppermute | solution.py:255
  64.8 8.7 %collective-permute-start.17 = (f16[272,512]{1,0:T(8,128)(2,1)S(1)}, f16[272,512]{1,0:T(8,128)(2,1)S(1)}, u32[]{:S(2)}, u32[]{:S(2)}) collective-permute-start(f16[272,512]{1,0:T(8,128)(2,1)S(1)} %add_convert_fusion), channel_id=1, source_target_pairs={{0,4},{4,0},{1,5},{5,1},{2,6},{6,2},{3,7},{7,3},{8,12},{12,8},{9,1... | collective-permute-start | bytes 835592 | tf_op jit(solution)/shard_map/ppermute | solution.py:255
  66.4 8.4 %collective-permute-start.18 = (f16[272,512]{1,0:T(8,128)(2,1)S(1)}, f16[272,512]{1,0:T(8,128)(2,1)S(1)}, u32[]{:S(2)}, u32[]{:S(2)}) collective-permute-start(f16[272,512]{1,0:T(8,128)(2,1)S(1)} %convert_element_type.21), channel_id=1, source_target_pairs={{0,2},{2,0},{1,3},{3,1},{4,6},{6,4},{5,7},{7,5},{8,10},{10,8},{9,1... | collective-permute-start | bytes 835592 | tf_op jit(solution)/shard_map/ppermute | solution.py:255
  75.1 8.8 %collective-permute-start.19 = (f16[144,512]{1,0:T(8,128)(2,1)S(1)}, f16[144,512]{1,0:T(8,128)(2,1)S(1)}, u32[]{:S(2)}, u32[]{:S(2)}) collective-permute-start(f16[144,512]{1,0:T(8,128)(2,1)S(1)} %get-tuple-element.64), channel_id=1, source_target_pairs={{0,16},{16,0},{1,17},{17,1},{2,18},{18,2},{3,19},{19,3},{4,20},{20... | collective-permute-start | bytes 442376 | tf_op jit(solution)/shard_map/ppermute | solution.py:255
  75.1 8.8 %collective-permute-start.20 = (f16[144,512]{1,0:T(8,128)(2,1)S(1)}, f16[144,512]{1,0:T(8,128)(2,1)S(1)}, u32[]{:S(2)}, u32[]{:S(2)}) collective-permute-start(f16[144,512]{1,0:T(8,128)(2,1)S(1)} %get-tuple-element.66), channel_id=1, source_target_pairs={{0,8},{8,0},{1,9},{9,1},{2,10},{10,2},{3,11},{11,3},{4,12},{12,4},... | collective-permute-start | bytes 442376 | tf_op jit(solution)/shard_map/ppermute | solution.py:255

commit v14 on v12

--- a/solution.py
+++ b/solution.py
@@ -313,7 +313,7 @@
     (cols,) = call(
         functools.partial(column_kernel, 2 * b), [((LINES, c), F32)], [tl, sl, peaks, image], (), 0, 2 * r * c
     )
-    row_parts, col_parts = exchange(others, rows + other), exchange(text_bits, cols)
+    row_parts, col_parts = exchange(others, together(rows, cols)[0] + other), exchange(text_bits, cols)
     pairs = b << (len(image_bits) + len(text_bits))
     row, extra = ((1, sw), F32), ((EXTRA, sw), F32)
     near_shape, keep_shape = ((r // 4 + EXTRA, sw), F32), ((c // 2 + EXTRA, sw), F32)

time: 84.9 us -> 84 us (0.989)
  waiting for transfers between devices: 40.7 us -> 38.5 us
  starting transfers between devices: 26.7 us -> 28.1 us
    ppermute x21, waiting for transfers between devices: 40.7 us -> 38.5 us  [swap(): return lax.ppermute(x, bits, perm)]
    ppermute x21, starting transfers between devices: 26.7 us -> 28.1 us  [swap(): return lax.ppermute(x, bits, perm)]
  transfers between devices with their start and end apart: 21 -> 21, of which waited for: 8 -> 7; matrix products, arithmetic and copies ran while one was open for 1% -> 1% of each run, Pallas kernels for 4% -> 4%
where the time goes in v14:
time: 84 us; the launch traced here: 83.8 us
  waiting for transfers between devices  38.5 us (46%)
  starting transfers between devices  28.1 us (33%)
  Pallas kernels  12.8 us (15%)
  local copies, waits for them, and re-layouts  2.78 us (3%)
  between operations  0.86 us (1%)
  other arithmetic  0.84 us (1%)
    ppermute x21, waiting for transfers between devices, swap(): return lax.ppermute(x, bits, perm)  38.5 us
    ppermute x21, starting transfers between devices, swap(): return lax.ppermute(x, bits, perm)  28.1 us
    pallas_call x7, Pallas kernels, call(): pl.pallas_call(kernel, out_shape=shapes, in_specs=[SMEM if x.dtype == jnp...  10.6 us
    unnamed x8, local copies, waits for them, and re-layouts  2.78 us
    pallas_call x1, Pallas kernels, local(): pl.pallas_call(send_kernel, out_shape=[whole, whole], in_specs=[pl.BlockS...  2.18 us
  transfers between devices with their start and end apart: 21, of which 7 were waited for; matrix products, arithmetic and copies ran while one was open for 1% of the time, Pallas kernels for 4%

profile of v14, /device:TPU:0, one launch (start us, length us, event | category | flops | bytes accessed | tf_op | source)
XLA Modules:
  0.0 83.8 jit_solution(8306565722174050950)
XLA Ops:
  0.6 2.2 %shard_map.67 = (bf16[128,1792]{1,0:T(8,128)(2,1)}, bf16[128,1792]{1,0:T(8,128)(2,1)}) custom-call(bf16[128,1280]{1,0:T(8,128)(2,1)} %teacher, bf16[128,512]{1,0:T(8,128)(2,1)} %student, bf16[128,1280]{1,0:T(8,128)(2,1)} %teacher.1, bf16[128,512]{1,0:T(8,128)(2,1)} %student.1), custom_call_target="tpu_custom_call" | custom-call | tf_op jit(solution)/shard_map/pallas_call | solution.py:294
  2.8 4.1 %collective-permute-start.2 = (bf16[128,1792]{1,0:T(8,128)(2,1)}, bf16[128,1792]{1,0:T(8,128)(2,1)S(1)}, u32[]{:S(2)}, u32[]{:S(2)}) collective-permute-start(bf16[128,1792]{1,0:T(8,128)(2,1)} %get-tuple-element.42), channel_id=1, source_target_pairs={{0,16},{16,0},{1,17},{17,1},{2,18},{18,2},{3,19},{19,3},{4,20},{20... | collective-permute-start | bytes 1376264 | tf_op jit(solution)/shard_map/ppermute | solution.py:255
  6.9 1.5 %collective-permute-start = (bf16[128,1792]{1,0:T(8,128)(2,1)}, bf16[128,1792]{1,0:T(8,128)(2,1)S(1)}, u32[]{:S(2)}, u32[]{:S(2)}) collective-permute-start(bf16[128,1792]{1,0:T(8,128)(2,1)} %get-tuple-element.42), channel_id=1, source_target_pairs={{0,4},{4,0},{1,5},{5,1},{2,6},{6,2},{3,7},{7,3},{8,12},{12,8},{9,1... | collective-permute-start | bytes 1376264 | tf_op jit(solution)/shard_map/ppermute | solution.py:255
  8.4 1.6 %collective-permute-start.8 = (bf16[128,1792]{1,0:T(8,128)(2,1)}, bf16[128,1792]{1,0:T(8,128)(2,1)S(1)}, u32[]{:S(2)}, u32[]{:S(2)}) collective-permute-start(bf16[128,1792]{1,0:T(8,128)(2,1)} %get-tuple-element.39), channel_id=1, source_target_pairs={{0,8},{8,0},{1,9},{9,1},{2,10},{10,2},{3,11},{11,3},{4,12},{12,4},... | collective-permute-start | bytes 1376264 | tf_op jit(solution)/shard_map/ppermute | solution.py:255
  10.0 1.5 %collective-permute-start.1 = (bf16[128,1792]{1,0:T(8,128)(2,1)}, bf16[128,1792]{1,0:T(8,128)(2,1)S(1)}, u32[]{:S(2)}, u32[]{:S(2)}) collective-permute-start(bf16[128,1792]{1,0:T(8,128)(2,1)} %get-tuple-element.39), channel_id=1, source_target_pairs={{0,2},{2,0},{1,3},{3,1},{4,6},{6,4},{5,7},{7,5},{8,10},{10,8},{9,1... | collective-permute-start | bytes 1376264 | tf_op jit(solution)/shard_map/ppermute | solution.py:255
  11.5 16.1 %collective-permute-done.2.refs_1_ = bf16[128,1792]{1,0:T(8,128)(2,1)S(1)} collective-permute-done((bf16[128,1792]{1,0:T(8,128)(2,1)}, bf16[128,1792]{1,0:T(8,128)(2,1)S(1)}, u32[]{:S(2)}, u32[]{:S(2)}) %collective-permute-start.2) | collective-permute-done | bytes 458784 | tf_op jit(solution)/shard_map/ppermute | solution.py:255
  27.6 1.6 %collective-permute-start.3 = (bf16[128,1792]{1,0:T(8,128)(2,1)S(1)}, bf16[128,1792]{1,0:T(8,128)(2,1)S(1)}, u32[]{:S(2)}, u32[]{:S(2)}) collective-permute-start(bf16[128,1792]{1,0:T(8,128)(2,1)S(1)} %collective-permute-done.2.refs_1_), channel_id=1, source_target_pairs={{0,4},{4,0},{1,5},{5,1},{2,6},{6,2},{3,7},{7,3},{8,12},{12,8},{9,1... | collective-permute-start | bytes 1376264 | tf_op jit(solution)/shard_map/ppermute | solution.py:255
  29.2 0.5 collective-permute-start.5
  29.7 1.5 %collective-permute-start.9 = (bf16[128,1792]{1,0:T(8,128)(2,1)S(1)}, bf16[128,1792]{1,0:T(8,128)(2,1)}, u32[]{:S(2)}, u32[]{:S(2)}) collective-permute-start(bf16[128,1792]{1,0:T(8,128)(2,1)S(1)} %collective-permute-done.8.refs_9_), channel_id=1, source_target_pairs={{0,2},{2,0},{1,3},{3,1},{4,6},{6,4},{5,7},{7,5},{8,10},{10,8},{9,1... | collective-permute-start | bytes 1376264 | tf_op jit(solution)/shard_map/ppermute | solution.py:255
  31.2 8.1 %collective-permute-done.3.refs_3_ = bf16[128,1792]{1,0:T(8,128)(2,1)S(1)} collective-permute-done((bf16[128,1792]{1,0:T(8,128)(2,1)S(1)}, bf16[128,1792]{1,0:T(8,128)(2,1)S(1)}, u32[]{:S(2)}, u32[]{:S(2)}) %collective-permute-start.3) | collective-permute-done | bytes 458784 | tf_op jit(solution)/shard_map/ppermute | solution.py:255
  39.3 1.0 %copy-done = bf16[128,1280]{1,0:T(8,128)(2,1)S(1)} copy-done((bf16[128,1280]{1,0:T(8,128)(2,1)S(1)}, bf16[128,1280]{1,0:T(8,128)(2,1)}, u32[]{:S(2)}) %copy-start) | copy-done | bytes 327704
  40.3 0.9 %copy-done.2 = bf16[128,512]{1,0:T(8,128)(2,1)S(1)} copy-done((bf16[128,512]{1,0:T(8,128)(2,1)S(1)}, bf16[128,512]{1,0:T(8,128)(2,1)}, u32[]{:S(2)}) %copy-start.2) | copy-done | bytes 131096
  41.3 0.9 %copy-done.3 = bf16[128,512]{1,0:T(8,128)(2,1)S(1)} copy-done((bf16[128,512]{1,0:T(8,128)(2,1)S(1)}, bf16[128,512]{1,0:T(8,128)(2,1)}, u32[]{:S(2)}) %copy-start.3) | copy-done | bytes 131096
  42.2 4.2 %shard_map.70 = (f32[1024,512]{1,0:T(8,128)S(1)}, f32[1024,512]{1,0:T(8,128)S(1)}, f32[8,1024]{1,0:T(8,128)S(1)}, f32[8,1024]{1,0:T(8,128)S(1)}, f32[8,512]{1,0:...) custom-call(s32[3]{0:T(128)S(1)} %pad_add_fusion.core.place, ...), custom_call_target="tpu_custom_call" | custom-call | flops 1879048192 | bytes 11354124 | tf_op jit(solution)/shard_map/pallas_call | solution.py:242
  46.4 0.5 collective-permute-start.10
  47.0 1.4 %shard_map.71.refs_6_ = f32[8,512]{1,0:T(8,128)S(1)} custom-call(f32[1024,512]{1,0:T(8,128)S(1)} %get-tuple-element.47.tl_ref.refs_1_, f32[1024,512]{1,0:T(8,128)S(1)} %get-tuple-element.48.sl_ref.refs_2_, f32[8,512]{1,0:T(8,128)S(1)} %get-tuple-element.50.peaks, bf16[1024,512]{1,0:T(8,128)(2,1)S(1)} %get-tuple-element.45.image), custom_call_target="tpu_custom_call" | custom-call | bytes 5275648 | tf_op jit(solution)/shard_map/pallas_call | solution.py:242
  48.5 4.8 %collective-permute-start.13 = (f32[8,512]{1,0:T(8,128)S(1)}, f32[8,512]{1,0:T(8,128)S(1)}, u32[]{:S(2)}, u32[]{:S(2)}) collective-permute-start(f32[8,512]{1,0:T(8,128)S(1)} %shard_map.71.refs_6_), channel_id=1, source_target_pairs={{0,8},{8,0},{1,9},{9,1},{2,10},{10,2},{3,11},{11,3},{4,12},{12,4},... | collective-permute-start | bytes 49160 | tf_op jit(solution)/shard_map/ppermute | solution.py:255
  53.3 1.5 %collective-permute-start.12 = (f32[16,1024]{1,0:T(8,128)S(1)}, f32[16,1024]{1,0:T(8,128)S(1)}, u32[]{:S(2)}, u32[]{:S(2)}) collective-permute-start(f32[16,1024]{1,0:T(8,128)S(1)} %pad_maximum_fusion.2), channel_id=1, source_target_pairs={{0,4},{4,0},{1,5},{5,1},{2,6},{6,2},{3,7},{7,3},{8,12},{12,8},{9,1... | collective-permute-start | bytes 196616 | tf_op jit(solution)/shard_map/ppermute | solution.py:255
  54.8 0.2 collective-permute-done.13.refs_7_
  55.0 1.5 %collective-permute-start.14 = (f32[16,512]{1,0:T(8,128)S(1)}, f32[16,512]{1,0:T(8,128)S(1)}, u32[]{:S(2)}, u32[]{:S(2)}) collective-permute-start(f32[16,512]{1,0:T(8,128)S(1)} %pad_maximum_fusion.3), channel_id=1, source_target_pairs={{0,2},{2,0},{1,3},{3,1},{4,6},{6,4},{5,7},{7,5},{8,10},{10,8},{9,1... | collective-permute-start | bytes 98312 | tf_op jit(solution)/shard_map/ppermute | solution.py:255
  56.5 2.4 %collective-permute-done.14.refs_8_ = f32[16,512]{1,0:T(8,128)S(1)} collective-permute-done((f32[16,512]{1,0:T(8,128)S(1)}, f32[16,512]{1,0:T(8,128)S(1)}, u32[]{:S(2)}, u32[]{:S(2)}) %collective-permute-start.14) | collective-permute-done | bytes 32800 | tf_op jit(solution)/shard_map/ppermute | solution.py:255
  58.9 2.3 %shard_map.72 = (f32[272,512]{1,0:T(8,128)S(1)}, f32[272,512]{1,0:T(8,128)S(1)}, bf16[1024,512]{1,0:T(8,128)(2,1)S(1)}, bf16[1024,512]{1,0:T(8,128)(2,1)S(1)}, f...) custom-call(s32[3]{0:T(128)S(1)} %pad_add_fusion.core.place, ...), custom_call_target="tpu_custom_call" | custom-call | flops 536870912 | bytes 8212492 | tf_op jit(solution)/shard_map/pallas_call | solution.py:242
  61.3 0.5 collective-permute-start.15
  61.8 1.8 %shard_map.73 = (f32[272,512]{1,0:T(8,128)S(1)}, f32[272,512]{1,0:T(8,128)S(1)}, f32[272,512]{1,0:T(8,128)S(1)}, f32[272,512]{1,0:T(8,128)S(1)}) custom-call(bf16[1024,512]{1,0:T(8,128)(2,1)S(1)} %get-tuple-element.45.image, bf16[512,512]{1,0:T(8,128)(2,1)S(1)} %get-tuple-element.46.refs_0_.text, bf16[1024,512]{1,0:T(8,128)(2,1)S(1)} %get-tuple-element.53.high_ref, ...), custom_call_target="tpu_custom_call" | custom-call | flops 1610612736 | bytes 5980160 | tf_op jit(solution)/shard_map/pallas_call | solution.py:242
  63.8 1.5 %collective-permute-start.17 = (f16[272,512]{1,0:T(8,128)(2,1)S(1)}, f16[272,512]{1,0:T(8,128)(2,1)S(1)}, u32[]{:S(2)}, u32[]{:S(2)}) collective-permute-start(f16[272,512]{1,0:T(8,128)(2,1)S(1)} %add_convert_fusion), channel_id=1, source_target_pairs={{0,4},{4,0},{1,5},{5,1},{2,6},{6,2},{3,7},{7,3},{8,12},{12,8},{9,1... | collective-permute-start | bytes 835592 | tf_op jit(solution)/shard_map/ppermute | solution.py:255
  65.4 1.5 %collective-permute-start.18 = (f16[272,512]{1,0:T(8,128)(2,1)S(1)}, f16[272,512]{1,0:T(8,128)(2,1)S(1)}, u32[]{:S(2)}, u32[]{:S(2)}) collective-permute-start(f16[272,512]{1,0:T(8,128)(2,1)S(1)} %convert_element_type.21), channel_id=1, source_target_pairs={{0,2},{2,0},{1,3},{3,1},{4,6},{6,4},{5,7},{7,5},{8,10},{10,8},{9,1... | collective-permute-start | bytes 835592 | tf_op jit(solution)/shard_map/ppermute | solution.py:255
  66.9 5.6 %collective-permute-done.17 = f16[272,512]{1,0:T(8,128)(2,1)S(1)} collective-permute-done((f16[272,512]{1,0:T(8,128)(2,1)S(1)}, f16[272,512]{1,0:T(8,128)(2,1)S(1)}, u32[]{:S(2)}, u32[]{:S(2)}) %collective-permute-start.17) | collective-permute-done | bytes 278560 | tf_op jit(solution)/shard_map/ppermute | solution.py:255
  72.7 1.0 %collective-permute-done.18 = f16[272,512]{1,0:T(8,128)(2,1)S(1)} collective-permute-done((f16[272,512]{1,0:T(8,128)(2,1)S(1)}, f16[272,512]{1,0:T(8,128)(2,1)S(1)}, u32[]{:S(2)}, u32[]{:S(2)}) %collective-permute-start.18) | collective-permute-done | bytes 278560 | tf_op jit(solution)/shard_map/ppermute | solution.py:255
  74.1 0.4 collective-permute-start.19
  74.5 3.3 %collective-permute-start.20 = (f16[144,512]{1,0:T(8,128)(2,1)S(1)}, f16[144,512]{1,0:T(8,128)(2,1)S(1)}, u32[]{:S(2)}, u32[]{:S(2)}) collective-permute-start(f16[144,512]{1,0:T(8,128)(2,1)S(1)} %get-tuple-element.68), channel_id=1, source_target_pairs={{0,8},{8,0},{1,9},{9,1},{2,10},{10,2},{3,11},{11,3},{4,12},{12,4},... | collective-permute-start | bytes 442376 | tf_op jit(solution)/shard_map/ppermute | solution.py:255
  77.8 5.1 %collective-permute-done.19 = f16[144,512]{1,0:T(8,128)(2,1)S(1)} collective-permute-done((f16[144,512]{1,0:T(8,128)(2,1)S(1)}, f16[144,512]{1,0:T(8,128)(2,1)S(1)}, u32[]{:S(2)}, u32[]{:S(2)}) %collective-permute-start.19) | collective-permute-done | bytes 147488 | tf_op jit(solution)/shard_map/ppermute | solution.py:255
  82.9 0.9 %shard_map.74 = (f32[128,512]{1,0:T(8,128)}, f32[128,512]{1,0:T(8,128)}, f32[1,1]{1,0:T(1,128)}) custom-call(f32[128,512]{1,0:T(8,128)S(1)} %get-tuple-element.80.refs_0_, f32[16,512]{1,0:T(8,128)S(1)} %get-tuple-element.76.refs_1_, f32[144,512]{1,0:T(8,128)S(1)} %convert_element_type.24.refs_2_, f32[1,512]{1,0:T(1,128)S(1)} %get-tuple-element.67.refs_3_, ...), custom_call_target="tpu_custom_call" | custom-call | bytes 1708036 | tf_op jit(solution)/shard_map/pallas_call | solution.py:242
  (44 shorter events, 1.1 us)
Async XLA Ops:
  0.6 40.6 %copy-start.1 = (bf16[128,1280]{1,0:T(8,128)(2,1)S(1)}, bf16[128,1280]{1,0:T(8,128)(2,1)}, u32[]{:S(2)}) copy-start(bf16[128,1280]{1,0:T(8,128)(2,1)} %teacher.1) | copy-start | bytes 983044
  2.8 24.8 %collective-permute-start.2 = (bf16[128,1792]{1,0:T(8,128)(2,1)}, bf16[128,1792]{1,0:T(8,128)(2,1)S(1)}, u32[]{:S(2)}, u32[]{:S(2)}) collective-permute-start(bf16[128,1792]{1,0:T(8,128)(2,1)} %get-tuple-element.42), channel_id=1, source_target_pairs={{0,16},{16,0},{1,17},{17,1},{2,18},{18,2},{3,19},{19,3},{4,20},{20... | collective-permute-start | bytes 1376264 | tf_op jit(solution)/shard_map/ppermute | solution.py:255
  6.9 22.2 %collective-permute-start = (bf16[128,1792]{1,0:T(8,128)(2,1)}, bf16[128,1792]{1,0:T(8,128)(2,1)S(1)}, u32[]{:S(2)}, u32[]{:S(2)}) collective-permute-start(bf16[128,1792]{1,0:T(8,128)(2,1)} %get-tuple-element.42), channel_id=1, source_target_pairs={{0,4},{4,0},{1,5},{5,1},{2,6},{6,2},{3,7},{7,3},{8,12},{12,8},{9,1... | collective-permute-start | bytes 1376264 | tf_op jit(solution)/shard_map/ppermute | solution.py:255
  8.4 21.2 %collective-permute-start.8 = (bf16[128,1792]{1,0:T(8,128)(2,1)}, bf16[128,1792]{1,0:T(8,128)(2,1)S(1)}, u32[]{:S(2)}, u32[]{:S(2)}) collective-permute-start(bf16[128,1792]{1,0:T(8,128)(2,1)} %get-tuple-element.39), channel_id=1, source_target_pairs={{0,8},{8,0},{1,9},{9,1},{2,10},{10,2},{3,11},{11,3},{4,12},{12,4},... | collective-permute-start | bytes 1376264 | tf_op jit(solution)/shard_map/ppermute | solution.py:255
  10.0 21.2 %collective-permute-start.1 = (bf16[128,1792]{1,0:T(8,128)(2,1)}, bf16[128,1792]{1,0:T(8,128)(2,1)S(1)}, u32[]{:S(2)}, u32[]{:S(2)}) collective-permute-start(bf16[128,1792]{1,0:T(8,128)(2,1)} %get-tuple-element.39), channel_id=1, source_target_pairs={{0,2},{2,0},{1,3},{3,1},{4,6},{6,4},{5,7},{7,5},{8,10},{10,8},{9,1... | collective-permute-start | bytes 1376264 | tf_op jit(solution)/shard_map/ppermute | solution.py:255
  27.6 11.6 %collective-permute-start.3 = (bf16[128,1792]{1,0:T(8,128)(2,1)S(1)}, bf16[128,1792]{1,0:T(8,128)(2,1)S(1)}, u32[]{:S(2)}, u32[]{:S(2)}) collective-permute-start(bf16[128,1792]{1,0:T(8,128)(2,1)S(1)} %collective-permute-done.2.refs_1_), channel_id=1, source_target_pairs={{0,4},{4,0},{1,5},{5,1},{2,6},{6,2},{3,7},{7,3},{8,12},{12,8},{9,1... | collective-permute-start | bytes 1376264 | tf_op jit(solution)/shard_map/ppermute | solution.py:255
  29.2 13.1 %collective-permute-start.4 = (bf16[128,1792]{1,0:T(8,128)(2,1)}, bf16[128,1792]{1,0:T(8,128)(2,1)S(1)}, u32[]{:S(2)}, u32[]{:S(2)}) collective-permute-start(bf16[128,1792]{1,0:T(8,128)(2,1)} %get-tuple-element.42), channel_id=1, source_target_pairs={{0,1},{1,0},{2,3},{3,2},{4,5},{5,4},{6,7},{7,6},{8,9},{9,8},{10,11... | collective-permute-start | bytes 1376264 | tf_op jit(solution)/shard_map/ppermute | solution.py:255
  29.2 13.0 %collective-permute-start.5 = (bf16[128,1792]{1,0:T(8,128)(2,1)S(1)}, bf16[128,1792]{1,0:T(8,128)(2,1)S(1)}, u32[]{:S(2)}, u32[]{:S(2)}) collective-permute-start(bf16[128,1792]{1,0:T(8,128)(2,1)S(1)} %collective-permute-done.2.refs_1_), channel_id=1, source_target_pairs={{0,1},{1,0},{2,3},{3,2},{4,5},{5,4},{6,7},{7,6},{8,9},{9,8},{10,11... | collective-permute-start | bytes 1376264 | tf_op jit(solution)/shard_map/ppermute | solution.py:255
  29.7 12.5 %collective-permute-start.9 = (bf16[128,1792]{1,0:T(8,128)(2,1)S(1)}, bf16[128,1792]{1,0:T(8,128)(2,1)}, u32[]{:S(2)}, u32[]{:S(2)}) collective-permute-start(bf16[128,1792]{1,0:T(8,128)(2,1)S(1)} %collective-permute-done.8.refs_9_), channel_id=1, source_target_pairs={{0,2},{2,0},{1,3},{3,1},{4,6},{6,4},{5,7},{7,5},{8,10},{10,8},{9,1... | collective-permute-start | bytes 1376264 | tf_op jit(solution)/shard_map/ppermute | solution.py:255
  31.2 11.0 %collective-permute-start.6 = (bf16[128,1792]{1,0:T(8,128)(2,1)S(1)}, bf16[128,1792]{1,0:T(8,128)(2,1)}, u32[]{:S(2)}, u32[]{:S(2)}) collective-permute-start(bf16[128,1792]{1,0:T(8,128)(2,1)S(1)} %collective-permute-done.refs_2_), channel_id=1, source_target_pairs={{0,1},{1,0},{2,3},{3,2},{4,5},{5,4},{6,7},{7,6},{8,9},{9,8},{10,11... | collective-permute-start | bytes 1376264 | tf_op jit(solution)/shard_map/ppermute | solution.py:255
  39.2 3.0 %collective-permute-start.7 = (bf16[128,1792]{1,0:T(8,128)(2,1)S(1)}, bf16[128,1792]{1,0:T(8,128)(2,1)}, u32[]{:S(2)}, u32[]{:S(2)}) collective-permute-start(bf16[128,1792]{1,0:T(8,128)(2,1)S(1)} %collective-permute-done.3.refs_3_), channel_id=1, source_target_pairs={{0,1},{1,0},{2,3},{3,2},{4,5},{5,4},{6,7},{7,6},{8,9},{9,8},{10,11... | collective-permute-start | bytes 1376264 | tf_op jit(solution)/shard_map/ppermute | solution.py:255
  39.3 1.0 %copy-start = (bf16[128,1280]{1,0:T(8,128)(2,1)S(1)}, bf16[128,1280]{1,0:T(8,128)(2,1)}, u32[]{:S(2)}) copy-start(bf16[128,1280]{1,0:T(8,128)(2,1)} %teacher) | copy-start | bytes 983044
  40.3 0.9 %copy-start.2 = (bf16[128,512]{1,0:T(8,128)(2,1)S(1)}, bf16[128,512]{1,0:T(8,128)(2,1)}, u32[]{:S(2)}) copy-start(bf16[128,512]{1,0:T(8,128)(2,1)} %student) | copy-start | bytes 393220
  41.2 0.9 %copy-start.3 = (bf16[128,512]{1,0:T(8,128)(2,1)S(1)}, bf16[128,512]{1,0:T(8,128)(2,1)}, u32[]{:S(2)}) copy-start(bf16[128,512]{1,0:T(8,128)(2,1)} %student.1) | copy-start | bytes 393220
  46.4 1.9 %collective-permute-start.10 = (f32[8,1024]{1,0:T(8,128)S(1)}, f32[8,1024]{1,0:T(8,128)S(1)}, u32[]{:S(2)}, u32[]{:S(2)}) collective-permute-start(f32[8,1024]{1,0:T(8,128)S(1)} %get-tuple-element.52), channel_id=1, source_target_pairs={{0,1},{1,0},{2,3},{3,2},{4,5},{5,4},{6,7},{7,6},{8,9},{9,8},{10,11... | collective-permute-start | bytes 98312 | tf_op jit(solution)/shard_map/ppermute | solution.py:255
  48.4 4.9 %collective-permute-start.11 = (f32[8,1024]{1,0:T(8,128)S(1)}, f32[8,1024]{1,0:T(8,128)S(1)}, u32[]{:S(2)}, u32[]{:S(2)}) collective-permute-start(f32[8,1024]{1,0:T(8,128)S(1)} %add.33.refs_3_), channel_id=1, source_target_pairs={{0,16},{16,0},{1,17},{17,1},{2,18},{18,2},{3,19},{19,3},{4,20},{20... | collective-permute-start | bytes 98312 | tf_op jit(solution)/shard_map/ppermute | solution.py:255
  48.5 6.5 %collective-permute-start.13 = (f32[8,512]{1,0:T(8,128)S(1)}, f32[8,512]{1,0:T(8,128)S(1)}, u32[]{:S(2)}, u32[]{:S(2)}) collective-permute-start(f32[8,512]{1,0:T(8,128)S(1)} %shard_map.71.refs_6_), channel_id=1, source_target_pairs={{0,8},{8,0},{1,9},{9,1},{2,10},{10,2},{3,11},{11,3},{4,12},{12,4},... | collective-permute-start | bytes 49160 | tf_op jit(solution)/shard_map/ppermute | solution.py:255
  53.3 5.6 %collective-permute-start.12 = (f32[16,1024]{1,0:T(8,128)S(1)}, f32[16,1024]{1,0:T(8,128)S(1)}, u32[]{:S(2)}, u32[]{:S(2)}) collective-permute-start(f32[16,1024]{1,0:T(8,128)S(1)} %pad_maximum_fusion.2), channel_id=1, source_target_pairs={{0,4},{4,0},{1,5},{5,1},{2,6},{6,2},{3,7},{7,3},{8,12},{12,8},{9,1... | collective-permute-start | bytes 196616 | tf_op jit(solution)/shard_map/ppermute | solution.py:255
  55.0 3.9 %collective-permute-start.14 = (f32[16,512]{1,0:T(8,128)S(1)}, f32[16,512]{1,0:T(8,128)S(1)}, u32[]{:S(2)}, u32[]{:S(2)}) collective-permute-start(f32[16,512]{1,0:T(8,128)S(1)} %pad_maximum_fusion.3), channel_id=1, source_target_pairs={{0,2},{2,0},{1,3},{3,1},{4,6},{6,4},{5,7},{7,5},{8,10},{10,8},{9,1... | collective-permute-start | bytes 98312 | tf_op jit(solution)/shard_map/ppermute | solution.py:255
  61.2 2.4 %collective-permute-start.16 = (f32[272,512]{1,0:T(8,128)S(1)}, f32[272,512]{1,0:T(8,128)S(1)}, u32[]{:S(2)}, u32[]{:S(2)}) collective-permute-start(f32[272,512]{1,0:T(8,128)S(1)} %get-tuple-element.61), channel_id=1, source_target_pairs={{0,1},{1,0},{2,3},{3,2},{4,5},{5,4},{6,7},{7,6},{8,9},{9,8},{10,11... | collective-permute-start | bytes 1671176 | tf_op jit(solution)/shard_map/ppermute | solution.py:255
  61.3 5.5 %collective-permute-start.15 = (f32[272,512]{1,0:T(8,128)S(1)}, f32[272,512]{1,0:T(8,128)S(1)}, u32[]{:S(2)}, u32[]{:S(2)}) collective-permute-start(f32[272,512]{1,0:T(8,128)S(1)} %get-tuple-element.59), channel_id=1, source_target_pairs={{0,1},{1,0},{2,3},{3,2},{4,5},{5,4},{6,7},{7,6},{8,9},{9,8},{10,11... | collective-permute-start | bytes 1671176 | tf_op jit(solution)/shard_map/ppermute | solution.py:255
  63.8 8.7 %collective-permute-start.17 = (f16[272,512]{1,0:T(8,128)(2,1)S(1)}, f16[272,512]{1,0:T(8,128)(2,1)S(1)}, u32[]{:S(2)}, u32[]{:S(2)}) collective-permute-start(f16[272,512]{1,0:T(8,128)(2,1)S(1)} %add_convert_fusion), channel_id=1, source_target_pairs={{0,4},{4,0},{1,5},{5,1},{2,6},{6,2},{3,7},{7,3},{8,12},{12,8},{9,1... | collective-permute-start | bytes 835592 | tf_op jit(solution)/shard_map/ppermute | solution.py:255
  65.4 8.4 %collective-permute-start.18 = (f16[272,512]{1,0:T(8,128)(2,1)S(1)}, f16[272,512]{1,0:T(8,128)(2,1)S(1)}, u32[]{:S(2)}, u32[]{:S(2)}) collective-permute-start(f16[272,512]{1,0:T(8,128)(2,1)S(1)} %convert_element_type.21), channel_id=1, source_target_pairs={{0,2},{2,0},{1,3},{3,1},{4,6},{6,4},{5,7},{7,5},{8,10},{10,8},{9,1... | collective-permute-start | bytes 835592 | tf_op jit(solution)/shard_map/ppermute | solution.py:255
  74.1 8.8 %collective-permute-start.19 = (f16[144,512]{1,0:T(8,128)(2,1)S(1)}, f16[144,512]{1,0:T(8,128)(2,1)S(1)}, u32[]{:S(2)}, u32[]{:S(2)}) collective-permute-start(f16[144,512]{1,0:T(8,128)(2,1)S(1)} %get-tuple-element.66), channel_id=1, source_target_pairs={{0,16},{16,0},{1,17},{17,1},{2,18},{18,2},{3,19},{19,3},{4,20},{20... | collective-permute-start | bytes 442376 | tf_op jit(solution)/shard_map/ppermute | solution.py:255
  74.5 8.4 %collective-permute-start.20 = (f16[144,512]{1,0:T(8,128)(2,1)S(1)}, f16[144,512]{1,0:T(8,128)(2,1)S(1)}, u32[]{:S(2)}, u32[]{:S(2)}) collective-permute-start(f16[144,512]{1,0:T(8,128)(2,1)S(1)} %get-tuple-element.68), channel_id=1, source_target_pairs={{0,8},{8,0},{1,9},{9,1},{2,10},{10,2},{3,11},{11,3},{4,12},{12,4},... | collective-permute-start | bytes 442376 | tf_op jit(solution)/shard_map/ppermute | solution.py:255
